TPU v7x, 512 devices: a whole 4x8x8 slice. The times are simulated.
512 devices in a mesh: section: 32 (over x, y_lo, core), dp: 16 (over z, y_hi).
Axes of the slice: x: 4, y: 8 (y_hi: 2, y_lo: 4; y = y_hi * 4 + y_lo), z: 8, core: 2. Of those that a mesh axis runs over, the one named last changes fastest.
Arguments:
- saved_inputs: bfloat16 [4, 32, 2048, 2560], P(None, 'section', 'dp'), may hold values from -24 to 24
- grad_in: bfloat16 [32, 2048, 2560], P('section', 'dp'), may hold values from -6 to 6
- adapter_down: bfloat16 [2, 32, 128, 2560], P(None, 'section', None, 'dp'), may hold values from -0.125 to 0.125
- adapter_up: bfloat16 [2, 32, 128, 2560], P(None, 'section', None, 'dp'), may hold values from -0.5 to 0.5
Outputs:
- grad_out: bfloat16 [32, 2048, 2560], P('section', 'dp')
- down_grad: float32 [2, 32, 128, 2560], P(None, 'section', None, 'dp')
- up_grad: float32 [2, 32, 128, 2560], P(None, 'section', None, 'dp')
All inputs are finite; a program needn't handle non-finite values.
Results may differ from a plain program's by a relative error of at most 0.024.
Values may be sent and summed in bfloat16 or wider, within the bound.
No kernel may reach another device: no remote copies, remote signals or barrier semaphores. Data moves between devices by JAX's collectives and lax.ppermute only.
A program may use at most 64 MiB of HBM per device.

v0:
```python
import jax
import jax.numpy as jnp
from jax import lax
from jax.sharding import PartitionSpec as P

EPS = 1e-06


def passed_along(value, axis, steps):
    count = lax.axis_size(axis)
    pairs = [(source, (source + steps) % count) for source in range(count)]
    return lax.ppermute(value, axis, pairs)


def layer_back(inputs_now, incoming, down_matrix, up_matrix):
    inputs_f32 = inputs_now.astype(jnp.float32)
    inverse_rms = lax.rsqrt(jnp.mean(inputs_f32 * inputs_f32, axis=-1, keepdims=True) + EPS)
    normed = inputs_f32 * inverse_rms
    normed_half = normed.astype(jnp.bfloat16)
    latent = lax.dot_general(
        normed_half, down_matrix, (((1,), (1,)), ((), ())), preferred_element_type=jnp.float32
    )
    gate_sig = jax.nn.sigmoid(latent)
    activated = (latent * gate_sig).astype(jnp.bfloat16)
    grad_act = lax.dot_general(
        incoming, up_matrix, (((1,), (1,)), ((), ())), preferred_element_type=jnp.float32
    )
    grad_latent = (grad_act * gate_sig * (1.0 + latent * (1.0 - gate_sig))).astype(jnp.bfloat16)
    grad_normed = jnp.dot(grad_latent, down_matrix, preferred_element_type=jnp.float32)
    inner = jnp.mean(grad_normed * normed, axis=-1, keepdims=True)
    outgoing = (incoming.astype(jnp.float32) + inverse_rms * (grad_normed - normed * inner)).astype(
        jnp.bfloat16
    )
    return (outgoing, grad_latent, activated, normed_half)


def on_device(saved_inputs, grad_in, adapter_down, adapter_up):
    section_count = lax.axis_size("section")
    position = lax.axis_index("section")
    ticks = saved_inputs.shape[0]
    levels_held = adapter_down.shape[0]
    full_down, full_up = (
        lax.all_gather(adapter_down, "dp", axis=3, tiled=True),
        lax.all_gather(adapter_up, "dp", axis=3, tiled=True),
    )
    current = grad_in[0]
    latents = []
    actives = []
    normals = []
    incomings = []
    levels = []
    for tick in range(ticks):
        level = levels_held - 1 - (position + tick) // section_count
        down_matrix = lax.dynamic_index_in_dim(full_down, level, 0, keepdims=False)[0]
        up_matrix = lax.dynamic_index_in_dim(full_up, level, 0, keepdims=False)[0]
        outgoing, grad_latent, activated, normed_half = layer_back(
            saved_inputs[tick, 0], current, down_matrix, up_matrix
        )
        latents.append(grad_latent)
        actives.append(activated)
        normals.append(normed_half)
        incomings.append(current)
        levels.append(level)
        current = passed_along(outgoing, "section", -1)
    latent_stack = jnp.stack(latents, axis=0)
    active_stack = jnp.stack(actives, axis=0)
    normal_stack = jnp.stack(normals, axis=0)
    incoming_stack = jnp.stack(incomings, axis=0)
    level_stack = jnp.stack(levels, axis=0)
    zero_half = jnp.zeros((), jnp.bfloat16)
    downs_made = []
    ups_made = []
    for level_now in range(levels_held):
        select = (level_stack == level_now)[:, None, None]
        latent_kept = jnp.where(select, latent_stack, zero_half)
        active_kept = jnp.where(select, active_stack, zero_half)
        downs_made.append(
            lax.dot_general(
                latent_kept,
                normal_stack,
                (((0, 1), (0, 1)), ((), ())),
                preferred_element_type=jnp.float32,
            )
        )
        ups_made.append(
            lax.dot_general(
                active_kept,
                incoming_stack,
                (((0, 1), (0, 1)), ((), ())),
                preferred_element_type=jnp.float32,
            )
        )
    totals_down = jnp.stack(downs_made, axis=0)
    totals_up = jnp.stack(ups_made, axis=0)
    summed_down, summed_up = (
        lax.psum_scatter(
            totals_down.astype(jnp.bfloat16), "dp", scatter_dimension=2, tiled=True
        ).astype(jnp.float32),
        lax.psum_scatter(
            totals_up.astype(jnp.bfloat16), "dp", scatter_dimension=2, tiled=True
        ).astype(jnp.float32),
    )
    return (current[None], summed_down[:, None], summed_up[:, None])


def solution(mesh):
    in_specs = (
        P(None, "section", "dp", None),
        P("section", "dp", None),
        P(None, "section", None, "dp"),
        P(None, "section", None, "dp"),
    )
    out_specs = (
        P("section", "dp", None),
        P(None, "section", None, "dp"),
        P(None, "section", None, "dp"),
    )
    return jax.shard_map(
        on_device, mesh=mesh, in_specs=in_specs, out_specs=out_specs, check_vma=False
    )
```

profile of v0, /device:TPU:12, one launch (start us, length us, event | category | flops | bytes accessed | tf_op | source)
XLA Modules:
  0.0 548.3 jit_solution(7851286428277804743)
XLA Ops:
  7.2 0.7 all-gather.5.cloned.1.call-update
  7.9 0.0 all-gather.3.cloned.1.call-start
  8.0 0.7 all-gather.3.cloned.1.call-update
  8.7 0.0 all-reduce.5.cloned.1.call-start
  8.7 0.1 broadcast_compare_fusion.1
  8.8 1.3 fusion.47
  10.2 101.1 %all-gather.5.cloned.1.call-done = bf16[2,1,128,2560]{2,3,1,0:T(8,128)(2,1)} async-done(((bf16[2,1,128,160]{2,3,1,0:T(8,128)(2,1)}), bf16[2,1,128,2560]{2,3,1,0:T(8,128)(2,1)}) %all-gather.5.cloned.1.call-update) | async-done | bytes 1310736 | tf_op jit(solution)/shard_map/all_gather | solution.py:43
  111.2 1.7 fusion.79
  113.0 90.8 %all-gather.3.cloned.1.call-done = bf16[2,1,128,2560]{2,3,1,0:T(8,128)(2,1)} async-done(((bf16[2,1,128,160]{2,3,1,0:T(8,128)(2,1)}), bf16[2,1,128,2560]{2,3,1,0:T(8,128)(2,1)}) %all-gather.3.cloned.1.call-update) | async-done | bytes 1310736 | tf_op jit(solution)/shard_map/all_gather | solution.py:44
  203.8 1.5 fusion.68
  205.3 1.9 fusion.44
  207.2 0.5 fusion.28
  207.7 2.1 collective-permute-start
  209.8 0.4 fusion.70
  210.3 0.4 fusion.76
  210.7 7.1 %collective-permute-done = bf16[128,2560]{1,0:T(8,128)(2,1)S(1)} collective-permute-done((bf16[128,2560]{1,0:T(8,128)(2,1)S(1)}, bf16[128,2560]{1,0:T(8,128)(2,1)S(1)}, u32[]{:S(2)}, u32[]{:S(2)}) %collective-permute-start) | collective-permute-done | bytes 655392 | tf_op jit(solution)/shard_map/ppermute | solution.py:12
  217.9 0.4 fusion.65
  218.3 0.4 fusion.29
  218.7 0.5 fusion.33
  219.2 3.8 collective-permute-start.1
  223.0 0.4 fusion.73
  223.5 7.6 %collective-permute-done.1 = bf16[128,2560]{1,0:T(8,128)(2,1)S(1)} collective-permute-done((bf16[128,2560]{1,0:T(8,128)(2,1)S(1)}, bf16[128,2560]{1,0:T(8,128)(2,1)S(1)}, u32[]{:S(2)}, u32[]{:S(2)}) %collective-permute-start.1) | collective-permute-done | bytes 655392 | tf_op jit(solution)/shard_map/ppermute | solution.py:12
  231.1 0.4 fusion.66
  231.5 0.4 fusion.34
  232.0 0.5 fusion.38
  232.5 3.9 collective-permute-start.2
  236.4 0.5 fusion.50
  236.9 7.6 %collective-permute-done.2 = bf16[128,2560]{1,0:T(8,128)(2,1)S(1)} collective-permute-done((bf16[128,2560]{1,0:T(8,128)(2,1)S(1)}, bf16[128,2560]{1,0:T(8,128)(2,1)S(1)}, u32[]{:S(2)}, u32[]{:S(2)}) %collective-permute-start.2) | collective-permute-done | bytes 655392 | tf_op jit(solution)/shard_map/ppermute | solution.py:12
  244.5 0.6 fusion.4
  245.1 0.6 fusion.5
  245.7 0.4 fusion.67
  246.2 1.5 fusion.6
  247.6 1.5 fusion.7
  249.1 1.2 pad_maximum_fusion.3
  250.3 4.3 copy.40
  254.6 2.5 pad_maximum_fusion.2
  257.1 4.3 copy.35
  261.3 1.5 fusion.39
  262.9 1.3 fusion.43
  264.2 3.8 collective-permute-start.3
  268.0 1.3 dynamic-slice
  269.9 6.5 %collective-permute-done.3 = bf16[128,2560]{1,0:T(8,128)(2,1)S(1)} collective-permute-done((bf16[128,2560]{1,0:T(8,128)(2,1)}, bf16[128,2560]{1,0:T(8,128)(2,1)S(1)}, u32[]{:S(2)}, u32[]{:S(2)}) %collective-permute-start.3) | collective-permute-done | bytes 655392 | tf_op jit(solution)/shard_map/ppermute | solution.py:12
  276.4 261.3 %all-reduce.5.cloned.1.call-done = (bf16[2,128,2560]{1,0,2:T(2,128)(2,1)}, bf16[2,128,2560]{1,0,2:T(2,128)(2,1)}) async-done(((bf16[2,128,2560]{1,0,2:T(2,128)(2,1)}, bf16[2,128,2560]{1,0,2:T(2,128)(2,1)}), (bf16[2,128,2560]{1,0,2:T(2,128)(2,1)}, bf16[2,128,2560]{1,0,2:T(2,128)(2,1)})) %all-reduce.5.cloned.1.call-update) | async-done | bytes 2621456
  537.7 0.9 bitcast_convert_fusion.1
  538.6 0.9 bitcast_convert_fusion
  539.6 0.7 copy.42
  540.3 0.7 copy.41
  541.0 0.8 copy.53
  (24 shorter events, 0.2 us)
Async XLA Ops:
  7.2 196.6 %copy-start.3 = (bf16[1,128,2560]{2,1,0:T(8,128)(2,1)S(1)}, bf16[1,128,2560]{2,1,0:T(8,128)(2,1)}, u32[]{:S(2)}) copy-start(bf16[1,128,2560]{2,1,0:T(8,128)(2,1)} %param.5) | copy-start | bytes 1966084
  7.2 104.0 %all-gather.5.cloned.1.call-start = ((), (), s32[]{:S(2)}) async-start(), calls=%async_computation.1 | async-start | bytes 1392640 | tf_op jit(solution)/shard_map/all_gather | solution.py:43
  7.9 195.9 %all-gather.3.cloned.1.call-start = ((), (), s32[]{:S(2)}) async-start(), calls=%async_computation | async-start | bytes 1392640 | tf_op jit(solution)/shard_map/all_gather | solution.py:44
  8.7 529.0 %all-reduce.5.cloned.1.call-start = ((), (), s32[]{:S(2)}) async-start(), calls=%async_computation.2 | async-start | bytes 5242880
  10.1 195.1 %copy-start = (bf16[4,1,128,2560]{3,2,1,0:T(8,128)(2,1)S(1)}, bf16[4,1,128,2560]{3,2,1,0:T(8,128)(2,1)}, u32[]{:S(2)}) copy-start(bf16[4,1,128,2560]{3,2,1,0:T(8,128)(2,1)} %param.4) | copy-start | bytes 7864324
  207.2 2.6 copy-start.2
  207.7 10.2 %copy-start.1 = (bf16[2,1,128,2560]{2,3,1,0:T(8,128)(2,1)S(1)}, bf16[2,1,128,2560]{2,3,1,0:T(8,128)(2,1)}, u32[]{:S(2)}) copy-start(bf16[2,1,128,2560]{2,3,1,0:T(8,128)(2,1)} %all-gather.3.cloned.1.call-done) | copy-start | bytes 3932164
  207.7 10.1 %collective-permute-start = (bf16[128,2560]{1,0:T(8,128)(2,1)S(1)}, bf16[128,2560]{1,0:T(8,128)(2,1)S(1)}, u32[]{:S(2)}, u32[]{:S(2)}) collective-permute-start(bf16[128,2560]{1,0:T(8,128)(2,1)S(1)} %fusion.28), channel_id=1, source_target_pairs={{0,496},{16,0},{32,16},{48,32},{64,48},{80,64},{96,80},{112,96},{1... | collective-permute-start | bytes 1966088 | tf_op jit(solution)/shard_map/ppermute | solution.py:12
  219.2 11.9 %collective-permute-start.1 = (bf16[128,2560]{1,0:T(8,128)(2,1)S(1)}, bf16[128,2560]{1,0:T(8,128)(2,1)S(1)}, u32[]{:S(2)}, u32[]{:S(2)}) collective-permute-start(bf16[128,2560]{1,0:T(8,128)(2,1)S(1)} %fusion.33), channel_id=1, source_target_pairs={{0,496},{16,0},{32,16},{48,32},{64,48},{80,64},{96,80},{112,96},{1... | collective-permute-start | bytes 1966088 | tf_op jit(solution)/shard_map/ppermute | solution.py:12
  232.5 12.1 %copy-start.4 = (bf16[1,128,2560]{2,1,0:T(8,128)(2,1)S(1)}, bf16[1,128,2560]{2,1,0:T(8,128)(2,1)}, u32[]{:S(2)}) copy-start(bf16[1,128,2560]{2,1,0:T(8,128)(2,1)} %param.5) | copy-start | bytes 1966084
  232.5 12.0 %collective-permute-start.2 = (bf16[128,2560]{1,0:T(8,128)(2,1)S(1)}, bf16[128,2560]{1,0:T(8,128)(2,1)S(1)}, u32[]{:S(2)}, u32[]{:S(2)}) collective-permute-start(bf16[128,2560]{1,0:T(8,128)(2,1)S(1)} %fusion.38), channel_id=1, source_target_pairs={{0,496},{16,0},{32,16},{48,32},{64,48},{80,64},{96,80},{112,96},{1... | collective-permute-start | bytes 1966088 | tf_op jit(solution)/shard_map/ppermute | solution.py:12
  264.2 12.2 %collective-permute-start.3 = (bf16[128,2560]{1,0:T(8,128)(2,1)}, bf16[128,2560]{1,0:T(8,128)(2,1)S(1)}, u32[]{:S(2)}, u32[]{:S(2)}) collective-permute-start(bf16[128,2560]{1,0:T(8,128)(2,1)} %fusion.43), channel_id=1, source_target_pairs={{0,496},{16,0},{32,16},{48,32},{64,48},{80,64},{96,80},{112,96},{1... | collective-permute-start | bytes 1966088 | tf_op jit(solution)/shard_map/ppermute | solution.py:12
Sparse Core Ops, SparseCore 0:
  11.2 99.9 all-gather.4
  114.4 89.3 all-gather.2
  261.5 276.1 all-reduce.4
where the time goes:
time: 549 us; the launch traced here: 548 us
  waiting for transfers between devices  483 us (88%)
  between operations  14.7 us (3%)
  matrix products  14.2 us (3%)
  starting transfers between devices  13.7 us (2%)
  local copies, waits for them, and re-layouts  12 us (2%)
  other arithmetic  10.4 us (2%)
    unnamed x4, waiting for transfers between devices  263 us
    all_gather x1, waiting for transfers between devices, on_device(): lax.all_gather(adapter_down, 'dp', axis=3, tiled=True)  101 us
    all_gather x1, waiting for transfers between devices, on_device(): lax.all_gather(adapter_up, 'dp', axis=3, tiled=True)  90.8 us
    ppermute x4, waiting for transfers between devices, passed_along(): return lax.ppermute(value, axis, pairs)  28.7 us
    ppermute x4, starting transfers between devices, passed_along(): return lax.ppermute(value, axis, pairs)  13.6 us
  transfers between devices with their start and end apart: 7, of which 7 were waited for; matrix products, arithmetic and copies ran while one was open for 2% of the time, Pallas kernels for 0%

commit v1 on v0

v1 whole, which is shorter than its diff:
```python
import jax
import jax.numpy as jnp
from jax import lax
from jax.sharding import PartitionSpec as P

EPS = 1e-06
F32 = jnp.float32
BF16 = jnp.bfloat16


def dp_pairs(n_z, step, flip):
    return [
        (2 * z + h, 2 * ((z + step) % n_z) + (h ^ flip)) for z in range(n_z) for h in range(2)
    ]


def shifted(value, n_z, step):
    return lax.ppermute(value, "dp", dp_pairs(n_z, step, 0))


def swapped(value, n_z):
    return lax.ppermute(value, "dp", dp_pairs(n_z, 0, 1))


def ring_gather(shard, n_z):
    index = lax.axis_index("dp")
    z, h = index // 2, index % 2
    other = swapped(shard, n_z)
    pair = jnp.stack([jnp.where(h == 0, shard, other), jnp.where(h == 0, other, shard)])
    full = jnp.zeros((n_z,) + pair.shape, pair.dtype)
    full = lax.dynamic_update_index_in_dim(full, pair, z, 0)
    right, left = pair, pair
    half = n_z // 2
    for step in range(1, half):
        right, left = shifted(right, n_z, 1), shifted(left, n_z, -1)
        full = lax.dynamic_update_index_in_dim(full, right, (z - step) % n_z, 0)
        full = lax.dynamic_update_index_in_dim(full, left, (z + step) % n_z, 0)
    right, left = shifted(right[:1], n_z, 1), shifted(left[1:], n_z, -1)
    last = jnp.concatenate([right, left], axis=0)
    return lax.dynamic_update_index_in_dim(full, last, (z + half) % n_z, 0)


def ring_reduce(parts, n_z):
    index = lax.axis_index("dp")
    z, h = index // 2, index % 2
    half = n_z // 2

    def at(offset):
        return lax.dynamic_index_in_dim(parts, (z + offset) % n_z, 0, keepdims=False)

    far = at(half)
    right, left = shifted(far[:1], n_z, 1), shifted(far[1:], n_z, -1)
    for step in range(half - 1, 0, -1):
        here, there = at(step), at(-step)
        if step == half - 1:
            here = jnp.concatenate([here[:1] + right, here[1:]], axis=0)
            there = jnp.concatenate([there[:1], there[1:] + left], axis=0)
        else:
            here, there = here + right, there + left
        right, left = shifted(here, n_z, 1), shifted(there, n_z, -1)
    total = at(0).astype(F32) + right.astype(F32) + left.astype(F32)
    mine = lax.dynamic_index_in_dim(total, h, 0, keepdims=False)
    other = lax.dynamic_index_in_dim(total, 1 - h, 0, keepdims=False)
    return mine + swapped(other.astype(BF16), n_z).astype(F32)


def on_device(saved_inputs, grad_in, adapter_down, adapter_up):
    n_sec = lax.axis_size("section")
    n_dp = lax.axis_size("dp")
    n_z = n_dp // 2
    position = lax.axis_index("section")
    ticks = saved_inputs.shape[0]
    rank, share = adapter_down.shape[2], adapter_down.shape[3]
    width = saved_inputs.shape[3]
    even = position % 2 == 0
    two_layers = position + ticks - 1 >= n_sec
    levels = [1 - (position + tick) // n_sec for tick in range(ticks)]

    x = saved_inputs[:, 0].astype(F32)
    inverse = lax.rsqrt(jnp.mean(x * x, axis=-1, keepdims=True) + EPS)
    normed = (x * inverse).astype(BF16)

    shard = jnp.concatenate(
        [jnp.swapaxes(adapter_down[:, 0], 1, 2), jnp.swapaxes(adapter_up[:, 0], 1, 2)], axis=2
    )

    def gather_two(shards):
        full = ring_gather(shards, n_z)
        full = jnp.moveaxis(full, 2, 0)
        return full.reshape(2, width, 2 * rank)

    def gather_one(shards):
        copies = jnp.broadcast_to(shards[1][None], (n_dp,) + shards.shape[1:])
        full = lax.all_to_all(copies, "dp", 0, 0, tiled=True).reshape(1, width, 2 * rank)
        return jnp.concatenate([full, full], axis=0)

    maps = lax.cond(two_layers, gather_two, gather_one, shard)

    latents, actives, slopes, downs, ups = [], [], [], [], []
    for tick in range(ticks):
        both = lax.dynamic_index_in_dim(maps, levels[tick], 0, keepdims=False)
        down, up = both[:, :rank], both[:, rank:]
        latent = jnp.dot(normed[tick], down, preferred_element_type=F32)
        gate = jax.nn.sigmoid(latent)
        downs.append(down)
        ups.append(up)
        latents.append(latent)
        actives.append((latent * gate).astype(BF16))
        slopes.append(gate * (1.0 + latent * (1.0 - gate)))

    def layer(tick, incoming):
        grad_act = jnp.dot(incoming, ups[tick], preferred_element_type=F32)
        grad_latent = (grad_act * slopes[tick]).astype(BF16)
        inner = jnp.sum(grad_latent.astype(F32) * latents[tick], axis=-1, keepdims=True) / width
        grad_normed = lax.dot_general(
            grad_latent, downs[tick], (((1,), (1,)), ((), ())), preferred_element_type=F32
        )
        inv = inverse[tick]
        sent = incoming.astype(F32) + inv * (grad_normed - x[tick] * (inv * inner))
        return sent.astype(BF16), grad_latent

    inside = [(s, s - 1) for s in range(1, n_sec, 2)]
    across = [(s, (s - 1) % n_sec) for s in range(0, n_sec, 2)]

    incoming = [grad_in[0]]
    sent, grad_latent = layer(0, grad_in[0])
    grad_latents = [grad_latent]
    over = lax.ppermute(sent, "section", across)
    core = lax.ppermute(sent, "section", inside)
    for tick in range(1, ticks):
        incoming.append(jnp.where(even, core, over))
        sent_even, latent_even = layer(tick, core)
        next_over = lax.ppermute(sent_even, "section", across)
        sent_odd, latent_odd = layer(tick, over)
        next_core = lax.ppermute(sent_odd, "section", inside)
        grad_latents.append(jnp.where(even, latent_even, latent_odd))
        over, core = next_over, next_core
    grad_out = jnp.where(even, core, over)

    normed_all = normed.reshape(-1, width)
    incoming_all = jnp.concatenate(incoming, axis=0)

    def partials(lats, acts):
        contract = (((0,), (0,)), ((), ()))
        down = lax.dot_general(normed_all, lats, contract, preferred_element_type=F32)
        up = lax.dot_general(incoming_all, acts, contract, preferred_element_type=F32)
        return jnp.concatenate([down.astype(BF16), up.astype(BF16)], axis=1)

    def reduce_one(stacks):
        parts = partials(*[s.reshape(-1, rank) for s in stacks])
        moved = lax.all_to_all(parts.reshape(n_dp, share, 2 * rank), "dp", 0, 0, tiled=True)
        total = jnp.sum(moved.astype(F32), axis=0)
        return jnp.stack([jnp.zeros_like(total), total])

    def reduce_two(stacks):
        level_stack = jnp.stack(levels)
        parts = []
        for level in range(2):
            keep = (level_stack == level)[:, None, None]
            parts.append(
                partials(*[jnp.where(keep, s, jnp.zeros((), BF16)).reshape(-1, rank) for s in stacks])
            )
        both = jnp.stack([p.reshape(n_z, 2, share, 2 * rank) for p in parts], axis=2)
        return ring_reduce(both, n_z)

    stacks = (jnp.stack(grad_latents), jnp.stack(actives))
    total = lax.cond(two_layers, reduce_two, reduce_one, stacks)
    total = jnp.swapaxes(total, 1, 2)
    return grad_out[None], total[:, None, :rank], total[:, None, rank:]


def solution(mesh):
    in_specs = (
        P(None, "section", "dp", None),
        P("section", "dp", None),
        P(None, "section", None, "dp"),
        P(None, "section", None, "dp"),
    )
    out_specs = (
        P("section", "dp", None),
        P(None, "section", None, "dp"),
        P(None, "section", None, "dp"),
    )
    return jax.shard_map(
        on_device, mesh=mesh, in_specs=in_specs, out_specs=out_specs, check_vma=False
    )
```

time: 549 us -> 221 us (0.40)
  the two profiles are of different devices: /device:TPU:12 before, /device:TPU:63 now
where the time goes in v1:
time: 221 us; the launch traced here: 220 us
  starting transfers between devices  86 us (39%)
  waiting for transfers between devices  65.3 us (30%)
  matrix products  22.5 us (10%)
  other arithmetic  22.4 us (10%)
  local copies, waits for them, and re-layouts  22 us (10%)
    ppermute x16, starting transfers between devices, shifted(): return lax.ppermute(value, 'dp', dp_pairs(n_z, step, 0))  56.1 us
    ppermute x3, waiting for transfers between devices, on_device(): next_over = lax.ppermute(sent_even, 'section', across)  25.6 us
    ppermute x16, waiting for transfers between devices, shifted(): return lax.ppermute(value, 'dp', dp_pairs(n_z, step, 0))  25 us
    ppermute x2, waiting for transfers between devices, swapped(): return lax.ppermute(value, 'dp', dp_pairs(n_z, 0, 1))  14.7 us
    ppermute x1, starting transfers between devices, on_device(): core = lax.ppermute(sent, 'section', inside)  11.5 us
    dot_general x7, matrix products, layer(): lax.dot_general(grad_latent, downs[tick], (((1,), (1,)), ((), ())), prefe...  9 us
    ppermute x2, starting transfers between devices, swapped(): return lax.ppermute(value, 'dp', dp_pairs(n_z, 0, 1))  7.76 us
    ppermute x3, starting transfers between devices, on_device(): next_core = lax.ppermute(sent_odd, 'section', inside)  5.31 us
  transfers between devices with their start and end apart: 26, of which 14 were waited for; matrix products, arithmetic and copies ran while one was open for 19% of the time, Pallas kernels for 0%

profile of v1, /device:TPU:63, one launch (start us, length us, event | category | flops | bytes accessed | tf_op | source)
XLA Modules:
  0.0 219.8 jit_solution(7430008616088570220)
XLA Ops:
  0.7 2.5 %fusion.18 = f32[4,128]{1,0:T(4,128)S(1)} fusion(bf16[4,1,128,2560]{3,2,1,0:T(8,128)(2,1)} %param.8), kind=kLoop, calls=%fused_computation.84 | loop fusion | flops 3931648 | bytes 2623488 | tf_op jit(solution)/shard_map/reduce_sum | solution.py:80
  3.2 3.0 %convert_element_type.173 = f32[4,1,128,2560]{3,2,1,0:T(8,128)} convert(bf16[4,1,128,2560]{3,2,1,0:T(8,128)(2,1)S(1)} %copy-done) | non-fusion elementwise | flops 1310720 | bytes 7864320 | tf_op jit(solution)/shard_map/convert_element_type | solution.py:79
  7.2 62.9 %conditional.2 = (bf16[2,2560,256]{2,1,0:T(8,128)(2,1)}) conditional(s32[]{:T(128)} %convert_element_type.175, bf16[2,160,256]{2,1,0:T(8,128)(2,1)S(1)} %pad_maximum_fusion.8, bf16[2,160,256]{2,1,0:T(8,128)(2,1)S(1)} %pad_maximum_fusion.8), branch_computations={%region_1.2_spmd, %region_2.3_spmd} | conditional | flops 1310720 | bytes 19990212 | solution.py:97
  7.2 4.4 %collective-permute-start.9 = (bf16[2,160,256]{2,1,0:T(8,128)(2,1)S(1)}, bf16[2,160,256]{2,1,0:T(8,128)(2,1)S(1)}, u32[]{:S(2)}, u32[]{:S(2)}) collective-permute-start(bf16[2,160,256]{2,1,0:T(8,128)(2,1)S(1)} %param.1), channel_id=1, source_target_pairs={{0,1},{1,0},{2,3},{3,2},{4,5},{5,4},{6,7},{7,6},{8,9},{9,8},{10,11... | collective-permute-start | bytes 491528 | tf_op jit(solution)/shard_map/cond/branch_1_fun/ppermute | solution.py:22
  11.6 6.4 %collective-permute-done.9 = bf16[2,160,256]{2,1,0:T(8,128)(2,1)S(1)} collective-permute-done((bf16[2,160,256]{2,1,0:T(8,128)(2,1)S(1)}, bf16[2,160,256]{2,1,0:T(8,128)(2,1)S(1)}, u32[]{:S(2)}, u32[]{:S(2)}) %collective-permute-start.9) | collective-permute-done | bytes 163872 | tf_op jit(solution)/shard_map/cond/branch_1_fun/ppermute | solution.py:22
  18.8 4.0 %collective-permute-start.10 = (bf16[2,2,160,256]{3,2,1,0:T(8,128)(2,1)}, bf16[2,2,160,256]{3,2,1,0:T(8,128)(2,1)}, u32[]{:S(2)}, u32[]{:S(2)}) collective-permute-start(bf16[2,2,160,256]{3,2,1,0:T(8,128)(2,1)} %get-tuple-element.79), channel_id=1, source_target_pairs={{0,2},{1,3},{2,4},{3,5},{4,6},{5,7},{6,8},{7,9},{8,10},{9,11},{10,... | collective-permute-start | bytes 983048 | tf_op jit(solution)/shard_map/cond/branch_1_fun/ppermute | solution.py:18
  22.8 8.6 %collective-permute-start.11 = (bf16[2,2,160,256]{3,2,1,0:T(8,128)(2,1)}, bf16[2,2,160,256]{3,2,1,0:T(8,128)(2,1)S(1)}, u32[]{:S(2)}, u32[]{:S(2)}) collective-permute-start(bf16[2,2,160,256]{3,2,1,0:T(8,128)(2,1)} %get-tuple-element.79), channel_id=1, source_target_pairs={{0,14},{1,15},{2,0},{3,1},{4,2},{5,3},{6,4},{7,5},{8,6},{9,7},{10,... | collective-permute-start | bytes 983048 | tf_op jit(solution)/shard_map/cond/branch_1_fun/ppermute | solution.py:18
  31.6 1.9 broadcast.115
  34.2 2.0 collective-permute-done.10
  36.2 1.9 collective-permute-start.12
  38.1 4.6 %collective-permute-start.13 = (bf16[2,2,160,256]{3,2,1,0:T(8,128)(2,1)S(1)}, bf16[2,2,160,256]{3,2,1,0:T(8,128)(2,1)S(1)}, u32[]{:S(2)}, u32[]{:S(2)}) collective-permute-start(bf16[2,2,160,256]{3,2,1,0:T(8,128)(2,1)S(1)} %collective-permute-done.11), channel_id=1, source_target_pairs={{0,14},{1,15},{2,0},{3,1},{4,2},{5,3},{6,4},{7,5},{8,6},{9,7},{10,... | collective-permute-start | bytes 983048 | tf_op jit(solution)/shard_map/cond/branch_1_fun/ppermute | solution.py:18
  42.7 1.7 copy_dynamic-update-slice_fusion.6
  46.4 1.9 collective-permute-start.14
  48.3 4.6 %collective-permute-start.15 = (bf16[2,2,160,256]{3,2,1,0:T(8,128)(2,1)S(1)}, bf16[2,2,160,256]{3,2,1,0:T(8,128)(2,1)S(1)}, u32[]{:S(2)}, u32[]{:S(2)}) collective-permute-start(bf16[2,2,160,256]{3,2,1,0:T(8,128)(2,1)S(1)} %collective-permute-done.13), channel_id=1, source_target_pairs={{0,14},{1,15},{2,0},{3,1},{4,2},{5,3},{6,4},{7,5},{8,6},{9,7},{10,... | collective-permute-start | bytes 983048 | tf_op jit(solution)/shard_map/cond/branch_1_fun/ppermute | solution.py:18
  54.4 2.5 %collective-permute-done.15 = bf16[2,2,160,256]{3,2,1,0:T(8,128)(2,1)S(1)} collective-permute-done((bf16[2,2,160,256]{3,2,1,0:T(8,128)(2,1)S(1)}, bf16[2,2,160,256]{3,2,1,0:T(8,128)(2,1)S(1)}, u32[]{:S(2)}, u32[]{:S(2)}) %collective-permute-start.15) | collective-permute-done | bytes 327712 | tf_op jit(solution)/shard_map/cond/branch_1_fun/ppermute | solution.py:18
  56.9 5.0 %collective-permute-start.17 = (bf16[1,2,160,256]{3,2,1,0:T(8,128)(2,1)S(1)}, bf16[1,2,160,256]{3,2,1,0:T(8,128)(2,1)S(1)}, u32[]{:S(2)}, u32[]{:S(2)}) collective-permute-start(bf16[1,2,160,256]{3,2,1,0:T(8,128)(2,1)S(1)} %slice.148), channel_id=1, source_target_pairs={{0,14},{1,15},{2,0},{3,1},{4,2},{5,3},{6,4},{7,5},{8,6},{9,7},{10,... | collective-permute-start | bytes 491528 | tf_op jit(solution)/shard_map/cond/branch_1_fun/ppermute | solution.py:18
  62.0 1.9 collective-permute-start.16
  65.5 3.8 %collective-permute-done.16 = bf16[1,2,160,256]{3,2,1,0:T(8,128)(2,1)S(1)} collective-permute-done((bf16[1,2,160,256]{3,2,1,0:T(8,128)(2,1)S(1)}, bf16[1,2,160,256]{3,2,1,0:T(8,128)(2,1)S(1)}, u32[]{:S(2)}, u32[]{:S(2)}) %collective-permute-start.16) | collective-permute-done | bytes 163872 | tf_op jit(solution)/shard_map/cond/branch_1_fun/ppermute | solution.py:18
  70.0 5.0 %dynamic-slice_bitcast_fusion = (bf16[2560,256]{1,0:T(8,128)(2,1)}, bf16[2560,256]{1,0:T(8,128)(2,1)}, bf16[2560,256]{1,0:T(8,128)(2,1)}, bf16[2560,256]{1,0:T(8,128)(2,1)S(1)}) fusion(bf16[2,2560,256]{2,1,0:T(8,128)(2,1)} %get-tuple-element.122, s32[]{:T(128)S(6)} %select_n.234, s32[]{:T(128)S(6)} %select_n.232, s32[]{:T(128)S(6)} %select_n.230, ...), kind=kLoop, calls=%fused_computation.112 | loop fusion | bytes 10485776 | tf_op jit(solution)/shard_map/jit(dynamic_index_in_dim)/squeeze | solution.py:101
  77.1 2.6 %fusion.28 = bf16[128,2560]{1,0:T(8,128)(2,1)} fusion(bf16[128,128]{0,1:T(8,128)(2,1)S(1)} %fusion.37, f32[4,1,128,2560]{3,2,1,0:T(8,128)} %convert_element_type.173, f32[128]{0:T(128)S(1)} %multiply_multiply_fusion.6, f32[128]{0:T(128)S(1)} %get-tuple-element.117, bf16[2560,256]{1,0:T(8,128)(2,1)S(1)} %get-tuple-element.102, ...), kind=kOutput, calls=%fused_computation.101 | convolution fusion | flops 85852160 | bytes 3310592 | tf_op jit(solution)/shard_map/dot_general | solution.py:115
  81.0 11.5 %collective-permute-start.22 = (bf16[128,2560]{1,0:T(8,128)(2,1)}, bf16[128,2560]{1,0:T(8,128)(2,1)}, u32[]{:S(2)}, u32[]{:S(2)}) collective-permute-start(bf16[128,2560]{1,0:T(8,128)(2,1)} %fusion.28), channel_id=1, source_target_pairs={{16,0},{48,32},{80,64},{112,96},{144,128},{176,160},{208,192},{240... | collective-permute-start | bytes 1966088 | tf_op jit(solution)/shard_map/ppermute | solution.py:129
  92.5 2.4 %fusion.17 = bf16[512,2560]{1,0:T(8,128)(2,1)S(1)} fusion(bf16[4,1,128,2560]{3,2,1,0:T(8,128)(2,1)} %param.8, f32[512]{0:T(512)S(1)} %get-tuple-element.110), kind=kLoop, calls=%fused_computation.81 | loop fusion | flops 3932160 | bytes 5244928 | tf_op jit(solution)/shard_map/convert_element_type | solution.py:81
  94.9 1.8 fusion.40
  102.1 1.7 collective-permute-start.19
  108.2 12.9 %collective-permute-done.23 = bf16[128,2560]{1,0:T(8,128)(2,1)S(1)} collective-permute-done((bf16[128,2560]{1,0:T(8,128)(2,1)S(1)}, bf16[128,2560]{1,0:T(8,128)(2,1)S(1)}, u32[]{:S(2)}, u32[]{:S(2)}) %collective-permute-start.23) | collective-permute-done | bytes 655392 | tf_op jit(solution)/shard_map/ppermute | solution.py:133
  125.2 12.6 %collective-permute-done.20 = bf16[128,2560]{1,0:T(8,128)(2,1)S(1)} collective-permute-done((bf16[128,2560]{1,0:T(8,128)(2,1)S(1)}, bf16[128,2560]{1,0:T(8,128)(2,1)S(1)}, u32[]{:S(2)}, u32[]{:S(2)}) %collective-permute-start.20) | collective-permute-done | bytes 655392 | tf_op jit(solution)/shard_map/ppermute | solution.py:133
  140.0 2.3 %collective-permute-start.21 = (bf16[128,2560]{1,0:T(8,128)(2,1)}, bf16[128,2560]{1,0:T(8,128)(2,1)}, u32[]{:S(2)}, u32[]{:S(2)}) collective-permute-start(bf16[128,2560]{1,0:T(8,128)(2,1)} %add_convert_fusion.3), channel_id=1, source_target_pairs={{16,0},{48,32},{80,64},{112,96},{144,128},{176,160},{208,192},{240... | collective-permute-start | bytes 1966088 | tf_op jit(solution)/shard_map/ppermute | solution.py:135
  146.8 69.3 %conditional.3 = (f32[2,160,256]{2,1,0:T(8,128)}) conditional(s32[]{:T(128)} %convert_element_type.175, (bf16[4,128,128]{1,2,0:T(8,128)(2,1)S(1)}, bf16[512,2560]{1,0:T(8,128)(2,1)S(1)}, bf16[4,128,128]{1,2,0:T(8,128)(2,1)S(1)}, bf16[512,2560]{1,0:T(8,128)(2,1)}) %tuple.20, (s32[]{:T(128)}, s32[]{:T(128)}, s32[]{:T(128)}, s32[]{:T(128)}, ...), branch_computations={%region_10.12_spmd, %region_12.13_spmd} | conditional | flops 1352433664 | bytes 62621692 | solution.py:167
  147.3 2.3 %fusion.2 = bf16[2560,128]{0,1:T(8,128)(2,1)S(1)} fusion(bf16[512,128]{1,0:T(8,128)(2,1)S(1)} %bitcast.267, bf16[512,2560]{1,0:T(8,128)(2,1)} %get-tuple-element.43), kind=kOutput, calls=%fused_computation.40 | convolution fusion | flops 335872000 | bytes 3407872 | tf_op jit(solution)/shard_map/cond/branch_1_fun/dot_general | solution.py:146
  151.3 2.4 %copy.31 = bf16[2560,256]{1,0:T(8,128)(2,1)} copy(bf16[2560,256]{0,1:T(8,128)(2,1)} %pad_maximum_fusion.3) | data formatting | bytes 2621440 | tf_op jit(solution)/shard_map/cond/branch_1_fun/concatenate | solution.py:147
  153.7 2.3 %fusion.4 = bf16[2560,128]{0,1:T(8,128)(2,1)S(1)} fusion(bf16[512,128]{1,0:T(8,128)(2,1)S(1)} %bitcast.265, bf16[512,2560]{1,0:T(8,128)(2,1)} %get-tuple-element.43), kind=kOutput, calls=%fused_computation.42 | convolution fusion | flops 335872000 | bytes 3407872 | tf_op jit(solution)/shard_map/cond/branch_1_fun/dot_general | solution.py:146
  157.7 1.7 copy.32
  161.1 1.9 collective-permute-start.4
  163.0 3.4 %collective-permute-start = (bf16[1,2,160,256]{3,2,1,0:T(8,128)(2,1)S(1)}, bf16[1,2,160,256]{3,2,1,0:T(8,128)(2,1)}, u32[]{:S(2)}, u32[]{:S(2)}) collective-permute-start(bf16[1,2,160,256]{3,2,1,0:T(8,128)(2,1)S(1)} %get-tuple-element.91), channel_id=1, source_target_pairs={{0,2},{1,3},{2,4},{3,5},{4,6},{5,7},{6,8},{7,9},{8,10},{9,11},{10,... | collective-permute-start | bytes 491528 | tf_op jit(solution)/shard_map/cond/branch_1_fun/ppermute | solution.py:18
  168.5 3.3 %collective-permute-start.5 = (bf16[2,2,160,256]{3,2,1,0:T(8,128)(2,1)S(1)}, bf16[2,2,160,256]{3,2,1,0:T(8,128)(2,1)S(1)}, u32[]{:S(2)}, u32[]{:S(2)}) collective-permute-start(bf16[2,2,160,256]{3,2,1,0:T(8,128)(2,1)S(1)} %pad_maximum_fusion.6), channel_id=1, source_target_pairs={{0,14},{1,15},{2,0},{3,1},{4,2},{5,3},{6,4},{7,5},{8,6},{9,7},{10,... | collective-permute-start | bytes 983048 | tf_op jit(solution)/shard_map/cond/branch_1_fun/ppermute | solution.py:18
  172.8 2.3 %collective-permute-start.1 = (bf16[2,2,160,256]{3,2,1,0:T(8,128)(2,1)S(1)}, bf16[2,2,160,256]{3,2,1,0:T(8,128)(2,1)S(1)}, u32[]{:S(2)}, u32[]{:S(2)}) collective-permute-start(bf16[2,2,160,256]{3,2,1,0:T(8,128)(2,1)S(1)} %pad_maximum_fusion.5), channel_id=1, source_target_pairs={{0,2},{1,3},{2,4},{3,5},{4,6},{5,7},{6,8},{7,9},{8,10},{9,11},{10,... | collective-permute-start | bytes 983048 | tf_op jit(solution)/shard_map/cond/branch_1_fun/ppermute | solution.py:18
  175.0 1.7 collective-permute-done.5
  176.8 4.0 %collective-permute-start.6 = (bf16[2,2,160,256]{3,2,1,0:T(8,128)(2,1)S(1)}, bf16[2,2,160,256]{3,2,1,0:T(8,128)(2,1)S(1)}, u32[]{:S(2)}, u32[]{:S(2)}) collective-permute-start(bf16[2,2,160,256]{3,2,1,0:T(8,128)(2,1)S(1)} %bitcast_add_fusion.1), channel_id=1, source_target_pairs={{0,14},{1,15},{2,0},{3,1},{4,2},{5,3},{6,4},{7,5},{8,6},{9,7},{10,... | collective-permute-start | bytes 983048 | tf_op jit(solution)/shard_map/cond/branch_1_fun/ppermute | solution.py:18
  182.0 1.9 collective-permute-start.2
  183.9 1.9 collective-permute-done.6
  185.8 5.0 %collective-permute-start.7 = (bf16[2,2,160,256]{3,2,1,0:T(8,128)(2,1)S(1)}, bf16[2,2,160,256]{3,2,1,0:T(8,128)(2,1)S(1)}, u32[]{:S(2)}, u32[]{:S(2)}) collective-permute-start(bf16[2,2,160,256]{3,2,1,0:T(8,128)(2,1)S(1)} %bitcast_add_fusion.2), channel_id=1, source_target_pairs={{0,14},{1,15},{2,0},{3,1},{4,2},{5,3},{6,4},{7,5},{8,6},{9,7},{10,... | collective-permute-start | bytes 983048 | tf_op jit(solution)/shard_map/cond/branch_1_fun/ppermute | solution.py:18
  192.2 1.9 collective-permute-start.3
  194.2 2.6 %collective-permute-done.7 = bf16[2,2,160,256]{3,2,1,0:T(8,128)(2,1)S(1)} collective-permute-done((bf16[2,2,160,256]{3,2,1,0:T(8,128)(2,1)S(1)}, bf16[2,2,160,256]{3,2,1,0:T(8,128)(2,1)S(1)}, u32[]{:S(2)}, u32[]{:S(2)}) %collective-permute-start.7) | collective-permute-done | bytes 327712 | tf_op jit(solution)/shard_map/cond/branch_1_fun/ppermute | solution.py:18
  196.8 6.7 %collective-permute-done.3 = bf16[2,2,160,256]{3,2,1,0:T(8,128)(2,1)S(1)} collective-permute-done((bf16[2,2,160,256]{3,2,1,0:T(8,128)(2,1)S(1)}, bf16[2,2,160,256]{3,2,1,0:T(8,128)(2,1)S(1)}, u32[]{:S(2)}, u32[]{:S(2)}) %collective-permute-start.3) | collective-permute-done | bytes 327712 | tf_op jit(solution)/shard_map/cond/branch_1_fun/ppermute | solution.py:18
  203.6 3.3 %collective-permute-start.8 = (bf16[2,160,256]{2,1,0:T(8,128)(2,1)S(1)}, bf16[2,160,256]{2,1,0:T(8,128)(2,1)S(1)}, u32[]{:S(2)}, u32[]{:S(2)}) collective-permute-start(bf16[2,160,256]{2,1,0:T(8,128)(2,1)S(1)} %fusion.14), channel_id=1, source_target_pairs={{0,1},{1,0},{2,3},{3,2},{4,5},{5,4},{6,7},{7,6},{8,9},{9,8},{10,11... | collective-permute-start | bytes 491528 | tf_op jit(solution)/shard_map/cond/branch_1_fun/ppermute | solution.py:22
  207.0 8.3 %collective-permute-done.8 = bf16[2,160,256]{2,1,0:T(8,128)(2,1)S(1)} collective-permute-done((bf16[2,160,256]{2,1,0:T(8,128)(2,1)S(1)}, bf16[2,160,256]{2,1,0:T(8,128)(2,1)S(1)}, u32[]{:S(2)}, u32[]{:S(2)}) %collective-permute-start.8) | collective-permute-done | bytes 163872 | tf_op jit(solution)/shard_map/cond/branch_1_fun/ppermute | solution.py:22
  216.1 1.7 slice_bitcast_fusion.19
  217.8 2.0 select_bitcast_fusion.2
  (126 shorter events, 44.1 us)
Async XLA Ops:
  0.7 2.5 %copy-start = (bf16[4,1,128,2560]{3,2,1,0:T(8,128)(2,1)S(1)}, bf16[4,1,128,2560]{3,2,1,0:T(8,128)(2,1)}, u32[]{:S(2)}) copy-start(bf16[4,1,128,2560]{3,2,1,0:T(8,128)(2,1)} %param.8) | copy-start | bytes 7864324
  6.2 0.9 copy-start.12
  6.2 0.9 copy-start.13
  6.7 68.3 %copy-start.5 = (bf16[4,128,2560]{2,1,0:T(8,128)(2,1)}, bf16[4,128,2560]{2,1,0:T(8,128)(2,1)S(1)}, u32[]{:S(2)}) copy-start(bf16[4,128,2560]{2,1,0:T(8,128)(2,1)S(1)} %fusion.19) | copy-start | bytes 7864324
  7.2 10.9 %collective-permute-start.9 = (bf16[2,160,256]{2,1,0:T(8,128)(2,1)S(1)}, bf16[2,160,256]{2,1,0:T(8,128)(2,1)S(1)}, u32[]{:S(2)}, u32[]{:S(2)}) collective-permute-start(bf16[2,160,256]{2,1,0:T(8,128)(2,1)S(1)} %param.1), channel_id=1, source_target_pairs={{0,1},{1,0},{2,3},{3,2},{4,5},{5,4},{6,7},{7,6},{8,9},{9,8},{10,11... | collective-permute-start | bytes 491528 | tf_op jit(solution)/shard_map/cond/branch_1_fun/ppermute | solution.py:22
  18.8 17.3 %collective-permute-start.10 = (bf16[2,2,160,256]{3,2,1,0:T(8,128)(2,1)}, bf16[2,2,160,256]{3,2,1,0:T(8,128)(2,1)}, u32[]{:S(2)}, u32[]{:S(2)}) collective-permute-start(bf16[2,2,160,256]{3,2,1,0:T(8,128)(2,1)} %get-tuple-element.79), channel_id=1, source_target_pairs={{0,2},{1,3},{2,4},{3,5},{4,6},{5,7},{6,8},{7,9},{8,10},{9,11},{10,... | collective-permute-start | bytes 983048 | tf_op jit(solution)/shard_map/cond/branch_1_fun/ppermute | solution.py:18
  22.8 15.3 %collective-permute-start.11 = (bf16[2,2,160,256]{3,2,1,0:T(8,128)(2,1)}, bf16[2,2,160,256]{3,2,1,0:T(8,128)(2,1)S(1)}, u32[]{:S(2)}, u32[]{:S(2)}) collective-permute-start(bf16[2,2,160,256]{3,2,1,0:T(8,128)(2,1)} %get-tuple-element.79), channel_id=1, source_target_pairs={{0,14},{1,15},{2,0},{3,1},{4,2},{5,3},{6,4},{7,5},{8,6},{9,7},{10,... | collective-permute-start | bytes 983048 | tf_op jit(solution)/shard_map/cond/branch_1_fun/ppermute | solution.py:18
  36.2 10.2 %collective-permute-start.12 = (bf16[2,2,160,256]{3,2,1,0:T(8,128)(2,1)}, bf16[2,2,160,256]{3,2,1,0:T(8,128)(2,1)S(1)}, u32[]{:S(2)}, u32[]{:S(2)}) collective-permute-start(bf16[2,2,160,256]{3,2,1,0:T(8,128)(2,1)} %collective-permute-done.10), channel_id=1, source_target_pairs={{0,2},{1,3},{2,4},{3,5},{4,6},{5,7},{6,8},{7,9},{8,10},{9,11},{10,... | collective-permute-start | bytes 983048 | tf_op jit(solution)/shard_map/cond/branch_1_fun/ppermute | solution.py:18
  38.1 10.2 %collective-permute-start.13 = (bf16[2,2,160,256]{3,2,1,0:T(8,128)(2,1)S(1)}, bf16[2,2,160,256]{3,2,1,0:T(8,128)(2,1)S(1)}, u32[]{:S(2)}, u32[]{:S(2)}) collective-permute-start(bf16[2,2,160,256]{3,2,1,0:T(8,128)(2,1)S(1)} %collective-permute-done.11), channel_id=1, source_target_pairs={{0,14},{1,15},{2,0},{3,1},{4,2},{5,3},{6,4},{7,5},{8,6},{9,7},{10,... | collective-permute-start | bytes 983048 | tf_op jit(solution)/shard_map/cond/branch_1_fun/ppermute | solution.py:18
  46.4 15.6 %collective-permute-start.14 = (bf16[2,2,160,256]{3,2,1,0:T(8,128)(2,1)S(1)}, bf16[2,2,160,256]{3,2,1,0:T(8,128)(2,1)S(1)}, u32[]{:S(2)}, u32[]{:S(2)}) collective-permute-start(bf16[2,2,160,256]{3,2,1,0:T(8,128)(2,1)S(1)} %collective-permute-done.12), channel_id=1, source_target_pairs={{0,2},{1,3},{2,4},{3,5},{4,6},{5,7},{6,8},{7,9},{8,10},{9,11},{10,... | collective-permute-start | bytes 983048 | tf_op jit(solution)/shard_map/cond/branch_1_fun/ppermute | solution.py:18
  48.3 8.6 %collective-permute-start.15 = (bf16[2,2,160,256]{3,2,1,0:T(8,128)(2,1)S(1)}, bf16[2,2,160,256]{3,2,1,0:T(8,128)(2,1)S(1)}, u32[]{:S(2)}, u32[]{:S(2)}) collective-permute-start(bf16[2,2,160,256]{3,2,1,0:T(8,128)(2,1)S(1)} %collective-permute-done.13), channel_id=1, source_target_pairs={{0,14},{1,15},{2,0},{3,1},{4,2},{5,3},{6,4},{7,5},{8,6},{9,7},{10,... | collective-permute-start | bytes 983048 | tf_op jit(solution)/shard_map/cond/branch_1_fun/ppermute | solution.py:18
  56.9 8.5 %collective-permute-start.17 = (bf16[1,2,160,256]{3,2,1,0:T(8,128)(2,1)S(1)}, bf16[1,2,160,256]{3,2,1,0:T(8,128)(2,1)S(1)}, u32[]{:S(2)}, u32[]{:S(2)}) collective-permute-start(bf16[1,2,160,256]{3,2,1,0:T(8,128)(2,1)S(1)} %slice.148), channel_id=1, source_target_pairs={{0,14},{1,15},{2,0},{3,1},{4,2},{5,3},{6,4},{7,5},{8,6},{9,7},{10,... | collective-permute-start | bytes 491528 | tf_op jit(solution)/shard_map/cond/branch_1_fun/ppermute | solution.py:18
  62.0 7.3 %collective-permute-start.16 = (bf16[1,2,160,256]{3,2,1,0:T(8,128)(2,1)S(1)}, bf16[1,2,160,256]{3,2,1,0:T(8,128)(2,1)S(1)}, u32[]{:S(2)}, u32[]{:S(2)}) collective-permute-start(bf16[1,2,160,256]{3,2,1,0:T(8,128)(2,1)S(1)} %slice.147), channel_id=1, source_target_pairs={{0,2},{1,3},{2,4},{3,5},{4,6},{5,7},{6,8},{7,9},{8,10},{9,11},{10,... | collective-permute-start | bytes 491528 | tf_op jit(solution)/shard_map/cond/branch_1_fun/ppermute | solution.py:18
  75.0 1.1 copy-start.7
  79.7 17.8 %collective-permute-start.18 = (bf16[128,2560]{1,0:T(8,128)(2,1)}, bf16[128,2560]{1,0:T(8,128)(2,1)}, u32[]{:S(2)}, u32[]{:S(2)}) collective-permute-start(bf16[128,2560]{1,0:T(8,128)(2,1)} %fusion.28), channel_id=1, source_target_pairs={{0,496},{32,16},{64,48},{96,80},{128,112},{160,144},{192,176},{224... | collective-permute-start | bytes 1966088 | tf_op jit(solution)/shard_map/ppermute | solution.py:128
  81.0 18.0 %collective-permute-start.22 = (bf16[128,2560]{1,0:T(8,128)(2,1)}, bf16[128,2560]{1,0:T(8,128)(2,1)}, u32[]{:S(2)}, u32[]{:S(2)}) collective-permute-start(bf16[128,2560]{1,0:T(8,128)(2,1)} %fusion.28), channel_id=1, source_target_pairs={{16,0},{48,32},{80,64},{112,96},{144,128},{176,160},{208,192},{240... | collective-permute-start | bytes 1966088 | tf_op jit(solution)/shard_map/ppermute | solution.py:129
  92.5 2.4 %copy-start.4 = (bf16[2560,256]{1,0:T(8,128)(2,1)S(1)}, bf16[2560,256]{1,0:T(8,128)(2,1)}, u32[]{:S(2)}) copy-start(bf16[2560,256]{1,0:T(8,128)(2,1)} %get-tuple-element.101) | copy-start | bytes 3932164
  92.5 4.2 %copy-start.3 = (bf16[2560,256]{1,0:T(8,128)(2,1)S(1)}, bf16[2560,256]{1,0:T(8,128)(2,1)}, u32[]{:S(2)}) copy-start(bf16[2560,256]{1,0:T(8,128)(2,1)} %get-tuple-element.100) | copy-start | bytes 3932164
  92.5 4.2 %copy-start.6 = (bf16[4,128,2560]{2,1,0:T(8,128)(2,1)S(1)}, bf16[4,128,2560]{2,1,0:T(8,128)(2,1)}, u32[]{:S(2)}) copy-start(bf16[4,128,2560]{2,1,0:T(8,128)(2,1)} %copy-done.5) | copy-start | bytes 7864324
  92.5 8.1 %slice-start = ((s8[5242880]{0:T(1024)(128)(4,1)}), s8[1048576]{0:T(1024)(128)(4,1)S(1)}, s32[]{:S(2)}) async-start(s8[5242880]{0:T(1024)(128)(4,1)} %bitcast.252), calls=%async_computation.2 | async-start | bytes 2097152
  94.9 2.2 %copy-start.2 = (bf16[2560,256]{1,0:T(8,128)(2,1)S(1)}, bf16[2560,256]{1,0:T(8,128)(2,1)}, u32[]{:S(2)}) copy-start(bf16[2560,256]{1,0:T(8,128)(2,1)} %get-tuple-element.99) | copy-start | bytes 3932164
  94.9 5.7 %slice-start.1 = ((s8[5242880]{0:T(1024)(128)(4,1)}), s8[4194304]{0:T(1024)(128)(4,1)S(1)}, s32[]{:S(2)}) async-start(s8[5242880]{0:T(1024)(128)(4,1)} %bitcast.252), calls=%async_computation.3 | async-start | bytes 8388608
  102.1 5.7 %collective-permute-start.19 = (bf16[128,2560]{1,0:T(8,128)(2,1)S(1)}, bf16[128,2560]{1,0:T(8,128)(2,1)S(1)}, u32[]{:S(2)}, u32[]{:S(2)}) collective-permute-start(bf16[128,2560]{1,0:T(8,128)(2,1)S(1)} %add_convert_fusion.5), channel_id=1, source_target_pairs={{16,0},{48,32},{80,64},{112,96},{144,128},{176,160},{208,192},{240... | collective-permute-start | bytes 1966088 | tf_op jit(solution)/shard_map/ppermute | solution.py:135
  105.3 15.8 %collective-permute-start.23 = (bf16[128,2560]{1,0:T(8,128)(2,1)S(1)}, bf16[128,2560]{1,0:T(8,128)(2,1)S(1)}, u32[]{:S(2)}, u32[]{:S(2)}) collective-permute-start(bf16[128,2560]{1,0:T(8,128)(2,1)S(1)} %add_convert_fusion.2), channel_id=1, source_target_pairs={{0,496},{32,16},{64,48},{96,80},{128,112},{160,144},{192,176},{224... | collective-permute-start | bytes 1966088 | tf_op jit(solution)/shard_map/ppermute | solution.py:133
  122.0 15.8 %collective-permute-start.20 = (bf16[128,2560]{1,0:T(8,128)(2,1)S(1)}, bf16[128,2560]{1,0:T(8,128)(2,1)S(1)}, u32[]{:S(2)}, u32[]{:S(2)}) collective-permute-start(bf16[128,2560]{1,0:T(8,128)(2,1)S(1)} %add_convert_fusion.4), channel_id=1, source_target_pairs={{0,496},{32,16},{64,48},{96,80},{128,112},{160,144},{192,176},{224... | collective-permute-start | bytes 1966088 | tf_op jit(solution)/shard_map/ppermute | solution.py:133
  123.8 14.5 %collective-permute-start.24 = (bf16[128,2560]{1,0:T(8,128)(2,1)S(1)}, bf16[128,2560]{1,0:T(8,128)(2,1)S(1)}, u32[]{:S(2)}, u32[]{:S(2)}) collective-permute-start(bf16[128,2560]{1,0:T(8,128)(2,1)S(1)} %add_convert_fusion.1), channel_id=1, source_target_pairs={{16,0},{48,32},{80,64},{112,96},{144,128},{176,160},{208,192},{240... | collective-permute-start | bytes 1966088 | tf_op jit(solution)/shard_map/ppermute | solution.py:135
  140.0 77.8 %collective-permute-start.21 = (bf16[128,2560]{1,0:T(8,128)(2,1)}, bf16[128,2560]{1,0:T(8,128)(2,1)}, u32[]{:S(2)}, u32[]{:S(2)}) collective-permute-start(bf16[128,2560]{1,0:T(8,128)(2,1)} %add_convert_fusion.3), channel_id=1, source_target_pairs={{16,0},{48,32},{80,64},{112,96},{144,128},{176,160},{208,192},{240... | collective-permute-start | bytes 1966088 | tf_op jit(solution)/shard_map/ppermute | solution.py:135
  143.6 1.5 copy-start.11
  143.6 74.3 %collective-permute-start.25 = (bf16[128,2560]{1,0:T(8,128)(2,1)}, bf16[128,2560]{1,0:T(8,128)(2,1)}, u32[]{:S(2)}, u32[]{:S(2)}) collective-permute-start(bf16[128,2560]{1,0:T(8,128)(2,1)} %add_convert_fusion), channel_id=1, source_target_pairs={{0,496},{32,16},{64,48},{96,80},{128,112},{160,144},{192,176},{224... | collective-permute-start | bytes 1966088 | tf_op jit(solution)/shard_map/ppermute | solution.py:133
  157.7 1.7 copy-start.1
  161.1 6.4 %collective-permute-start.4 = (bf16[1,2,160,256]{3,2,1,0:T(8,128)(2,1)}, bf16[1,2,160,256]{3,2,1,0:T(8,128)(2,1)}, u32[]{:S(2)}, u32[]{:S(2)}) collective-permute-start(bf16[1,2,160,256]{3,2,1,0:T(8,128)(2,1)} %get-tuple-element.92), channel_id=1, source_target_pairs={{0,14},{1,15},{2,0},{3,1},{4,2},{5,3},{6,4},{7,5},{8,6},{9,7},{10,... | collective-permute-start | bytes 491528 | tf_op jit(solution)/shard_map/cond/branch_1_fun/ppermute | solution.py:18
  163.0 8.7 %collective-permute-start = (bf16[1,2,160,256]{3,2,1,0:T(8,128)(2,1)S(1)}, bf16[1,2,160,256]{3,2,1,0:T(8,128)(2,1)}, u32[]{:S(2)}, u32[]{:S(2)}) collective-permute-start(bf16[1,2,160,256]{3,2,1,0:T(8,128)(2,1)S(1)} %get-tuple-element.91), channel_id=1, source_target_pairs={{0,2},{1,3},{2,4},{3,5},{4,6},{5,7},{6,8},{7,9},{8,10},{9,11},{10,... | collective-permute-start | bytes 491528 | tf_op jit(solution)/shard_map/cond/branch_1_fun/ppermute | solution.py:18
  166.5 1.0 copy-start.10
  168.4 13.5 %copy-start.9 = (bf16[1,2,2,160,256]{4,3,1,0,2:T(8,128)(2,1)S(1)}, bf16[1,2,2,160,256]{4,3,1,0,2:T(8,128)(2,1)}, u32[]{:S(2)}) copy-start(bf16[1,2,2,160,256]{4,3,1,0,2:T(8,128)(2,1)} %get-tuple-element.85) | copy-start | bytes 983044 | tf_op jit(solution)/shard_map/cond
  168.5 8.3 %collective-permute-start.5 = (bf16[2,2,160,256]{3,2,1,0:T(8,128)(2,1)S(1)}, bf16[2,2,160,256]{3,2,1,0:T(8,128)(2,1)S(1)}, u32[]{:S(2)}, u32[]{:S(2)}) collective-permute-start(bf16[2,2,160,256]{3,2,1,0:T(8,128)(2,1)S(1)} %pad_maximum_fusion.6), channel_id=1, source_target_pairs={{0,14},{1,15},{2,0},{3,1},{4,2},{5,3},{6,4},{7,5},{8,6},{9,7},{10,... | collective-permute-start | bytes 983048 | tf_op jit(solution)/shard_map/cond/branch_1_fun/ppermute | solution.py:18
  172.7 13.1 %copy-start.8 = (bf16[1,2,2,160,256]{4,3,1,0,2:T(8,128)(2,1)S(1)}, bf16[1,2,2,160,256]{4,3,1,0,2:T(8,128)(2,1)}, u32[]{:S(2)}) copy-start(bf16[1,2,2,160,256]{4,3,1,0,2:T(8,128)(2,1)} %get-tuple-element.88) | copy-start | bytes 983044 | tf_op jit(solution)/shard_map/cond
  172.8 9.2 %collective-permute-start.1 = (bf16[2,2,160,256]{3,2,1,0:T(8,128)(2,1)S(1)}, bf16[2,2,160,256]{3,2,1,0:T(8,128)(2,1)S(1)}, u32[]{:S(2)}, u32[]{:S(2)}) collective-permute-start(bf16[2,2,160,256]{3,2,1,0:T(8,128)(2,1)S(1)} %pad_maximum_fusion.5), channel_id=1, source_target_pairs={{0,2},{1,3},{2,4},{3,5},{4,6},{5,7},{6,8},{7,9},{8,10},{9,11},{10,... | collective-permute-start | bytes 983048 | tf_op jit(solution)/shard_map/cond/branch_1_fun/ppermute | solution.py:18
  176.8 9.0 %collective-permute-start.6 = (bf16[2,2,160,256]{3,2,1,0:T(8,128)(2,1)S(1)}, bf16[2,2,160,256]{3,2,1,0:T(8,128)(2,1)S(1)}, u32[]{:S(2)}, u32[]{:S(2)}) collective-permute-start(bf16[2,2,160,256]{3,2,1,0:T(8,128)(2,1)S(1)} %bitcast_add_fusion.1), channel_id=1, source_target_pairs={{0,14},{1,15},{2,0},{3,1},{4,2},{5,3},{6,4},{7,5},{8,6},{9,7},{10,... | collective-permute-start | bytes 983048 | tf_op jit(solution)/shard_map/cond/branch_1_fun/ppermute | solution.py:18
  182.0 10.2 %collective-permute-start.2 = (bf16[2,2,160,256]{3,2,1,0:T(8,128)(2,1)S(1)}, bf16[2,2,160,256]{3,2,1,0:T(8,128)(2,1)S(1)}, u32[]{:S(2)}, u32[]{:S(2)}) collective-permute-start(bf16[2,2,160,256]{3,2,1,0:T(8,128)(2,1)S(1)} %bitcast_add_fusion.3), channel_id=1, source_target_pairs={{0,2},{1,3},{2,4},{3,5},{4,6},{5,7},{6,8},{7,9},{8,10},{9,11},{10,... | collective-permute-start | bytes 983048 | tf_op jit(solution)/shard_map/cond/branch_1_fun/ppermute | solution.py:18
  185.8 11.0 %collective-permute-start.7 = (bf16[2,2,160,256]{3,2,1,0:T(8,128)(2,1)S(1)}, bf16[2,2,160,256]{3,2,1,0:T(8,128)(2,1)S(1)}, u32[]{:S(2)}, u32[]{:S(2)}) collective-permute-start(bf16[2,2,160,256]{3,2,1,0:T(8,128)(2,1)S(1)} %bitcast_add_fusion.2), channel_id=1, source_target_pairs={{0,14},{1,15},{2,0},{3,1},{4,2},{5,3},{6,4},{7,5},{8,6},{9,7},{10,... | collective-permute-start | bytes 983048 | tf_op jit(solution)/shard_map/cond/branch_1_fun/ppermute | solution.py:18
  192.2 11.3 %collective-permute-start.3 = (bf16[2,2,160,256]{3,2,1,0:T(8,128)(2,1)S(1)}, bf16[2,2,160,256]{3,2,1,0:T(8,128)(2,1)S(1)}, u32[]{:S(2)}, u32[]{:S(2)}) collective-permute-start(bf16[2,2,160,256]{3,2,1,0:T(8,128)(2,1)S(1)} %bitcast_add_fusion.4), channel_id=1, source_target_pairs={{0,2},{1,3},{2,4},{3,5},{4,6},{5,7},{6,8},{7,9},{8,10},{9,11},{10,... | collective-permute-start | bytes 983048 | tf_op jit(solution)/shard_map/cond/branch_1_fun/ppermute | solution.py:18
  203.6 11.7 %collective-permute-start.8 = (bf16[2,160,256]{2,1,0:T(8,128)(2,1)S(1)}, bf16[2,160,256]{2,1,0:T(8,128)(2,1)S(1)}, u32[]{:S(2)}, u32[]{:S(2)}) collective-permute-start(bf16[2,160,256]{2,1,0:T(8,128)(2,1)S(1)} %fusion.14), channel_id=1, source_target_pairs={{0,1},{1,0},{2,3},{3,2},{4,5},{5,4},{6,7},{7,6},{8,9},{9,8},{10,11... | collective-permute-start | bytes 491528 | tf_op jit(solution)/shard_map/cond/branch_1_fun/ppermute | solution.py:22

commit v2 on v1

v2 whole, which is shorter than its diff:
```python
import functools

import jax
import jax.numpy as jnp
from jax import lax
from jax.experimental import pallas as pl
from jax.experimental.pallas import tpu as pltpu
from jax.sharding import PartitionSpec as P

EPS = 1e-06
F32 = jnp.float32
BF16 = jnp.bfloat16
LIMIT = pltpu.CompilerParams(vmem_limit_bytes=24 * 1024 * 1024)
IN_VMEM = pl.BlockSpec(memory_space=pltpu.VMEM)
ANYWHERE = pl.BlockSpec(memory_space=pl.ANY)
SCALAR = pl.BlockSpec(memory_space=pltpu.SMEM)


def dp_pairs(n_z, step, flip):
    return [
        (2 * z + h, 2 * ((z + step) % n_z) + (h ^ flip)) for z in range(n_z) for h in range(2)
    ]


def shifted(value, n_z, step):
    return lax.ppermute(value, "dp", dp_pairs(n_z, step, 0))


def swapped(value, n_z):
    return lax.ppermute(value, "dp", dp_pairs(n_z, 0, 1))


def place_kernel(n_z, place_ref, *refs):
    half = n_z // 2
    pieces, outs = refs[: n_z + 1], refs[n_z + 1 :]
    z = place_ref[0]
    offsets = [0] + list(range(-1, -half, -1)) + list(range(1, half))
    for level, out in enumerate(outs):
        lanes = slice(level * out.shape[2], (level + 1) * out.shape[2])
        for piece, offset in zip(pieces, offsets):
            at = lax.rem(z + (offset + n_z), n_z) * 2
            out[pl.ds(at, 2)] = piece[:, :, lanes]
        far = lax.rem(z + half, n_z) * 2
        for h in range(2):
            out[pl.ds(far + h, 1)] = pieces[n_z - 1 + h][:, :, lanes]


def ring_gather(shard, n_z):
    index = lax.axis_index("dp")
    z, h = index // 2, index % 2
    other = swapped(shard, n_z)
    pair = jnp.stack([jnp.where(h == 0, shard, other), jnp.where(h == 0, other, shard)])
    half = n_z // 2
    rights, lefts = [], []
    right, left = pair, pair
    for _ in range(1, half):
        right, left = shifted(right, n_z, 1), shifted(left, n_z, -1)
        rights.append(right)
        lefts.append(left)
    pieces = [pair] + rights + lefts + [shifted(right[:1], n_z, 1), shifted(left[1:], n_z, -1)]
    share, lanes = shard.shape[0], shard.shape[1] // 2
    whole = jax.ShapeDtypeStruct((2 * n_z, share, lanes), shard.dtype)
    return pl.pallas_call(
        functools.partial(place_kernel, n_z),
        out_shape=[whole, whole],
        in_specs=[SCALAR] + [IN_VMEM] * len(pieces),
        out_specs=[IN_VMEM] * 2,
        compiler_params=LIMIT,
        name="place_maps",
    )(z.astype(jnp.int32)[None], *pieces)


def ring_reduce(parts, n_z):
    index = lax.axis_index("dp")
    z, h = index // 2, index % 2
    half = n_z // 2

    def at(offset):
        return lax.dynamic_index_in_dim(parts, (z + offset) % n_z, 0, keepdims=False)

    far = at(half)
    right, left = shifted(far[:1], n_z, 1), shifted(far[1:], n_z, -1)
    for step in range(half - 1, 0, -1):
        here, there = at(step), at(-step)
        if step == half - 1:
            here = jnp.concatenate([here[:1] + right, here[1:]], axis=0)
            there = jnp.concatenate([there[:1], there[1:] + left], axis=0)
        else:
            here, there = here + right, there + left
        here, there = lax.optimization_barrier((here, there))
        right, left = shifted(here, n_z, 1), shifted(there, n_z, -1)
    total = at(0).astype(F32) + right.astype(F32) + left.astype(F32)
    mine = lax.dynamic_index_in_dim(total, h, 0, keepdims=False)
    other = lax.dynamic_index_in_dim(total, 1 - h, 0, keepdims=False).astype(BF16)
    return mine, swapped(other, n_z)


def empty_kernel(out_ref):
    pass


def unset(shape, dtype):
    return pl.pallas_call(
        empty_kernel,
        out_shape=jax.ShapeDtypeStruct(shape, dtype),
        out_specs=ANYWHERE,
        name="unset",
    )()


def relay(incoming_ref, x_ref, map_ref, latent, slope, inverse, sent_ref, grad_latent_ref):
    width, rank = x_ref.shape[-1], latent.shape[1]
    grad_act = jnp.dot(incoming_ref[...], map_ref[:, rank:], preferred_element_type=F32)
    grad_latent = (grad_act * slope).astype(BF16)
    grad_latent_ref[...] = grad_latent
    inner = jnp.sum(grad_latent.astype(F32) * latent, axis=-1, keepdims=True) / width
    scale = inverse * inverse * inner
    run = width // 4
    for start in range(0, width, run):
        at = pl.ds(start, run)
        grad_normed = lax.dot_general(
            grad_latent, map_ref[at, :rank], (((1,), (1,)), ((), ())), preferred_element_type=F32
        )
        x = x_ref[0, 0, :, at].astype(F32)
        sent = incoming_ref[:, at].astype(F32) + (inverse * grad_normed - x * scale)
        sent_ref[:, at] = sent.astype(BF16)


def normalise(x_ref, normed_ref):
    x = x_ref[0, 0].astype(F32)
    inverse = lax.rsqrt(jnp.mean(x * x, axis=-1, keepdims=True) + EPS)
    normed_ref[...] = (x * inverse).astype(BF16)
    return inverse


def first_kernel(x_ref, incoming_ref, map_ref, sent_ref, grad_latent_ref, active_ref, normed_ref):
    rank = active_ref.shape[1]
    inverse = normalise(x_ref, normed_ref)
    latent = jnp.dot(normed_ref[...], map_ref[:, :rank], preferred_element_type=F32)
    gate = jax.nn.sigmoid(latent)
    active_ref[...] = (latent * gate).astype(BF16)
    slope = gate * (1.0 + latent * (1.0 - gate))
    relay(incoming_ref, x_ref, map_ref, latent, slope, inverse, sent_ref, grad_latent_ref)


def first_tick(saved_inputs, incoming, maps):
    ticks, _, rows, width = saved_inputs.shape
    rank = maps.shape[1] // 2
    wide = jax.ShapeDtypeStruct((rows, width), BF16)
    narrow = jax.ShapeDtypeStruct((rows, rank), BF16)
    return pl.pallas_call(
        first_kernel,
        grid=(1,),
        out_shape=[wide, narrow, narrow, wide],
        in_specs=[pl.BlockSpec((1, 1, rows, width), lambda i: (0, 0, 0, 0)), IN_VMEM, IN_VMEM],
        out_specs=[IN_VMEM] * 4,
        compiler_params=LIMIT,
        cost_estimate=pl.CostEstimate(flops=6 * rows * width * rank, bytes_accessed=4 * 2 * rows * width, transcendentals=0),
        name="first_tick",
    )(saved_inputs, incoming, maps)


def forward_kernel(level_ref, x_ref, first_ref, second_ref, dep_ref, normed_ref, active_ref, latent_ref, slope_ref, inverse_ref):
    rank = active_ref.shape[2]
    inverse = normalise(x_ref, normed_ref.at[0])
    inverse_ref[0] = jnp.broadcast_to(inverse, inverse_ref.shape[1:])
    level = level_ref[pl.program_id(0) + 1]
    for value, map_ref in ((1, first_ref), (0, second_ref)):

        @pl.when(level == value)
        def _():
            latent_ref[0] = jnp.dot(
                normed_ref[0], map_ref[:, :rank], preferred_element_type=F32
            )

    latent = latent_ref[0]
    gate = jax.nn.sigmoid(latent)
    active_ref[0] = (latent * gate).astype(BF16)
    slope_ref[0] = gate * (1.0 + latent * (1.0 - gate))


def forward_rest(levels, saved_inputs, first, second, dep):
    ticks, _, rows, width = saved_inputs.shape
    rank = first.shape[1] // 2
    rest = ticks - 1

    def made(lanes, dtype):
        return jax.ShapeDtypeStruct((rest, rows, lanes), dtype)

    def block(lanes):
        return pl.BlockSpec((1, rows, lanes), lambda i: (i, 0, 0))

    return pl.pallas_call(
        forward_kernel,
        grid=(rest,),
        out_shape=[made(width, BF16), made(rank, BF16), made(rank, F32), made(rank, F32), made(rank, F32)],
        in_specs=[
            SCALAR,
            pl.BlockSpec((1, 1, rows, width), lambda i: (i + 1, 0, 0, 0)),
            IN_VMEM,
            IN_VMEM,
            ANYWHERE,
        ],
        out_specs=[block(width)] + [block(rank)] * 4,
        compiler_params=LIMIT,
        cost_estimate=pl.CostEstimate(flops=rest * 2 * rows * width * rank, bytes_accessed=rest * 4 * rows * width, transcendentals=0),
        name="forward_rest",
    )(levels, saved_inputs, first, second, dep)


def tick_kernel(flags_ref, incoming_ref, x_ref, first_ref, second_ref, latent_ref, slope_ref, inverse_ref, dep_ref, sent_ref, grad_latent_ref):
    for value, map_ref in ((1, first_ref), (0, second_ref)):

        @pl.when((flags_ref[0] == 1) & (flags_ref[1] == value))
        def _():
            relay(
                incoming_ref,
                x_ref,
                map_ref,
                latent_ref[0],
                slope_ref[0],
                inverse_ref[0][:, :1],
                sent_ref,
                grad_latent_ref,
            )


def later_tick(tick, works, level, incoming, saved_inputs, first, second, latents, slopes, inverses, dep):
    _, _, rows, width = saved_inputs.shape
    rank = first.shape[1] // 2
    narrow = pl.BlockSpec((1, rows, rank), lambda i: (tick - 1, 0, 0))
    return pl.pallas_call(
        tick_kernel,
        grid=(1,),
        out_shape=[
            jax.ShapeDtypeStruct((rows, width), BF16),
            jax.ShapeDtypeStruct((rows, rank), BF16),
        ],
        in_specs=[
            SCALAR,
            IN_VMEM,
            pl.BlockSpec((1, 1, rows, width), lambda i: (tick, 0, 0, 0)),
            IN_VMEM,
            IN_VMEM,
            narrow,
            narrow,
            narrow,
            ANYWHERE,
        ],
        out_specs=[IN_VMEM] * 2,
        compiler_params=LIMIT,
        cost_estimate=pl.CostEstimate(flops=4 * rows * width * rank, bytes_accessed=3 * 2 * rows * width, transcendentals=0),
        name="later_tick",
    )(
        jnp.stack([works.astype(jnp.int32), level.astype(jnp.int32)]),
        incoming,
        saved_inputs,
        first,
        second,
        latents,
        slopes,
        inverses,
        dep,
    )


def turned(block):
    share, rank = block.shape
    room = -(-share // 128) * 128
    if room != share:
        block = jnp.concatenate([block, jnp.zeros((room - share, rank), block.dtype)], axis=0)
    return block.T[:, :share]


def finish_one_kernel(moved_ref, down_ref, up_ref):
    rank = down_ref.shape[1]
    total = jnp.sum(moved_ref[...].astype(F32), axis=0)
    down_ref[0] = jnp.zeros(down_ref.shape[1:], F32)
    up_ref[0] = jnp.zeros(up_ref.shape[1:], F32)
    down_ref[1] = turned(total[:, :rank])
    up_ref[1] = turned(total[:, rank:])


def finish_two_kernel(mine_ref, other_ref, down_ref, up_ref):
    rank = down_ref.shape[1]
    total = mine_ref[...] + other_ref[...].astype(F32)
    for i, out in enumerate((down_ref, up_ref)):
        for j, level in enumerate((1, 0)):
            at = (2 * i + j) * rank
            out[level] = turned(total[:, at : at + rank])


def finish(kernel, rank, share, *args):
    made = jax.ShapeDtypeStruct((2, rank, share), F32)
    return pl.pallas_call(
        kernel,
        out_shape=[made, made],
        in_specs=[IN_VMEM] * len(args),
        out_specs=[IN_VMEM] * 2,
        compiler_params=LIMIT,
        name="finish_sums",
    )(*args)


def on_device(saved_inputs, grad_in, adapter_down, adapter_up):
    n_sec = lax.axis_size("section")
    n_dp = lax.axis_size("dp")
    n_z = n_dp // 2
    position = lax.axis_index("section")
    ticks = saved_inputs.shape[0]
    rank, share = adapter_down.shape[2], adapter_down.shape[3]
    width = saved_inputs.shape[3]
    even = position % 2 == 0
    two_layers = position + ticks - 1 >= n_sec
    levels = [1 - (position + tick) // n_sec for tick in range(ticks)]

    def gather_two(down, up):
        shard = jnp.concatenate([down[1].T, up[1].T, down[0].T, up[0].T], axis=1)
        first, second = ring_gather(shard, n_z)
        return first.reshape(width, 2 * rank), second.reshape(width, 2 * rank)

    def gather_one(down, up):
        shard = jnp.concatenate([down[1].T, up[1].T], axis=1)
        copies = jnp.broadcast_to(shard[None], (n_dp,) + shard.shape)
        full = lax.all_to_all(copies, "dp", 0, 0, tiled=True)
        full = full.reshape(width, 2 * rank)
        return full, unset(full.shape, full.dtype)

    first, second = lax.cond(
        two_layers, gather_two, gather_one, adapter_down[:, 0], adapter_up[:, 0]
    )

    sent, grad_latent, active, normed = first_tick(saved_inputs, grad_in[0], first)
    level_stack = jnp.stack(levels).astype(jnp.int32)
    normeds, actives, latents, slopes, inverses = forward_rest(
        level_stack, saved_inputs, first, second, grad_latent
    )

    inside = [(s, s - 1) for s in range(1, n_sec, 2)]
    across = [(s, (s - 1) % n_sec) for s in range(0, n_sec, 2)]

    grads = [grad_in[0]]
    grad_latents = [grad_latent]
    over = lax.ppermute(sent, "section", across)
    core = lax.ppermute(sent, "section", inside)
    for tick in range(1, ticks):

        def layer(works, incoming, dep):
            return later_tick(
                tick,
                works,
                levels[tick],
                incoming,
                saved_inputs,
                first,
                second,
                latents,
                slopes,
                inverses,
                dep,
            )

        sent_even, latent_even = layer(even, core, normeds)
        next_over = lax.ppermute(sent_even, "section", across)
        sent_odd, latent_odd = layer(~even, over, latent_even)
        next_core = lax.ppermute(sent_odd, "section", inside)
        grads.append(jnp.where(even, core, over))
        grad_latents.append(jnp.where(even, latent_even, latent_odd))
        over, core = next_over, next_core

    normed_all = jnp.concatenate([normed[None], normeds], axis=0).reshape(-1, width)
    grads_all = jnp.concatenate(grads, axis=0)
    actives_all = jnp.concatenate([active[None], actives], axis=0)

    def products(lats, acts):
        contract = (((0,), (0,)), ((), ()))
        down = lax.dot_general(normed_all, lats, contract, preferred_element_type=F32)
        up = lax.dot_general(grads_all, acts, contract, preferred_element_type=F32)
        return jnp.concatenate([down.astype(BF16), up.astype(BF16)], axis=1)

    def reduce_one(lats, acts):
        parts = products(lats.reshape(-1, rank), acts.reshape(-1, rank))
        moved = lax.all_to_all(parts.reshape(n_dp, share, 2 * rank), "dp", 0, 0, tiled=True)
        return finish(finish_one_kernel, rank, share, moved)

    def reduce_two(lats, acts):
        level = level_stack[:, None, None]
        zero = jnp.zeros((), BF16)

        def split(value):
            both = [jnp.where(level == 1, value, zero), jnp.where(level == 0, value, zero)]
            return jnp.concatenate(both, axis=2).reshape(-1, 2 * rank)

        parts = products(split(lats), split(acts))
        mine, other = ring_reduce(parts.reshape(n_z, 2, share, 4 * rank), n_z)
        return finish(finish_two_kernel, rank, share, mine, other)

    down_grad, up_grad = lax.cond(
        two_layers, reduce_two, reduce_one, jnp.stack(grad_latents), actives_all
    )
    grad_out = jnp.where(even, core, over)
    return grad_out[None], down_grad[:, None], up_grad[:, None]


def solution(mesh):
    in_specs = (
        P(None, "section", "dp", None),
        P("section", "dp", None),
        P(None, "section", None, "dp"),
        P(None, "section", None, "dp"),
    )
    out_specs = (
        P("section", "dp", None),
        P(None, "section", None, "dp"),
        P(None, "section", None, "dp"),
    )
    return jax.shard_map(
        on_device, mesh=mesh, in_specs=in_specs, out_specs=out_specs, check_vma=False
    )
```

time: 221 us -> 223 us (level)
  the two profiles are of different devices: /device:TPU:63 before, /device:TPU:62 now
where the time goes in v2:
time: 223 us; the launch traced here: 222 us
  starting transfers between devices  84.6 us (38%)
  waiting for transfers between devices  72.4 us (32%)
  Pallas kernels  21.2 us (10%)
  local copies, waits for them, and re-layouts  20.2 us (9%)
  other arithmetic  16.5 us (7%)
  matrix products  5.2 us (2%)
    ppermute x16, starting transfers between devices, shifted(): return lax.ppermute(value, 'dp', dp_pairs(n_z, step, 0))  59.2 us
    ppermute x16, waiting for transfers between devices, shifted(): return lax.ppermute(value, 'dp', dp_pairs(n_z, step, 0))  45.6 us
    ppermute x2, waiting for transfers between devices, swapped(): return lax.ppermute(value, 'dp', dp_pairs(n_z, 0, 1))  14.3 us
    cond x32, local copies, waits for them, and re-layouts  12.9 us
    pallas_call x6, Pallas kernels, later_tick(): pl.pallas_call(tick_kernel, grid=(1,), out_shape=[jax.ShapeDtypeStruct((r...  11.6 us
    ppermute x3, waiting for transfers between devices, on_device(): next_core = lax.ppermute(sent_odd, 'section', inside)  8.33 us
    ppermute x2, starting transfers between devices, swapped(): return lax.ppermute(value, 'dp', dp_pairs(n_z, 0, 1))  7.85 us
    ppermute x3, starting transfers between devices, on_device(): next_over = lax.ppermute(sent_even, 'section', across)  6.63 us
  transfers between devices with their start and end apart: 26, of which 17 were waited for; matrix products, arithmetic and copies ran while one was open for 11% of the time, Pallas kernels for 5%

profile of v2, /device:TPU:62, one launch (start us, length us, event | category | flops | bytes accessed | tf_op | source)
XLA Modules:
  0.0 221.6 jit_solution(11696354285920351441)
XLA Ops:
  0.7 76.2 %conditional.2 = (bf16[2560,256]{1,0:T(8,128)(2,1)}, bf16[2560,256]{1,0:T(8,128)(2,1)}) conditional(s32[]{:T(128)} %convert_element_type.46, (bf16[2,128,160]{1,2,0:T(8,128)(2,1)}, bf16[2,128,160]{1,2,0:T(8,128)(2,1)}) %tuple.65, (bf16[2,128,160]{1,2,0:T(8,128)(2,1)}, bf16[2,128,160]{1,2,0:T(8,128)(2,1)}) %tuple.66), branch_computations={%region_0.1_spmd, %region_1.2_spmd} | conditional | flops 1638422 | bytes 30802904 | solution.py:329
  2.4 4.7 %collective-permute-start = (bf16[160,512]{1,0:T(8,128)(2,1)}, bf16[160,512]{1,0:T(8,128)(2,1)}, u32[]{:S(2)}, u32[]{:S(2)}) collective-permute-start(bf16[160,512]{1,0:T(8,128)(2,1)} %pad_maximum_fusion.2), channel_id=1, source_target_pairs={{0,1},{1,0},{2,3},{3,2},{4,5},{5,4},{6,7},{7,6},{8,9},{9,8},{10,11... | collective-permute-start | bytes 491528 | tf_op jit(solution)/shard_map/cond/branch_1_fun/ppermute | solution.py:30
  7.1 7.3 %collective-permute-done = bf16[160,512]{1,0:T(8,128)(2,1)} collective-permute-done((bf16[160,512]{1,0:T(8,128)(2,1)}, bf16[160,512]{1,0:T(8,128)(2,1)}, u32[]{:S(2)}, u32[]{:S(2)}) %collective-permute-start) | collective-permute-done | bytes 163872 | tf_op jit(solution)/shard_map/cond/branch_1_fun/ppermute | solution.py:30
  15.5 4.3 %collective-permute-start.1 = (bf16[2,160,512]{2,1,0:T(8,128)(2,1)S(1)}, bf16[2,160,512]{2,1,0:T(8,128)(2,1)S(1)}, u32[]{:S(2)}, u32[]{:S(2)}) collective-permute-start(bf16[2,160,512]{2,1,0:T(8,128)(2,1)S(1)} %pad_maximum_fusion.1.refs_0_), channel_id=1, source_target_pairs={{0,2},{1,3},{2,4},{3,5},{4,6},{5,7},{6,8},{7,9},{8,10},{9,11},{10,... | collective-permute-start | bytes 983048 | tf_op jit(solution)/shard_map/cond/branch_1_fun/ppermute | solution.py:26
  19.7 8.6 %collective-permute-start.4 = (bf16[2,160,512]{2,1,0:T(8,128)(2,1)S(1)}, bf16[2,160,512]{2,1,0:T(8,128)(2,1)S(1)}, u32[]{:S(2)}, u32[]{:S(2)}) collective-permute-start(bf16[2,160,512]{2,1,0:T(8,128)(2,1)S(1)} %pad_maximum_fusion.1.refs_0_), channel_id=1, source_target_pairs={{0,14},{1,15},{2,0},{3,1},{4,2},{5,3},{6,4},{7,5},{8,6},{9,7},{10,... | collective-permute-start | bytes 983048 | tf_op jit(solution)/shard_map/cond/branch_1_fun/ppermute | solution.py:26
  29.1 4.2 %collective-permute-done.1.refs_1_ = bf16[2,160,512]{2,1,0:T(8,128)(2,1)S(1)} collective-permute-done((bf16[2,160,512]{2,1,0:T(8,128)(2,1)S(1)}, bf16[2,160,512]{2,1,0:T(8,128)(2,1)S(1)}, u32[]{:S(2)}, u32[]{:S(2)}) %collective-permute-start.1) | collective-permute-done | bytes 327712 | tf_op jit(solution)/shard_map/cond/branch_1_fun/ppermute | solution.py:26
  35.9 5.1 %collective-permute-start.5 = (bf16[2,160,512]{2,1,0:T(8,128)(2,1)S(1)}, bf16[2,160,512]{2,1,0:T(8,128)(2,1)S(1)}, u32[]{:S(2)}, u32[]{:S(2)}) collective-permute-start(bf16[2,160,512]{2,1,0:T(8,128)(2,1)S(1)} %collective-permute-done.4.refs_4_), channel_id=1, source_target_pairs={{0,14},{1,15},{2,0},{3,1},{4,2},{5,3},{6,4},{7,5},{8,6},{9,7},{10,... | collective-permute-start | bytes 983048 | tf_op jit(solution)/shard_map/cond/branch_1_fun/ppermute | solution.py:26
  41.8 2.5 %collective-permute-done.2.refs_2_ = bf16[2,160,512]{2,1,0:T(8,128)(2,1)S(1)} collective-permute-done((bf16[2,160,512]{2,1,0:T(8,128)(2,1)S(1)}, bf16[2,160,512]{2,1,0:T(8,128)(2,1)S(1)}, u32[]{:S(2)}, u32[]{:S(2)}) %collective-permute-start.2) | collective-permute-done | bytes 327712 | tf_op jit(solution)/shard_map/cond/branch_1_fun/ppermute | solution.py:26
  46.2 5.6 %collective-permute-start.6 = (bf16[2,160,512]{2,1,0:T(8,128)(2,1)S(1)}, bf16[2,160,512]{2,1,0:T(8,128)(2,1)S(1)}, u32[]{:S(2)}, u32[]{:S(2)}) collective-permute-start(bf16[2,160,512]{2,1,0:T(8,128)(2,1)S(1)} %collective-permute-done.5.refs_5_), channel_id=1, source_target_pairs={{0,14},{1,15},{2,0},{3,1},{4,2},{5,3},{6,4},{7,5},{8,6},{9,7},{10,... | collective-permute-start | bytes 983048 | tf_op jit(solution)/shard_map/cond/branch_1_fun/ppermute | solution.py:26
  52.5 1.9 collective-permute-done.3.refs_3_
  59.2 5.1 %collective-permute-start.8 = (bf16[1,160,512]{2,1,0:T(8,128)(2,1)}, bf16[1,160,512]{2,1,0:T(8,128)(2,1)}, u32[]{:S(2)}, u32[]{:S(2)}) collective-permute-start(bf16[1,160,512]{2,1,0:T(8,128)(2,1)} %slice.63), channel_id=1, source_target_pairs={{0,14},{1,15},{2,0},{3,1},{4,2},{5,3},{6,4},{7,5},{8,6},{9,7},{10,... | collective-permute-start | bytes 491528 | tf_op jit(solution)/shard_map/cond/branch_1_fun/ppermute | solution.py:26
  64.5 3.0 %collective-permute-done.8.refs_8_ = bf16[1,160,512]{2,1,0:T(8,128)(2,1)} collective-permute-done((bf16[1,160,512]{2,1,0:T(8,128)(2,1)}, bf16[1,160,512]{2,1,0:T(8,128)(2,1)}, u32[]{:S(2)}, u32[]{:S(2)}) %collective-permute-start.8) | collective-permute-done | bytes 163872 | tf_op jit(solution)/shard_map/cond/branch_1_fun/ppermute | solution.py:26
  74.3 2.6 %place_maps.1 = (bf16[16,160,256]{2,1,0:T(8,128)(2,1)}, bf16[16,160,256]{2,1,0:T(8,128)(2,1)}) custom-call(s32[1]{0:T(128)} %bitcast.5.place_ref, bf16[2,160,512]{2,1,0:T(8,128)(2,1)S(1)} %copy-done.4, bf16[2,160,512]{2,1,0:T(8,128)(2,1)S(1)} %copy-done.12, bf16[2,160,512]{2,1,0:T(8,128)(2,1)S(1)} %copy-done.16, bf16[2,160,512]{2,1,0:T(8,128)(2,1)S(1)} %copy-done.6, ...), custom_call_target="tpu_custom_call" | custom-call | tf_op jit(solution)/shard_map/cond/branch_1_fun/place_maps/pallas_call | solution.py:63
  76.8 3.3 %first_tick.1 = (bf16[128,2560]{1,0:T(8,128)(2,1)}, bf16[128,128]{1,0:T(8,128)(2,1)S(1)}, bf16[128,128]{1,0:T(8,128)(2,1)S(1)}, bf16[128,2560]{1,0:T(8,128)(2,1)S(1)}) custom-call(bf16[4,1,128,2560]{3,2,1,0:T(8,128)(2,1)S(1)} %copy-done, bf16[128,2560]{1,0:T(8,128)(2,1)S(1)} %bitcast.106, bf16[2560,256]{1,0:T(8,128)(2,1)} %get-tuple-element.85.map_ref.first_ref), custom_call_target="tpu_custom_call" | custom-call | flops 251658240 | bytes 2621440 | tf_op jit(solution)/shard_map/first_tick/pallas_call | solution.py:151
  81.0 5.7 %collective-permute-start.18 = (bf16[128,2560]{1,0:T(8,128)(2,1)}, bf16[128,2560]{1,0:T(8,128)(2,1)}, u32[]{:S(2)}, u32[]{:S(2)}) collective-permute-start(bf16[128,2560]{1,0:T(8,128)(2,1)} %get-tuple-element.86), channel_id=1, source_target_pairs={{0,496},{32,16},{64,48},{96,80},{128,112},{160,144},{192,176},{224... | collective-permute-start | bytes 1966088 | tf_op jit(solution)/shard_map/ppermute | solution.py:344
  88.4 3.6 %forward_rest.1 = (bf16[3,128,2560]{2,1,0:T(8,128)(2,1)S(1)}, bf16[3,128,128]{2,1,0:T(8,128)(2,1)S(1)}, f32[3,128,128]{2,1,0:T(8,128)S(1)}, f32[3,128,128]{2,1,0:T(8,128)S(1)}, f32[3,128,128]{2,1,0:T(8,128)S(1)}) custom-call(s32[4]{0:T(128)S(1)} %pad_add_fusion.level_ref, bf16[4,1,128,2560]{3,2,1,0:T(8,128)(2,1)S(1)} %copy-done, ...), custom_call_target="tpu_custom_call" | custom-call | flops 251658240 | bytes 3932160 | tf_op jit(solution)/shard_map/forward_rest/pallas_call | solution.py:193
  93.8 2.1 later_tick.6
  98.8 2.9 %collective-permute-start.22 = (bf16[128,2560]{1,0:T(8,128)(2,1)S(1)}, bf16[128,2560]{1,0:T(8,128)(2,1)S(1)}, u32[]{:S(2)}, u32[]{:S(2)}) collective-permute-start(bf16[128,2560]{1,0:T(8,128)(2,1)S(1)} %get-tuple-element.96), channel_id=1, source_target_pairs={{0,496},{32,16},{64,48},{96,80},{128,112},{160,144},{192,176},{224... | collective-permute-start | bytes 1966088 | tf_op jit(solution)/shard_map/ppermute | solution.py:364
  101.8 2.1 later_tick.8
  105.5 4.2 %collective-permute-done.22.incoming_ref = bf16[128,2560]{1,0:T(8,128)(2,1)S(1)} collective-permute-done((bf16[128,2560]{1,0:T(8,128)(2,1)S(1)}, bf16[128,2560]{1,0:T(8,128)(2,1)S(1)}, u32[]{:S(2)}, u32[]{:S(2)}) %collective-permute-start.22) | collective-permute-done | bytes 655392 | tf_op jit(solution)/shard_map/ppermute | solution.py:364
  112.5 8.3 %collective-permute-done.23.incoming_ref = bf16[128,2560]{1,0:T(8,128)(2,1)S(1)} collective-permute-done((bf16[128,2560]{1,0:T(8,128)(2,1)S(1)}, bf16[128,2560]{1,0:T(8,128)(2,1)S(1)}, u32[]{:S(2)}, u32[]{:S(2)}) %collective-permute-start.23) | collective-permute-done | bytes 655392 | tf_op jit(solution)/shard_map/ppermute | solution.py:366
  120.8 2.3 %later_tick.10 = (bf16[128,2560]{1,0:T(8,128)(2,1)S(1)}, bf16[128,128]{1,0:T(8,128)(2,1)S(1)}) custom-call(s32[2]{0:T(128)S(1)} %pad_add_fusion.1.flags_ref, bf16[128,2560]{1,0:T(8,128)(2,1)S(1)} %collective-permute-done.23.incoming_ref, bf16[4,1,128,2560]{3,2,1,0:T(8,128)(2,1)S(1)} %copy-done, bf16[2560,256]{1,0:T(8,128)(2,1)} %get-tuple-element.85.map_ref.first_ref, ...), custom_call_target="tpu_custom_call" | custom-call | flops 167772160 | bytes 1966080 | tf_op jit(solution)/shard_map/later_tick/pallas_call | solution.py:232
  123.1 2.2 later_tick.11
  126.7 2.1 collective-permute-start.25
  130.6 88.8 %conditional.3 = (f32[2,1,128,160]{2,3,1,0:T(8,128)}, f32[2,1,128,160]{2,3,1,0:T(8,128)S(1)}) conditional(s32[]{:T(128)} %convert_element_type.46, (bf16[4,128,128]{2,1,0:T(8,128)(2,1)S(1)}, bf16[512,2560]{1,0:T(8,128)(2,1)}, bf16[4,128,128]{2,1,0:T(8,128)(2,1)S(1)}, bf16[512,2560]{1,0:T(8,128)(2,1)}) %tuple.32, (s32[4]{0:T(128)S(1)}, ...), branch_computations={%region_2.3_spmd, %region_3.4_spmd} | conditional | flops 1352007680 | bytes 43976608 | solution.py:398
  130.8 2.6 %fusion.1 = bf16[2560,256]{0,1:T(8,128)(2,1)S(1)} fusion(bf16[512,256]{1,0:T(8,128)(2,1)S(1)} %bitcast.125, bf16[512,2560]{1,0:T(8,128)(2,1)} %get-tuple-element.48), kind=kOutput, calls=%fused_computation.17 | convolution fusion | flops 671744000 | bytes 4194304 | tf_op jit(solution)/shard_map/cond/branch_1_fun/dot_general | solution.py:378
  133.4 2.6 %fusion = bf16[2560,256]{0,1:T(8,128)(2,1)S(1)} fusion(bf16[512,256]{1,0:T(8,128)(2,1)S(1)} %bitcast.124, bf16[512,2560]{1,0:T(8,128)(2,1)} %get-tuple-element.46), kind=kOutput, calls=%fused_computation.16 | convolution fusion | flops 671744000 | bytes 4194304 | tf_op jit(solution)/shard_map/cond/branch_1_fun/dot_general | solution.py:377
  137.8 3.0 %copy.9 = bf16[2560,512]{1,0:T(8,128)(2,1)S(1)} copy(bf16[2560,512]{0,1:T(8,128)(2,1)} %pad_maximum_fusion.4) | data formatting | bytes 5242880 | tf_op jit(solution)/shard_map/cond/branch_1_fun/concatenate | solution.py:379
  140.9 5.3 %collective-permute-start.10 = (bf16[1,160,512]{2,1,0:T(8,128)(2,1)S(1)}, bf16[1,160,512]{2,1,0:T(8,128)(2,1)S(1)}, u32[]{:S(2)}, u32[]{:S(2)}) collective-permute-start(bf16[1,160,512]{2,1,0:T(8,128)(2,1)S(1)} %get-tuple-element.133), channel_id=1, source_target_pairs={{0,14},{1,15},{2,0},{3,1},{4,2},{5,3},{6,4},{7,5},{8,6},{9,7},{10,... | collective-permute-start | bytes 491528 | tf_op jit(solution)/shard_map/cond/branch_1_fun/ppermute | solution.py:26
  146.2 1.9 collective-permute-start.9
  148.1 2.5 %collective-permute-done.10 = bf16[1,160,512]{2,1,0:T(8,128)(2,1)S(1)} collective-permute-done((bf16[1,160,512]{2,1,0:T(8,128)(2,1)S(1)}, bf16[1,160,512]{2,1,0:T(8,128)(2,1)S(1)}, u32[]{:S(2)}, u32[]{:S(2)}) %collective-permute-start.10) | collective-permute-done | bytes 163872 | tf_op jit(solution)/shard_map/cond/branch_1_fun/ppermute | solution.py:26
  150.5 5.7 %collective-permute-done.9 = bf16[1,160,512]{2,1,0:T(8,128)(2,1)S(1)} collective-permute-done((bf16[1,160,512]{2,1,0:T(8,128)(2,1)S(1)}, bf16[1,160,512]{2,1,0:T(8,128)(2,1)S(1)}, u32[]{:S(2)}, u32[]{:S(2)}) %collective-permute-start.9) | collective-permute-done | bytes 163872 | tf_op jit(solution)/shard_map/cond/branch_1_fun/ppermute | solution.py:26
  157.8 1.9 collective-permute-start.12
  159.7 3.9 %collective-permute-start.11 = (bf16[2,160,512]{2,1,0:T(8,128)(2,1)}, bf16[2,160,512]{2,1,0:T(8,128)(2,1)}, u32[]{:S(2)}, u32[]{:S(2)}) collective-permute-start(bf16[2,160,512]{2,1,0:T(8,128)(2,1)} %pad_maximum_fusion.5), channel_id=1, source_target_pairs={{0,2},{1,3},{2,4},{3,5},{4,6},{5,7},{6,8},{7,9},{8,10},{9,11},{10,... | collective-permute-start | bytes 983048 | tf_op jit(solution)/shard_map/cond/branch_1_fun/ppermute | solution.py:26
  163.7 5.9 %collective-permute-done.12 = bf16[2,160,512]{2,1,0:T(8,128)(2,1)} collective-permute-done((bf16[2,160,512]{2,1,0:T(8,128)(2,1)}, bf16[2,160,512]{2,1,0:T(8,128)(2,1)}, u32[]{:S(2)}, u32[]{:S(2)}) %collective-permute-start.12) | collective-permute-done | bytes 327712 | tf_op jit(solution)/shard_map/cond/branch_1_fun/ppermute | solution.py:26
  169.6 3.1 %collective-permute-done.11 = bf16[2,160,512]{2,1,0:T(8,128)(2,1)} collective-permute-done((bf16[2,160,512]{2,1,0:T(8,128)(2,1)}, bf16[2,160,512]{2,1,0:T(8,128)(2,1)}, u32[]{:S(2)}, u32[]{:S(2)}) %collective-permute-start.11) | collective-permute-done | bytes 327712 | tf_op jit(solution)/shard_map/cond/branch_1_fun/ppermute | solution.py:26
  172.8 2.0 bitcast_add_fusion.1
  176.7 3.9 %collective-permute-start.13 = (bf16[2,160,512]{2,1,0:T(8,128)(2,1)}, bf16[2,160,512]{2,1,0:T(8,128)(2,1)}, u32[]{:S(2)}, u32[]{:S(2)}) collective-permute-start(bf16[2,160,512]{2,1,0:T(8,128)(2,1)} %get-tuple-element.51), channel_id=1, source_target_pairs={{0,2},{1,3},{2,4},{3,5},{4,6},{5,7},{6,8},{7,9},{8,10},{9,11},{10,... | collective-permute-start | bytes 983048 | tf_op jit(solution)/shard_map/cond/branch_1_fun/ppermute | solution.py:26
  180.7 5.1 %collective-permute-done.14 = bf16[2,160,512]{2,1,0:T(8,128)(2,1)} collective-permute-done((bf16[2,160,512]{2,1,0:T(8,128)(2,1)}, bf16[2,160,512]{2,1,0:T(8,128)(2,1)}, u32[]{:S(2)}, u32[]{:S(2)}) %collective-permute-start.14) | collective-permute-done | bytes 327712 | tf_op jit(solution)/shard_map/cond/branch_1_fun/ppermute | solution.py:26
  185.8 3.1 %collective-permute-done.13 = bf16[2,160,512]{2,1,0:T(8,128)(2,1)} collective-permute-done((bf16[2,160,512]{2,1,0:T(8,128)(2,1)}, bf16[2,160,512]{2,1,0:T(8,128)(2,1)}, u32[]{:S(2)}, u32[]{:S(2)}) %collective-permute-start.13) | collective-permute-done | bytes 327712 | tf_op jit(solution)/shard_map/cond/branch_1_fun/ppermute | solution.py:26
  188.9 2.0 bitcast_add_fusion
  190.9 3.5 %collective-permute-start.16 = (bf16[2,160,512]{2,1,0:T(8,128)(2,1)}, bf16[2,160,512]{2,1,0:T(8,128)(2,1)}, u32[]{:S(2)}, u32[]{:S(2)}) collective-permute-start(bf16[2,160,512]{2,1,0:T(8,128)(2,1)} %get-tuple-element.54), channel_id=1, source_target_pairs={{0,14},{1,15},{2,0},{3,1},{4,2},{5,3},{6,4},{7,5},{8,6},{9,7},{10,... | collective-permute-start | bytes 983048 | tf_op jit(solution)/shard_map/cond/branch_1_fun/ppermute | solution.py:26
  194.4 2.3 %collective-permute-start.15 = (bf16[2,160,512]{2,1,0:T(8,128)(2,1)}, bf16[2,160,512]{2,1,0:T(8,128)(2,1)}, u32[]{:S(2)}, u32[]{:S(2)}) collective-permute-start(bf16[2,160,512]{2,1,0:T(8,128)(2,1)} %get-tuple-element.53), channel_id=1, source_target_pairs={{0,2},{1,3},{2,4},{3,5},{4,6},{5,7},{6,8},{7,9},{8,10},{9,11},{10,... | collective-permute-start | bytes 983048 | tf_op jit(solution)/shard_map/cond/branch_1_fun/ppermute | solution.py:26
  196.8 4.2 %collective-permute-done.16 = bf16[2,160,512]{2,1,0:T(8,128)(2,1)} collective-permute-done((bf16[2,160,512]{2,1,0:T(8,128)(2,1)}, bf16[2,160,512]{2,1,0:T(8,128)(2,1)}, u32[]{:S(2)}, u32[]{:S(2)}) %collective-permute-start.16) | collective-permute-done | bytes 327712 | tf_op jit(solution)/shard_map/cond/branch_1_fun/ppermute | solution.py:26
  200.9 4.2 %collective-permute-done.15 = bf16[2,160,512]{2,1,0:T(8,128)(2,1)} collective-permute-done((bf16[2,160,512]{2,1,0:T(8,128)(2,1)}, bf16[2,160,512]{2,1,0:T(8,128)(2,1)}, u32[]{:S(2)}, u32[]{:S(2)}) %collective-permute-start.15) | collective-permute-done | bytes 327712 | tf_op jit(solution)/shard_map/cond/branch_1_fun/ppermute | solution.py:26
  207.2 3.1 %collective-permute-start.17 = (bf16[160,512]{1,0:T(8,128)(2,1)S(1)}, bf16[160,512]{1,0:T(8,128)(2,1)S(1)}, u32[]{:S(2)}, u32[]{:S(2)}) collective-permute-start(bf16[160,512]{1,0:T(8,128)(2,1)S(1)} %fusion.3), channel_id=1, source_target_pairs={{0,1},{1,0},{2,3},{3,2},{4,5},{5,4},{6,7},{7,6},{8,9},{9,8},{10,11... | collective-permute-start | bytes 491528 | tf_op jit(solution)/shard_map/cond/branch_1_fun/ppermute | solution.py:30
  211.4 7.0 %collective-permute-done.17.other_ref = bf16[160,512]{1,0:T(8,128)(2,1)S(1)} collective-permute-done((bf16[160,512]{1,0:T(8,128)(2,1)S(1)}, bf16[160,512]{1,0:T(8,128)(2,1)S(1)}, u32[]{:S(2)}, u32[]{:S(2)}) %collective-permute-start.17) | collective-permute-done | bytes 163872 | tf_op jit(solution)/shard_map/cond/branch_1_fun/ppermute | solution.py:30
  219.5 2.0 select_bitcast_fusion.2
  (102 shorter events, 45.5 us)
Async XLA Ops:
  0.6 76.2 %copy-start = (bf16[4,1,128,2560]{3,2,1,0:T(8,128)(2,1)S(1)}, bf16[4,1,128,2560]{3,2,1,0:T(8,128)(2,1)}, u32[]{:S(2)}) copy-start(bf16[4,1,128,2560]{3,2,1,0:T(8,128)(2,1)} %x_ref.15) | copy-start | bytes 7864324
  0.6 76.2 %copy-start.1 = (bf16[1,128,2560]{2,1,0:T(8,128)(2,1)S(1)}, bf16[1,128,2560]{2,1,0:T(8,128)(2,1)}, u32[]{:S(2)}) copy-start(bf16[1,128,2560]{2,1,0:T(8,128)(2,1)} %param.9) | copy-start | bytes 1966084
  2.4 12.0 %collective-permute-start = (bf16[160,512]{1,0:T(8,128)(2,1)}, bf16[160,512]{1,0:T(8,128)(2,1)}, u32[]{:S(2)}, u32[]{:S(2)}) collective-permute-start(bf16[160,512]{1,0:T(8,128)(2,1)} %pad_maximum_fusion.2), channel_id=1, source_target_pairs={{0,1},{1,0},{2,3},{3,2},{4,5},{5,4},{6,7},{7,6},{8,9},{9,8},{10,11... | collective-permute-start | bytes 491528 | tf_op jit(solution)/shard_map/cond/branch_1_fun/ppermute | solution.py:30
  15.5 17.8 %collective-permute-start.1 = (bf16[2,160,512]{2,1,0:T(8,128)(2,1)S(1)}, bf16[2,160,512]{2,1,0:T(8,128)(2,1)S(1)}, u32[]{:S(2)}, u32[]{:S(2)}) collective-permute-start(bf16[2,160,512]{2,1,0:T(8,128)(2,1)S(1)} %pad_maximum_fusion.1.refs_0_), channel_id=1, source_target_pairs={{0,2},{1,3},{2,4},{3,5},{4,6},{5,7},{6,8},{7,9},{8,10},{9,11},{10,... | collective-permute-start | bytes 983048 | tf_op jit(solution)/shard_map/cond/branch_1_fun/ppermute | solution.py:26
  19.7 16.2 %collective-permute-start.4 = (bf16[2,160,512]{2,1,0:T(8,128)(2,1)S(1)}, bf16[2,160,512]{2,1,0:T(8,128)(2,1)S(1)}, u32[]{:S(2)}, u32[]{:S(2)}) collective-permute-start(bf16[2,160,512]{2,1,0:T(8,128)(2,1)S(1)} %pad_maximum_fusion.1.refs_0_), channel_id=1, source_target_pairs={{0,14},{1,15},{2,0},{3,1},{4,2},{5,3},{6,4},{7,5},{8,6},{9,7},{10,... | collective-permute-start | bytes 983048 | tf_op jit(solution)/shard_map/cond/branch_1_fun/ppermute | solution.py:26
  28.3 0.7 copy-start.3
  33.2 11.0 %collective-permute-start.2 = (bf16[2,160,512]{2,1,0:T(8,128)(2,1)S(1)}, bf16[2,160,512]{2,1,0:T(8,128)(2,1)S(1)}, u32[]{:S(2)}, u32[]{:S(2)}) collective-permute-start(bf16[2,160,512]{2,1,0:T(8,128)(2,1)S(1)} %collective-permute-done.1.refs_1_), channel_id=1, source_target_pairs={{0,2},{1,3},{2,4},{3,5},{4,6},{5,7},{6,8},{7,9},{8,10},{9,11},{10,... | collective-permute-start | bytes 983048 | tf_op jit(solution)/shard_map/cond/branch_1_fun/ppermute | solution.py:26
  35.1 0.7 copy-start.11
  35.9 10.3 %collective-permute-start.5 = (bf16[2,160,512]{2,1,0:T(8,128)(2,1)S(1)}, bf16[2,160,512]{2,1,0:T(8,128)(2,1)S(1)}, u32[]{:S(2)}, u32[]{:S(2)}) collective-permute-start(bf16[2,160,512]{2,1,0:T(8,128)(2,1)S(1)} %collective-permute-done.4.refs_4_), channel_id=1, source_target_pairs={{0,14},{1,15},{2,0},{3,1},{4,2},{5,3},{6,4},{7,5},{8,6},{9,7},{10,... | collective-permute-start | bytes 983048 | tf_op jit(solution)/shard_map/cond/branch_1_fun/ppermute | solution.py:26
  41.0 0.7 copy-start.13
  44.2 14.2 %copy-start.15 = (bf16[2,160,512]{2,1,0:T(8,128)(2,1)}, bf16[2,160,512]{2,1,0:T(8,128)(2,1)S(1)}, u32[]{:S(2)}) copy-start(bf16[2,160,512]{2,1,0:T(8,128)(2,1)S(1)} %collective-permute-done.2.refs_2_) | copy-start | bytes 983044 | tf_op jit(solution)/shard_map/cond
  44.3 10.2 %collective-permute-start.3 = (bf16[2,160,512]{2,1,0:T(8,128)(2,1)S(1)}, bf16[2,160,512]{2,1,0:T(8,128)(2,1)S(1)}, u32[]{:S(2)}, u32[]{:S(2)}) collective-permute-start(bf16[2,160,512]{2,1,0:T(8,128)(2,1)S(1)} %collective-permute-done.2.refs_2_), channel_id=1, source_target_pairs={{0,2},{1,3},{2,4},{3,5},{4,6},{5,7},{6,8},{7,9},{8,10},{9,11},{10,... | collective-permute-start | bytes 983048 | tf_op jit(solution)/shard_map/cond/branch_1_fun/ppermute | solution.py:26
  46.2 11.6 %collective-permute-start.6 = (bf16[2,160,512]{2,1,0:T(8,128)(2,1)S(1)}, bf16[2,160,512]{2,1,0:T(8,128)(2,1)S(1)}, u32[]{:S(2)}, u32[]{:S(2)}) collective-permute-start(bf16[2,160,512]{2,1,0:T(8,128)(2,1)S(1)} %collective-permute-done.5.refs_5_), channel_id=1, source_target_pairs={{0,14},{1,15},{2,0},{3,1},{4,2},{5,3},{6,4},{7,5},{8,6},{9,7},{10,... | collective-permute-start | bytes 983048 | tf_op jit(solution)/shard_map/cond/branch_1_fun/ppermute | solution.py:26
  51.8 0.7 copy-start.17
  55.1 0.7 copy-start.5
  55.8 8.6 %collective-permute-start.7 = (bf16[1,160,512]{2,1,0:T(8,128)(2,1)}, bf16[1,160,512]{2,1,0:T(8,128)(2,1)S(1)}, u32[]{:S(2)}, u32[]{:S(2)}) collective-permute-start(bf16[1,160,512]{2,1,0:T(8,128)(2,1)} %slice.62), channel_id=1, source_target_pairs={{0,2},{1,3},{2,4},{3,5},{4,6},{5,7},{6,8},{7,9},{8,10},{9,11},{10,... | collective-permute-start | bytes 491528 | tf_op jit(solution)/shard_map/cond/branch_1_fun/ppermute | solution.py:26
  58.4 0.7 copy-start.7
  59.2 8.3 %collective-permute-start.8 = (bf16[1,160,512]{2,1,0:T(8,128)(2,1)}, bf16[1,160,512]{2,1,0:T(8,128)(2,1)}, u32[]{:S(2)}, u32[]{:S(2)}) collective-permute-start(bf16[1,160,512]{2,1,0:T(8,128)(2,1)} %slice.63), channel_id=1, source_target_pairs={{0,14},{1,15},{2,0},{3,1},{4,2},{5,3},{6,4},{7,5},{8,6},{9,7},{10,... | collective-permute-start | bytes 491528 | tf_op jit(solution)/shard_map/cond/branch_1_fun/ppermute | solution.py:26
  67.4 1.0 copy-start.4
  68.4 1.0 copy-start.6
  69.4 1.0 copy-start.8
  70.4 1.0 copy-start.12
  71.3 1.0 copy-start.14
  72.3 1.0 copy-start.16
  73.3 1.0 copy-start.18
  80.1 0.9 copy-start.9
  81.0 15.0 %collective-permute-start.18 = (bf16[128,2560]{1,0:T(8,128)(2,1)}, bf16[128,2560]{1,0:T(8,128)(2,1)}, u32[]{:S(2)}, u32[]{:S(2)}) collective-permute-start(bf16[128,2560]{1,0:T(8,128)(2,1)} %get-tuple-element.86), channel_id=1, source_target_pairs={{0,496},{32,16},{64,48},{96,80},{128,112},{160,144},{192,176},{224... | collective-permute-start | bytes 1966088 | tf_op jit(solution)/shard_map/ppermute | solution.py:344
  86.6 7.2 %collective-permute-start.19 = (bf16[128,2560]{1,0:T(8,128)(2,1)}, bf16[128,2560]{1,0:T(8,128)(2,1)S(1)}, u32[]{:S(2)}, u32[]{:S(2)}) collective-permute-start(bf16[128,2560]{1,0:T(8,128)(2,1)} %get-tuple-element.86), channel_id=1, source_target_pairs={{16,0},{48,32},{80,64},{112,96},{144,128},{176,160},{208,192},{240... | collective-permute-start | bytes 1966088 | tf_op jit(solution)/shard_map/ppermute | solution.py:345
  88.4 3.7 %copy-start.10 = (bf16[128,2560]{1,0:T(8,128)(2,1)S(1)}, bf16[128,2560]{1,0:T(8,128)(2,1)}, u32[]{:S(2)}) copy-start(bf16[128,2560]{1,0:T(8,128)(2,1)} %copy-done.9) | copy-start | bytes 1966084
  92.1 1.7 copy-start.19
  97.5 4.3 %collective-permute-start.20 = (bf16[128,2560]{1,0:T(8,128)(2,1)S(1)}, bf16[128,2560]{1,0:T(8,128)(2,1)S(1)}, u32[]{:S(2)}, u32[]{:S(2)}) collective-permute-start(bf16[128,2560]{1,0:T(8,128)(2,1)S(1)} %get-tuple-element.94), channel_id=1, source_target_pairs={{16,0},{48,32},{80,64},{112,96},{144,128},{176,160},{208,192},{240... | collective-permute-start | bytes 1966088 | tf_op jit(solution)/shard_map/ppermute | solution.py:366
  98.8 10.9 %collective-permute-start.22 = (bf16[128,2560]{1,0:T(8,128)(2,1)S(1)}, bf16[128,2560]{1,0:T(8,128)(2,1)S(1)}, u32[]{:S(2)}, u32[]{:S(2)}) collective-permute-start(bf16[128,2560]{1,0:T(8,128)(2,1)S(1)} %get-tuple-element.96), channel_id=1, source_target_pairs={{0,496},{32,16},{64,48},{96,80},{128,112},{160,144},{192,176},{224... | collective-permute-start | bytes 1966088 | tf_op jit(solution)/shard_map/ppermute | solution.py:364
  103.9 19.2 %collective-permute-start.21 = (bf16[128,2560]{1,0:T(8,128)(2,1)S(1)}, bf16[128,2560]{1,0:T(8,128)(2,1)S(1)}, u32[]{:S(2)}, u32[]{:S(2)}) collective-permute-start(bf16[128,2560]{1,0:T(8,128)(2,1)S(1)} %get-tuple-element.95), channel_id=1, source_target_pairs={{0,496},{32,16},{64,48},{96,80},{128,112},{160,144},{192,176},{224... | collective-permute-start | bytes 1966088 | tf_op jit(solution)/shard_map/ppermute | solution.py:364
  111.1 9.7 %collective-permute-start.23 = (bf16[128,2560]{1,0:T(8,128)(2,1)S(1)}, bf16[128,2560]{1,0:T(8,128)(2,1)S(1)}, u32[]{:S(2)}, u32[]{:S(2)}) collective-permute-start(bf16[128,2560]{1,0:T(8,128)(2,1)S(1)} %get-tuple-element.98), channel_id=1, source_target_pairs={{16,0},{48,32},{80,64},{112,96},{144,128},{176,160},{208,192},{240... | collective-permute-start | bytes 1966088 | tf_op jit(solution)/shard_map/ppermute | solution.py:366
  125.3 3.7 %copy-start.2 = (bf16[1,128,2560]{2,1,0:T(8,128)(2,1)S(1)}, bf16[1,128,2560]{2,1,0:T(8,128)(2,1)}, u32[]{:S(2)}) copy-start(bf16[1,128,2560]{2,1,0:T(8,128)(2,1)} %param.9) | copy-start | bytes 1966084
  125.3 94.2 %collective-permute-start.24 = (bf16[128,2560]{1,0:T(8,128)(2,1)}, bf16[128,2560]{1,0:T(8,128)(2,1)}, u32[]{:S(2)}, u32[]{:S(2)}) collective-permute-start(bf16[128,2560]{1,0:T(8,128)(2,1)} %get-tuple-element.100), channel_id=1, source_target_pairs={{16,0},{48,32},{80,64},{112,96},{144,128},{176,160},{208,192},{240... | collective-permute-start | bytes 1966088 | tf_op jit(solution)/shard_map/ppermute | solution.py:366
  126.7 92.8 %collective-permute-start.25 = (bf16[128,2560]{1,0:T(8,128)(2,1)S(1)}, bf16[128,2560]{1,0:T(8,128)(2,1)}, u32[]{:S(2)}, u32[]{:S(2)}) collective-permute-start(bf16[128,2560]{1,0:T(8,128)(2,1)S(1)} %get-tuple-element.101), channel_id=1, source_target_pairs={{0,496},{32,16},{64,48},{96,80},{128,112},{160,144},{192,176},{224... | collective-permute-start | bytes 1966088 | tf_op jit(solution)/shard_map/ppermute | solution.py:364
  140.9 9.7 %collective-permute-start.10 = (bf16[1,160,512]{2,1,0:T(8,128)(2,1)S(1)}, bf16[1,160,512]{2,1,0:T(8,128)(2,1)S(1)}, u32[]{:S(2)}, u32[]{:S(2)}) collective-permute-start(bf16[1,160,512]{2,1,0:T(8,128)(2,1)S(1)} %get-tuple-element.133), channel_id=1, source_target_pairs={{0,14},{1,15},{2,0},{3,1},{4,2},{5,3},{6,4},{7,5},{8,6},{9,7},{10,... | collective-permute-start | bytes 491528 | tf_op jit(solution)/shard_map/cond/branch_1_fun/ppermute | solution.py:26
  146.2 10.1 %collective-permute-start.9 = (bf16[1,160,512]{2,1,0:T(8,128)(2,1)S(1)}, bf16[1,160,512]{2,1,0:T(8,128)(2,1)S(1)}, u32[]{:S(2)}, u32[]{:S(2)}) collective-permute-start(bf16[1,160,512]{2,1,0:T(8,128)(2,1)S(1)} %get-tuple-element.132), channel_id=1, source_target_pairs={{0,2},{1,3},{2,4},{3,5},{4,6},{5,7},{6,8},{7,9},{8,10},{9,11},{10,... | collective-permute-start | bytes 491528 | tf_op jit(solution)/shard_map/cond/branch_1_fun/ppermute | solution.py:26
  157.8 11.8 %collective-permute-start.12 = (bf16[2,160,512]{2,1,0:T(8,128)(2,1)}, bf16[2,160,512]{2,1,0:T(8,128)(2,1)}, u32[]{:S(2)}, u32[]{:S(2)}) collective-permute-start(bf16[2,160,512]{2,1,0:T(8,128)(2,1)} %pad_maximum_fusion.6), channel_id=1, source_target_pairs={{0,14},{1,15},{2,0},{3,1},{4,2},{5,3},{6,4},{7,5},{8,6},{9,7},{10,... | collective-permute-start | bytes 983048 | tf_op jit(solution)/shard_map/cond/branch_1_fun/ppermute | solution.py:26
  159.7 13.1 %collective-permute-start.11 = (bf16[2,160,512]{2,1,0:T(8,128)(2,1)}, bf16[2,160,512]{2,1,0:T(8,128)(2,1)}, u32[]{:S(2)}, u32[]{:S(2)}) collective-permute-start(bf16[2,160,512]{2,1,0:T(8,128)(2,1)} %pad_maximum_fusion.5), channel_id=1, source_target_pairs={{0,2},{1,3},{2,4},{3,5},{4,6},{5,7},{6,8},{7,9},{8,10},{9,11},{10,... | collective-permute-start | bytes 983048 | tf_op jit(solution)/shard_map/cond/branch_1_fun/ppermute | solution.py:26
  174.8 11.0 %collective-permute-start.14 = (bf16[2,160,512]{2,1,0:T(8,128)(2,1)}, bf16[2,160,512]{2,1,0:T(8,128)(2,1)}, u32[]{:S(2)}, u32[]{:S(2)}) collective-permute-start(bf16[2,160,512]{2,1,0:T(8,128)(2,1)} %get-tuple-element.52), channel_id=1, source_target_pairs={{0,14},{1,15},{2,0},{3,1},{4,2},{5,3},{6,4},{7,5},{8,6},{9,7},{10,... | collective-permute-start | bytes 983048 | tf_op jit(solution)/shard_map/cond/branch_1_fun/ppermute | solution.py:26
  176.7 12.2 %collective-permute-start.13 = (bf16[2,160,512]{2,1,0:T(8,128)(2,1)}, bf16[2,160,512]{2,1,0:T(8,128)(2,1)}, u32[]{:S(2)}, u32[]{:S(2)}) collective-permute-start(bf16[2,160,512]{2,1,0:T(8,128)(2,1)} %get-tuple-element.51), channel_id=1, source_target_pairs={{0,2},{1,3},{2,4},{3,5},{4,6},{5,7},{6,8},{7,9},{8,10},{9,11},{10,... | collective-permute-start | bytes 983048 | tf_op jit(solution)/shard_map/cond/branch_1_fun/ppermute | solution.py:26
  190.9 10.1 %collective-permute-start.16 = (bf16[2,160,512]{2,1,0:T(8,128)(2,1)}, bf16[2,160,512]{2,1,0:T(8,128)(2,1)}, u32[]{:S(2)}, u32[]{:S(2)}) collective-permute-start(bf16[2,160,512]{2,1,0:T(8,128)(2,1)} %get-tuple-element.54), channel_id=1, source_target_pairs={{0,14},{1,15},{2,0},{3,1},{4,2},{5,3},{6,4},{7,5},{8,6},{9,7},{10,... | collective-permute-start | bytes 983048 | tf_op jit(solution)/shard_map/cond/branch_1_fun/ppermute | solution.py:26
  194.4 10.7 %collective-permute-start.15 = (bf16[2,160,512]{2,1,0:T(8,128)(2,1)}, bf16[2,160,512]{2,1,0:T(8,128)(2,1)}, u32[]{:S(2)}, u32[]{:S(2)}) collective-permute-start(bf16[2,160,512]{2,1,0:T(8,128)(2,1)} %get-tuple-element.53), channel_id=1, source_target_pairs={{0,2},{1,3},{2,4},{3,5},{4,6},{5,7},{6,8},{7,9},{8,10},{9,11},{10,... | collective-permute-start | bytes 983048 | tf_op jit(solution)/shard_map/cond/branch_1_fun/ppermute | solution.py:26
  206.3 0.8 copy-start.20
  207.2 11.1 %collective-permute-start.17 = (bf16[160,512]{1,0:T(8,128)(2,1)S(1)}, bf16[160,512]{1,0:T(8,128)(2,1)S(1)}, u32[]{:S(2)}, u32[]{:S(2)}) collective-permute-start(bf16[160,512]{1,0:T(8,128)(2,1)S(1)} %fusion.3), channel_id=1, source_target_pairs={{0,1},{1,0},{2,3},{3,2},{4,5},{5,4},{6,7},{7,6},{8,9},{9,8},{10,11... | collective-permute-start | bytes 491528 | tf_op jit(solution)/shard_map/cond/branch_1_fun/ppermute | solution.py:30
  219.5 2.1 copy-start.21

commit v3 on v1

v3 whole, which is shorter than its diff:
```python
import functools

import jax
import jax.numpy as jnp
from jax import lax
from jax.experimental import pallas as pl
from jax.experimental.pallas import tpu as pltpu
from jax.sharding import PartitionSpec as P

EPS = 1e-06
F32 = jnp.float32
BF16 = jnp.bfloat16
LIMIT = pltpu.CompilerParams(vmem_limit_bytes=24 * 1024 * 1024)
IN_VMEM = pl.BlockSpec(memory_space=pltpu.VMEM)
ANYWHERE = pl.BlockSpec(memory_space=pl.ANY)
SCALAR = pl.BlockSpec(memory_space=pltpu.SMEM)


def dp_pairs(sections, n_dp, step, flip):
    n_z = n_dp // 2
    return [
        (s * n_dp + 2 * z + h, s * n_dp + 2 * ((z + step) % n_z) + (h ^ flip))
        for s in sections
        for z in range(n_z)
        for h in range(2)
    ]


def shifted(value, ring, step):
    return lax.ppermute(value, ("section", "dp"), dp_pairs(*ring, step, 0))


def swapped(value, ring):
    return lax.ppermute(value, ("section", "dp"), dp_pairs(*ring, 0, 1))


def ring_gather(shard, ring):
    h = lax.axis_index("dp") % 2
    other = swapped(shard, ring)
    pair = jnp.stack([jnp.where(h == 0, shard, other), jnp.where(h == 0, other, shard)])
    rights, lefts = [], []
    right, left = pair, pair
    for _ in range(1, ring[1] // 4):
        right, left = shifted(right, ring, 1), shifted(left, ring, -1)
        rights.append(right)
        lefts.append(left)
    return [pair] + rights + lefts + [shifted(right[:1], ring, 1), shifted(left[1:], ring, -1)]


def ring_reduce(parts, ring):
    n_z = ring[1] // 2
    index = lax.axis_index("dp")
    z, h = index // 2, index % 2
    half = n_z // 2

    def at(offset):
        return lax.dynamic_index_in_dim(parts, (z + offset) % n_z, 0, keepdims=False)

    far = at(half)
    right, left = shifted(far[:1], ring, 1), shifted(far[1:], ring, -1)
    for step in range(half - 1, 0, -1):
        here, there = at(step), at(-step)
        if step == half - 1:
            here = jnp.concatenate([here[:1] + right, here[1:]], axis=0)
            there = jnp.concatenate([there[:1], there[1:] + left], axis=0)
        else:
            here, there = here + right, there + left
        here, there = lax.optimization_barrier((here, there))
        right, left = shifted(here, ring, 1), shifted(there, ring, -1)
    total = at(0).astype(F32) + right.astype(F32) + left.astype(F32)
    mine = lax.dynamic_index_in_dim(total, h, 0, keepdims=False)
    other = lax.dynamic_index_in_dim(total, 1 - h, 0, keepdims=False).astype(BF16)
    return mine, swapped(other, ring)


def norm_kernel(x_ref, normed_ref, inverse_ref):
    x = x_ref[0, 0].astype(F32)
    inverse = lax.rsqrt(jnp.mean(x * x, axis=-1, keepdims=True) + EPS)
    normed_ref[0] = (x * inverse).astype(BF16)
    inverse_ref[0] = jnp.broadcast_to(inverse, inverse_ref.shape[1:])


def norms(saved_inputs):
    ticks, _, rows, width = saved_inputs.shape
    return pl.pallas_call(
        norm_kernel,
        grid=(ticks,),
        out_shape=[
            jax.ShapeDtypeStruct((ticks, rows, width), BF16),
            jax.ShapeDtypeStruct((ticks, rows, 128), F32),
        ],
        in_specs=[pl.BlockSpec((1, 1, rows, width), lambda i: (i, 0, 0, 0))],
        out_specs=[
            pl.BlockSpec((1, rows, width), lambda i: (i, 0, 0)),
            pl.BlockSpec((1, rows, 128), lambda i: (i, 0, 0)),
        ],
        compiler_params=LIMIT,
        cost_estimate=pl.CostEstimate(
            flops=8 * ticks * rows * width, bytes_accessed=4 * ticks * rows * width, transcendentals=0
        ),
        name="norms",
    )(saved_inputs)


def tick_kernel(tick, n_pieces, flags_ref, *refs):
    incoming_ref, normed_ref, inverse_ref, first_ref = refs[:4]
    pieces = refs[4 : 4 + n_pieces]
    sent_ref, grad_latent_ref, active_ref = refs[5 + n_pieces : 8 + n_pieces]
    incoming, normed, inverse, down, up, sent, sems = refs[8 + n_pieces :]
    n_dp, share, rank = down.shape
    width = n_dp * share

    @pl.when(flags_ref[0] == 1)
    def _():
        gets = [
            pltpu.make_async_copy(normed_ref.at[tick], normed, sems.at[0]),
            pltpu.make_async_copy(first_ref.at[:, 0], down, sems.at[1]),
            pltpu.make_async_copy(first_ref.at[:, 1], up, sems.at[2]),
            pltpu.make_async_copy(incoming_ref, incoming, sems.at[3]),
            pltpu.make_async_copy(inverse_ref.at[tick], inverse, sems.at[4]),
        ]
        gets[0].start()
        gets[3].start()
        gets[4].start()

        def from_first():
            gets[1].start()
            gets[2].start()

        if n_pieces:
            n_z = n_dp // 2
            half = n_z // 2
            offsets = [0] + list(range(-1, -half, -1)) + list(range(1, half))
            z = flags_ref[2]
            pl.when(flags_ref[1] == 1)(from_first)

            @pl.when(flags_ref[1] == 0)
            def _():
                for which, target in enumerate((down, up)):
                    sem = sems.at[1 + which]
                    for piece, offset in zip(pieces, offsets):
                        at = lax.rem(z + (offset + n_z), n_z) * 2
                        pltpu.make_async_copy(
                            piece.at[:, which], target.at[pl.ds(at, 2)], sem
                        ).start()
                    far = lax.rem(z + half, n_z) * 2
                    for h in range(2):
                        pltpu.make_async_copy(
                            pieces[n_z - 1 + h].at[:, which], target.at[pl.ds(far + h, 1)], sem
                        ).start()
        else:
            from_first()

        gets[0].wait()
        gets[1].wait()
        down_map = down[...].reshape(width, rank)
        latent = jnp.dot(normed[...], down_map, preferred_element_type=F32)
        gate = jax.nn.sigmoid(latent)
        active_ref[...] = (latent * gate).astype(BF16)
        slope = gate * (1.0 + latent * (1.0 - gate))
        gets[2].wait()
        gets[3].wait()
        gets[4].wait()
        up_map = up[...].reshape(width, rank)
        grad_act = jnp.dot(incoming[...], up_map, preferred_element_type=F32)
        grad_latent = (grad_act * slope).astype(BF16)
        grad_latent_ref[...] = grad_latent
        inner = jnp.sum(grad_latent.astype(F32) * latent, axis=-1, keepdims=True) / width
        inv = inverse[:, :1]
        scale = inv * inner
        blocks = 4
        run = width // blocks
        for block in range(blocks):
            at = pl.ds(block * run, run)
            piece = down[pl.ds(block * n_dp // blocks, n_dp // blocks)].reshape(run, rank)
            grad_normed = lax.dot_general(
                grad_latent, piece, (((1,), (1,)), ((), ())), preferred_element_type=F32
            )
            new = incoming[:, at].astype(F32) + (
                inv * grad_normed - normed[:, at].astype(F32) * scale
            )
            sent[:, at] = new.astype(BF16)
        put = pltpu.make_async_copy(sent, sent_ref, sems.at[5])
        put.start()
        put.wait()


def tick_layer(tick, works, level, z, incoming, normed, inverse, first, pieces, dep):
    _, rows, width = normed.shape
    n_dp, _, share, rank = first.shape
    wide = jax.ShapeDtypeStruct((rows, width), BF16)
    narrow = jax.ShapeDtypeStruct((rows, rank), BF16)
    flags = jnp.stack([works.astype(jnp.int32), level.astype(jnp.int32), z.astype(jnp.int32)])
    return pl.pallas_call(
        functools.partial(tick_kernel, tick, len(pieces)),
        out_shape=[wide, narrow, narrow],
        in_specs=[SCALAR] + [ANYWHERE] * (5 + len(pieces)),
        out_specs=[ANYWHERE, IN_VMEM, IN_VMEM],
        scratch_shapes=[
            pltpu.VMEM((rows, width), BF16),
            pltpu.VMEM((rows, width), BF16),
            pltpu.VMEM((rows, 128), F32),
            pltpu.VMEM((n_dp, share, rank), BF16),
            pltpu.VMEM((n_dp, share, rank), BF16),
            pltpu.VMEM((rows, width), BF16),
            pltpu.SemaphoreType.DMA((6,)),
        ],
        compiler_params=LIMIT,
        cost_estimate=pl.CostEstimate(
            flops=40 * rows * width * rank, bytes_accessed=40 * rows * width, transcendentals=0
        ),
        name="tick_layer",
    )(flags, incoming, normed, inverse, first, *pieces, dep)


def turned(block):
    share, rank = block.shape
    room = -(-share // 128) * 128
    if room != share:
        block = jnp.concatenate([block, jnp.zeros((room - share, rank), block.dtype)], axis=0)
    return block.T[:, :share]


def finish_kernel(level_ref, moved_ref, mine_ref, other_ref, down_ref, up_ref):
    rank = down_ref.shape[1]
    level = level_ref[0]
    main = jnp.sum(moved_ref[...].astype(F32), axis=0)
    rest = mine_ref[...] + other_ref[...].astype(F32)
    for i, out in enumerate((down_ref, up_ref)):
        out[level] = turned(main[i])
        out[1 - level] = turned(rest[i])


def finish(level, moved, mine, other):
    _, share, rank = mine.shape
    made = jax.ShapeDtypeStruct((2, rank, share), F32)
    return pl.pallas_call(
        finish_kernel,
        out_shape=[made, made],
        in_specs=[SCALAR] + [IN_VMEM] * 3,
        out_specs=[IN_VMEM] * 2,
        compiler_params=LIMIT,
        name="finish_sums",
    )(level.astype(jnp.int32)[None], moved, mine, other)


def on_device(saved_inputs, grad_in, adapter_down, adapter_up):
    n_sec = lax.axis_size("section")
    n_dp = lax.axis_size("dp")
    n_z = n_dp // 2
    position = lax.axis_index("section")
    z = lax.axis_index("dp") // 2
    ticks = saved_inputs.shape[0]
    rank, share = adapter_down.shape[2], adapter_down.shape[3]
    width = saved_inputs.shape[3]
    even = position % 2 == 0
    levels = [1 - (position + tick) // n_sec for tick in range(ticks)]
    ring = (list(range(n_sec - ticks + 1, n_sec)), n_dp)

    def shard_of(level):
        return jnp.stack([adapter_down[level, 0].T, adapter_up[level, 0].T])

    shard = shard_of(1)
    copies = jnp.broadcast_to(shard[None], (n_dp,) + shard.shape)
    first = lax.all_to_all(copies, "dp", 0, 0, tiled=True)
    pieces = ring_gather(shard_of(0), ring)
    normed, inverse = norms(saved_inputs)

    def layer(tick, works, incoming, dep):
        met = any(s % 2 == (0 if works is even else 1) for s in range(n_sec - tick, n_sec))
        return tick_layer(
            tick,
            jnp.ones((), jnp.int32) if works is None else works,
            levels[tick],
            z,
            incoming,
            normed,
            inverse,
            first,
            pieces if met else [],
            dep,
        )

    inside = [(s, s - 1) for s in range(1, n_sec, 2)]
    across = [(s, (s - 1) % n_sec) for s in range(0, n_sec, 2)]
    odd = ~even

    sent, latent, active = layer(0, None, grad_in[0], inverse)
    grads, latents, actives = [grad_in[0]], [latent], [active]
    over = lax.ppermute(sent, "section", across)
    core = lax.ppermute(sent, "section", inside)
    for tick in range(1, ticks):
        sent_even, latent_even, active_even = layer(tick, even, core, latent)
        next_over = lax.ppermute(sent_even, "section", across)
        sent_odd, latent_odd, active_odd = layer(tick, odd, over, latent_even)
        next_core = lax.ppermute(sent_odd, "section", inside)
        grads.append(jnp.where(even, core, over))
        latents.append(jnp.where(even, latent_even, latent_odd))
        actives.append(jnp.where(even, active_even, active_odd))
        latent = latent_odd
        over, core = next_over, next_core
    grad_out = jnp.where(even, core, over)

    def product(wide, narrow):
        return lax.dot_general(wide, narrow, (((0,), (0,)), ((), ())), preferred_element_type=F32)

    last = ticks - 1
    zero = jnp.zeros((), BF16)

    def split(values):
        same = [jnp.where(levels[t] == levels[last], values[t], zero) for t in range(last)]
        differ = [jnp.where(levels[t] == levels[last], zero, values[t]) for t in range(last)]
        return jnp.concatenate([jnp.concatenate(same), jnp.concatenate(differ)], axis=1)

    early_down = product(normed[:last].reshape(-1, width), split(latents))
    early_up = product(jnp.concatenate(grads[:last]), split(actives))
    rest = jnp.stack([v[:, rank:].reshape(n_dp, share, rank) for v in (early_down, early_up)], axis=1)
    mine, other = ring_reduce(rest.astype(BF16).reshape(n_z, 2, 2, share, rank), ring)
    down = early_down[:, :rank] + product(normed[last], latents[last])
    up = early_up[:, :rank] + product(grads[last], actives[last])
    main = jnp.stack([v.astype(BF16).reshape(n_dp, share, rank) for v in (down, up)], axis=1)
    moved = lax.all_to_all(main, "dp", 0, 0, tiled=True)
    down_grad, up_grad = finish(levels[last], moved, mine, other)
    return grad_out[None], down_grad[:, None], up_grad[:, None]


def solution(mesh):
    in_specs = (
        P(None, "section", "dp", None),
        P("section", "dp", None),
        P(None, "section", None, "dp"),
        P(None, "section", None, "dp"),
    )
    out_specs = (
        P("section", "dp", None),
        P(None, "section", None, "dp"),
        P(None, "section", None, "dp"),
    )
    return jax.shard_map(
        on_device, mesh=mesh, in_specs=in_specs, out_specs=out_specs, check_vma=False
    )
```

time: 221 us -> 266 us (1.20)
  starting transfers between devices: 86 us -> 118 us
  Pallas kernels: 0 us -> 18.4 us
  matrix products: 22.5 us -> 4.89 us
  waiting for transfers between devices: 65.3 us -> 81.9 us
  other arithmetic: 22.4 us -> 13.9 us
    all_to_all x0 -> x2, starting transfers between devices: none -> 30.3 us  [the longest x1 15.4 us: on_device(): first = lax.all_to_all(copies, 'dp', 0, 0, tiled=True)]
    ppermute x18, waiting for transfers between devices: 39.7 us -> 66.8 us  [the longest x16 44.2 us: shifted(): return lax.ppermute(value, ('section', 'dp'), dp_pairs(*ring, step, 0))]
    pallas_call x0 -> x9, Pallas kernels: none -> 18.4 us  [the longest x7 17.1 us: tick_layer(): pl.pallas_call(functools.partial(tick_kernel, tick, len(pieces)), out_sha...]
    dot_general x22 -> x4, matrix products: 22.5 us -> 4.89 us  [product(): lax.dot_general(wide, narrow, (((0,), (0,)), ((), ())), preferred_element...]
    ppermute x3, waiting for transfers between devices: 25.6 us -> 14.8 us  [on_device(): next_over = lax.ppermute(sent_even, 'section', across)]
    ppermute x1, starting transfers between devices: 11.5 us -> 21.5 us  [on_device(): core = lax.ppermute(sent, 'section', inside)]
    ppermute x18, starting transfers between devices: 63.9 us -> 54.3 us  [the longest x16 49.7 us: shifted(): return lax.ppermute(value, ('section', 'dp'), dp_pairs(*ring, step, 0))]
    unnamed x24 -> x60, local copies, waits for them, and re-layouts: 1.15 us -> 10.5 us
  transfers between devices with their start and end apart: 26 -> 28, of which waited for: 14 -> 12; matrix products, arithmetic and copies ran while one was open for 19% -> 11% of each run, Pallas kernels for 0% -> 4%
where the time goes in v3:
time: 266 us; the launch traced here: 263 us
  starting transfers between devices  118 us (44%)
  waiting for transfers between devices  81.9 us (31%)
  local copies, waits for them, and re-layouts  24.3 us (9%)
  Pallas kernels  18.4 us (7%)
  other arithmetic  13.9 us (5%)
  matrix products  4.89 us (2%)
    ppermute x16, starting transfers between devices, shifted(): return lax.ppermute(value, ('section', 'dp'), dp_pairs(*ring, step, 0))  49.7 us
    ppermute x16, waiting for transfers between devices, shifted(): return lax.ppermute(value, ('section', 'dp'), dp_pairs(*ring, step, 0))  44.2 us
    ppermute x2, waiting for transfers between devices, swapped(): return lax.ppermute(value, ('section', 'dp'), dp_pairs(*ring, 0, 1))  22.6 us
    ppermute x1, starting transfers between devices, on_device(): core = lax.ppermute(sent, 'section', inside)  21.5 us
    pallas_call x7, Pallas kernels, tick_layer(): pl.pallas_call(functools.partial(tick_kernel, tick, len(pieces)), out_sha...  17.1 us
    all_to_all x1, starting transfers between devices, on_device(): first = lax.all_to_all(copies, 'dp', 0, 0, tiled=True)  15.4 us
    all_to_all x1, starting transfers between devices, on_device(): moved = lax.all_to_all(main, 'dp', 0, 0, tiled=True)  14.9 us
    ppermute x3, waiting for transfers between devices, on_device(): next_over = lax.ppermute(sent_even, 'section', across)  14.8 us
  transfers between devices with their start and end apart: 28, of which 12 were waited for; matrix products, arithmetic and copies ran while one was open for 11% of the time, Pallas kernels for 4%

profile of v3, /device:TPU:63, one launch (start us, length us, event | category | flops | bytes accessed | tf_op | source)
XLA Modules:
  0.0 262.7 jit_solution(11104123077830276303)
XLA Ops:
  2.3 1.3 broadcast_in_dim.32
  3.6 15.4 %all-to-all-start = ((bf16[16,2,160,128]{3,2,1,0:T(8,128)(2,1)}), bf16[16,2,160,128]{3,2,1,0:T(8,128)(2,1)}, u32[]{:S(2)}, u32[]{:S(2)}) async-start(bf16[16,2,160,128]{3,2,1,0:T(8,128)(2,1)} %broadcast_in_dim.32), calls=%async_computation | async-start | bytes 2621440 | tf_op jit(solution)/shard_map/all_to_all | solution.py:265
  19.0 2.1 collective-permute-start.1
  21.2 18.2 %collective-permute-done.1 = bf16[2,160,128]{2,1,0:T(8,128)(2,1)S(1)} collective-permute-done((bf16[2,160,128]{2,1,0:T(8,128)(2,1)S(1)}, bf16[2,160,128]{2,1,0:T(8,128)(2,1)S(1)}, u32[]{:S(2)}, u32[]{:S(2)}) %collective-permute-start.1) | collective-permute-done | bytes 81952 | tf_op jit(solution)/shard_map/ppermute | solution.py:34
  39.4 3.2 %collective-permute-start.5 = (bf16[2,2,160,128]{3,2,1,0:T(8,128)(2,1)S(1)}, bf16[2,2,160,128]{3,2,1,0:T(8,128)(2,1)}, u32[]{:S(2)}, u32[]{:S(2)}) collective-permute-start(bf16[2,2,160,128]{3,2,1,0:T(8,128)(2,1)S(1)} %pad_maximum_fusion.1.refs_4_), channel_id=1, source_target_pairs={{464,478},{465,479},{466,464},{467,465},{468,466},{469,467},{470,4... | collective-permute-start | bytes 491528 | tf_op jit(solution)/shard_map/ppermute | solution.py:30
  42.6 2.0 collective-permute-start.2
  44.9 8.4 %collective-permute-done.5.refs_8_ = bf16[2,2,160,128]{3,2,1,0:T(8,128)(2,1)} collective-permute-done((bf16[2,2,160,128]{3,2,1,0:T(8,128)(2,1)S(1)}, bf16[2,2,160,128]{3,2,1,0:T(8,128)(2,1)}, u32[]{:S(2)}, u32[]{:S(2)}) %collective-permute-start.5) | collective-permute-done | bytes 163872 | tf_op jit(solution)/shard_map/ppermute | solution.py:30
  53.3 1.9 collective-permute-start.6
  55.2 2.4 collective-permute-done.2.refs_5_
  57.6 1.9 collective-permute-start.3
  60.6 1.5 copy-done.1
  62.9 4.6 %collective-permute-start.7 = (bf16[2,2,160,128]{3,2,1,0:T(8,128)(2,1)}, bf16[2,2,160,128]{3,2,1,0:T(8,128)(2,1)}, u32[]{:S(2)}, u32[]{:S(2)}) collective-permute-start(bf16[2,2,160,128]{3,2,1,0:T(8,128)(2,1)} %collective-permute-done.6.refs_9_), channel_id=1, source_target_pairs={{464,478},{465,479},{466,464},{467,465},{468,466},{469,467},{470,4... | collective-permute-start | bytes 491528 | tf_op jit(solution)/shard_map/ppermute | solution.py:30
  67.4 3.0 %collective-permute-start.4 = (bf16[2,2,160,128]{3,2,1,0:T(8,128)(2,1)}, bf16[2,2,160,128]{3,2,1,0:T(8,128)(2,1)}, u32[]{:S(2)}, u32[]{:S(2)}) collective-permute-start(bf16[2,2,160,128]{3,2,1,0:T(8,128)(2,1)} %collective-permute-done.3.refs_6_), channel_id=1, source_target_pairs={{464,466},{465,467},{466,468},{467,469},{468,470},{469,471},{470,4... | collective-permute-start | bytes 491528 | tf_op jit(solution)/shard_map/ppermute | solution.py:30
  70.5 1.7 copy-done.2
  73.2 4.1 %tick_layer.7 = (bf16[128,2560]{1,0:T(8,128)(2,1)}, bf16[128,128]{1,0:T(8,128)(2,1)S(1)}, bf16[128,128]{1,0:T(8,128)(2,1)S(1)}) custom-call(s32[3]{0:T(128)S(1)} %add_add_fusion.3.flags_ref, bf16[128,2560]{1,0:T(8,128)(2,1)S(1)} %bitcast.90, bf16[4,128,2560]{2,1,0:T(8,128)(2,1)S(1)} %copy-done.2, f32[4,128,128]{2,1,0:T(8,128)S(1)} %copy-done.11, ...), custom_call_target="tpu_custom_call" | custom-call | flops 1677721600 | bytes 13107200 | tf_op jit(solution)/shard_map/tick_layer/pallas_call | solution.py:194
  77.3 21.5 %collective-permute-start.10 = (bf16[128,2560]{1,0:T(8,128)(2,1)}, bf16[128,2560]{1,0:T(8,128)(2,1)S(1)}, u32[]{:S(2)}, u32[]{:S(2)}) collective-permute-start(bf16[128,2560]{1,0:T(8,128)(2,1)} %get-tuple-element.36), channel_id=1, source_target_pairs={{16,0},{48,32},{80,64},{112,96},{144,128},{176,160},{208,192},{240... | collective-permute-start | bytes 1966088 | tf_op jit(solution)/shard_map/ppermute | solution.py:291
  100.3 1.4 slice.80
  102.7 4.8 %collective-permute-start.9 = (bf16[1,2,160,128]{3,2,1,0:T(8,128)(2,1)S(1)}, bf16[1,2,160,128]{3,2,1,0:T(8,128)(2,1)S(1)}, u32[]{:S(2)}, u32[]{:S(2)}) collective-permute-start(bf16[1,2,160,128]{3,2,1,0:T(8,128)(2,1)S(1)} %slice.99), channel_id=1, source_target_pairs={{464,478},{465,479},{466,464},{467,465},{468,466},{469,467},{470,4... | collective-permute-start | bytes 245768 | tf_op jit(solution)/shard_map/ppermute | solution.py:30
  108.4 1.9 collective-permute-start.8
  112.0 2.8 %collective-permute-done.8.refs_11_ = bf16[1,2,160,128]{3,2,1,0:T(8,128)(2,1)S(1)} collective-permute-done((bf16[1,2,160,128]{3,2,1,0:T(8,128)(2,1)S(1)}, bf16[1,2,160,128]{3,2,1,0:T(8,128)(2,1)S(1)}, u32[]{:S(2)}, u32[]{:S(2)}) %collective-permute-start.8) | collective-permute-done | bytes 81952 | tf_op jit(solution)/shard_map/ppermute | solution.py:30
  115.1 3.4 %tick_layer.9 = (bf16[128,2560]{1,0:T(8,128)(2,1)S(1)}, bf16[128,128]{1,0:T(8,128)(2,1)S(1)}, bf16[128,128]{1,0:T(8,128)(2,1)S(1)}) custom-call(s32[3]{0:T(128)S(1)} %add_add_fusion.2.flags_ref, bf16[128,2560]{1,0:T(8,128)(2,1)} %collective-permute-done.refs_0_, bf16[4,128,2560]{2,1,0:T(8,128)(2,1)S(1)} %copy-done.3, f32[4,128,128]{2,1,0:T(8,128)S(1)} %copy-done.12, ...), custom_call_target="tpu_custom_call" | custom-call | flops 1677721600 | bytes 13107200 | tf_op jit(solution)/shard_map/tick_layer/pallas_call | solution.py:194
  122.9 12.7 %collective-permute-done.13.refs_0_ = bf16[128,2560]{1,0:T(8,128)(2,1)S(1)} collective-permute-done((bf16[128,2560]{1,0:T(8,128)(2,1)S(1)}, bf16[128,2560]{1,0:T(8,128)(2,1)S(1)}, u32[]{:S(2)}, u32[]{:S(2)}) %collective-permute-start.13) | collective-permute-done | bytes 655392 | tf_op jit(solution)/shard_map/ppermute | solution.py:294
  135.6 4.2 %tick_layer.11 = (bf16[128,2560]{1,0:T(8,128)(2,1)}, bf16[128,128]{1,0:T(8,128)(2,1)S(1)}, bf16[128,128]{1,0:T(8,128)(2,1)S(1)}) custom-call(s32[3]{0:T(128)S(1)} %add_add_fusion.6.flags_ref, bf16[128,2560]{1,0:T(8,128)(2,1)S(1)} %collective-permute-done.13.refs_0_, bf16[4,128,2560]{2,1,0:T(8,128)(2,1)S(1)} %copy-done.3, f32[4,128,128]{2,1,0:T(8,128)S(1)} %copy-done.12, ...), custom_call_target="tpu_custom_call" | custom-call | flops 1677721600 | bytes 13107200 | tf_op jit(solution)/shard_map/tick_layer/pallas_call | solution.py:194
  139.8 1.5 collective-permute-start.14
  145.6 1.5 copy-done.19
  148.1 2.2 copy.8
  152.8 4.8 %collective-permute-start.18 = (bf16[1,2,160,128]{3,2,1,0:T(8,128)(2,1)S(1)}, bf16[1,2,160,128]{3,2,1,0:T(8,128)(2,1)S(1)}, u32[]{:S(2)}, u32[]{:S(2)}) collective-permute-start(bf16[1,2,160,128]{3,2,1,0:T(8,128)(2,1)S(1)} %get-tuple-element.75), channel_id=1, source_target_pairs={{464,478},{465,479},{466,464},{467,465},{468,466},{469,467},{470,4... | collective-permute-start | bytes 245768 | tf_op jit(solution)/shard_map/ppermute | solution.py:30
  158.3 1.9 collective-permute-start.17
  161.5 2.2 collective-permute-done.12.refs_0_
  163.7 3.6 %tick_layer.13 = (bf16[128,2560]{1,0:T(8,128)(2,1)S(1)}, bf16[128,128]{1,0:T(8,128)(2,1)S(1)}, bf16[128,128]{1,0:T(8,128)(2,1)S(1)}) custom-call(s32[3]{0:T(128)S(1)} %add_add_fusion.flags_ref, bf16[128,2560]{1,0:T(8,128)(2,1)} %collective-permute-done.12.refs_0_, bf16[4,128,2560]{2,1,0:T(8,128)(2,1)S(1)} %copy-done.3, f32[4,128,128]{2,1,0:T(8,128)S(1)} %copy-done.13, ...), custom_call_target="tpu_custom_call" | custom-call | flops 1677721600 | bytes 13107200 | tf_op jit(solution)/shard_map/tick_layer/pallas_call | solution.py:194
  169.3 1.4 copy.7
  170.7 1.9 fusion.8
  173.9 14.9 %all-to-all-start.1 = ((bf16[16,2,160,128]{3,2,1,0:T(8,128)(2,1)}), bf16[16,2,160,128]{3,2,1,0:T(8,128)(2,1)S(1)}, u32[]{:S(2)}, u32[]{:S(2)}) async-start(bf16[16,2,160,128]{3,2,1,0:T(8,128)(2,1)} %pad_maximum_fusion), calls=%async_computation.1 | async-start | bytes 2621440 | tf_op jit(solution)/shard_map/all_to_all | solution.py:322
  191.1 3.1 %collective-permute-start.19 = (bf16[2,2,160,128]{3,2,1,0:T(8,128)(2,1)}, bf16[2,2,160,128]{3,2,1,0:T(8,128)(2,1)S(1)}, u32[]{:S(2)}, u32[]{:S(2)}) collective-permute-start(bf16[2,2,160,128]{3,2,1,0:T(8,128)(2,1)} %pad_maximum_fusion.2), channel_id=1, source_target_pairs={{464,466},{465,467},{466,468},{467,469},{468,470},{469,471},{470,4... | collective-permute-start | bytes 491528 | tf_op jit(solution)/shard_map/ppermute | solution.py:30
  194.1 3.4 %collective-permute-start.20 = (bf16[2,2,160,128]{3,2,1,0:T(8,128)(2,1)}, bf16[2,2,160,128]{3,2,1,0:T(8,128)(2,1)}, u32[]{:S(2)}, u32[]{:S(2)}) collective-permute-start(bf16[2,2,160,128]{3,2,1,0:T(8,128)(2,1)} %pad_maximum_fusion.3), channel_id=1, source_target_pairs={{464,478},{465,479},{466,464},{467,465},{468,466},{469,467},{470,4... | collective-permute-start | bytes 491528 | tf_op jit(solution)/shard_map/ppermute | solution.py:30
  197.6 22.8 %collective-permute-done.19 = bf16[2,2,160,128]{3,2,1,0:T(8,128)(2,1)S(1)} collective-permute-done((bf16[2,2,160,128]{3,2,1,0:T(8,128)(2,1)}, bf16[2,2,160,128]{3,2,1,0:T(8,128)(2,1)S(1)}, u32[]{:S(2)}, u32[]{:S(2)}) %collective-permute-start.19) | collective-permute-done | bytes 163872 | tf_op jit(solution)/shard_map/ppermute | solution.py:30
  221.1 4.2 %collective-permute-done.20 = bf16[2,2,160,128]{3,2,1,0:T(8,128)(2,1)} collective-permute-done((bf16[2,2,160,128]{3,2,1,0:T(8,128)(2,1)}, bf16[2,2,160,128]{3,2,1,0:T(8,128)(2,1)}, u32[]{:S(2)}, u32[]{:S(2)}) %collective-permute-start.20) | collective-permute-done | bytes 163872 | tf_op jit(solution)/shard_map/ppermute | solution.py:30
  225.3 1.8 bitcast_add_fusion.1
  227.1 2.8 %collective-permute-start.21 = (bf16[2,2,160,128]{3,2,1,0:T(8,128)(2,1)}, bf16[2,2,160,128]{3,2,1,0:T(8,128)(2,1)}, u32[]{:S(2)}, u32[]{:S(2)}) collective-permute-start(bf16[2,2,160,128]{3,2,1,0:T(8,128)(2,1)} %get-tuple-element.59), channel_id=1, source_target_pairs={{464,466},{465,467},{466,468},{467,469},{468,470},{469,471},{470,4... | collective-permute-start | bytes 491528 | tf_op jit(solution)/shard_map/ppermute | solution.py:30
  229.9 3.7 %collective-permute-start.22 = (bf16[2,2,160,128]{3,2,1,0:T(8,128)(2,1)S(1)}, bf16[2,2,160,128]{3,2,1,0:T(8,128)(2,1)}, u32[]{:S(2)}, u32[]{:S(2)}) collective-permute-start(bf16[2,2,160,128]{3,2,1,0:T(8,128)(2,1)S(1)} %get-tuple-element.60), channel_id=1, source_target_pairs={{464,478},{465,479},{466,464},{467,465},{468,466},{469,467},{470,4... | collective-permute-start | bytes 491528 | tf_op jit(solution)/shard_map/ppermute | solution.py:30
  234.9 3.8 %collective-permute-start.15 = (bf16[128,2560]{1,0:T(8,128)(2,1)S(1)}, bf16[128,2560]{1,0:T(8,128)(2,1)}, u32[]{:S(2)}, u32[]{:S(2)}) collective-permute-start(bf16[128,2560]{1,0:T(8,128)(2,1)S(1)} %copy-done.9), channel_id=1, source_target_pairs={{16,0},{48,32},{80,64},{112,96},{144,128},{176,160},{208,192},{240... | collective-permute-start | bytes 1966088 | tf_op jit(solution)/shard_map/ppermute | solution.py:296
  238.7 1.8 bitcast_add_fusion
  240.5 2.0 collective-permute-start.23
  242.5 4.5 %collective-permute-start.24 = (bf16[2,2,160,128]{3,2,1,0:T(8,128)(2,1)S(1)}, bf16[2,2,160,128]{3,2,1,0:T(8,128)(2,1)}, u32[]{:S(2)}, u32[]{:S(2)}) collective-permute-start(bf16[2,2,160,128]{3,2,1,0:T(8,128)(2,1)S(1)} %get-tuple-element.62), channel_id=1, source_target_pairs={{464,478},{465,479},{466,464},{467,465},{468,466},{469,467},{470,4... | collective-permute-start | bytes 491528 | tf_op jit(solution)/shard_map/ppermute | solution.py:30
  247.1 2.8 %collective-permute-done.23 = bf16[2,2,160,128]{3,2,1,0:T(8,128)(2,1)} collective-permute-done((bf16[2,2,160,128]{3,2,1,0:T(8,128)(2,1)}, bf16[2,2,160,128]{3,2,1,0:T(8,128)(2,1)}, u32[]{:S(2)}, u32[]{:S(2)}) %collective-permute-start.23) | collective-permute-done | bytes 163872 | tf_op jit(solution)/shard_map/ppermute | solution.py:30
  251.7 2.6 collective-permute-start.25
  254.3 2.0 select_bitcast_fusion
  256.3 4.4 %collective-permute-done.25.other_ref = bf16[2,160,128]{2,1,0:T(8,128)(2,1)S(1)} collective-permute-done((bf16[2,160,128]{2,1,0:T(8,128)(2,1)S(1)}, bf16[2,160,128]{2,1,0:T(8,128)(2,1)S(1)}, u32[]{:S(2)}, u32[]{:S(2)}) %collective-permute-start.25) | collective-permute-done | bytes 81952 | tf_op jit(solution)/shard_map/ppermute | solution.py:34
  (124 shorter events, 35.0 us)
Async XLA Ops:
  3.6 56.0 %copy-start = (bf16[4,1,128,2560]{3,2,1,0:T(8,128)(2,1)S(1)}, bf16[4,1,128,2560]{3,2,1,0:T(8,128)(2,1)}, u32[]{:S(2)}) copy-start(bf16[4,1,128,2560]{3,2,1,0:T(8,128)(2,1)} %x_ref.1) | copy-start | bytes 7864324
  3.6 66.9 %all-to-all-start = ((bf16[16,2,160,128]{3,2,1,0:T(8,128)(2,1)}), bf16[16,2,160,128]{3,2,1,0:T(8,128)(2,1)}, u32[]{:S(2)}, u32[]{:S(2)}) async-start(bf16[16,2,160,128]{3,2,1,0:T(8,128)(2,1)} %broadcast_in_dim.32), calls=%async_computation | async-start | bytes 2621440 | tf_op jit(solution)/shard_map/all_to_all | solution.py:265
  19.0 20.3 %collective-permute-start.1 = (bf16[2,160,128]{2,1,0:T(8,128)(2,1)S(1)}, bf16[2,160,128]{2,1,0:T(8,128)(2,1)S(1)}, u32[]{:S(2)}, u32[]{:S(2)}) collective-permute-start(bf16[2,160,128]{2,1,0:T(8,128)(2,1)S(1)} %pad_maximum_fusion.5), channel_id=1, source_target_pairs={{464,465},{465,464},{466,467},{467,466},{468,469},{469,468},{470,4... | collective-permute-start | bytes 245768 | tf_op jit(solution)/shard_map/ppermute | solution.py:34
  39.4 13.9 %collective-permute-start.5 = (bf16[2,2,160,128]{3,2,1,0:T(8,128)(2,1)S(1)}, bf16[2,2,160,128]{3,2,1,0:T(8,128)(2,1)}, u32[]{:S(2)}, u32[]{:S(2)}) collective-permute-start(bf16[2,2,160,128]{3,2,1,0:T(8,128)(2,1)S(1)} %pad_maximum_fusion.1.refs_4_), channel_id=1, source_target_pairs={{464,478},{465,479},{466,464},{467,465},{468,466},{469,467},{470,4... | collective-permute-start | bytes 491528 | tf_op jit(solution)/shard_map/ppermute | solution.py:30
  42.6 14.9 %collective-permute-start.2 = (bf16[2,2,160,128]{3,2,1,0:T(8,128)(2,1)S(1)}, bf16[2,2,160,128]{3,2,1,0:T(8,128)(2,1)}, u32[]{:S(2)}, u32[]{:S(2)}) collective-permute-start(bf16[2,2,160,128]{3,2,1,0:T(8,128)(2,1)S(1)} %pad_maximum_fusion.1.refs_4_), channel_id=1, source_target_pairs={{464,466},{465,467},{466,468},{467,469},{468,470},{469,471},{470,4... | collective-permute-start | bytes 491528 | tf_op jit(solution)/shard_map/ppermute | solution.py:30
  53.3 9.6 %collective-permute-start.6 = (bf16[2,2,160,128]{3,2,1,0:T(8,128)(2,1)}, bf16[2,2,160,128]{3,2,1,0:T(8,128)(2,1)}, u32[]{:S(2)}, u32[]{:S(2)}) collective-permute-start(bf16[2,2,160,128]{3,2,1,0:T(8,128)(2,1)} %collective-permute-done.5.refs_8_), channel_id=1, source_target_pairs={{464,478},{465,479},{466,464},{467,465},{468,466},{469,467},{470,4... | collective-permute-start | bytes 491528 | tf_op jit(solution)/shard_map/ppermute | solution.py:30
  57.6 9.8 %collective-permute-start.3 = (bf16[2,2,160,128]{3,2,1,0:T(8,128)(2,1)}, bf16[2,2,160,128]{3,2,1,0:T(8,128)(2,1)}, u32[]{:S(2)}, u32[]{:S(2)}) collective-permute-start(bf16[2,2,160,128]{3,2,1,0:T(8,128)(2,1)} %collective-permute-done.2.refs_5_), channel_id=1, source_target_pairs={{464,466},{465,467},{466,468},{467,469},{468,470},{469,471},{470,4... | collective-permute-start | bytes 491528 | tf_op jit(solution)/shard_map/ppermute | solution.py:30
  59.6 10.9 %copy-start.4 = (bf16[1,128,2560]{2,1,0:T(8,128)(2,1)S(1)}, bf16[1,128,2560]{2,1,0:T(8,128)(2,1)}, u32[]{:S(2)}) copy-start(bf16[1,128,2560]{2,1,0:T(8,128)(2,1)} %param.5) | copy-start | bytes 1966084
  62.9 38.9 %collective-permute-start.7 = (bf16[2,2,160,128]{3,2,1,0:T(8,128)(2,1)}, bf16[2,2,160,128]{3,2,1,0:T(8,128)(2,1)}, u32[]{:S(2)}, u32[]{:S(2)}) collective-permute-start(bf16[2,2,160,128]{3,2,1,0:T(8,128)(2,1)} %collective-permute-done.6.refs_9_), channel_id=1, source_target_pairs={{464,478},{465,479},{466,464},{467,465},{468,466},{469,467},{470,4... | collective-permute-start | bytes 491528 | tf_op jit(solution)/shard_map/ppermute | solution.py:30
  67.4 40.1 %collective-permute-start.4 = (bf16[2,2,160,128]{3,2,1,0:T(8,128)(2,1)}, bf16[2,2,160,128]{3,2,1,0:T(8,128)(2,1)}, u32[]{:S(2)}, u32[]{:S(2)}) collective-permute-start(bf16[2,2,160,128]{3,2,1,0:T(8,128)(2,1)} %collective-permute-done.3.refs_6_), channel_id=1, source_target_pairs={{464,466},{465,467},{466,468},{467,469},{468,470},{469,471},{470,4... | collective-permute-start | bytes 491528 | tf_op jit(solution)/shard_map/ppermute | solution.py:30
  73.2 27.1 %copy-start.3 = (bf16[4,128,2560]{2,1,0:T(8,128)(2,1)S(1)}, bf16[4,128,2560]{2,1,0:T(8,128)(2,1)}, u32[]{:S(2)}) copy-start(bf16[4,128,2560]{2,1,0:T(8,128)(2,1)} %copy-done.1) | copy-start | bytes 7864324
  77.3 33.1 %collective-permute-start.10 = (bf16[128,2560]{1,0:T(8,128)(2,1)}, bf16[128,2560]{1,0:T(8,128)(2,1)S(1)}, u32[]{:S(2)}, u32[]{:S(2)}) collective-permute-start(bf16[128,2560]{1,0:T(8,128)(2,1)} %get-tuple-element.36), channel_id=1, source_target_pairs={{16,0},{48,32},{80,64},{112,96},{144,128},{176,160},{208,192},{240... | collective-permute-start | bytes 1966088 | tf_op jit(solution)/shard_map/ppermute | solution.py:291
  98.9 16.1 %collective-permute-start = (bf16[128,2560]{1,0:T(8,128)(2,1)}, bf16[128,2560]{1,0:T(8,128)(2,1)}, u32[]{:S(2)}, u32[]{:S(2)}) collective-permute-start(bf16[128,2560]{1,0:T(8,128)(2,1)} %get-tuple-element.36), channel_id=1, source_target_pairs={{0,496},{32,16},{64,48},{96,80},{128,112},{160,144},{192,176},{224... | collective-permute-start | bytes 1966088 | tf_op jit(solution)/shard_map/ppermute | solution.py:290
  102.7 9.3 %collective-permute-start.9 = (bf16[1,2,160,128]{3,2,1,0:T(8,128)(2,1)S(1)}, bf16[1,2,160,128]{3,2,1,0:T(8,128)(2,1)S(1)}, u32[]{:S(2)}, u32[]{:S(2)}) collective-permute-start(bf16[1,2,160,128]{3,2,1,0:T(8,128)(2,1)S(1)} %slice.99), channel_id=1, source_target_pairs={{464,478},{465,479},{466,464},{467,465},{468,466},{469,467},{470,4... | collective-permute-start | bytes 245768 | tf_op jit(solution)/shard_map/ppermute | solution.py:30
  108.4 6.4 %collective-permute-start.8 = (bf16[1,2,160,128]{3,2,1,0:T(8,128)(2,1)S(1)}, bf16[1,2,160,128]{3,2,1,0:T(8,128)(2,1)S(1)}, u32[]{:S(2)}, u32[]{:S(2)}) collective-permute-start(bf16[1,2,160,128]{3,2,1,0:T(8,128)(2,1)S(1)} %slice.98), channel_id=1, source_target_pairs={{464,466},{465,467},{466,468},{467,469},{468,470},{469,471},{470,4... | collective-permute-start | bytes 245768 | tf_op jit(solution)/shard_map/ppermute | solution.py:30
  112.0 23.6 %copy-start.14 = (bf16[1,2,160,128]{3,2,1,0:T(8,128)(2,1)}, bf16[1,2,160,128]{3,2,1,0:T(8,128)(2,1)S(1)}, u32[]{:S(2)}) copy-start(bf16[1,2,160,128]{3,2,1,0:T(8,128)(2,1)S(1)} %collective-permute-done.9.refs_12_) | copy-start | bytes 245764
  114.8 20.8 %copy-start.16 = (bf16[1,2,160,128]{3,2,1,0:T(8,128)(2,1)}, bf16[1,2,160,128]{3,2,1,0:T(8,128)(2,1)S(1)}, u32[]{:S(2)}) copy-start(bf16[1,2,160,128]{3,2,1,0:T(8,128)(2,1)S(1)} %collective-permute-done.8.refs_11_) | copy-start | bytes 245764
  118.4 3.9 %collective-permute-start.11 = (bf16[128,2560]{1,0:T(8,128)(2,1)S(1)}, bf16[128,2560]{1,0:T(8,128)(2,1)S(1)}, u32[]{:S(2)}, u32[]{:S(2)}) collective-permute-start(bf16[128,2560]{1,0:T(8,128)(2,1)S(1)} %get-tuple-element.39), channel_id=1, source_target_pairs={{16,0},{48,32},{80,64},{112,96},{144,128},{176,160},{208,192},{240... | collective-permute-start | bytes 1966088 | tf_op jit(solution)/shard_map/ppermute | solution.py:296
  119.8 15.8 %collective-permute-start.13 = (bf16[128,2560]{1,0:T(8,128)(2,1)S(1)}, bf16[128,2560]{1,0:T(8,128)(2,1)S(1)}, u32[]{:S(2)}, u32[]{:S(2)}) collective-permute-start(bf16[128,2560]{1,0:T(8,128)(2,1)S(1)} %get-tuple-element.42), channel_id=1, source_target_pairs={{0,496},{32,16},{64,48},{96,80},{128,112},{160,144},{192,176},{224... | collective-permute-start | bytes 1966088 | tf_op jit(solution)/shard_map/ppermute | solution.py:294
  139.8 2.9 %copy-start.5 = (bf16[1,128,2560]{2,1,0:T(8,128)(2,1)S(1)}, bf16[1,128,2560]{2,1,0:T(8,128)(2,1)}, u32[]{:S(2)}) copy-start(bf16[1,128,2560]{2,1,0:T(8,128)(2,1)} %param.5) | copy-start | bytes 1966084
  139.8 21.0 %collective-permute-start.14 = (bf16[128,2560]{1,0:T(8,128)(2,1)}, bf16[128,2560]{1,0:T(8,128)(2,1)S(1)}, u32[]{:S(2)}, u32[]{:S(2)}) collective-permute-start(bf16[128,2560]{1,0:T(8,128)(2,1)} %get-tuple-element.44), channel_id=1, source_target_pairs={{16,0},{48,32},{80,64},{112,96},{144,128},{176,160},{208,192},{240... | collective-permute-start | bytes 1966088 | tf_op jit(solution)/shard_map/ppermute | solution.py:296
  141.3 22.4 %collective-permute-start.12 = (bf16[128,2560]{1,0:T(8,128)(2,1)}, bf16[128,2560]{1,0:T(8,128)(2,1)}, u32[]{:S(2)}, u32[]{:S(2)}) collective-permute-start(bf16[128,2560]{1,0:T(8,128)(2,1)} %get-tuple-element.41), channel_id=1, source_target_pairs={{0,496},{32,16},{64,48},{96,80},{128,112},{160,144},{192,176},{224... | collective-permute-start | bytes 1966088 | tf_op jit(solution)/shard_map/ppermute | solution.py:294
  142.7 2.0 copy-start.21
  150.3 10.6 %copy-start.13 = (f32[4,128,128]{2,1,0:T(8,128)S(1)}, f32[4,128,128]{2,1,0:T(8,128)}, u32[]{:S(2)}) copy-start(f32[4,128,128]{2,1,0:T(8,128)} %copy-done.10) | copy-start | bytes 786436
  150.3 10.6 %copy-start.15 = (bf16[1,2,160,128]{3,2,1,0:T(8,128)(2,1)S(1)}, bf16[1,2,160,128]{3,2,1,0:T(8,128)(2,1)}, u32[]{:S(2)}) copy-start(bf16[1,2,160,128]{3,2,1,0:T(8,128)(2,1)} %copy-done.14) | copy-start | bytes 245764
  150.3 10.6 %copy-start.17 = (bf16[1,2,160,128]{3,2,1,0:T(8,128)(2,1)S(1)}, bf16[1,2,160,128]{3,2,1,0:T(8,128)(2,1)}, u32[]{:S(2)}) copy-start(bf16[1,2,160,128]{3,2,1,0:T(8,128)(2,1)} %copy-done.16) | copy-start | bytes 245764
  151.5 9.4 %copy-start.23 = (bf16[1,2,2,160,128]{4,3,2,1,0:T(8,128)(2,1)}, bf16[1,2,2,160,128]{4,3,2,1,0:T(8,128)(2,1)S(1)}, u32[]{:S(2)}) copy-start(bf16[1,2,2,160,128]{4,3,2,1,0:T(8,128)(2,1)S(1)} %get-tuple-element.73) | copy-start | bytes 491524
  152.8 7.4 %collective-permute-start.18 = (bf16[1,2,160,128]{3,2,1,0:T(8,128)(2,1)S(1)}, bf16[1,2,160,128]{3,2,1,0:T(8,128)(2,1)S(1)}, u32[]{:S(2)}, u32[]{:S(2)}) collective-permute-start(bf16[1,2,160,128]{3,2,1,0:T(8,128)(2,1)S(1)} %get-tuple-element.75), channel_id=1, source_target_pairs={{464,478},{465,479},{466,464},{467,465},{468,466},{469,467},{470,4... | collective-permute-start | bytes 245768 | tf_op jit(solution)/shard_map/ppermute | solution.py:30
  158.3 30.5 %collective-permute-start.17 = (bf16[1,2,160,128]{3,2,1,0:T(8,128)(2,1)}, bf16[1,2,160,128]{3,2,1,0:T(8,128)(2,1)}, u32[]{:S(2)}, u32[]{:S(2)}) collective-permute-start(bf16[1,2,160,128]{3,2,1,0:T(8,128)(2,1)} %get-tuple-element.76), channel_id=1, source_target_pairs={{464,466},{465,467},{466,468},{467,469},{468,470},{469,471},{470,4... | collective-permute-start | bytes 245768 | tf_op jit(solution)/shard_map/ppermute | solution.py:30
  161.5 5.8 %copy-start.6 = (bf16[128,2560]{1,0:T(8,128)(2,1)}, bf16[128,2560]{1,0:T(8,128)(2,1)S(1)}, u32[]{:S(2)}) copy-start(bf16[128,2560]{1,0:T(8,128)(2,1)S(1)} %get-tuple-element.48) | copy-start | bytes 1966084
  163.7 4.4 %copy-start.20 = (f32[2560,256]{0,1:T(8,128)S(1)}, f32[2560,256]{0,1:T(8,128)}, u32[]{:S(2)}) copy-start(f32[2560,256]{0,1:T(8,128)} %copy-done.19) | copy-start | bytes 7864324
  173.8 14.9 %copy-start.24 = (bf16[1,2,2,160,128]{4,3,2,1,0:T(8,128)(2,1)S(1)}, bf16[1,2,2,160,128]{4,3,2,1,0:T(8,128)(2,1)}, u32[]{:S(2)}) copy-start(bf16[1,2,2,160,128]{4,3,2,1,0:T(8,128)(2,1)} %copy-done.23) | copy-start | bytes 491524
  173.8 15.8 %copy-start.25 = (bf16[1,2,160,128]{3,2,1,0:T(8,128)(2,1)S(1)}, bf16[1,2,160,128]{3,2,1,0:T(8,128)(2,1)}, u32[]{:S(2)}) copy-start(bf16[1,2,160,128]{3,2,1,0:T(8,128)(2,1)} %slice_bitcast_fusion.2) | copy-start | bytes 245764
  173.8 15.8 %copy-start.27 = (bf16[1,2,160,128]{3,2,1,0:T(8,128)(2,1)S(1)}, bf16[1,2,160,128]{3,2,1,0:T(8,128)(2,1)}, u32[]{:S(2)}) copy-start(bf16[1,2,160,128]{3,2,1,0:T(8,128)(2,1)} %fusion.48) | copy-start | bytes 245764
  173.9 16.5 %copy-start.26 = (bf16[1,2,160,128]{3,2,1,0:T(8,128)(2,1)S(1)}, bf16[1,2,160,128]{3,2,1,0:T(8,128)(2,1)}, u32[]{:S(2)}) copy-start(bf16[1,2,160,128]{3,2,1,0:T(8,128)(2,1)} %slice_bitcast_fusion.3) | copy-start | bytes 245764
  173.9 51.4 %copy-start.18 = (bf16[2560,128]{1,0:T(8,128)(2,1)S(1)}, bf16[2560,128]{1,0:T(8,128)(2,1)}, u32[]{:S(2)}) copy-start(bf16[2560,128]{1,0:T(8,128)(2,1)} %slice.134) | copy-start | bytes 1966084
  173.9 86.9 %all-to-all-start.1 = ((bf16[16,2,160,128]{3,2,1,0:T(8,128)(2,1)}), bf16[16,2,160,128]{3,2,1,0:T(8,128)(2,1)S(1)}, u32[]{:S(2)}, u32[]{:S(2)}) async-start(bf16[16,2,160,128]{3,2,1,0:T(8,128)(2,1)} %pad_maximum_fusion), calls=%async_computation.1 | async-start | bytes 2621440 | tf_op jit(solution)/shard_map/all_to_all | solution.py:322
  189.7 44.0 %copy-start.7 = (bf16[128,2560]{1,0:T(8,128)(2,1)S(1)}, bf16[128,2560]{1,0:T(8,128)(2,1)}, u32[]{:S(2)}) copy-start(bf16[128,2560]{1,0:T(8,128)(2,1)} %copy-done.6) | copy-start | bytes 1966084
  189.7 45.3 %copy-start.9 = (bf16[128,2560]{1,0:T(8,128)(2,1)S(1)}, bf16[128,2560]{1,0:T(8,128)(2,1)}, u32[]{:S(2)}) copy-start(bf16[128,2560]{1,0:T(8,128)(2,1)} %copy-done.8) | copy-start | bytes 1966084
  191.1 29.3 %collective-permute-start.19 = (bf16[2,2,160,128]{3,2,1,0:T(8,128)(2,1)}, bf16[2,2,160,128]{3,2,1,0:T(8,128)(2,1)S(1)}, u32[]{:S(2)}, u32[]{:S(2)}) collective-permute-start(bf16[2,2,160,128]{3,2,1,0:T(8,128)(2,1)} %pad_maximum_fusion.2), channel_id=1, source_target_pairs={{464,466},{465,467},{466,468},{467,469},{468,470},{469,471},{470,4... | collective-permute-start | bytes 491528 | tf_op jit(solution)/shard_map/ppermute | solution.py:30
  194.1 31.2 %collective-permute-start.20 = (bf16[2,2,160,128]{3,2,1,0:T(8,128)(2,1)}, bf16[2,2,160,128]{3,2,1,0:T(8,128)(2,1)}, u32[]{:S(2)}, u32[]{:S(2)}) collective-permute-start(bf16[2,2,160,128]{3,2,1,0:T(8,128)(2,1)} %pad_maximum_fusion.3), channel_id=1, source_target_pairs={{464,478},{465,479},{466,464},{467,465},{468,466},{469,467},{470,4... | collective-permute-start | bytes 491528 | tf_op jit(solution)/shard_map/ppermute | solution.py:30
  227.1 11.6 %collective-permute-start.21 = (bf16[2,2,160,128]{3,2,1,0:T(8,128)(2,1)}, bf16[2,2,160,128]{3,2,1,0:T(8,128)(2,1)}, u32[]{:S(2)}, u32[]{:S(2)}) collective-permute-start(bf16[2,2,160,128]{3,2,1,0:T(8,128)(2,1)} %get-tuple-element.59), channel_id=1, source_target_pairs={{464,466},{465,467},{466,468},{467,469},{468,470},{469,471},{470,4... | collective-permute-start | bytes 491528 | tf_op jit(solution)/shard_map/ppermute | solution.py:30
  229.9 8.8 %collective-permute-start.22 = (bf16[2,2,160,128]{3,2,1,0:T(8,128)(2,1)S(1)}, bf16[2,2,160,128]{3,2,1,0:T(8,128)(2,1)}, u32[]{:S(2)}, u32[]{:S(2)}) collective-permute-start(bf16[2,2,160,128]{3,2,1,0:T(8,128)(2,1)S(1)} %get-tuple-element.60), channel_id=1, source_target_pairs={{464,478},{465,479},{466,464},{467,465},{468,466},{469,467},{470,4... | collective-permute-start | bytes 491528 | tf_op jit(solution)/shard_map/ppermute | solution.py:30
  233.6 20.7 %collective-permute-start.16 = (bf16[128,2560]{1,0:T(8,128)(2,1)S(1)}, bf16[128,2560]{1,0:T(8,128)(2,1)}, u32[]{:S(2)}, u32[]{:S(2)}) collective-permute-start(bf16[128,2560]{1,0:T(8,128)(2,1)S(1)} %copy-done.7), channel_id=1, source_target_pairs={{0,496},{32,16},{64,48},{96,80},{128,112},{160,144},{192,176},{224... | collective-permute-start | bytes 1966088 | tf_op jit(solution)/shard_map/ppermute | solution.py:294
  234.9 19.4 %collective-permute-start.15 = (bf16[128,2560]{1,0:T(8,128)(2,1)S(1)}, bf16[128,2560]{1,0:T(8,128)(2,1)}, u32[]{:S(2)}, u32[]{:S(2)}) collective-permute-start(bf16[128,2560]{1,0:T(8,128)(2,1)S(1)} %copy-done.9), channel_id=1, source_target_pairs={{16,0},{48,32},{80,64},{112,96},{144,128},{176,160},{208,192},{240... | collective-permute-start | bytes 1966088 | tf_op jit(solution)/shard_map/ppermute | solution.py:296
  240.5 9.3 %collective-permute-start.23 = (bf16[2,2,160,128]{3,2,1,0:T(8,128)(2,1)}, bf16[2,2,160,128]{3,2,1,0:T(8,128)(2,1)}, u32[]{:S(2)}, u32[]{:S(2)}) collective-permute-start(bf16[2,2,160,128]{3,2,1,0:T(8,128)(2,1)} %get-tuple-element.61), channel_id=1, source_target_pairs={{464,466},{465,467},{466,468},{467,469},{468,470},{469,471},{470,4... | collective-permute-start | bytes 491528 | tf_op jit(solution)/shard_map/ppermute | solution.py:30
  242.5 8.0 %collective-permute-start.24 = (bf16[2,2,160,128]{3,2,1,0:T(8,128)(2,1)S(1)}, bf16[2,2,160,128]{3,2,1,0:T(8,128)(2,1)}, u32[]{:S(2)}, u32[]{:S(2)}) collective-permute-start(bf16[2,2,160,128]{3,2,1,0:T(8,128)(2,1)S(1)} %get-tuple-element.62), channel_id=1, source_target_pairs={{464,478},{465,479},{466,464},{467,465},{468,466},{469,467},{470,4... | collective-permute-start | bytes 491528 | tf_op jit(solution)/shard_map/ppermute | solution.py:30
  251.7 9.1 %collective-permute-start.25 = (bf16[2,160,128]{2,1,0:T(8,128)(2,1)S(1)}, bf16[2,160,128]{2,1,0:T(8,128)(2,1)S(1)}, u32[]{:S(2)}, u32[]{:S(2)}) collective-permute-start(bf16[2,160,128]{2,1,0:T(8,128)(2,1)S(1)} %fusion.47), channel_id=1, source_target_pairs={{464,465},{465,464},{466,467},{467,466},{468,469},{469,468},{470,4... | collective-permute-start | bytes 245768 | tf_op jit(solution)/shard_map/ppermute | solution.py:34
  (9 other events, 10.8 us)

commit v4 on v3

v4 whole, which is shorter than its diff:
```python
import functools

import jax
import jax.numpy as jnp
from jax import lax
from jax.experimental import pallas as pl
from jax.experimental.pallas import tpu as pltpu
from jax.sharding import PartitionSpec as P

EPS = 1e-06
F32 = jnp.float32
BF16 = jnp.bfloat16
LIMIT = pltpu.CompilerParams(vmem_limit_bytes=24 * 1024 * 1024)
IN_VMEM = pl.BlockSpec(memory_space=pltpu.VMEM)
ANYWHERE = pl.BlockSpec(memory_space=pl.ANY)
SCALAR = pl.BlockSpec(memory_space=pltpu.SMEM)


def dp_pairs(sections, n_dp):
    return [(s * n_dp + d, s * n_dp + (d ^ 1)) for s in sections for d in range(n_dp)]


def swapped(value, ring):
    return lax.ppermute(value, ("section", "dp"), dp_pairs(*ring))


def z_groups(n_dp):
    return [[2 * z + h for z in range(n_dp // 2)] for h in range(2)]


def paired(shard, ring):
    h = lax.axis_index("dp") % 2
    other = swapped(shard, ring)
    return jnp.stack([jnp.where(h == 0, shard, other), jnp.where(h == 0, other, shard)])


def reduced(parts, ring):
    h = lax.axis_index("dp") % 2
    total = lax.psum_scatter(
        parts, "dp", scatter_dimension=0, tiled=False, axis_index_groups=z_groups(ring[1])
    )
    mine = lax.dynamic_index_in_dim(total, h, 0, keepdims=False)
    other = lax.dynamic_index_in_dim(total, 1 - h, 0, keepdims=False)
    return mine, swapped(other, ring)


def norm_kernel(x_ref, normed_ref, inverse_ref):
    x = x_ref[0, 0].astype(F32)
    inverse = lax.rsqrt(jnp.mean(x * x, axis=-1, keepdims=True) + EPS)
    normed_ref[0] = (x * inverse).astype(BF16)
    inverse_ref[0] = jnp.broadcast_to(inverse, inverse_ref.shape[1:])


def norms(saved_inputs):
    ticks, _, rows, width = saved_inputs.shape
    return pl.pallas_call(
        norm_kernel,
        grid=(ticks,),
        out_shape=[
            jax.ShapeDtypeStruct((ticks, rows, width), BF16),
            jax.ShapeDtypeStruct((ticks, rows, 128), F32),
        ],
        in_specs=[pl.BlockSpec((1, 1, rows, width), lambda i: (i, 0, 0, 0))],
        out_specs=[
            pl.BlockSpec((1, rows, width), lambda i: (i, 0, 0)),
            pl.BlockSpec((1, rows, 128), lambda i: (i, 0, 0)),
        ],
        compiler_params=LIMIT,
        cost_estimate=pl.CostEstimate(
            flops=8 * ticks * rows * width, bytes_accessed=4 * ticks * rows * width, transcendentals=0
        ),
        name="norms",
    )(saved_inputs)


def tick_kernel(tick, flags_ref, *refs):
    incoming_ref, normed_ref, inverse_ref = refs[:3]
    level_refs = refs[3:-11]
    sent_ref, grad_latent_ref, active_ref = refs[-10:-7]
    incoming, normed, inverse, down, up, sent, sems = refs[-7:]
    n_dp, share, rank = down.shape
    width = n_dp * share

    @pl.when(flags_ref[0] == 1)
    def _():
        get_incoming = pltpu.make_async_copy(incoming_ref, incoming, sems.at[3])
        get_normed = pltpu.make_async_copy(normed_ref.at[tick], normed, sems.at[0])
        get_inverse = pltpu.make_async_copy(inverse_ref.at[tick], inverse, sems.at[4])
        get_incoming.start()
        for value, maps_ref in zip((1, 0), level_refs):

            @pl.when(flags_ref[1] == value)
            def _():
                pltpu.make_async_copy(maps_ref.at[:, 1], up, sems.at[2]).start()
                pltpu.make_async_copy(maps_ref.at[:, 0], down, sems.at[1]).start()

        get_normed.start()
        get_inverse.start()
        get_incoming.wait()
        pltpu.make_async_copy(level_refs[0].at[:, 1], up, sems.at[2]).wait()
        grad_act = jnp.dot(
            incoming[...], up[...].reshape(width, rank), preferred_element_type=F32
        )
        pltpu.make_async_copy(level_refs[0].at[:, 0], down, sems.at[1]).wait()
        get_normed.wait()
        get_inverse.wait()
        latent = jnp.dot(
            normed[...], down[...].reshape(width, rank), preferred_element_type=F32
        )
        gate = jax.nn.sigmoid(latent)
        active_ref[...] = (latent * gate).astype(BF16)
        slope = gate * (1.0 + latent * (1.0 - gate))
        grad_latent = (grad_act * slope).astype(BF16)
        grad_latent_ref[...] = grad_latent
        inner = jnp.sum(grad_latent.astype(F32) * latent, axis=-1, keepdims=True) / width
        inv = inverse[:, :1]
        scale = inv * inner
        blocks = 4
        run = width // blocks
        puts = []
        for block in range(blocks):
            at = pl.ds(block * run, run)
            piece = down[pl.ds(block * n_dp // blocks, n_dp // blocks)].reshape(run, rank)
            grad_normed = lax.dot_general(
                grad_latent, piece, (((1,), (1,)), ((), ())), preferred_element_type=F32
            )
            new = incoming[:, at].astype(F32) + (
                inv * grad_normed - normed[:, at].astype(F32) * scale
            )
            sent[:, at] = new.astype(BF16)
            puts.append(
                pltpu.make_async_copy(sent.at[:, at], sent_ref.at[:, at], sems.at[5 + block])
            )
            puts[-1].start()
        for put in puts:
            put.wait()


def tick_layer(tick, works, level, incoming, normed, inverse, maps, dep):
    _, rows, width = normed.shape
    n_dp, _, share, rank = maps[0].shape
    wide = jax.ShapeDtypeStruct((rows, width), BF16)
    narrow = jax.ShapeDtypeStruct((rows, rank), BF16)
    flags = jnp.stack([works.astype(jnp.int32), level.astype(jnp.int32)])
    return pl.pallas_call(
        functools.partial(tick_kernel, tick),
        out_shape=[wide, narrow, narrow],
        in_specs=[SCALAR] + [ANYWHERE] * (4 + len(maps)),
        out_specs=[ANYWHERE, IN_VMEM, IN_VMEM],
        scratch_shapes=[
            pltpu.VMEM((rows, width), BF16),
            pltpu.VMEM((rows, width), BF16),
            pltpu.VMEM((rows, 128), F32),
            pltpu.VMEM((n_dp, share, rank), BF16),
            pltpu.VMEM((n_dp, share, rank), BF16),
            pltpu.VMEM((rows, width), BF16),
            pltpu.SemaphoreType.DMA((9,)),
        ],
        compiler_params=LIMIT,
        cost_estimate=pl.CostEstimate(
            flops=40 * rows * width * rank, bytes_accessed=40 * rows * width, transcendentals=0
        ),
        name="tick_layer",
    )(flags, incoming, normed, inverse, *maps, dep)


def turned(block):
    share, rank = block.shape
    room = -(-share // 128) * 128
    if room != share:
        block = jnp.concatenate([block, jnp.zeros((room - share, rank), block.dtype)], axis=0)
    return block.T[:, :share]


def finish_kernel(level_ref, moved_ref, mine_ref, other_ref, down_ref, up_ref):
    rank = down_ref.shape[1]
    level = level_ref[0]
    main = jnp.sum(moved_ref[...].astype(F32), axis=0)
    rest = mine_ref[...].astype(F32) + other_ref[...].astype(F32)
    for i, out in enumerate((down_ref, up_ref)):
        lanes = slice(i * rank, (i + 1) * rank)
        out[level] = turned(main[:, lanes])
        out[1 - level] = turned(rest[:, lanes])


def finish(level, moved, mine, other):
    share, lanes = mine.shape
    rank = lanes // 2
    made = jax.ShapeDtypeStruct((2, rank, share), F32)
    return pl.pallas_call(
        finish_kernel,
        out_shape=[made, made],
        in_specs=[SCALAR] + [IN_VMEM] * 3,
        out_specs=[IN_VMEM] * 2,
        compiler_params=LIMIT,
        name="finish_sums",
    )(level.astype(jnp.int32)[None], moved, mine, other)


def on_device(saved_inputs, grad_in, adapter_down, adapter_up):
    n_sec = lax.axis_size("section")
    n_dp = lax.axis_size("dp")
    position = lax.axis_index("section")
    ticks = saved_inputs.shape[0]
    rank, share = adapter_down.shape[2], adapter_down.shape[3]
    width = saved_inputs.shape[3]
    even = position % 2 == 0
    levels = [1 - (position + tick) // n_sec for tick in range(ticks)]
    ring = (list(range(n_sec - ticks + 1, n_sec)), n_dp)

    def shard_of(level):
        return jnp.stack([adapter_down[level, 0].T, adapter_up[level, 0].T])

    pair = paired(shard_of(0), ring)
    shard = lax.optimization_barrier((shard_of(1), pair))[0]
    copies = jnp.broadcast_to(shard[None], (n_dp,) + shard.shape)
    first = lax.all_to_all(copies, "dp", 0, 0, tiled=True)
    second = lax.all_gather(pair, "dp", axis=0, axis_index_groups=z_groups(n_dp))
    second = second.reshape(first.shape)
    normed, inverse = norms(saved_inputs)

    def layer(tick, works, incoming, dep):
        met = any(s % 2 == (0 if works is even else 1) for s in range(n_sec - tick, n_sec))
        return tick_layer(
            tick,
            jnp.ones((), jnp.int32) if works is None else works,
            levels[tick],
            incoming,
            normed,
            inverse,
            [first, second] if met else [first],
            dep,
        )

    inside = [(s, s - 1) for s in range(1, n_sec, 2)]
    across = [(s, (s - 1) % n_sec) for s in range(0, n_sec, 2)]
    odd = ~even

    sent, latent, active = layer(0, None, grad_in[0], inverse)
    grads, latents, actives = [grad_in[0]], [latent], [active]
    over = lax.ppermute(sent, "section", across)
    core = lax.ppermute(sent, "section", inside)
    for tick in range(1, ticks):
        sent_even, latent_even, active_even = layer(tick, even, core, latent)
        next_over = lax.ppermute(sent_even, "section", across)
        sent_odd, latent_odd, active_odd = layer(tick, odd, over, latent_even)
        next_core = lax.ppermute(sent_odd, "section", inside)
        grads.append(jnp.where(even, core, over))
        latents.append(jnp.where(even, latent_even, latent_odd))
        actives.append(jnp.where(even, active_even, active_odd))
        latent = latent_odd
        over, core = next_over, next_core
    grad_out = jnp.where(even, core, over)

    def product(wide, narrow):
        return lax.dot_general(wide, narrow, (((0,), (0,)), ((), ())), preferred_element_type=F32)

    last = ticks - 1
    zero = jnp.zeros((), BF16)

    def kept(values, count, same):
        pick = [levels[t] == levels[last] for t in range(count)]
        return jnp.concatenate(
            [jnp.where(p if same else ~p, v, zero) for p, v in zip(pick, values)]
        )

    early = jnp.concatenate(grads[:last])
    early_normed = normed[:last].reshape(-1, width)
    rest = jnp.concatenate(
        [
            product(early_normed, kept(latents, last, False)).astype(BF16),
            product(early, kept(actives, last, False)).astype(BF16),
        ],
        axis=1,
    )
    mine, other = reduced(rest.reshape(n_dp // 2, 2, share, 2 * rank), ring)
    early_up = product(early, kept(actives, last, True))
    down = product(normed.reshape(-1, width), kept(latents, ticks, True))
    up = early_up + product(grads[last], actives[last])
    main = jnp.concatenate([down.astype(BF16), up.astype(BF16)], axis=1)
    moved = lax.all_to_all(main.reshape(n_dp, share, 2 * rank), "dp", 0, 0, tiled=True)
    down_grad, up_grad = finish(levels[last], moved, mine, other)
    return grad_out[None], down_grad[:, None], up_grad[:, None]


def solution(mesh):
    in_specs = (
        P(None, "section", "dp", None),
        P("section", "dp", None),
        P(None, "section", None, "dp"),
        P(None, "section", None, "dp"),
    )
    out_specs = (
        P("section", "dp", None),
        P(None, "section", None, "dp"),
        P(None, "section", None, "dp"),
    )
    return jax.shard_map(
        on_device, mesh=mesh, in_specs=in_specs, out_specs=out_specs, check_vma=False
    )
```

time: 266 us -> 233 us (0.88)
  the two profiles are of different devices: /device:TPU:63 before, /device:TPU:55 now
where the time goes in v4:
time: 233 us; the launch traced here: 232 us
  waiting for transfers between devices  122 us (52%)
  starting transfers between devices  44.2 us (19%)
  local copies, waits for them, and re-layouts  22.1 us (9%)
  Pallas kernels  17.6 us (8%)
  between operations  14.6 us (6%)
  other arithmetic  7.65 us (3%)
  matrix products  3.9 us (2%)
    reduce_scatter x1, waiting for transfers between devices, reduced(): lax.psum_scatter(parts, 'dp', scatter_dimension=0, tiled=False, axis_inde...  52.6 us
    all_to_all x1, waiting for transfers between devices, on_device(): first = lax.all_to_all(copies, 'dp', 0, 0, tiled=True)  41.5 us
    pallas_call x7, Pallas kernels, tick_layer(): pl.pallas_call(functools.partial(tick_kernel, tick), out_shape=[wide, nar...  16.4 us
    all_to_all x1, starting transfers between devices, on_device(): first = lax.all_to_all(copies, 'dp', 0, 0, tiled=True)  15.3 us
    unnamed x58, local copies, waits for them, and re-layouts  12.9 us
    all_to_all x1, starting transfers between devices, on_device(): lax.all_to_all(main.reshape(n_dp, share, 2 * rank), 'dp', 0, 0, tiled=True)  10.8 us
    ppermute x2, waiting for transfers between devices, swapped(): return lax.ppermute(value, ('section', 'dp'), dp_pairs(*ring))  10.7 us
    ppermute x3, waiting for transfers between devices, on_device(): next_over = lax.ppermute(sent_even, 'section', across)  9.96 us
  transfers between devices with their start and end apart: 14, of which 8 were waited for; matrix products, arithmetic and copies ran while one was open for 7% of the time, Pallas kernels for 4%

profile of v4, /device:TPU:55, one launch (start us, length us, event | category | flops | bytes accessed | tf_op | source)
XLA Modules:
  0.0 231.8 jit_solution(8377398923671318215)
XLA Ops:
  7.2 0.8 slice_bitcast_fusion.1
  8.0 0.8 slice_bitcast_fusion
  8.8 3.5 %collective-permute-start = (bf16[2,160,128]{2,1,0:T(8,128)(2,1)S(1)}, bf16[2,160,128]{2,1,0:T(8,128)(2,1)S(1)}, u32[]{:S(2)}, u32[]{:S(2)}) collective-permute-start(bf16[2,160,128]{2,1,0:T(8,128)(2,1)S(1)} %pad_maximum_fusion.7), channel_id=1, source_target_pairs={{464,465},{465,464},{466,467},{467,466},{468,469},{469,468},{470,4... | collective-permute-start | bytes 245768 | tf_op jit(solution)/shard_map/ppermute | solution.py:24
  12.4 5.5 %collective-permute-done = bf16[2,160,128]{2,1,0:T(8,128)(2,1)S(1)} collective-permute-done((bf16[2,160,128]{2,1,0:T(8,128)(2,1)S(1)}, bf16[2,160,128]{2,1,0:T(8,128)(2,1)S(1)}, u32[]{:S(2)}, u32[]{:S(2)}) %collective-permute-start) | collective-permute-done | bytes 81952 | tf_op jit(solution)/shard_map/ppermute | solution.py:24
  17.9 0.7 pad_maximum_fusion.5
  18.6 1.3 broadcast_in_dim.32
  19.9 15.3 %all-to-all-start = ((bf16[16,2,160,128]{3,2,1,0:T(8,128)(2,1)}), bf16[16,2,160,128]{3,2,1,0:T(8,128)(2,1)}, u32[]{:S(2)}, u32[]{:S(2)}) async-start(bf16[16,2,160,128]{3,2,1,0:T(8,128)(2,1)} %broadcast_in_dim.32), calls=%async_computation | async-start | bytes 2621440 | tf_op jit(solution)/shard_map/all_to_all | solution.py:217
  35.2 0.7 all-gather.3.cloned.1.call-update
  36.0 1.7 copy-done
  37.8 1.0 norms.1
  39.8 41.5 %all-to-all-done.refs_3_ = bf16[16,2,160,128]{3,2,1,0:T(8,128)(2,1)} async-done(((bf16[16,2,160,128]{3,2,1,0:T(8,128)(2,1)}), bf16[16,2,160,128]{3,2,1,0:T(8,128)(2,1)}, u32[]{:S(2)}, u32[]{:S(2)}) %all-to-all-start) | async-done | bytes 1310752 | tf_op jit(solution)/shard_map/all_to_all | solution.py:217
  81.3 0.9 copy-done.14
  82.3 3.7 %tick_layer.7 = (bf16[128,2560]{1,0:T(8,128)(2,1)}, bf16[128,128]{1,0:T(8,128)(2,1)S(1)}, bf16[128,128]{1,0:T(8,128)(2,1)S(1)}) custom-call(s32[2]{0:T(128)S(1)} %pad_add_fusion.flags_ref, bf16[128,2560]{1,0:T(8,128)(2,1)S(1)} %bitcast.56, bf16[4,128,2560]{2,1,0:T(8,128)(2,1)S(1)} %get-tuple-element.29.refs_1_, f32[4,128,128]{2,1,0:T(8,128)S(1)} %copy-done.14, ...), custom_call_target="tpu_custom_call" | custom-call | flops 1677721600 | bytes 13107200 | tf_op jit(solution)/shard_map/tick_layer/pallas_call | solution.py:145
  86.0 1.3 collective-permute-start.2
  87.4 1.3 collective-permute-start.1
  88.8 1.5 slice.19
  90.9 0.9 copy-done.15
  92.5 0.8 copy-done.11
  93.3 0.8 all-gather.3.cloned.1.call-done.refs_4_
  94.1 5.5 %collective-permute-done.1.refs_0_ = bf16[128,2560]{1,0:T(8,128)(2,1)} collective-permute-done((bf16[128,2560]{1,0:T(8,128)(2,1)}, bf16[128,2560]{1,0:T(8,128)(2,1)}, u32[]{:S(2)}, u32[]{:S(2)}) %collective-permute-start.1) | collective-permute-done | bytes 655392 | tf_op jit(solution)/shard_map/ppermute | solution.py:241
  99.6 1.3 copy-done.1
  100.9 0.9 copy-done.16
  101.9 3.5 %tick_layer.9 = (bf16[128,2560]{1,0:T(8,128)(2,1)S(1)}, bf16[128,128]{1,0:T(8,128)(2,1)S(1)}, bf16[128,128]{1,0:T(8,128)(2,1)S(1)}) custom-call(s32[2]{0:T(128)S(1)} %pad_add_fusion.6.flags_ref, bf16[128,2560]{1,0:T(8,128)(2,1)} %collective-permute-done.1.refs_0_, bf16[4,128,2560]{2,1,0:T(8,128)(2,1)S(1)} %get-tuple-element.29.refs_1_, ...), custom_call_target="tpu_custom_call" | custom-call | flops 1677721600 | bytes 13107200 | tf_op jit(solution)/shard_map/tick_layer/pallas_call | solution.py:145
  105.4 1.5 collective-permute-start.3
  106.9 1.3 collective-permute-start.5
  108.8 1.2 broadcast_select_fusion.1
  110.7 8.1 %collective-permute-done.5.refs_0_ = bf16[128,2560]{1,0:T(8,128)(2,1)S(1)} collective-permute-done((bf16[128,2560]{1,0:T(8,128)(2,1)S(1)}, bf16[128,2560]{1,0:T(8,128)(2,1)S(1)}, u32[]{:S(2)}, u32[]{:S(2)}) %collective-permute-start.5) | collective-permute-done | bytes 655392 | tf_op jit(solution)/shard_map/ppermute | solution.py:245
  118.8 3.8 %tick_layer.11 = (bf16[128,2560]{1,0:T(8,128)(2,1)}, bf16[128,128]{1,0:T(8,128)(2,1)S(1)}, bf16[128,128]{1,0:T(8,128)(2,1)S(1)}) custom-call(s32[2]{0:T(128)S(1)} %pad_add_fusion.3.flags_ref, bf16[128,2560]{1,0:T(8,128)(2,1)S(1)} %collective-permute-done.5.refs_0_, bf16[4,128,2560]{2,1,0:T(8,128)(2,1)S(1)} %get-tuple-element.29.refs_1_, ...), custom_call_target="tpu_custom_call" | custom-call | flops 1677721600 | bytes 13107200 | tf_op jit(solution)/shard_map/tick_layer/pallas_call | solution.py:145
  122.6 1.5 collective-permute-start.6
  124.1 1.3 collective-permute-start.4
  127.9 1.2 pad_maximum_fusion.2
  129.1 2.4 %copy.16 = bf16[2560,256]{1,0:T(8,128)(2,1)} copy(bf16[2560,256]{0,1:T(8,128)(2,1)} %pad_maximum_fusion.2) | data formatting | bytes 2621440 | tf_op jit(solution)/shard_map/concatenate | solution.py:269
  131.6 1.3 copy-done.3
  132.9 0.9 copy-done.18
  134.5 1.8 collective-permute-done.4.refs_0_
  136.3 3.5 %tick_layer.13 = (bf16[128,2560]{1,0:T(8,128)(2,1)S(1)}, bf16[128,128]{1,0:T(8,128)(2,1)S(1)}, bf16[128,128]{1,0:T(8,128)(2,1)S(1)}) custom-call(s32[2]{0:T(128)S(1)} %pad_add_fusion.2.flags_ref, bf16[128,2560]{1,0:T(8,128)(2,1)} %collective-permute-done.4.refs_0_, bf16[4,128,2560]{2,1,0:T(8,128)(2,1)S(1)} %get-tuple-element.29.refs_1_, ...), custom_call_target="tpu_custom_call" | custom-call | flops 1677721600 | bytes 13107200 | tf_op jit(solution)/shard_map/tick_layer/pallas_call | solution.py:145
  139.8 1.7 fusion.3
  143.7 1.4 copy.15
  145.1 10.8 %all-to-all-start.1 = ((bf16[16,160,256]{2,1,0:T(8,128)(2,1)}), bf16[16,160,256]{2,1,0:T(8,128)(2,1)S(1)}, u32[]{:S(2)}, u32[]{:S(2)}) async-start(bf16[16,160,256]{2,1,0:T(8,128)(2,1)} %bitcast.61), calls=%async_computation.1 | async-start | bytes 2621440 | tf_op jit(solution)/shard_map/all_to_all | solution.py:281
  156.0 1.3 collective-permute-start.8
  157.3 3.1 %collective-permute-start.7 = (bf16[128,2560]{1,0:T(8,128)(2,1)S(1)}, bf16[128,2560]{1,0:T(8,128)(2,1)}, u32[]{:S(2)}, u32[]{:S(2)}) collective-permute-start(bf16[128,2560]{1,0:T(8,128)(2,1)S(1)} %copy-done.10), channel_id=1, source_target_pairs={{16,0},{48,32},{80,64},{112,96},{144,128},{176,160},{208,192},{240... | collective-permute-start | bytes 1966088 | tf_op jit(solution)/shard_map/ppermute | solution.py:247
  160.4 52.6 %reduce-scatter.2.cloned.1.call-done = bf16[1,2,160,256]{3,2,1,0:T(8,128)(2,1)} async-done(((bf16[8,2,160,256]{3,2,1,0:T(8,128)(2,1)}), bf16[1,2,160,256]{3,2,1,0:T(8,128)(2,1)}) %reduce-scatter.2.cloned.1.call-update) | async-done | bytes 163856 | tf_op jit(solution)/shard_map/reduce_scatter | solution.py:39
  213.1 0.9 dynamic-slice_bitcast_fusion
  214.0 1.9 collective-permute-start.9
  215.9 2.0 select_bitcast_fusion
  218.0 5.1 %collective-permute-done.9.other_ref = bf16[160,256]{1,0:T(8,128)(2,1)S(1)} collective-permute-done((bf16[160,256]{1,0:T(8,128)(2,1)S(1)}, bf16[160,256]{1,0:T(8,128)(2,1)S(1)}, u32[]{:S(2)}, u32[]{:S(2)}) %collective-permute-start.9) | collective-permute-done | bytes 81952 | tf_op jit(solution)/shard_map/ppermute | solution.py:24
  223.4 0.8 copy.17
  224.2 0.8 copy.18
  (82 shorter events, 9.4 us)
Async XLA Ops:
  8.8 9.1 %collective-permute-start = (bf16[2,160,128]{2,1,0:T(8,128)(2,1)S(1)}, bf16[2,160,128]{2,1,0:T(8,128)(2,1)S(1)}, u32[]{:S(2)}, u32[]{:S(2)}) collective-permute-start(bf16[2,160,128]{2,1,0:T(8,128)(2,1)S(1)} %pad_maximum_fusion.7), channel_id=1, source_target_pairs={{464,465},{465,464},{466,467},{467,466},{468,469},{469,468},{470,4... | collective-permute-start | bytes 245768 | tf_op jit(solution)/shard_map/ppermute | solution.py:24
  19.9 61.4 %copy-start.4 = (bf16[1,128,2560]{2,1,0:T(8,128)(2,1)S(1)}, bf16[1,128,2560]{2,1,0:T(8,128)(2,1)}, u32[]{:S(2)}) copy-start(bf16[1,128,2560]{2,1,0:T(8,128)(2,1)} %param.5) | copy-start | bytes 1966084
  19.9 61.4 %all-to-all-start = ((bf16[16,2,160,128]{3,2,1,0:T(8,128)(2,1)}), bf16[16,2,160,128]{3,2,1,0:T(8,128)(2,1)}, u32[]{:S(2)}, u32[]{:S(2)}) async-start(bf16[16,2,160,128]{3,2,1,0:T(8,128)(2,1)} %broadcast_in_dim.32), calls=%async_computation | async-start | bytes 2621440 | tf_op jit(solution)/shard_map/all_to_all | solution.py:217
  35.2 58.9 %all-gather.3.cloned.1.call-start = ((), (), s32[]{:S(2)}) async-start(), calls=%async_computation.4 | async-start | bytes 1474560 | tf_op jit(solution)/shard_map/all_gather | solution.py:218
  35.9 177.1 %reduce-scatter.2.cloned.1.call-start = ((), (), s32[]{:S(2)}) async-start(), calls=%async_computation.3 | async-start | bytes 1474560 | tf_op jit(solution)/shard_map/reduce_scatter | solution.py:39
  36.0 1.7 copy-start
  38.7 0.7 copy-start.13
  81.3 1.0 copy-start.14
  86.0 4.9 %collective-permute-start.2 = (bf16[128,2560]{1,0:T(8,128)(2,1)}, bf16[128,2560]{1,0:T(8,128)(2,1)S(1)}, u32[]{:S(2)}, u32[]{:S(2)}) collective-permute-start(bf16[128,2560]{1,0:T(8,128)(2,1)} %get-tuple-element.32), channel_id=1, source_target_pairs={{16,0},{48,32},{80,64},{112,96},{144,128},{176,160},{208,192},{240... | collective-permute-start | bytes 1966088 | tf_op jit(solution)/shard_map/ppermute | solution.py:242
  87.4 12.2 %collective-permute-start.1 = (bf16[128,2560]{1,0:T(8,128)(2,1)}, bf16[128,2560]{1,0:T(8,128)(2,1)}, u32[]{:S(2)}, u32[]{:S(2)}) collective-permute-start(bf16[128,2560]{1,0:T(8,128)(2,1)} %get-tuple-element.32), channel_id=1, source_target_pairs={{0,496},{32,16},{64,48},{96,80},{128,112},{160,144},{192,176},{224... | collective-permute-start | bytes 1966088 | tf_op jit(solution)/shard_map/ppermute | solution.py:241
  90.9 1.0 copy-start.15
  92.5 0.9 copy-start.11
  99.6 1.3 copy-start.1
  100.9 0.9 copy-start.16
  101.9 5.0 %copy-start.12 = (bf16[128,2560]{1,0:T(8,128)(2,1)S(1)}, bf16[128,2560]{1,0:T(8,128)(2,1)}, u32[]{:S(2)}) copy-start(bf16[128,2560]{1,0:T(8,128)(2,1)} %copy-done.11) | copy-start | bytes 1966084
  105.4 4.6 %copy-start.2 = (bf16[16,2,160,128]{3,2,1,0:T(8,128)(2,1)S(1)}, bf16[16,2,160,128]{3,2,1,0:T(8,128)(2,1)}, u32[]{:S(2)}) copy-start(bf16[16,2,160,128]{3,2,1,0:T(8,128)(2,1)} %all-gather.3.cloned.1.call-done.refs_4_) | copy-start | bytes 3932164
  105.4 4.6 %copy-start.17 = (f32[4,128,128]{2,1,0:T(8,128)S(1)}, f32[4,128,128]{2,1,0:T(8,128)}, u32[]{:S(2)}) copy-start(f32[4,128,128]{2,1,0:T(8,128)} %copy-done.13) | copy-start | bytes 786436
  105.4 4.6 %collective-permute-start.3 = (bf16[128,2560]{1,0:T(8,128)(2,1)S(1)}, bf16[128,2560]{1,0:T(8,128)(2,1)S(1)}, u32[]{:S(2)}, u32[]{:S(2)}) collective-permute-start(bf16[128,2560]{1,0:T(8,128)(2,1)S(1)} %get-tuple-element.35), channel_id=1, source_target_pairs={{16,0},{48,32},{80,64},{112,96},{144,128},{176,160},{208,192},{240... | collective-permute-start | bytes 1966088 | tf_op jit(solution)/shard_map/ppermute | solution.py:247
  106.9 11.9 %collective-permute-start.5 = (bf16[128,2560]{1,0:T(8,128)(2,1)S(1)}, bf16[128,2560]{1,0:T(8,128)(2,1)S(1)}, u32[]{:S(2)}, u32[]{:S(2)}) collective-permute-start(bf16[128,2560]{1,0:T(8,128)(2,1)S(1)} %copy-done.12), channel_id=1, source_target_pairs={{0,496},{32,16},{64,48},{96,80},{128,112},{160,144},{192,176},{224... | collective-permute-start | bytes 1966088 | tf_op jit(solution)/shard_map/ppermute | solution.py:245
  110.0 16.7 %copy-start.21 = (bf16[128,2560]{1,0:T(8,128)(2,1)}, bf16[128,2560]{1,0:T(8,128)(2,1)S(1)}, u32[]{:S(2)}) copy-start(bf16[128,2560]{1,0:T(8,128)(2,1)S(1)} %broadcast_select_fusion.1) | copy-start | bytes 1966084
  122.6 3.5 %copy-start.20 = (bf16[3,128,2560]{2,1,0:T(8,128)(2,1)S(1)}, bf16[3,128,2560]{2,1,0:T(8,128)(2,1)}, u32[]{:S(2)}) copy-start(bf16[3,128,2560]{2,1,0:T(8,128)(2,1)} %slice.19) | copy-start | bytes 5898244
  122.6 8.9 %collective-permute-start.6 = (bf16[128,2560]{1,0:T(8,128)(2,1)}, bf16[128,2560]{1,0:T(8,128)(2,1)S(1)}, u32[]{:S(2)}, u32[]{:S(2)}) collective-permute-start(bf16[128,2560]{1,0:T(8,128)(2,1)} %get-tuple-element.40), channel_id=1, source_target_pairs={{16,0},{48,32},{80,64},{112,96},{144,128},{176,160},{208,192},{240... | collective-permute-start | bytes 1966088 | tf_op jit(solution)/shard_map/ppermute | solution.py:247
  124.1 12.2 %collective-permute-start.4 = (bf16[128,2560]{1,0:T(8,128)(2,1)}, bf16[128,2560]{1,0:T(8,128)(2,1)}, u32[]{:S(2)}, u32[]{:S(2)}) collective-permute-start(bf16[128,2560]{1,0:T(8,128)(2,1)} %get-tuple-element.37), channel_id=1, source_target_pairs={{0,496},{32,16},{64,48},{96,80},{128,112},{160,144},{192,176},{224... | collective-permute-start | bytes 1966088 | tf_op jit(solution)/shard_map/ppermute | solution.py:245
  126.0 1.3 copy-start.5
  126.0 1.3 copy-start.25
  126.1 1.8 copy-start.23
  131.6 1.3 copy-start.3
  132.9 0.9 copy-start.18
  133.8 2.5 %copy-start.19 = (f32[4,128,128]{2,1,0:T(8,128)S(1)}, f32[4,128,128]{2,1,0:T(8,128)}, u32[]{:S(2)}) copy-start(f32[4,128,128]{2,1,0:T(8,128)} %copy-done.13) | copy-start | bytes 786436
  134.5 5.3 %copy-start.7 = (bf16[128,2560]{1,0:T(8,128)(2,1)}, bf16[128,2560]{1,0:T(8,128)(2,1)S(1)}, u32[]{:S(2)}) copy-start(bf16[128,2560]{1,0:T(8,128)(2,1)S(1)} %get-tuple-element.44) | copy-start | bytes 1966084
  139.8 2.3 %copy-start.9 = (bf16[128,2560]{1,0:T(8,128)(2,1)}, bf16[128,2560]{1,0:T(8,128)(2,1)S(1)}, u32[]{:S(2)}) copy-start(bf16[128,2560]{1,0:T(8,128)(2,1)S(1)} %get-tuple-element.43) | copy-start | bytes 1966084
  141.5 1.1 copy-start.6
  141.5 1.3 copy-start.22
  141.6 1.5 copy-start.24
  141.6 1.5 copy-start.26
  141.6 1.4 copy-start.27
  145.1 10.8 %copy-start.8 = (bf16[128,2560]{1,0:T(8,128)(2,1)S(1)}, bf16[128,2560]{1,0:T(8,128)(2,1)}, u32[]{:S(2)}) copy-start(bf16[128,2560]{1,0:T(8,128)(2,1)} %copy-done.7) | copy-start | bytes 1966084
  145.1 12.1 %copy-start.10 = (bf16[128,2560]{1,0:T(8,128)(2,1)S(1)}, bf16[128,2560]{1,0:T(8,128)(2,1)}, u32[]{:S(2)}) copy-start(bf16[128,2560]{1,0:T(8,128)(2,1)} %copy-done.9) | copy-start | bytes 1966084
  145.1 78.0 %all-to-all-start.1 = ((bf16[16,160,256]{2,1,0:T(8,128)(2,1)}), bf16[16,160,256]{2,1,0:T(8,128)(2,1)S(1)}, u32[]{:S(2)}, u32[]{:S(2)}) async-start(bf16[16,160,256]{2,1,0:T(8,128)(2,1)} %bitcast.61), calls=%async_computation.1 | async-start | bytes 2621440 | tf_op jit(solution)/shard_map/all_to_all | solution.py:281
  156.0 60.0 %collective-permute-start.8 = (bf16[128,2560]{1,0:T(8,128)(2,1)S(1)}, bf16[128,2560]{1,0:T(8,128)(2,1)}, u32[]{:S(2)}, u32[]{:S(2)}) collective-permute-start(bf16[128,2560]{1,0:T(8,128)(2,1)S(1)} %copy-done.8), channel_id=1, source_target_pairs={{0,496},{32,16},{64,48},{96,80},{128,112},{160,144},{192,176},{224... | collective-permute-start | bytes 1966088 | tf_op jit(solution)/shard_map/ppermute | solution.py:245
  157.3 58.7 %collective-permute-start.7 = (bf16[128,2560]{1,0:T(8,128)(2,1)S(1)}, bf16[128,2560]{1,0:T(8,128)(2,1)}, u32[]{:S(2)}, u32[]{:S(2)}) collective-permute-start(bf16[128,2560]{1,0:T(8,128)(2,1)S(1)} %copy-done.10), channel_id=1, source_target_pairs={{16,0},{48,32},{80,64},{112,96},{144,128},{176,160},{208,192},{240... | collective-permute-start | bytes 1966088 | tf_op jit(solution)/shard_map/ppermute | solution.py:247
  214.0 9.1 %collective-permute-start.9 = (bf16[160,256]{1,0:T(8,128)(2,1)S(1)}, bf16[160,256]{1,0:T(8,128)(2,1)S(1)}, u32[]{:S(2)}, u32[]{:S(2)}) collective-permute-start(bf16[160,256]{1,0:T(8,128)(2,1)S(1)} %get-tuple-element.64), channel_id=1, source_target_pairs={{464,465},{465,464},{466,467},{467,466},{468,469},{469,468},{470,4... | collective-permute-start | bytes 245768 | tf_op jit(solution)/shard_map/ppermute | solution.py:24
Sparse Core Ops, SparseCore 0:
  38.7 55.3 all-gather.2
  131.7 81.3 reduce-scatter.1

commit v5 on v4

--- a/solution.py
+++ b/solution.py
@@ -16,32 +16,85 @@
 SCALAR = pl.BlockSpec(memory_space=pltpu.SMEM)
 
 
-def dp_pairs(sections, n_dp):
-    return [(s * n_dp + d, s * n_dp + (d ^ 1)) for s in sections for d in range(n_dp)]
+def dp_pairs(sections, n_dp, step, flip):
+    n_z = n_dp // 2
+    return [
+        (s * n_dp + 2 * z + h, s * n_dp + 2 * ((z + step) % n_z) + (h ^ flip))
+        for s in sections
+        for z in range(n_z)
+        for h in range(2)
+    ]
+
+
+def shifted(value, ring, step):
+    return lax.ppermute(value, ("section", "dp"), dp_pairs(*ring, step, 0))
 
 
 def swapped(value, ring):
-    return lax.ppermute(value, ("section", "dp"), dp_pairs(*ring))
-
-
-def z_groups(n_dp):
-    return [[2 * z + h for z in range(n_dp // 2)] for h in range(2)]
-
-
-def paired(shard, ring):
+    return lax.ppermute(value, ("section", "dp"), dp_pairs(*ring, 0, 1))
+
+
+def together(*lists):
+    flat = iter(lax.optimization_barrier(tuple(v for values in lists for v in values)))
+    return [[next(flat) for _ in values] for values in lists]
+
+
+def gathered(shards, rings):
     h = lax.axis_index("dp") % 2
-    other = swapped(shard, ring)
-    return jnp.stack([jnp.where(h == 0, shard, other), jnp.where(h == 0, other, shard)])
-
-
-def reduced(parts, ring):
-    h = lax.axis_index("dp") % 2
-    total = lax.psum_scatter(
-        parts, "dp", scatter_dimension=0, tiled=False, axis_index_groups=z_groups(ring[1])
-    )
-    mine = lax.dynamic_index_in_dim(total, h, 0, keepdims=False)
-    other = lax.dynamic_index_in_dim(total, 1 - h, 0, keepdims=False)
-    return mine, swapped(other, ring)
+    pairs = []
+    for shard, ring in zip(shards, rings):
+        other = swapped(shard, ring)
+        pairs.append(
+            jnp.stack([jnp.where(h == 0, shard, other), jnp.where(h == 0, other, shard)])
+        )
+    steps = rings[0][1] // 4
+    rights, lefts = [pairs], [pairs]
+    for step in range(1, steps):
+        right = [shifted(v, ring, 1) for v, ring in zip(rights[-1], rings)]
+        left = [shifted(v, ring, -1) for v, ring in zip(lefts[-1], rings)]
+        if step < steps - 1:
+            right, left = together(right, left)
+        rights.append(right)
+        lefts.append(left)
+    return [
+        [pairs[i]]
+        + [right[i] for right in rights[1:]]
+        + [left[i] for left in lefts[1:]]
+        + [shifted(rights[-1][i][:1], ring, 1), shifted(lefts[-1][i][1:], ring, -1)]
+        for i, ring in enumerate(rings)
+    ]
+
+
+def reduced(parts, rings):
+    n_z = rings[0][1] // 2
+    index = lax.axis_index("dp")
+    z, h = index // 2, index % 2
+    half = n_z // 2
+
+    def at(part, offset):
+        return lax.dynamic_index_in_dim(part, (z + offset) % n_z, 0, keepdims=False)
+
+    right = [shifted(at(part, half)[:1], ring, 1) for part, ring in zip(parts, rings)]
+    left = [shifted(at(part, half)[1:], ring, -1) for part, ring in zip(parts, rings)]
+    for step in range(half - 1, 0, -1):
+        right, left = together(right, left)
+        here = [at(part, step) for part in parts]
+        there = [at(part, -step) for part in parts]
+        if step == half - 1:
+            here = [jnp.concatenate([v[:1] + r, v[1:]], axis=0) for v, r in zip(here, right)]
+            there = [jnp.concatenate([v[:1], v[1:] + r], axis=0) for v, r in zip(there, left)]
+        else:
+            here = [v + r for v, r in zip(here, right)]
+            there = [v + r for v, r in zip(there, left)]
+        right = [shifted(v, ring, 1) for v, ring in zip(here, rings)]
+        left = [shifted(v, ring, -1) for v, ring in zip(there, rings)]
+    terms = []
+    for part, ring, r, v in zip(parts, rings, right, left):
+        total = at(part, 0).astype(F32) + r.astype(F32) + v.astype(F32)
+        mine = lax.dynamic_index_in_dim(total, h, 0, keepdims=False)
+        other = lax.dynamic_index_in_dim(total, 1 - h, 0, keepdims=False).astype(BF16)
+        terms += [mine, swapped(other, ring)]
+    return terms
 
 
 def norm_kernel(x_ref, normed_ref, inverse_ref):
@@ -75,11 +128,27 @@
 
 def tick_kernel(tick, flags_ref, *refs):
     incoming_ref, normed_ref, inverse_ref = refs[:3]
-    level_refs = refs[3:-11]
+    pieces = refs[3:-11]
     sent_ref, grad_latent_ref, active_ref = refs[-10:-7]
     incoming, normed, inverse, down, up, sent, sems = refs[-7:]
     n_dp, share, rank = down.shape
     width = n_dp * share
+    n_z = n_dp // 2
+    half = n_z // 2
+    offsets = [0] + list(range(-1, -half, -1)) + list(range(1, half))
+
+    def place(level_pieces, which, target, sem):
+        z = flags_ref[2]
+        for piece, offset in zip(level_pieces, offsets):
+            at = lax.rem(z + (offset + n_z), n_z) * 2
+            pltpu.make_async_copy(piece.at[:, which], target.at[pl.ds(at, 2)], sem).start()
+        far = lax.rem(z + half, n_z) * 2
+        for h in range(2):
+            piece = level_pieces[n_z - 1 + h]
+            pltpu.make_async_copy(piece.at[:, which], target.at[pl.ds(far + h, 1)], sem).start()
+
+    def placed(target, sem):
+        pltpu.make_async_copy(target, target, sem).wait()
 
     @pl.when(flags_ref[0] == 1)
     def _():
@@ -87,21 +156,22 @@
         get_normed = pltpu.make_async_copy(normed_ref.at[tick], normed, sems.at[0])
         get_inverse = pltpu.make_async_copy(inverse_ref.at[tick], inverse, sems.at[4])
         get_incoming.start()
-        for value, maps_ref in zip((1, 0), level_refs):
-
-            @pl.when(flags_ref[1] == value)
-            def _():
-                pltpu.make_async_copy(maps_ref.at[:, 1], up, sems.at[2]).start()
-                pltpu.make_async_copy(maps_ref.at[:, 0], down, sems.at[1]).start()
+        for value, start in ((1, 0), (0, n_z + 1)):
+            if start < len(pieces):
+
+                @pl.when(flags_ref[1] == value)
+                def _():
+                    place(pieces[start : start + n_z + 1], 1, up, sems.at[2])
+                    place(pieces[start : start + n_z + 1], 0, down, sems.at[1])
 
         get_normed.start()
         get_inverse.start()
         get_incoming.wait()
-        pltpu.make_async_copy(level_refs[0].at[:, 1], up, sems.at[2]).wait()
+        placed(up, sems.at[2])
         grad_act = jnp.dot(
             incoming[...], up[...].reshape(width, rank), preferred_element_type=F32
         )
-        pltpu.make_async_copy(level_refs[0].at[:, 0], down, sems.at[1]).wait()
+        placed(down, sems.at[1])
         get_normed.wait()
         get_inverse.wait()
         latent = jnp.dot(
@@ -136,16 +206,17 @@
             put.wait()
 
 
-def tick_layer(tick, works, level, incoming, normed, inverse, maps, dep):
+def tick_layer(tick, works, level, z, incoming, normed, inverse, pieces, dep):
     _, rows, width = normed.shape
-    n_dp, _, share, rank = maps[0].shape
+    _, _, share, rank = pieces[0].shape
+    n_dp = width // share
     wide = jax.ShapeDtypeStruct((rows, width), BF16)
     narrow = jax.ShapeDtypeStruct((rows, rank), BF16)
-    flags = jnp.stack([works.astype(jnp.int32), level.astype(jnp.int32)])
+    flags = jnp.stack([works.astype(jnp.int32), level.astype(jnp.int32), z.astype(jnp.int32)])
     return pl.pallas_call(
         functools.partial(tick_kernel, tick),
         out_shape=[wide, narrow, narrow],
-        in_specs=[SCALAR] + [ANYWHERE] * (4 + len(maps)),
+        in_specs=[SCALAR] + [ANYWHERE] * (4 + len(pieces)),
         out_specs=[ANYWHERE, IN_VMEM, IN_VMEM],
         scratch_shapes=[
             pltpu.VMEM((rows, width), BF16),
@@ -161,7 +232,7 @@
             flops=40 * rows * width * rank, bytes_accessed=40 * rows * width, transcendentals=0
         ),
         name="tick_layer",
-    )(flags, incoming, normed, inverse, *maps, dep)
+    )(flags, incoming, normed, inverse, *pieces, dep)
 
 
 def turned(block):
@@ -172,35 +243,36 @@
     return block.T[:, :share]
 
 
-def finish_kernel(level_ref, moved_ref, mine_ref, other_ref, down_ref, up_ref):
+def finish_kernel(level_ref, mine_ref, other_ref, rest_mine_ref, rest_other_ref, down_ref, up_ref):
     rank = down_ref.shape[1]
     level = level_ref[0]
-    main = jnp.sum(moved_ref[...].astype(F32), axis=0)
-    rest = mine_ref[...].astype(F32) + other_ref[...].astype(F32)
+    main = mine_ref[...] + other_ref[...].astype(F32)
+    rest = rest_mine_ref[...] + rest_other_ref[...].astype(F32)
     for i, out in enumerate((down_ref, up_ref)):
         lanes = slice(i * rank, (i + 1) * rank)
         out[level] = turned(main[:, lanes])
         out[1 - level] = turned(rest[:, lanes])
 
 
-def finish(level, moved, mine, other):
-    share, lanes = mine.shape
+def finish(level, terms):
+    share, lanes = terms[0].shape
     rank = lanes // 2
     made = jax.ShapeDtypeStruct((2, rank, share), F32)
     return pl.pallas_call(
         finish_kernel,
         out_shape=[made, made],
-        in_specs=[SCALAR] + [IN_VMEM] * 3,
+        in_specs=[SCALAR] + [IN_VMEM] * 4,
         out_specs=[IN_VMEM] * 2,
         compiler_params=LIMIT,
         name="finish_sums",
-    )(level.astype(jnp.int32)[None], moved, mine, other)
+    )(level.astype(jnp.int32)[None], *terms)
 
 
 def on_device(saved_inputs, grad_in, adapter_down, adapter_up):
     n_sec = lax.axis_size("section")
     n_dp = lax.axis_size("dp")
     position = lax.axis_index("section")
+    z = lax.axis_index("dp") // 2
     ticks = saved_inputs.shape[0]
     rank, share = adapter_down.shape[2], adapter_down.shape[3]
     width = saved_inputs.shape[3]
@@ -211,12 +283,8 @@
     def shard_of(level):
         return jnp.stack([adapter_down[level, 0].T, adapter_up[level, 0].T])
 
-    pair = paired(shard_of(0), ring)
-    shard = lax.optimization_barrier((shard_of(1), pair))[0]
-    copies = jnp.broadcast_to(shard[None], (n_dp,) + shard.shape)
-    first = lax.all_to_all(copies, "dp", 0, 0, tiled=True)
-    second = lax.all_gather(pair, "dp", axis=0, axis_index_groups=z_groups(n_dp))
-    second = second.reshape(first.shape)
+    rings = [(list(range(n_sec)), n_dp), ring]
+    first, second = gathered([shard_of(1), shard_of(0)], rings)
     normed, inverse = norms(saved_inputs)
 
     def layer(tick, works, incoming, dep):
@@ -225,10 +293,11 @@
             tick,
             jnp.ones((), jnp.int32) if works is None else works,
             levels[tick],
+            z,
             incoming,
             normed,
             inverse,
-            [first, second] if met else [first],
+            first + second if met else first,
             dep,
         )
 
@@ -264,8 +333,8 @@
             [jnp.where(p if same else ~p, v, zero) for p, v in zip(pick, values)]
         )
 
-    early = jnp.concatenate(grads[:last])
-    early_normed = normed[:last].reshape(-1, width)
+    early = lax.optimization_barrier((jnp.concatenate(grads[:last]), latent_even))[0]
+    early_normed = lax.optimization_barrier((normed[:last].reshape(-1, width), latent_even))[0]
     rest = jnp.concatenate(
         [
             product(early_normed, kept(latents, last, False)).astype(BF16),
@@ -273,13 +342,12 @@
         ],
         axis=1,
     )
-    mine, other = reduced(rest.reshape(n_dp // 2, 2, share, 2 * rank), ring)
     early_up = product(early, kept(actives, last, True))
     down = product(normed.reshape(-1, width), kept(latents, ticks, True))
     up = early_up + product(grads[last], actives[last])
     main = jnp.concatenate([down.astype(BF16), up.astype(BF16)], axis=1)
-    moved = lax.all_to_all(main.reshape(n_dp, share, 2 * rank), "dp", 0, 0, tiled=True)
-    down_grad, up_grad = finish(levels[last], moved, mine, other)
+    parts = [v.reshape(n_dp // 2, 2, share, 2 * rank) for v in (main, rest)]
+    down_grad, up_grad = finish(levels[last], reduced(parts, rings))
     return grad_out[None], down_grad[:, None], up_grad[:, None]
 
 

time: 233 us -> 257 us (1.10)
  the two profiles are of different devices: /device:TPU:55 before, /device:TPU:31 now
where the time goes in v5:
time: 257 us; the launch traced here: 255 us
  starting transfers between devices  148 us (58%)
  waiting for transfers between devices  42.8 us (17%)
  local copies, waits for them, and re-layouts  25.9 us (10%)
  Pallas kernels  17.8 us (7%)
  other arithmetic  15.2 us (6%)
  matrix products  3.36 us (1%)
    ppermute x32, starting transfers between devices, shifted(): return lax.ppermute(value, ('section', 'dp'), dp_pairs(*ring, step, 0))  110 us
    ppermute x3, waiting for transfers between devices, on_device(): next_over = lax.ppermute(sent_even, 'section', across)  23.2 us
    ppermute x4, starting transfers between devices, swapped(): return lax.ppermute(value, ('section', 'dp'), dp_pairs(*ring, 0, 1))  18.4 us
    pallas_call x7, Pallas kernels, tick_layer(): pl.pallas_call(functools.partial(tick_kernel, tick), out_shape=[wide, nar...  16.6 us
    ppermute x32, waiting for transfers between devices, shifted(): return lax.ppermute(value, ('section', 'dp'), dp_pairs(*ring, step, 0))  15 us
    unnamed x70, local copies, waits for them, and re-layouts  13.1 us
    ppermute x1, starting transfers between devices, on_device(): core = lax.ppermute(sent, 'section', inside)  8.99 us
    ppermute x3, starting transfers between devices, on_device(): next_core = lax.ppermute(sent_odd, 'section', inside)  5.35 us
  transfers between devices with their start and end apart: 44, of which 9 were waited for; matrix products, arithmetic and copies ran while one was open for 8% of the time, Pallas kernels for 3%

profile of v5, /device:TPU:31, one launch (start us, length us, event | category | flops | bytes accessed | tf_op | source)
XLA Modules:
  0.0 254.6 jit_solution(13994505953301351666)
XLA Ops:
  2.3 4.8 %collective-permute-start.2 = (bf16[2,160,128]{2,1,0:T(8,128)(2,1)S(1)}, bf16[2,160,128]{2,1,0:T(8,128)(2,1)S(1)}, u32[]{:S(2)}, u32[]{:S(2)}) collective-permute-start(bf16[2,160,128]{2,1,0:T(8,128)(2,1)S(1)} %pad_maximum_fusion.10), channel_id=1, source_target_pairs={{464,465},{465,464},{466,467},{467,466},{468,469},{469,468},{470,4... | collective-permute-start | bytes 245768 | tf_op jit(solution)/shard_map/ppermute | solution.py:34
  7.0 4.4 %collective-permute-start = (bf16[2,160,128]{2,1,0:T(8,128)(2,1)S(1)}, bf16[2,160,128]{2,1,0:T(8,128)(2,1)S(1)}, u32[]{:S(2)}, u32[]{:S(2)}) collective-permute-start(bf16[2,160,128]{2,1,0:T(8,128)(2,1)S(1)} %pad_maximum_fusion.9), channel_id=1, source_target_pairs={{0,1},{1,0},{2,3},{3,2},{4,5},{5,4},{6,7},{7,6},{8,9},{9,8},{10,11... | collective-permute-start | bytes 245768 | tf_op jit(solution)/shard_map/ppermute | solution.py:34
  11.6 10.8 %collective-permute-start.5 = (bf16[2,2,160,128]{3,2,1,0:T(8,128)(2,1)S(1)}, bf16[2,2,160,128]{3,2,1,0:T(8,128)(2,1)S(1)}, u32[]{:S(2)}, u32[]{:S(2)}) collective-permute-start(bf16[2,2,160,128]{3,2,1,0:T(8,128)(2,1)S(1)} %pad_maximum_fusion.4.refs_12_), channel_id=1, source_target_pairs={{464,478},{465,479},{466,464},{467,465},{468,466},{469,467},{470,4... | collective-permute-start | bytes 491528 | tf_op jit(solution)/shard_map/ppermute | solution.py:30
  22.4 1.9 collective-permute-start.3
  24.4 4.6 %collective-permute-start.4 = (bf16[2,2,160,128]{3,2,1,0:T(8,128)(2,1)S(1)}, bf16[2,2,160,128]{3,2,1,0:T(8,128)(2,1)S(1)}, u32[]{:S(2)}, u32[]{:S(2)}) collective-permute-start(bf16[2,2,160,128]{3,2,1,0:T(8,128)(2,1)S(1)} %pad_maximum_fusion.3.refs_3_), channel_id=1, source_target_pairs={{0,14},{1,15},{2,0},{3,1},{4,2},{5,3},{6,4},{7,5},{8,6},{9,7},{10,... | collective-permute-start | bytes 491528 | tf_op jit(solution)/shard_map/ppermute | solution.py:30
  29.0 1.9 collective-permute-start.1
  31.2 5.0 %collective-permute-done.1.refs_4_ = bf16[2,2,160,128]{3,2,1,0:T(8,128)(2,1)S(1)} collective-permute-done((bf16[2,2,160,128]{3,2,1,0:T(8,128)(2,1)S(1)}, bf16[2,2,160,128]{3,2,1,0:T(8,128)(2,1)S(1)}, u32[]{:S(2)}, u32[]{:S(2)}) %collective-permute-start.1) | collective-permute-done | bytes 163872 | tf_op jit(solution)/shard_map/ppermute | solution.py:30
  36.2 1.9 collective-permute-start.7
  38.8 4.6 %collective-permute-start.9 = (bf16[2,2,160,128]{3,2,1,0:T(8,128)(2,1)S(1)}, bf16[2,2,160,128]{3,2,1,0:T(8,128)(2,1)}, u32[]{:S(2)}, u32[]{:S(2)}) collective-permute-start(bf16[2,2,160,128]{3,2,1,0:T(8,128)(2,1)S(1)} %collective-permute-done.5.refs_16_), channel_id=1, source_target_pairs={{464,478},{465,479},{466,464},{467,465},{468,466},{469,467},{470,4... | collective-permute-start | bytes 491528 | tf_op jit(solution)/shard_map/ppermute | solution.py:30
  44.0 1.9 collective-permute-start.6
  46.6 4.6 %collective-permute-start.8 = (bf16[2,2,160,128]{3,2,1,0:T(8,128)(2,1)S(1)}, bf16[2,2,160,128]{3,2,1,0:T(8,128)(2,1)}, u32[]{:S(2)}, u32[]{:S(2)}) collective-permute-start(bf16[2,2,160,128]{3,2,1,0:T(8,128)(2,1)S(1)} %collective-permute-done.4.refs_7_), channel_id=1, source_target_pairs={{0,14},{1,15},{2,0},{3,1},{4,2},{5,3},{6,4},{7,5},{8,6},{9,7},{10,... | collective-permute-start | bytes 491528 | tf_op jit(solution)/shard_map/ppermute | solution.py:30
  53.4 1.9 collective-permute-start.10
  55.4 5.1 %collective-permute-start.11 = (bf16[2,2,160,128]{3,2,1,0:T(8,128)(2,1)}, bf16[2,2,160,128]{3,2,1,0:T(8,128)(2,1)}, u32[]{:S(2)}, u32[]{:S(2)}) collective-permute-start(bf16[2,2,160,128]{3,2,1,0:T(8,128)(2,1)} %collective-permute-done.8.refs_8_), channel_id=1, source_target_pairs={{0,14},{1,15},{2,0},{3,1},{4,2},{5,3},{6,4},{7,5},{8,6},{9,7},{10,... | collective-permute-start | bytes 491528 | tf_op jit(solution)/shard_map/ppermute | solution.py:30
  64.3 1.9 collective-permute-start.12
  67.1 4.6 %collective-permute-start.13 = (bf16[1,2,160,128]{3,2,1,0:T(8,128)(2,1)S(1)}, bf16[1,2,160,128]{3,2,1,0:T(8,128)(2,1)S(1)}, u32[]{:S(2)}, u32[]{:S(2)}) collective-permute-start(bf16[1,2,160,128]{3,2,1,0:T(8,128)(2,1)S(1)} %slice.133), channel_id=1, source_target_pairs={{0,14},{1,15},{2,0},{3,1},{4,2},{5,3},{6,4},{7,5},{8,6},{9,7},{10,... | collective-permute-start | bytes 245768 | tf_op jit(solution)/shard_map/ppermute | solution.py:30
  71.8 1.9 collective-permute-start.15
  73.7 4.6 %collective-permute-start.16 = (bf16[2,2,160,128]{3,2,1,0:T(8,128)(2,1)}, bf16[2,2,160,128]{3,2,1,0:T(8,128)(2,1)}, u32[]{:S(2)}, u32[]{:S(2)}) collective-permute-start(bf16[2,2,160,128]{3,2,1,0:T(8,128)(2,1)} %collective-permute-done.9.refs_17_), channel_id=1, source_target_pairs={{464,478},{465,479},{466,464},{467,465},{468,466},{469,467},{470,4... | collective-permute-start | bytes 491528 | tf_op jit(solution)/shard_map/ppermute | solution.py:30
  78.4 3.8 %tick_layer.7 = (bf16[128,2560]{1,0:T(8,128)(2,1)}, bf16[128,128]{1,0:T(8,128)(2,1)S(1)}, bf16[128,128]{1,0:T(8,128)(2,1)S(1)}) custom-call(s32[3]{0:T(128)S(1)} %add_add_fusion.3.flags_ref, bf16[128,2560]{1,0:T(8,128)(2,1)S(1)} %bitcast.117, bf16[4,128,2560]{2,1,0:T(8,128)(2,1)S(1)} %get-tuple-element.50.refs_1_, ...), custom_call_target="tpu_custom_call" | custom-call | flops 1677721600 | bytes 13107200 | tf_op jit(solution)/shard_map/tick_layer/pallas_call | solution.py:216
  82.2 9.0 %collective-permute-start.19 = (bf16[128,2560]{1,0:T(8,128)(2,1)}, bf16[128,2560]{1,0:T(8,128)(2,1)S(1)}, u32[]{:S(2)}, u32[]{:S(2)}) collective-permute-start(bf16[128,2560]{1,0:T(8,128)(2,1)} %get-tuple-element.58), channel_id=1, source_target_pairs={{16,0},{48,32},{80,64},{112,96},{144,128},{176,160},{208,192},{240... | collective-permute-start | bytes 1966088 | tf_op jit(solution)/shard_map/ppermute | solution.py:311
  97.8 4.6 %collective-permute-start.18 = (bf16[1,2,160,128]{3,2,1,0:T(8,128)(2,1)S(1)}, bf16[1,2,160,128]{3,2,1,0:T(8,128)(2,1)S(1)}, u32[]{:S(2)}, u32[]{:S(2)}) collective-permute-start(bf16[1,2,160,128]{3,2,1,0:T(8,128)(2,1)S(1)} %slice.135), channel_id=1, source_target_pairs={{464,478},{465,479},{466,464},{467,465},{468,466},{469,467},{470,4... | collective-permute-start | bytes 245768 | tf_op jit(solution)/shard_map/ppermute | solution.py:30
  109.5 3.4 %tick_layer.9 = (bf16[128,2560]{1,0:T(8,128)(2,1)S(1)}, bf16[128,128]{1,0:T(8,128)(2,1)S(1)}, bf16[128,128]{1,0:T(8,128)(2,1)S(1)}) custom-call(s32[3]{0:T(128)S(1)} %add_add_fusion.2.flags_ref, bf16[128,2560]{1,0:T(8,128)(2,1)} %collective-permute-done.14.refs_0_, bf16[4,128,2560]{2,1,0:T(8,128)(2,1)S(1)} %get-tuple-element.50.refs_1_, ...), custom_call_target="tpu_custom_call" | custom-call | flops 1677721600 | bytes 13107200 | tf_op jit(solution)/shard_map/tick_layer/pallas_call | solution.py:216
  112.9 2.6 %collective-permute-start.20 = (bf16[128,2560]{1,0:T(8,128)(2,1)S(1)}, bf16[128,2560]{1,0:T(8,128)(2,1)S(1)}, u32[]{:S(2)}, u32[]{:S(2)}) collective-permute-start(bf16[128,2560]{1,0:T(8,128)(2,1)S(1)} %get-tuple-element.63), channel_id=1, source_target_pairs={{16,0},{48,32},{80,64},{112,96},{144,128},{176,160},{208,192},{240... | collective-permute-start | bytes 1966088 | tf_op jit(solution)/shard_map/ppermute | solution.py:316
  119.8 11.5 %collective-permute-done.22.refs_0_ = bf16[128,2560]{1,0:T(8,128)(2,1)S(1)} collective-permute-done((bf16[128,2560]{1,0:T(8,128)(2,1)S(1)}, bf16[128,2560]{1,0:T(8,128)(2,1)S(1)}, u32[]{:S(2)}, u32[]{:S(2)}) %collective-permute-start.22) | collective-permute-done | bytes 655392 | tf_op jit(solution)/shard_map/ppermute | solution.py:314
  131.3 3.7 %tick_layer.11 = (bf16[128,2560]{1,0:T(8,128)(2,1)S(1)}, bf16[128,128]{1,0:T(8,128)(2,1)S(1)}, bf16[128,128]{1,0:T(8,128)(2,1)S(1)}) custom-call(s32[3]{0:T(128)S(1)} %add_add_fusion.6.flags_ref, bf16[128,2560]{1,0:T(8,128)(2,1)S(1)} %collective-permute-done.22.refs_0_, bf16[4,128,2560]{2,1,0:T(8,128)(2,1)S(1)} %get-tuple-element.50.refs_1_, ...), custom_call_target="tpu_custom_call" | custom-call | flops 1677721600 | bytes 13107200 | tf_op jit(solution)/shard_map/tick_layer/pallas_call | solution.py:216
  140.5 11.7 %collective-permute-done.21.refs_0_ = bf16[128,2560]{1,0:T(8,128)(2,1)S(1)} collective-permute-done((bf16[128,2560]{1,0:T(8,128)(2,1)S(1)}, bf16[128,2560]{1,0:T(8,128)(2,1)S(1)}, u32[]{:S(2)}, u32[]{:S(2)}) %collective-permute-start.21) | collective-permute-done | bytes 655392 | tf_op jit(solution)/shard_map/ppermute | solution.py:314
  152.2 3.7 %tick_layer.13 = (bf16[128,2560]{1,0:T(8,128)(2,1)S(1)}, bf16[128,128]{1,0:T(8,128)(2,1)S(1)}, bf16[128,128]{1,0:T(8,128)(2,1)S(1)}) custom-call(s32[3]{0:T(128)S(1)} %add_add_fusion.flags_ref, bf16[128,2560]{1,0:T(8,128)(2,1)S(1)} %collective-permute-done.21.refs_0_, bf16[4,128,2560]{2,1,0:T(8,128)(2,1)S(1)} %get-tuple-element.50.refs_1_, ...), custom_call_target="tpu_custom_call" | custom-call | flops 1677721600 | bytes 13107200 | tf_op jit(solution)/shard_map/tick_layer/pallas_call | solution.py:216
  158.8 2.6 %copy.7 = bf16[2560,256]{1,0:T(8,128)(2,1)} copy(bf16[2560,256]{0,1:T(8,128)(2,1)} %pad_maximum_fusion.1) | data formatting | bytes 2621440 | tf_op jit(solution)/shard_map/concatenate | solution.py:348
  163.2 1.9 collective-permute-start.26
  165.2 4.6 %collective-permute-start.28 = (bf16[1,160,256]{2,1,0:T(8,128)(2,1)}, bf16[1,160,256]{2,1,0:T(8,128)(2,1)}, u32[]{:S(2)}, u32[]{:S(2)}) collective-permute-start(bf16[1,160,256]{2,1,0:T(8,128)(2,1)} %get-tuple-element.116), channel_id=1, source_target_pairs={{0,14},{1,15},{2,0},{3,1},{4,2},{5,3},{6,4},{7,5},{8,6},{9,7},{10,... | collective-permute-start | bytes 245768 | tf_op jit(solution)/shard_map/ppermute | solution.py:30
  174.5 1.9 collective-permute-start.27
  176.4 4.6 %collective-permute-start.29 = (bf16[1,160,256]{2,1,0:T(8,128)(2,1)S(1)}, bf16[1,160,256]{2,1,0:T(8,128)(2,1)S(1)}, u32[]{:S(2)}, u32[]{:S(2)}) collective-permute-start(bf16[1,160,256]{2,1,0:T(8,128)(2,1)S(1)} %get-tuple-element.111), channel_id=1, source_target_pairs={{464,478},{465,479},{466,464},{467,465},{468,466},{469,467},{470,4... | collective-permute-start | bytes 245768 | tf_op jit(solution)/shard_map/ppermute | solution.py:30
  182.5 2.1 collective-permute-start.31
  185.6 1.9 collective-permute-start.30
  187.6 4.9 %collective-permute-start.32 = (bf16[2,160,256]{2,1,0:T(8,128)(2,1)S(1)}, bf16[2,160,256]{2,1,0:T(8,128)(2,1)}, u32[]{:S(2)}, u32[]{:S(2)}) collective-permute-start(bf16[2,160,256]{2,1,0:T(8,128)(2,1)S(1)} %pad_maximum_fusion.7), channel_id=1, source_target_pairs={{0,14},{1,15},{2,0},{3,1},{4,2},{5,3},{6,4},{7,5},{8,6},{9,7},{10,... | collective-permute-start | bytes 491528 | tf_op jit(solution)/shard_map/ppermute | solution.py:30
  193.2 3.3 %collective-permute-start.33 = (bf16[2,160,256]{2,1,0:T(8,128)(2,1)}, bf16[2,160,256]{2,1,0:T(8,128)(2,1)S(1)}, u32[]{:S(2)}, u32[]{:S(2)}) collective-permute-start(bf16[2,160,256]{2,1,0:T(8,128)(2,1)} %pad_maximum_fusion.8), channel_id=1, source_target_pairs={{464,478},{465,479},{466,464},{467,465},{468,466},{469,467},{470,4... | collective-permute-start | bytes 491528 | tf_op jit(solution)/shard_map/ppermute | solution.py:30
  196.6 4.0 %collective-permute-done.33 = bf16[2,160,256]{2,1,0:T(8,128)(2,1)S(1)} collective-permute-done((bf16[2,160,256]{2,1,0:T(8,128)(2,1)}, bf16[2,160,256]{2,1,0:T(8,128)(2,1)S(1)}, u32[]{:S(2)}, u32[]{:S(2)}) %collective-permute-start.33) | collective-permute-done | bytes 163872 | tf_op jit(solution)/shard_map/ppermute | solution.py:30
  202.5 4.5 %collective-permute-start.36 = (bf16[2,160,256]{2,1,0:T(8,128)(2,1)}, bf16[2,160,256]{2,1,0:T(8,128)(2,1)S(1)}, u32[]{:S(2)}, u32[]{:S(2)}) collective-permute-start(bf16[2,160,256]{2,1,0:T(8,128)(2,1)} %get-tuple-element.106), channel_id=1, source_target_pairs={{0,14},{1,15},{2,0},{3,1},{4,2},{5,3},{6,4},{7,5},{8,6},{9,7},{10,... | collective-permute-start | bytes 491528 | tf_op jit(solution)/shard_map/ppermute | solution.py:30
  207.0 1.9 collective-permute-start.34
  210.6 4.6 %collective-permute-start.37 = (bf16[2,160,256]{2,1,0:T(8,128)(2,1)}, bf16[2,160,256]{2,1,0:T(8,128)(2,1)S(1)}, u32[]{:S(2)}, u32[]{:S(2)}) collective-permute-start(bf16[2,160,256]{2,1,0:T(8,128)(2,1)} %get-tuple-element.104), channel_id=1, source_target_pairs={{464,478},{465,479},{466,464},{467,465},{468,466},{469,467},{470,4... | collective-permute-start | bytes 491528 | tf_op jit(solution)/shard_map/ppermute | solution.py:30
  215.2 1.9 collective-permute-start.35
  219.9 2.8 %collective-permute-done.35 = bf16[2,160,256]{2,1,0:T(8,128)(2,1)S(1)} collective-permute-done((bf16[2,160,256]{2,1,0:T(8,128)(2,1)}, bf16[2,160,256]{2,1,0:T(8,128)(2,1)S(1)}, u32[]{:S(2)}, u32[]{:S(2)}) %collective-permute-start.35) | collective-permute-done | bytes 163872 | tf_op jit(solution)/shard_map/ppermute | solution.py:30
  223.7 1.9 collective-permute-start.38
  225.6 4.6 %collective-permute-start.39 = (bf16[2,160,256]{2,1,0:T(8,128)(2,1)S(1)}, bf16[2,160,256]{2,1,0:T(8,128)(2,1)S(1)}, u32[]{:S(2)}, u32[]{:S(2)}) collective-permute-start(bf16[2,160,256]{2,1,0:T(8,128)(2,1)S(1)} %get-tuple-element.103), channel_id=1, source_target_pairs={{0,14},{1,15},{2,0},{3,1},{4,2},{5,3},{6,4},{7,5},{8,6},{9,7},{10,... | collective-permute-start | bytes 491528 | tf_op jit(solution)/shard_map/ppermute | solution.py:30
  230.3 1.9 collective-permute-start.41
  232.2 4.6 %collective-permute-start.42 = (bf16[2,160,256]{2,1,0:T(8,128)(2,1)S(1)}, bf16[2,160,256]{2,1,0:T(8,128)(2,1)S(1)}, u32[]{:S(2)}, u32[]{:S(2)}) collective-permute-start(bf16[2,160,256]{2,1,0:T(8,128)(2,1)S(1)} %get-tuple-element.101), channel_id=1, source_target_pairs={{464,478},{465,479},{466,464},{467,465},{468,466},{469,467},{470,4... | collective-permute-start | bytes 491528 | tf_op jit(solution)/shard_map/ppermute | solution.py:30
  237.8 5.7 %collective-permute-start.40 = (bf16[160,256]{1,0:T(8,128)(2,1)S(1)}, bf16[160,256]{1,0:T(8,128)(2,1)S(1)}, u32[]{:S(2)}, u32[]{:S(2)}) collective-permute-start(bf16[160,256]{1,0:T(8,128)(2,1)S(1)} %fusion.29), channel_id=1, source_target_pairs={{0,1},{1,0},{2,3},{3,2},{4,5},{5,4},{6,7},{7,6},{8,9},{9,8},{10,11... | collective-permute-start | bytes 245768 | tf_op jit(solution)/shard_map/ppermute | solution.py:34
  243.6 3.5 %collective-permute-start.43 = (bf16[160,256]{1,0:T(8,128)(2,1)S(1)}, bf16[160,256]{1,0:T(8,128)(2,1)S(1)}, u32[]{:S(2)}, u32[]{:S(2)}) collective-permute-start(bf16[160,256]{1,0:T(8,128)(2,1)S(1)} %fusion.30), channel_id=1, source_target_pairs={{464,465},{465,464},{466,467},{467,466},{468,469},{469,468},{470,4... | collective-permute-start | bytes 245768 | tf_op jit(solution)/shard_map/ppermute | solution.py:34
  248.1 4.6 %collective-permute-done.43.rest_other_ref = bf16[160,256]{1,0:T(8,128)(2,1)S(1)} collective-permute-done((bf16[160,256]{1,0:T(8,128)(2,1)S(1)}, bf16[160,256]{1,0:T(8,128)(2,1)S(1)}, u32[]{:S(2)}, u32[]{:S(2)}) %collective-permute-start.43) | collective-permute-done | bytes 81952 | tf_op jit(solution)/shard_map/ppermute | solution.py:34
  (176 shorter events, 58.2 us)
Async XLA Ops:
  2.3 9.2 %collective-permute-start.2 = (bf16[2,160,128]{2,1,0:T(8,128)(2,1)S(1)}, bf16[2,160,128]{2,1,0:T(8,128)(2,1)S(1)}, u32[]{:S(2)}, u32[]{:S(2)}) collective-permute-start(bf16[2,160,128]{2,1,0:T(8,128)(2,1)S(1)} %pad_maximum_fusion.10), channel_id=1, source_target_pairs={{464,465},{465,464},{466,467},{467,466},{468,469},{469,468},{470,4... | collective-permute-start | bytes 245768 | tf_op jit(solution)/shard_map/ppermute | solution.py:34
  7.0 17.3 %collective-permute-start = (bf16[2,160,128]{2,1,0:T(8,128)(2,1)S(1)}, bf16[2,160,128]{2,1,0:T(8,128)(2,1)S(1)}, u32[]{:S(2)}, u32[]{:S(2)}) collective-permute-start(bf16[2,160,128]{2,1,0:T(8,128)(2,1)S(1)} %pad_maximum_fusion.9), channel_id=1, source_target_pairs={{0,1},{1,0},{2,3},{3,2},{4,5},{5,4},{6,7},{7,6},{8,9},{9,8},{10,11... | collective-permute-start | bytes 245768 | tf_op jit(solution)/shard_map/ppermute | solution.py:34
  11.6 66.8 %copy-start.1 = (bf16[1,128,2560]{2,1,0:T(8,128)(2,1)S(1)}, bf16[1,128,2560]{2,1,0:T(8,128)(2,1)}, u32[]{:S(2)}) copy-start(bf16[1,128,2560]{2,1,0:T(8,128)(2,1)} %param.5) | copy-start | bytes 1966084
  11.6 19.4 %collective-permute-start.5 = (bf16[2,2,160,128]{3,2,1,0:T(8,128)(2,1)S(1)}, bf16[2,2,160,128]{3,2,1,0:T(8,128)(2,1)S(1)}, u32[]{:S(2)}, u32[]{:S(2)}) collective-permute-start(bf16[2,2,160,128]{3,2,1,0:T(8,128)(2,1)S(1)} %pad_maximum_fusion.4.refs_12_), channel_id=1, source_target_pairs={{464,478},{465,479},{466,464},{467,465},{468,466},{469,467},{470,4... | collective-permute-start | bytes 491528 | tf_op jit(solution)/shard_map/ppermute | solution.py:30
  22.4 8.6 %collective-permute-start.3 = (bf16[2,2,160,128]{3,2,1,0:T(8,128)(2,1)S(1)}, bf16[2,2,160,128]{3,2,1,0:T(8,128)(2,1)S(1)}, u32[]{:S(2)}, u32[]{:S(2)}) collective-permute-start(bf16[2,2,160,128]{3,2,1,0:T(8,128)(2,1)S(1)} %pad_maximum_fusion.4.refs_12_), channel_id=1, source_target_pairs={{464,466},{465,467},{466,468},{467,469},{468,470},{469,471},{470,4... | collective-permute-start | bytes 491528 | tf_op jit(solution)/shard_map/ppermute | solution.py:30
  24.4 36.2 %copy-start.3 = (bf16[2,2,160,128]{3,2,1,0:T(8,128)(2,1)}, bf16[2,2,160,128]{3,2,1,0:T(8,128)(2,1)S(1)}, u32[]{:S(2)}) copy-start(bf16[2,2,160,128]{3,2,1,0:T(8,128)(2,1)S(1)} %pad_maximum_fusion.3.refs_3_) | copy-start | bytes 491524
  24.4 6.8 %collective-permute-start.4 = (bf16[2,2,160,128]{3,2,1,0:T(8,128)(2,1)S(1)}, bf16[2,2,160,128]{3,2,1,0:T(8,128)(2,1)S(1)}, u32[]{:S(2)}, u32[]{:S(2)}) collective-permute-start(bf16[2,2,160,128]{3,2,1,0:T(8,128)(2,1)S(1)} %pad_maximum_fusion.3.refs_3_), channel_id=1, source_target_pairs={{0,14},{1,15},{2,0},{3,1},{4,2},{5,3},{6,4},{7,5},{8,6},{9,7},{10,... | collective-permute-start | bytes 491528 | tf_op jit(solution)/shard_map/ppermute | solution.py:30
  29.0 7.3 %collective-permute-start.1 = (bf16[2,2,160,128]{3,2,1,0:T(8,128)(2,1)S(1)}, bf16[2,2,160,128]{3,2,1,0:T(8,128)(2,1)S(1)}, u32[]{:S(2)}, u32[]{:S(2)}) collective-permute-start(bf16[2,2,160,128]{3,2,1,0:T(8,128)(2,1)S(1)} %pad_maximum_fusion.3.refs_3_), channel_id=1, source_target_pairs={{0,2},{1,3},{2,4},{3,5},{4,6},{5,7},{6,8},{7,9},{8,10},{9,11},{10,... | collective-permute-start | bytes 491528 | tf_op jit(solution)/shard_map/ppermute | solution.py:30
  36.2 15.8 %collective-permute-start.7 = (bf16[2,2,160,128]{3,2,1,0:T(8,128)(2,1)S(1)}, bf16[2,2,160,128]{3,2,1,0:T(8,128)(2,1)}, u32[]{:S(2)}, u32[]{:S(2)}) collective-permute-start(bf16[2,2,160,128]{3,2,1,0:T(8,128)(2,1)S(1)} %collective-permute-done.3.refs_13_), channel_id=1, source_target_pairs={{464,466},{465,467},{466,468},{467,469},{468,470},{469,471},{470,4... | collective-permute-start | bytes 491528 | tf_op jit(solution)/shard_map/ppermute | solution.py:30
  38.8 13.2 %collective-permute-start.9 = (bf16[2,2,160,128]{3,2,1,0:T(8,128)(2,1)S(1)}, bf16[2,2,160,128]{3,2,1,0:T(8,128)(2,1)}, u32[]{:S(2)}, u32[]{:S(2)}) collective-permute-start(bf16[2,2,160,128]{3,2,1,0:T(8,128)(2,1)S(1)} %collective-permute-done.5.refs_16_), channel_id=1, source_target_pairs={{464,478},{465,479},{466,464},{467,465},{468,466},{469,467},{470,4... | collective-permute-start | bytes 491528 | tf_op jit(solution)/shard_map/ppermute | solution.py:30
  44.0 8.0 %collective-permute-start.6 = (bf16[2,2,160,128]{3,2,1,0:T(8,128)(2,1)S(1)}, bf16[2,2,160,128]{3,2,1,0:T(8,128)(2,1)}, u32[]{:S(2)}, u32[]{:S(2)}) collective-permute-start(bf16[2,2,160,128]{3,2,1,0:T(8,128)(2,1)S(1)} %collective-permute-done.1.refs_4_), channel_id=1, source_target_pairs={{0,2},{1,3},{2,4},{3,5},{4,6},{5,7},{6,8},{7,9},{8,10},{9,11},{10,... | collective-permute-start | bytes 491528 | tf_op jit(solution)/shard_map/ppermute | solution.py:30
  46.6 6.8 %collective-permute-start.8 = (bf16[2,2,160,128]{3,2,1,0:T(8,128)(2,1)S(1)}, bf16[2,2,160,128]{3,2,1,0:T(8,128)(2,1)}, u32[]{:S(2)}, u32[]{:S(2)}) collective-permute-start(bf16[2,2,160,128]{3,2,1,0:T(8,128)(2,1)S(1)} %collective-permute-done.4.refs_7_), channel_id=1, source_target_pairs={{0,14},{1,15},{2,0},{3,1},{4,2},{5,3},{6,4},{7,5},{8,6},{9,7},{10,... | collective-permute-start | bytes 491528 | tf_op jit(solution)/shard_map/ppermute | solution.py:30
  53.4 10.0 %collective-permute-start.10 = (bf16[2,2,160,128]{3,2,1,0:T(8,128)(2,1)}, bf16[2,2,160,128]{3,2,1,0:T(8,128)(2,1)}, u32[]{:S(2)}, u32[]{:S(2)}) collective-permute-start(bf16[2,2,160,128]{3,2,1,0:T(8,128)(2,1)} %collective-permute-done.6.refs_5_), channel_id=1, source_target_pairs={{0,2},{1,3},{2,4},{3,5},{4,6},{5,7},{6,8},{7,9},{8,10},{9,11},{10,... | collective-permute-start | bytes 491528 | tf_op jit(solution)/shard_map/ppermute | solution.py:30
  55.4 10.9 %collective-permute-start.11 = (bf16[2,2,160,128]{3,2,1,0:T(8,128)(2,1)}, bf16[2,2,160,128]{3,2,1,0:T(8,128)(2,1)}, u32[]{:S(2)}, u32[]{:S(2)}) collective-permute-start(bf16[2,2,160,128]{3,2,1,0:T(8,128)(2,1)} %collective-permute-done.8.refs_8_), channel_id=1, source_target_pairs={{0,14},{1,15},{2,0},{3,1},{4,2},{5,3},{6,4},{7,5},{8,6},{9,7},{10,... | collective-permute-start | bytes 491528 | tf_op jit(solution)/shard_map/ppermute | solution.py:30
  63.3 18.8 %copy-start.9 = (f32[4,128,128]{2,1,0:T(8,128)}, f32[4,128,128]{2,1,0:T(8,128)S(1)}, u32[]{:S(2)}) copy-start(f32[4,128,128]{2,1,0:T(8,128)S(1)} %get-tuple-element.51.refs_2_.refs_12_) | copy-start | bytes 786436
  64.3 14.0 %collective-permute-start.12 = (bf16[1,2,160,128]{3,2,1,0:T(8,128)(2,1)S(1)}, bf16[1,2,160,128]{3,2,1,0:T(8,128)(2,1)S(1)}, u32[]{:S(2)}, u32[]{:S(2)}) collective-permute-start(bf16[1,2,160,128]{3,2,1,0:T(8,128)(2,1)S(1)} %slice.132), channel_id=1, source_target_pairs={{0,2},{1,3},{2,4},{3,5},{4,6},{5,7},{6,8},{7,9},{8,10},{9,11},{10,... | collective-permute-start | bytes 245768 | tf_op jit(solution)/shard_map/ppermute | solution.py:30
  67.1 11.2 %collective-permute-start.13 = (bf16[1,2,160,128]{3,2,1,0:T(8,128)(2,1)S(1)}, bf16[1,2,160,128]{3,2,1,0:T(8,128)(2,1)S(1)}, u32[]{:S(2)}, u32[]{:S(2)}) collective-permute-start(bf16[1,2,160,128]{3,2,1,0:T(8,128)(2,1)S(1)} %slice.133), channel_id=1, source_target_pairs={{0,14},{1,15},{2,0},{3,1},{4,2},{5,3},{6,4},{7,5},{8,6},{9,7},{10,... | collective-permute-start | bytes 245768 | tf_op jit(solution)/shard_map/ppermute | solution.py:30
  71.8 22.3 %collective-permute-start.15 = (bf16[2,2,160,128]{3,2,1,0:T(8,128)(2,1)}, bf16[2,2,160,128]{3,2,1,0:T(8,128)(2,1)}, u32[]{:S(2)}, u32[]{:S(2)}) collective-permute-start(bf16[2,2,160,128]{3,2,1,0:T(8,128)(2,1)} %collective-permute-done.7.refs_14_), channel_id=1, source_target_pairs={{464,466},{465,467},{466,468},{467,469},{468,470},{469,471},{470,4... | collective-permute-start | bytes 491528 | tf_op jit(solution)/shard_map/ppermute | solution.py:30
  73.7 23.2 %collective-permute-start.16 = (bf16[2,2,160,128]{3,2,1,0:T(8,128)(2,1)}, bf16[2,2,160,128]{3,2,1,0:T(8,128)(2,1)}, u32[]{:S(2)}, u32[]{:S(2)}) collective-permute-start(bf16[2,2,160,128]{3,2,1,0:T(8,128)(2,1)} %collective-permute-done.9.refs_17_), channel_id=1, source_target_pairs={{464,478},{465,479},{466,464},{467,465},{468,466},{469,467},{470,4... | collective-permute-start | bytes 491528 | tf_op jit(solution)/shard_map/ppermute | solution.py:30
  82.2 20.8 %collective-permute-start.19 = (bf16[128,2560]{1,0:T(8,128)(2,1)}, bf16[128,2560]{1,0:T(8,128)(2,1)S(1)}, u32[]{:S(2)}, u32[]{:S(2)}) collective-permute-start(bf16[128,2560]{1,0:T(8,128)(2,1)} %get-tuple-element.58), channel_id=1, source_target_pairs={{16,0},{48,32},{80,64},{112,96},{144,128},{176,160},{208,192},{240... | collective-permute-start | bytes 1966088 | tf_op jit(solution)/shard_map/ppermute | solution.py:311
  91.3 17.9 %collective-permute-start.14 = (bf16[128,2560]{1,0:T(8,128)(2,1)}, bf16[128,2560]{1,0:T(8,128)(2,1)}, u32[]{:S(2)}, u32[]{:S(2)}) collective-permute-start(bf16[128,2560]{1,0:T(8,128)(2,1)} %get-tuple-element.58), channel_id=1, source_target_pairs={{0,496},{32,16},{64,48},{96,80},{128,112},{160,144},{192,176},{224... | collective-permute-start | bytes 1966088 | tf_op jit(solution)/shard_map/ppermute | solution.py:310
  95.0 14.1 %collective-permute-start.17 = (bf16[1,2,160,128]{3,2,1,0:T(8,128)(2,1)S(1)}, bf16[1,2,160,128]{3,2,1,0:T(8,128)(2,1)S(1)}, u32[]{:S(2)}, u32[]{:S(2)}) collective-permute-start(bf16[1,2,160,128]{3,2,1,0:T(8,128)(2,1)S(1)} %slice.134), channel_id=1, source_target_pairs={{464,466},{465,467},{466,468},{467,469},{468,470},{469,471},{470,4... | collective-permute-start | bytes 245768 | tf_op jit(solution)/shard_map/ppermute | solution.py:30
  97.8 11.3 %collective-permute-start.18 = (bf16[1,2,160,128]{3,2,1,0:T(8,128)(2,1)S(1)}, bf16[1,2,160,128]{3,2,1,0:T(8,128)(2,1)S(1)}, u32[]{:S(2)}, u32[]{:S(2)}) collective-permute-start(bf16[1,2,160,128]{3,2,1,0:T(8,128)(2,1)S(1)} %slice.135), channel_id=1, source_target_pairs={{464,478},{465,479},{466,464},{467,465},{468,466},{469,467},{470,4... | collective-permute-start | bytes 245768 | tf_op jit(solution)/shard_map/ppermute | solution.py:30
  112.9 6.3 %collective-permute-start.20 = (bf16[128,2560]{1,0:T(8,128)(2,1)S(1)}, bf16[128,2560]{1,0:T(8,128)(2,1)S(1)}, u32[]{:S(2)}, u32[]{:S(2)}) collective-permute-start(bf16[128,2560]{1,0:T(8,128)(2,1)S(1)} %get-tuple-element.63), channel_id=1, source_target_pairs={{16,0},{48,32},{80,64},{112,96},{144,128},{176,160},{208,192},{240... | collective-permute-start | bytes 1966088 | tf_op jit(solution)/shard_map/ppermute | solution.py:316
  115.5 15.8 %collective-permute-start.22 = (bf16[128,2560]{1,0:T(8,128)(2,1)S(1)}, bf16[128,2560]{1,0:T(8,128)(2,1)S(1)}, u32[]{:S(2)}, u32[]{:S(2)}) collective-permute-start(bf16[128,2560]{1,0:T(8,128)(2,1)S(1)} %get-tuple-element.66), channel_id=1, source_target_pairs={{0,496},{32,16},{64,48},{96,80},{128,112},{160,144},{192,176},{224... | collective-permute-start | bytes 1966088 | tf_op jit(solution)/shard_map/ppermute | solution.py:314
  135.0 3.7 %collective-permute-start.23 = (bf16[128,2560]{1,0:T(8,128)(2,1)S(1)}, bf16[128,2560]{1,0:T(8,128)(2,1)S(1)}, u32[]{:S(2)}, u32[]{:S(2)}) collective-permute-start(bf16[128,2560]{1,0:T(8,128)(2,1)S(1)} %get-tuple-element.68), channel_id=1, source_target_pairs={{16,0},{48,32},{80,64},{112,96},{144,128},{176,160},{208,192},{240... | collective-permute-start | bytes 1966088 | tf_op jit(solution)/shard_map/ppermute | solution.py:316
  136.4 15.8 %collective-permute-start.21 = (bf16[128,2560]{1,0:T(8,128)(2,1)S(1)}, bf16[128,2560]{1,0:T(8,128)(2,1)S(1)}, u32[]{:S(2)}, u32[]{:S(2)}) collective-permute-start(bf16[128,2560]{1,0:T(8,128)(2,1)S(1)} %get-tuple-element.65), channel_id=1, source_target_pairs={{0,496},{32,16},{64,48},{96,80},{128,112},{160,144},{192,176},{224... | collective-permute-start | bytes 1966088 | tf_op jit(solution)/shard_map/ppermute | solution.py:314
  163.2 17.7 %collective-permute-start.26 = (bf16[1,160,256]{2,1,0:T(8,128)(2,1)}, bf16[1,160,256]{2,1,0:T(8,128)(2,1)}, u32[]{:S(2)}, u32[]{:S(2)}) collective-permute-start(bf16[1,160,256]{2,1,0:T(8,128)(2,1)} %get-tuple-element.115), channel_id=1, source_target_pairs={{0,2},{1,3},{2,4},{3,5},{4,6},{5,7},{6,8},{7,9},{8,10},{9,11},{10,... | collective-permute-start | bytes 245768 | tf_op jit(solution)/shard_map/ppermute | solution.py:30
  165.2 15.8 %collective-permute-start.28 = (bf16[1,160,256]{2,1,0:T(8,128)(2,1)}, bf16[1,160,256]{2,1,0:T(8,128)(2,1)}, u32[]{:S(2)}, u32[]{:S(2)}) collective-permute-start(bf16[1,160,256]{2,1,0:T(8,128)(2,1)} %get-tuple-element.116), channel_id=1, source_target_pairs={{0,14},{1,15},{2,0},{3,1},{4,2},{5,3},{6,4},{7,5},{8,6},{9,7},{10,... | collective-permute-start | bytes 245768 | tf_op jit(solution)/shard_map/ppermute | solution.py:30
  174.5 6.5 %collective-permute-start.27 = (bf16[1,160,256]{2,1,0:T(8,128)(2,1)S(1)}, bf16[1,160,256]{2,1,0:T(8,128)(2,1)S(1)}, u32[]{:S(2)}, u32[]{:S(2)}) collective-permute-start(bf16[1,160,256]{2,1,0:T(8,128)(2,1)S(1)} %get-tuple-element.109), channel_id=1, source_target_pairs={{464,466},{465,467},{466,468},{467,469},{468,470},{469,471},{470,4... | collective-permute-start | bytes 245768 | tf_op jit(solution)/shard_map/ppermute | solution.py:30
  176.4 6.0 %collective-permute-start.29 = (bf16[1,160,256]{2,1,0:T(8,128)(2,1)S(1)}, bf16[1,160,256]{2,1,0:T(8,128)(2,1)S(1)}, u32[]{:S(2)}, u32[]{:S(2)}) collective-permute-start(bf16[1,160,256]{2,1,0:T(8,128)(2,1)S(1)} %get-tuple-element.111), channel_id=1, source_target_pairs={{464,478},{465,479},{466,464},{467,465},{468,466},{469,467},{470,4... | collective-permute-start | bytes 245768 | tf_op jit(solution)/shard_map/ppermute | solution.py:30
  182.5 36.1 %copy-start.8 = (bf16[128,2560]{1,0:T(8,128)(2,1)S(1)}, bf16[128,2560]{1,0:T(8,128)(2,1)}, u32[]{:S(2)}) copy-start(bf16[128,2560]{1,0:T(8,128)(2,1)} %copy-done.7) | copy-start | bytes 1966084
  182.5 14.1 %collective-permute-start.31 = (bf16[2,160,256]{2,1,0:T(8,128)(2,1)S(1)}, bf16[2,160,256]{2,1,0:T(8,128)(2,1)}, u32[]{:S(2)}, u32[]{:S(2)}) collective-permute-start(bf16[2,160,256]{2,1,0:T(8,128)(2,1)S(1)} %pad_maximum_fusion.6), channel_id=1, source_target_pairs={{464,466},{465,467},{466,468},{467,469},{468,470},{469,471},{470,4... | collective-permute-start | bytes 491528 | tf_op jit(solution)/shard_map/ppermute | solution.py:30
  185.6 11.0 %collective-permute-start.30 = (bf16[2,160,256]{2,1,0:T(8,128)(2,1)S(1)}, bf16[2,160,256]{2,1,0:T(8,128)(2,1)}, u32[]{:S(2)}, u32[]{:S(2)}) collective-permute-start(bf16[2,160,256]{2,1,0:T(8,128)(2,1)S(1)} %pad_maximum_fusion.5), channel_id=1, source_target_pairs={{0,2},{1,3},{2,4},{3,5},{4,6},{5,7},{6,8},{7,9},{8,10},{9,11},{10,... | collective-permute-start | bytes 491528 | tf_op jit(solution)/shard_map/ppermute | solution.py:30
  187.6 9.0 %collective-permute-start.32 = (bf16[2,160,256]{2,1,0:T(8,128)(2,1)S(1)}, bf16[2,160,256]{2,1,0:T(8,128)(2,1)}, u32[]{:S(2)}, u32[]{:S(2)}) collective-permute-start(bf16[2,160,256]{2,1,0:T(8,128)(2,1)S(1)} %pad_maximum_fusion.7), channel_id=1, source_target_pairs={{0,14},{1,15},{2,0},{3,1},{4,2},{5,3},{6,4},{7,5},{8,6},{9,7},{10,... | collective-permute-start | bytes 491528 | tf_op jit(solution)/shard_map/ppermute | solution.py:30
  193.2 7.4 %collective-permute-start.33 = (bf16[2,160,256]{2,1,0:T(8,128)(2,1)}, bf16[2,160,256]{2,1,0:T(8,128)(2,1)S(1)}, u32[]{:S(2)}, u32[]{:S(2)}) collective-permute-start(bf16[2,160,256]{2,1,0:T(8,128)(2,1)} %pad_maximum_fusion.8), channel_id=1, source_target_pairs={{464,478},{465,479},{466,464},{467,465},{468,466},{469,467},{470,4... | collective-permute-start | bytes 491528 | tf_op jit(solution)/shard_map/ppermute | solution.py:30
  202.5 16.0 %collective-permute-start.36 = (bf16[2,160,256]{2,1,0:T(8,128)(2,1)}, bf16[2,160,256]{2,1,0:T(8,128)(2,1)S(1)}, u32[]{:S(2)}, u32[]{:S(2)}) collective-permute-start(bf16[2,160,256]{2,1,0:T(8,128)(2,1)} %get-tuple-element.106), channel_id=1, source_target_pairs={{0,14},{1,15},{2,0},{3,1},{4,2},{5,3},{6,4},{7,5},{8,6},{9,7},{10,... | collective-permute-start | bytes 491528 | tf_op jit(solution)/shard_map/ppermute | solution.py:30
  207.0 12.8 %collective-permute-start.34 = (bf16[2,160,256]{2,1,0:T(8,128)(2,1)S(1)}, bf16[2,160,256]{2,1,0:T(8,128)(2,1)S(1)}, u32[]{:S(2)}, u32[]{:S(2)}) collective-permute-start(bf16[2,160,256]{2,1,0:T(8,128)(2,1)S(1)} %get-tuple-element.107), channel_id=1, source_target_pairs={{0,2},{1,3},{2,4},{3,5},{4,6},{5,7},{6,8},{7,9},{8,10},{9,11},{10,... | collective-permute-start | bytes 491528 | tf_op jit(solution)/shard_map/ppermute | solution.py:30
  210.6 9.2 %collective-permute-start.37 = (bf16[2,160,256]{2,1,0:T(8,128)(2,1)}, bf16[2,160,256]{2,1,0:T(8,128)(2,1)S(1)}, u32[]{:S(2)}, u32[]{:S(2)}) collective-permute-start(bf16[2,160,256]{2,1,0:T(8,128)(2,1)} %get-tuple-element.104), channel_id=1, source_target_pairs={{464,478},{465,479},{466,464},{467,465},{468,466},{469,467},{470,4... | collective-permute-start | bytes 491528 | tf_op jit(solution)/shard_map/ppermute | solution.py:30
  215.2 7.5 %collective-permute-start.35 = (bf16[2,160,256]{2,1,0:T(8,128)(2,1)}, bf16[2,160,256]{2,1,0:T(8,128)(2,1)S(1)}, u32[]{:S(2)}, u32[]{:S(2)}) collective-permute-start(bf16[2,160,256]{2,1,0:T(8,128)(2,1)} %get-tuple-element.105), channel_id=1, source_target_pairs={{464,466},{465,467},{466,468},{467,469},{468,470},{469,471},{470,4... | collective-permute-start | bytes 491528 | tf_op jit(solution)/shard_map/ppermute | solution.py:30
  217.2 30.0 %collective-permute-start.25 = (bf16[128,2560]{1,0:T(8,128)(2,1)S(1)}, bf16[128,2560]{1,0:T(8,128)(2,1)S(1)}, u32[]{:S(2)}, u32[]{:S(2)}) collective-permute-start(bf16[128,2560]{1,0:T(8,128)(2,1)S(1)} %get-tuple-element.72), channel_id=1, source_target_pairs={{0,496},{32,16},{64,48},{96,80},{128,112},{160,144},{192,176},{224... | collective-permute-start | bytes 1966088 | tf_op jit(solution)/shard_map/ppermute | solution.py:314
  218.5 28.7 %collective-permute-start.24 = (bf16[128,2560]{1,0:T(8,128)(2,1)S(1)}, bf16[128,2560]{1,0:T(8,128)(2,1)S(1)}, u32[]{:S(2)}, u32[]{:S(2)}) collective-permute-start(bf16[128,2560]{1,0:T(8,128)(2,1)S(1)} %copy-done.8), channel_id=1, source_target_pairs={{16,0},{48,32},{80,64},{112,96},{144,128},{176,160},{208,192},{240... | collective-permute-start | bytes 1966088 | tf_op jit(solution)/shard_map/ppermute | solution.py:316
  223.7 8.5 %collective-permute-start.38 = (bf16[2,160,256]{2,1,0:T(8,128)(2,1)S(1)}, bf16[2,160,256]{2,1,0:T(8,128)(2,1)S(1)}, u32[]{:S(2)}, u32[]{:S(2)}) collective-permute-start(bf16[2,160,256]{2,1,0:T(8,128)(2,1)S(1)} %get-tuple-element.102), channel_id=1, source_target_pairs={{0,2},{1,3},{2,4},{3,5},{4,6},{5,7},{6,8},{7,9},{8,10},{9,11},{10,... | collective-permute-start | bytes 491528 | tf_op jit(solution)/shard_map/ppermute | solution.py:30
  225.6 11.2 %collective-permute-start.39 = (bf16[2,160,256]{2,1,0:T(8,128)(2,1)S(1)}, bf16[2,160,256]{2,1,0:T(8,128)(2,1)S(1)}, u32[]{:S(2)}, u32[]{:S(2)}) collective-permute-start(bf16[2,160,256]{2,1,0:T(8,128)(2,1)S(1)} %get-tuple-element.103), channel_id=1, source_target_pairs={{0,14},{1,15},{2,0},{3,1},{4,2},{5,3},{6,4},{7,5},{8,6},{9,7},{10,... | collective-permute-start | bytes 491528 | tf_op jit(solution)/shard_map/ppermute | solution.py:30
  230.3 13.3 %collective-permute-start.41 = (bf16[2,160,256]{2,1,0:T(8,128)(2,1)S(1)}, bf16[2,160,256]{2,1,0:T(8,128)(2,1)S(1)}, u32[]{:S(2)}, u32[]{:S(2)}) collective-permute-start(bf16[2,160,256]{2,1,0:T(8,128)(2,1)S(1)} %get-tuple-element.100), channel_id=1, source_target_pairs={{464,466},{465,467},{466,468},{467,469},{468,470},{469,471},{470,4... | collective-permute-start | bytes 491528 | tf_op jit(solution)/shard_map/ppermute | solution.py:30
  232.2 11.3 %collective-permute-start.42 = (bf16[2,160,256]{2,1,0:T(8,128)(2,1)S(1)}, bf16[2,160,256]{2,1,0:T(8,128)(2,1)S(1)}, u32[]{:S(2)}, u32[]{:S(2)}) collective-permute-start(bf16[2,160,256]{2,1,0:T(8,128)(2,1)S(1)} %get-tuple-element.101), channel_id=1, source_target_pairs={{464,478},{465,479},{466,464},{467,465},{468,466},{469,467},{470,4... | collective-permute-start | bytes 491528 | tf_op jit(solution)/shard_map/ppermute | solution.py:30
  237.8 10.3 %collective-permute-start.40 = (bf16[160,256]{1,0:T(8,128)(2,1)S(1)}, bf16[160,256]{1,0:T(8,128)(2,1)S(1)}, u32[]{:S(2)}, u32[]{:S(2)}) collective-permute-start(bf16[160,256]{1,0:T(8,128)(2,1)S(1)} %fusion.29), channel_id=1, source_target_pairs={{0,1},{1,0},{2,3},{3,2},{4,5},{5,4},{6,7},{7,6},{8,9},{9,8},{10,11... | collective-permute-start | bytes 245768 | tf_op jit(solution)/shard_map/ppermute | solution.py:34
  243.6 9.1 %collective-permute-start.43 = (bf16[160,256]{1,0:T(8,128)(2,1)S(1)}, bf16[160,256]{1,0:T(8,128)(2,1)S(1)}, u32[]{:S(2)}, u32[]{:S(2)}) collective-permute-start(bf16[160,256]{1,0:T(8,128)(2,1)S(1)} %fusion.30), channel_id=1, source_target_pairs={{464,465},{465,464},{466,467},{467,466},{468,469},{469,468},{470,4... | collective-permute-start | bytes 245768 | tf_op jit(solution)/shard_map/ppermute | solution.py:34
  (30 other events, 154.3 us)

commit v6 on v2

--- a/solution.py
+++ b/solution.py
@@ -32,17 +32,25 @@
 
 def place_kernel(n_z, place_ref, *refs):
     half = n_z // 2
-    pieces, outs = refs[: n_z + 1], refs[n_z + 1 :]
+    pieces, outs, sem = refs[: n_z + 1], refs[n_z + 1 : n_z + 3], refs[n_z + 3]
     z = place_ref[0]
     offsets = [0] + list(range(-1, -half, -1)) + list(range(1, half))
+    copies = []
     for level, out in enumerate(outs):
-        lanes = slice(level * out.shape[2], (level + 1) * out.shape[2])
         for piece, offset in zip(pieces, offsets):
             at = lax.rem(z + (offset + n_z), n_z) * 2
-            out[pl.ds(at, 2)] = piece[:, :, lanes]
+            copies.append((piece.at[:, level], out.at[pl.ds(at, 2)]))
         far = lax.rem(z + half, n_z) * 2
         for h in range(2):
-            out[pl.ds(far + h, 1)] = pieces[n_z - 1 + h][:, :, lanes]
+            copies.append((pieces[n_z - 1 + h].at[:, level], out.at[pl.ds(far + h, 1)]))
+    started = [
+        pltpu.make_async_copy(source, target, sem.at[i])
+        for i, (source, target) in enumerate(copies)
+    ]
+    for copy in started:
+        copy.start()
+    for copy in started:
+        copy.wait()
 
 
 def ring_gather(shard, n_z):
@@ -58,41 +66,16 @@
         rights.append(right)
         lefts.append(left)
     pieces = [pair] + rights + lefts + [shifted(right[:1], n_z, 1), shifted(left[1:], n_z, -1)]
-    share, lanes = shard.shape[0], shard.shape[1] // 2
+    _, share, lanes = shard.shape
     whole = jax.ShapeDtypeStruct((2 * n_z, share, lanes), shard.dtype)
     return pl.pallas_call(
         functools.partial(place_kernel, n_z),
         out_shape=[whole, whole],
-        in_specs=[SCALAR] + [IN_VMEM] * len(pieces),
-        out_specs=[IN_VMEM] * 2,
-        compiler_params=LIMIT,
+        in_specs=[SCALAR] + [ANYWHERE] * len(pieces),
+        out_specs=[ANYWHERE] * 2,
+        scratch_shapes=[pltpu.SemaphoreType.DMA((2 * (n_z + 1),))],
         name="place_maps",
     )(z.astype(jnp.int32)[None], *pieces)
-
-
-def ring_reduce(parts, n_z):
-    index = lax.axis_index("dp")
-    z, h = index // 2, index % 2
-    half = n_z // 2
-
-    def at(offset):
-        return lax.dynamic_index_in_dim(parts, (z + offset) % n_z, 0, keepdims=False)
-
-    far = at(half)
-    right, left = shifted(far[:1], n_z, 1), shifted(far[1:], n_z, -1)
-    for step in range(half - 1, 0, -1):
-        here, there = at(step), at(-step)
-        if step == half - 1:
-            here = jnp.concatenate([here[:1] + right, here[1:]], axis=0)
-            there = jnp.concatenate([there[:1], there[1:] + left], axis=0)
-        else:
-            here, there = here + right, there + left
-        here, there = lax.optimization_barrier((here, there))
-        right, left = shifted(here, n_z, 1), shifted(there, n_z, -1)
-    total = at(0).astype(F32) + right.astype(F32) + left.astype(F32)
-    mine = lax.dynamic_index_in_dim(total, h, 0, keepdims=False)
-    other = lax.dynamic_index_in_dim(total, 1 - h, 0, keepdims=False).astype(BF16)
-    return mine, swapped(other, n_z)
 
 
 def empty_kernel(out_ref):
@@ -151,9 +134,10 @@
     return pl.pallas_call(
         first_kernel,
         grid=(1,),
-        out_shape=[wide, narrow, narrow, wide],
+        out_shape=[wide, narrow, narrow],
         in_specs=[pl.BlockSpec((1, 1, rows, width), lambda i: (0, 0, 0, 0)), IN_VMEM, IN_VMEM],
-        out_specs=[IN_VMEM] * 4,
+        out_specs=[IN_VMEM] * 3,
+        scratch_shapes=[pltpu.VMEM((rows, width), BF16)],
         compiler_params=LIMIT,
         cost_estimate=pl.CostEstimate(flops=6 * rows * width * rank, bytes_accessed=4 * 2 * rows * width, transcendentals=0),
         name="first_tick",
@@ -164,7 +148,7 @@
     rank = active_ref.shape[2]
     inverse = normalise(x_ref, normed_ref.at[0])
     inverse_ref[0] = jnp.broadcast_to(inverse, inverse_ref.shape[1:])
-    level = level_ref[pl.program_id(0) + 1]
+    level = level_ref[pl.program_id(0)]
     for value, map_ref in ((1, first_ref), (0, second_ref)):
 
         @pl.when(level == value)
@@ -179,10 +163,10 @@
     slope_ref[0] = gate * (1.0 + latent * (1.0 - gate))
 
 
-def forward_rest(levels, saved_inputs, first, second, dep):
+def forward_all(levels, saved_inputs, first, second, dep):
     ticks, _, rows, width = saved_inputs.shape
     rank = first.shape[1] // 2
-    rest = ticks - 1
+    rest = ticks
 
     def made(lanes, dtype):
         return jax.ShapeDtypeStruct((rest, rows, lanes), dtype)
@@ -196,7 +180,7 @@
         out_shape=[made(width, BF16), made(rank, BF16), made(rank, F32), made(rank, F32), made(rank, F32)],
         in_specs=[
             SCALAR,
-            pl.BlockSpec((1, 1, rows, width), lambda i: (i + 1, 0, 0, 0)),
+            pl.BlockSpec((1, 1, rows, width), lambda i: (i, 0, 0, 0)),
             IN_VMEM,
             IN_VMEM,
             ANYWHERE,
@@ -204,33 +188,47 @@
         out_specs=[block(width)] + [block(rank)] * 4,
         compiler_params=LIMIT,
         cost_estimate=pl.CostEstimate(flops=rest * 2 * rows * width * rank, bytes_accessed=rest * 4 * rows * width, transcendentals=0),
-        name="forward_rest",
+        name="forward_all",
     )(levels, saved_inputs, first, second, dep)
 
 
-def tick_kernel(flags_ref, incoming_ref, x_ref, first_ref, second_ref, latent_ref, slope_ref, inverse_ref, dep_ref, sent_ref, grad_latent_ref):
-    for value, map_ref in ((1, first_ref), (0, second_ref)):
-
-        @pl.when((flags_ref[0] == 1) & (flags_ref[1] == value))
+def tick_kernel(tick, flags_ref, incoming_ref, x_ref, first_ref, second_ref, latent_ref, slope_ref, inverse_ref, dep_ref, sent_ref, grad_latent_ref, x, second, sems):
+    level = flags_ref[1]
+    get_x = pltpu.make_async_copy(x_ref.at[pl.ds(tick, 1)], x, sems.at[0])
+    get_second = pltpu.make_async_copy(second_ref, second, sems.at[1])
+
+    @pl.when(flags_ref[0] == 1)
+    def _():
+        get_x.start()
+
+        @pl.when(level == 0)
         def _():
-            relay(
-                incoming_ref,
-                x_ref,
-                map_ref,
-                latent_ref[0],
-                slope_ref[0],
-                inverse_ref[0][:, :1],
-                sent_ref,
-                grad_latent_ref,
-            )
+            get_second.start()
+            get_second.wait()
+
+        get_x.wait()
+        for value, map_ref in ((1, first_ref), (0, second)):
+
+            @pl.when(level == value)
+            def _():
+                relay(
+                    incoming_ref,
+                    x,
+                    map_ref,
+                    latent_ref[0],
+                    slope_ref[0],
+                    inverse_ref[0][:, :1],
+                    sent_ref,
+                    grad_latent_ref,
+                )
 
 
 def later_tick(tick, works, level, incoming, saved_inputs, first, second, latents, slopes, inverses, dep):
     _, _, rows, width = saved_inputs.shape
     rank = first.shape[1] // 2
-    narrow = pl.BlockSpec((1, rows, rank), lambda i: (tick - 1, 0, 0))
-    return pl.pallas_call(
-        tick_kernel,
+    narrow = pl.BlockSpec((1, rows, rank), lambda i: (tick, 0, 0))
+    return pl.pallas_call(
+        functools.partial(tick_kernel, tick),
         grid=(1,),
         out_shape=[
             jax.ShapeDtypeStruct((rows, width), BF16),
@@ -239,17 +237,24 @@
         in_specs=[
             SCALAR,
             IN_VMEM,
-            pl.BlockSpec((1, 1, rows, width), lambda i: (tick, 0, 0, 0)),
+            ANYWHERE,
             IN_VMEM,
-            IN_VMEM,
+            ANYWHERE,
             narrow,
             narrow,
             narrow,
             ANYWHERE,
         ],
         out_specs=[IN_VMEM] * 2,
-        compiler_params=LIMIT,
-        cost_estimate=pl.CostEstimate(flops=4 * rows * width * rank, bytes_accessed=3 * 2 * rows * width, transcendentals=0),
+        scratch_shapes=[
+            pltpu.VMEM((1, 1, rows, width), BF16),
+            pltpu.VMEM(second.shape, BF16),
+            pltpu.SemaphoreType.DMA((2,)),
+        ],
+        compiler_params=LIMIT,
+        cost_estimate=pl.CostEstimate(
+            flops=40 * rows * width * rank, bytes_accessed=40 * rows * width, transcendentals=0
+        ),
         name="later_tick",
     )(
         jnp.stack([works.astype(jnp.int32), level.astype(jnp.int32)]),
@@ -272,34 +277,74 @@
     return block.T[:, :share]
 
 
-def finish_one_kernel(moved_ref, down_ref, up_ref):
-    rank = down_ref.shape[1]
+def beside_kernel(left_ref, right_ref, out_ref):
+    lanes = left_ref.shape[1]
+    out_ref[:, :lanes] = left_ref[...]
+    out_ref[:, lanes:] = right_ref[...]
+
+
+def beside(left, right):
+    rows, lanes = left.shape
+    run = rows // 4
+    block = pl.BlockSpec((run, lanes), lambda i: (i, 0))
+    return pl.pallas_call(
+        beside_kernel,
+        grid=(rows // run,),
+        out_shape=jax.ShapeDtypeStruct((rows, 2 * lanes), left.dtype),
+        in_specs=[block, block],
+        out_specs=pl.BlockSpec((run, 2 * lanes), lambda i: (i, 0)),
+        compiler_params=LIMIT,
+        name="side_by_side",
+    )(left, right)
+
+
+def sum_kernel(moved_ref, out_ref):
     total = jnp.sum(moved_ref[...].astype(F32), axis=0)
-    down_ref[0] = jnp.zeros(down_ref.shape[1:], F32)
-    up_ref[0] = jnp.zeros(up_ref.shape[1:], F32)
-    down_ref[1] = turned(total[:, :rank])
-    up_ref[1] = turned(total[:, rank:])
-
-
-def finish_two_kernel(mine_ref, other_ref, down_ref, up_ref):
-    rank = down_ref.shape[1]
-    total = mine_ref[...] + other_ref[...].astype(F32)
+    if total.shape == out_ref.shape:
+        out_ref[...] = total
+    else:
+        rank = total.shape[1] // 2
+        zeros = jnp.zeros((total.shape[0], rank), F32)
+        out_ref[...] = jnp.concatenate([total[:, :rank], zeros, total[:, rank:], zeros], axis=1)
+
+
+def summed(moved, lanes):
+    return pl.pallas_call(
+        sum_kernel,
+        out_shape=jax.ShapeDtypeStruct((moved.shape[1], lanes), F32),
+        in_specs=[IN_VMEM],
+        out_specs=IN_VMEM,
+        compiler_params=LIMIT,
+        name="sum_partials",
+    )(moved)
+
+
+def finish_kernel(even_ref, total_ref, core_ref, over_ref, grad_ref, down_ref, up_ref, sem):
+    for value, source in ((1, core_ref), (0, over_ref)):
+
+        @pl.when(even_ref[0] == value)
+        def _():
+            pltpu.make_async_copy(source, grad_ref.at[0], sem).start()
+
+    rank = down_ref.shape[2]
     for i, out in enumerate((down_ref, up_ref)):
         for j, level in enumerate((1, 0)):
             at = (2 * i + j) * rank
-            out[level] = turned(total[:, at : at + rank])
-
-
-def finish(kernel, rank, share, *args):
-    made = jax.ShapeDtypeStruct((2, rank, share), F32)
-    return pl.pallas_call(
-        kernel,
-        out_shape=[made, made],
-        in_specs=[IN_VMEM] * len(args),
-        out_specs=[IN_VMEM] * 2,
-        compiler_params=LIMIT,
-        name="finish_sums",
-    )(*args)
+            out[level, 0] = turned(total_ref[:, at : at + rank])
+    pltpu.make_async_copy(core_ref, grad_ref.at[0], sem).wait()
+
+
+def finish(flag, total, core, over, share, rank):
+    made = jax.ShapeDtypeStruct((2, 1, rank, share), F32)
+    return pl.pallas_call(
+        finish_kernel,
+        out_shape=[jax.ShapeDtypeStruct((1,) + core.shape, core.dtype), made, made],
+        in_specs=[SCALAR, IN_VMEM, ANYWHERE, ANYWHERE],
+        out_specs=[ANYWHERE, IN_VMEM, IN_VMEM],
+        scratch_shapes=[pltpu.SemaphoreType.DMA],
+        compiler_params=LIMIT,
+        name="finish",
+    )(flag, total, core, over)
 
 
 def on_device(saved_inputs, grad_in, adapter_down, adapter_up):
@@ -315,7 +360,9 @@
     levels = [1 - (position + tick) // n_sec for tick in range(ticks)]
 
     def gather_two(down, up):
-        shard = jnp.concatenate([down[1].T, up[1].T, down[0].T, up[0].T], axis=1)
+        shard = jnp.stack(
+            [jnp.concatenate([down[v].T, up[v].T], axis=1) for v in (1, 0)]
+        )
         first, second = ring_gather(shard, n_z)
         return first.reshape(width, 2 * rank), second.reshape(width, 2 * rank)
 
@@ -330,9 +377,9 @@
         two_layers, gather_two, gather_one, adapter_down[:, 0], adapter_up[:, 0]
     )
 
-    sent, grad_latent, active, normed = first_tick(saved_inputs, grad_in[0], first)
+    sent, grad_latent, _ = first_tick(saved_inputs, grad_in[0], first)
     level_stack = jnp.stack(levels).astype(jnp.int32)
-    normeds, actives, latents, slopes, inverses = forward_rest(
+    normeds, actives, latents, slopes, inverses = forward_all(
         level_stack, saved_inputs, first, second, grad_latent
     )
 
@@ -360,7 +407,7 @@
                 dep,
             )
 
-        sent_even, latent_even = layer(even, core, normeds)
+        sent_even, latent_even = layer(even, core, grad_latent)
         next_over = lax.ppermute(sent_even, "section", across)
         sent_odd, latent_odd = layer(~even, over, latent_even)
         next_core = lax.ppermute(sent_odd, "section", inside)
@@ -368,20 +415,19 @@
         grad_latents.append(jnp.where(even, latent_even, latent_odd))
         over, core = next_over, next_core
 
-    normed_all = jnp.concatenate([normed[None], normeds], axis=0).reshape(-1, width)
+    normed_all = normeds.reshape(-1, width)
     grads_all = jnp.concatenate(grads, axis=0)
-    actives_all = jnp.concatenate([active[None], actives], axis=0)
 
     def products(lats, acts):
         contract = (((0,), (0,)), ((), ()))
         down = lax.dot_general(normed_all, lats, contract, preferred_element_type=F32)
         up = lax.dot_general(grads_all, acts, contract, preferred_element_type=F32)
-        return jnp.concatenate([down.astype(BF16), up.astype(BF16)], axis=1)
+        both = beside(down.astype(BF16), up.astype(BF16))
+        moved = lax.all_to_all(both.reshape(n_dp, share, -1), "dp", 0, 0, tiled=True)
+        return summed(moved, 4 * rank)
 
     def reduce_one(lats, acts):
-        parts = products(lats.reshape(-1, rank), acts.reshape(-1, rank))
-        moved = lax.all_to_all(parts.reshape(n_dp, share, 2 * rank), "dp", 0, 0, tiled=True)
-        return finish(finish_one_kernel, rank, share, moved)
+        return products(lats.reshape(-1, rank), acts.reshape(-1, rank))
 
     def reduce_two(lats, acts):
         level = level_stack[:, None, None]
@@ -391,15 +437,11 @@
             both = [jnp.where(level == 1, value, zero), jnp.where(level == 0, value, zero)]
             return jnp.concatenate(both, axis=2).reshape(-1, 2 * rank)
 
-        parts = products(split(lats), split(acts))
-        mine, other = ring_reduce(parts.reshape(n_z, 2, share, 4 * rank), n_z)
-        return finish(finish_two_kernel, rank, share, mine, other)
-
-    down_grad, up_grad = lax.cond(
-        two_layers, reduce_two, reduce_one, jnp.stack(grad_latents), actives_all
-    )
-    grad_out = jnp.where(even, core, over)
-    return grad_out[None], down_grad[:, None], up_grad[:, None]
+        return products(split(lats), split(acts))
+
+    total = lax.cond(two_layers, reduce_two, reduce_one, jnp.stack(grad_latents), actives)
+    flag = even.astype(jnp.int32)[None]
+    return tuple(finish(flag, total, core, over, share, rank))
 
 
 def solution(mesh):

time: 223 us -> 285 us (1.28)
  the two profiles are of different devices: /device:TPU:62 before, /device:TPU:63 now
where the time goes in v6:
time: 285 us; the launch traced here: 284 us
  Pallas kernels  104 us (36%)
  blocking collectives  61.6 us (22%)
  starting transfers between devices  59.8 us (21%)
  waiting for transfers between devices  44.5 us (16%)
  local copies, waits for them, and re-layouts  6.16 us (2%)
  other arithmetic  3.98 us (1%)
    pallas_call x1, Pallas kernels, ring_gather(): pl.pallas_call(functools.partial(place_kernel, n_z), out_shape=[whole, wh...  80.7 us
    all_to_all x1, blocking collectives, products(): lax.all_to_all(both.reshape(n_dp, share, -1), 'dp', 0, 0, tiled=True)  61.6 us
    ppermute x8, starting transfers between devices, shifted(): return lax.ppermute(value, 'dp', dp_pairs(n_z, step, 0))  34 us
    ppermute x3, waiting for transfers between devices, on_device(): next_over = lax.ppermute(sent_even, 'section', across)  23.7 us
    ppermute x8, waiting for transfers between devices, shifted(): return lax.ppermute(value, 'dp', dp_pairs(n_z, step, 0))  13.7 us
    pallas_call x6, Pallas kernels, later_tick(): pl.pallas_call(functools.partial(tick_kernel, tick), grid=(1,), out_shape...  13.6 us
    ppermute x1, starting transfers between devices, on_device(): core = lax.ppermute(sent, 'section', inside)  12.3 us
    ppermute x1, waiting for transfers between devices, swapped(): return lax.ppermute(value, 'dp', dp_pairs(n_z, 0, 1))  6.73 us
  transfers between devices with their start and end apart: 17, of which 8 were waited for; matrix products, arithmetic and copies ran while one was open for 2% of the time, Pallas kernels for 4%

profile of v6, /device:TPU:63, one launch (start us, length us, event | category | flops | bytes accessed | tf_op | source)
XLA Modules:
  0.0 283.8 jit_solution(5708743396882369757)
XLA Ops:
  0.7 145.3 %conditional.2 = (bf16[2560,256]{1,0:T(8,128)(2,1)}, bf16[2560,256]{1,0:T(8,128)(2,1)}) conditional(s32[]{:T(128)} %convert_element_type.27, (bf16[2,128,160]{1,2,0:T(8,128)(2,1)}, bf16[2,128,160]{1,2,0:T(8,128)(2,1)}) %tuple.46, (bf16[2,128,160]{1,2,0:T(8,128)(2,1)}, bf16[2,128,160]{1,2,0:T(8,128)(2,1)}) %tuple.47), branch_computations={%region_0.1_spmd, %region_1.2_spmd} | conditional | flops 819222 | bytes 22610736 | solution.py:376
  0.7 1.0 slice_bitcast_fusion.4
  1.7 0.7 pad_maximum_fusion.2
  2.4 4.4 %collective-permute-start = (bf16[2,160,256]{2,1,0:T(8,128)(2,1)}, bf16[2,160,256]{2,1,0:T(8,128)(2,1)}, u32[]{:S(2)}, u32[]{:S(2)}) collective-permute-start(bf16[2,160,256]{2,1,0:T(8,128)(2,1)} %pad_maximum_fusion.2), channel_id=1, source_target_pairs={{0,1},{1,0},{2,3},{3,2},{4,5},{5,4},{6,7},{7,6},{8,9},{9,8},{10,11... | collective-permute-start | bytes 491528 | tf_op jit(solution)/shard_map/cond/branch_1_fun/ppermute | solution.py:30
  6.9 6.7 %collective-permute-done = bf16[2,160,256]{2,1,0:T(8,128)(2,1)} collective-permute-done((bf16[2,160,256]{2,1,0:T(8,128)(2,1)}, bf16[2,160,256]{2,1,0:T(8,128)(2,1)}, u32[]{:S(2)}, u32[]{:S(2)}) %collective-permute-start) | collective-permute-done | bytes 163872 | tf_op jit(solution)/shard_map/cond/branch_1_fun/ppermute | solution.py:30
  13.6 0.9 select_bitcast_fusion.1
  14.6 10.7 %collective-permute-start.4 = (bf16[2,2,160,256]{3,2,1,0:T(8,128)(2,1)S(1)}, bf16[2,2,160,256]{3,2,1,0:T(8,128)(2,1)S(1)}, u32[]{:S(2)}, u32[]{:S(2)}) collective-permute-start(bf16[2,2,160,256]{3,2,1,0:T(8,128)(2,1)S(1)} %pad_maximum_fusion.1.refs_0_), channel_id=1, source_target_pairs={{0,14},{1,15},{2,0},{3,1},{4,2},{5,3},{6,4},{7,5},{8,6},{9,7},{10,... | collective-permute-start | bytes 983048 | tf_op jit(solution)/shard_map/cond/branch_1_fun/ppermute | solution.py:26
  25.3 1.9 collective-permute-start.1
  27.2 3.5 %collective-permute-done.4.refs_4_ = bf16[2,2,160,256]{3,2,1,0:T(8,128)(2,1)S(1)} collective-permute-done((bf16[2,2,160,256]{3,2,1,0:T(8,128)(2,1)S(1)}, bf16[2,2,160,256]{3,2,1,0:T(8,128)(2,1)S(1)}, u32[]{:S(2)}, u32[]{:S(2)}) %collective-permute-start.4) | collective-permute-done | bytes 327712 | tf_op jit(solution)/shard_map/cond/branch_1_fun/ppermute | solution.py:26
  30.7 5.3 %collective-permute-start.5 = (bf16[2,2,160,256]{3,2,1,0:T(8,128)(2,1)S(1)}, bf16[2,2,160,256]{3,2,1,0:T(8,128)(2,1)S(1)}, u32[]{:S(2)}, u32[]{:S(2)}) collective-permute-start(bf16[2,2,160,256]{3,2,1,0:T(8,128)(2,1)S(1)} %collective-permute-done.4.refs_4_), channel_id=1, source_target_pairs={{0,14},{1,15},{2,0},{3,1},{4,2},{5,3},{6,4},{7,5},{8,6},{9,7},{10,... | collective-permute-start | bytes 983048 | tf_op jit(solution)/shard_map/cond/branch_1_fun/ppermute | solution.py:26
  36.0 1.9 collective-permute-start.2
  37.9 2.5 collective-permute-done.5.refs_5_
  40.5 5.3 %collective-permute-start.6 = (bf16[2,2,160,256]{3,2,1,0:T(8,128)(2,1)S(1)}, bf16[2,2,160,256]{3,2,1,0:T(8,128)(2,1)S(1)}, u32[]{:S(2)}, u32[]{:S(2)}) collective-permute-start(bf16[2,2,160,256]{3,2,1,0:T(8,128)(2,1)S(1)} %collective-permute-done.5.refs_5_), channel_id=1, source_target_pairs={{0,14},{1,15},{2,0},{3,1},{4,2},{5,3},{6,4},{7,5},{8,6},{9,7},{10,... | collective-permute-start | bytes 983048 | tf_op jit(solution)/shard_map/cond/branch_1_fun/ppermute | solution.py:26
  45.8 1.9 collective-permute-start.3
  47.8 2.0 collective-permute-done.6.refs_6_
  49.8 0.7 copy-done.5
  51.2 5.0 %collective-permute-start.8 = (bf16[1,2,160,256]{3,2,1,0:T(8,128)(2,1)}, bf16[1,2,160,256]{3,2,1,0:T(8,128)(2,1)S(1)}, u32[]{:S(2)}, u32[]{:S(2)}) collective-permute-start(bf16[1,2,160,256]{3,2,1,0:T(8,128)(2,1)} %slice.27), channel_id=1, source_target_pairs={{0,14},{1,15},{2,0},{3,1},{4,2},{5,3},{6,4},{7,5},{8,6},{9,7},{10,... | collective-permute-start | bytes 491528 | tf_op jit(solution)/shard_map/cond/branch_1_fun/ppermute | solution.py:26
  56.2 0.7 copy-done.6
  57.7 1.9 collective-permute-start.7
  59.6 5.6 %collective-permute-done.7.refs_7_ = bf16[1,2,160,256]{3,2,1,0:T(8,128)(2,1)} collective-permute-done((bf16[1,2,160,256]{3,2,1,0:T(8,128)(2,1)}, bf16[1,2,160,256]{3,2,1,0:T(8,128)(2,1)}, u32[]{:S(2)}, u32[]{:S(2)}) %collective-permute-start.7) | collective-permute-done | bytes 163872 | tf_op jit(solution)/shard_map/cond/branch_1_fun/ppermute | solution.py:26
  65.2 80.7 %place_maps.1 = (bf16[16,160,256]{2,1,0:T(8,128)(2,1)}, bf16[16,160,256]{2,1,0:T(8,128)(2,1)}) custom-call(s32[1]{0:T(128)} %bitcast.5.place_ref, bf16[2,2,160,256]{3,2,1,0:T(8,128)(2,1)} %copy-done.4, bf16[2,2,160,256]{3,2,1,0:T(8,128)(2,1)} %copy-done.8, bf16[2,2,160,256]{3,2,1,0:T(8,128)(2,1)} %copy-done.10, bf16[2,2,160,256]{3,2,1,0:T(8,128)(2,1)} %copy-done.6, ...), custom_call_target="tpu_custom_call" | custom-call | tf_op jit(solution)/shard_map/cond/branch_1_fun/place_maps/pallas_call | solution.py:71
  145.9 3.3 %first_tick.1 = (bf16[128,2560]{1,0:T(8,128)(2,1)}, bf16[128,128]{1,0:T(8,128)(2,1)S(1)}, bf16[128,128]{1,0:T(8,128)(2,1)}) custom-call(bf16[4,1,128,2560]{3,2,1,0:T(8,128)(2,1)S(1)} %copy-done, bf16[128,2560]{1,0:T(8,128)(2,1)S(1)} %bitcast.73, bf16[2560,256]{1,0:T(8,128)(2,1)} %get-tuple-element.68.map_ref.first_ref), custom_call_target="tpu_custom_call" | custom-call | flops 251658240 | bytes 2621440 | tf_op jit(solution)/shard_map/first_tick/pallas_call | solution.py:134
  149.2 1.3 collective-permute-start.10
  150.5 12.3 %collective-permute-start.9 = (bf16[128,2560]{1,0:T(8,128)(2,1)}, bf16[128,2560]{1,0:T(8,128)(2,1)}, u32[]{:S(2)}, u32[]{:S(2)}) collective-permute-start(bf16[128,2560]{1,0:T(8,128)(2,1)} %get-tuple-element.70), channel_id=1, source_target_pairs={{16,0},{48,32},{80,64},{112,96},{144,128},{176,160},{208,192},{240... | collective-permute-start | bytes 1966088 | tf_op jit(solution)/shard_map/ppermute | solution.py:392
  163.0 4.2 %forward_all.1 = (bf16[4,128,2560]{2,1,0:T(8,128)(2,1)S(1)}, bf16[4,128,128]{2,1,0:T(8,128)(2,1)S(1)}, f32[4,128,128]{2,1,0:T(8,128)S(1)}, f32[4,128,128]{2,1,0:T(8,128)S(1)}, f32[4,128,128]{2,1,0:T(8,128)S(1)}) custom-call(s32[4]{0:T(128)S(1)} %pad_add_fusion.level_ref, bf16[4,1,128,2560]{3,2,1,0:T(8,128)(2,1)S(1)} %copy-done, ...), custom_call_target="tpu_custom_call" | custom-call | flops 335544320 | bytes 5242880 | tf_op jit(solution)/shard_map/forward_all/pallas_call | solution.py:177
  167.6 1.6 later_tick.6
  169.2 2.6 later_tick.7
  171.8 1.3 collective-permute-start.11
  173.2 1.3 collective-permute-start.12
  174.5 1.2 broadcast_select_fusion.6
  175.7 1.4 later_tick.8
  177.0 12.0 %collective-permute-done.12.incoming_ref = bf16[128,2560]{1,0:T(8,128)(2,1)S(1)} collective-permute-done((bf16[128,2560]{1,0:T(8,128)(2,1)S(1)}, bf16[128,2560]{1,0:T(8,128)(2,1)S(1)}, u32[]{:S(2)}, u32[]{:S(2)}) %collective-permute-start.12) | collective-permute-done | bytes 655392 | tf_op jit(solution)/shard_map/ppermute | solution.py:411
  189.0 2.4 later_tick.9
  191.4 1.3 collective-permute-start.13
  192.8 1.3 collective-permute-start.14
  194.4 2.4 later_tick.10
  196.8 11.8 %collective-permute-done.14.incoming_ref = bf16[128,2560]{1,0:T(8,128)(2,1)S(1)} collective-permute-done((bf16[128,2560]{1,0:T(8,128)(2,1)S(1)}, bf16[128,2560]{1,0:T(8,128)(2,1)S(1)}, u32[]{:S(2)}, u32[]{:S(2)}) %collective-permute-start.14) | collective-permute-done | bytes 655392 | tf_op jit(solution)/shard_map/ppermute | solution.py:411
  208.6 3.3 %later_tick.11 = (bf16[128,2560]{1,0:T(8,128)(2,1)}, bf16[128,128]{1,0:T(8,128)(2,1)S(1)}) custom-call(s32[2]{0:T(128)S(1)} %pad_add_fusion.5.flags_ref, bf16[128,2560]{1,0:T(8,128)(2,1)S(1)} %collective-permute-done.14.incoming_ref, bf16[4,1,128,2560]{3,2,1,0:T(8,128)(2,1)S(1)} %copy-done, bf16[2560,256]{1,0:T(8,128)(2,1)} %get-tuple-element.68.map_ref.first_ref, ...), custom_call_target="tpu_custom_call" | custom-call | flops 1677721600 | bytes 13107200 | tf_op jit(solution)/shard_map/later_tick/pallas_call | solution.py:230
  211.9 1.3 collective-permute-start.15
  213.2 1.3 collective-permute-start.16
  214.9 64.8 %conditional.3 = (f32[160,512]{1,0:T(8,128)S(1)}) conditional(s32[]{:T(128)} %convert_element_type.27, (bf16[4,128,128]{2,1,0:T(8,128)(2,1)S(1)}, bf16[512,2560]{1,0:T(8,128)(2,1)S(1)}, bf16[4,128,128]{2,1,0:T(8,128)(2,1)S(1)}, bf16[512,2560]{1,0:T(8,128)(2,1)S(1)}) %tuple.42, (s32[4]{0:T(128)S(1)}, bf16[4,128,128]{2,1,0:T(8,128)(2,1)S(1)}, ...), branch_computations={%region_2.3_spmd, %region_3.4_spmd} | conditional | flops 1344798720 | bytes 15466536 | solution.py:442
  215.1 1.1 fusion.left_ref
  216.2 1.2 fusion.1.right_ref
  217.7 61.6 %all_to_all.13.moved_ref = bf16[16,160,512]{2,1,0:T(8,128)(2,1)S(1)} all-to-all(bf16[16,160,512]{2,1,0:T(8,128)(2,1)S(1)} %bitcast.71), channel_id=1, replica_groups=mesh['section'=32,'dp'=16] {'dp'}, dimensions={0} | all-to-all | bytes 5242880 | tf_op jit(solution)/shard_map/cond/branch_1_fun/all_to_all | solution.py:426
  279.6 0.7 copy-done.3
  280.4 1.8 finish.1
  282.2 0.8 copy.12
  283.0 0.8 copy.13
  (55 shorter events, 3.5 us)
Async XLA Ops:
  0.6 145.3 %copy-start = (bf16[4,1,128,2560]{3,2,1,0:T(8,128)(2,1)S(1)}, bf16[4,1,128,2560]{3,2,1,0:T(8,128)(2,1)}, u32[]{:S(2)}) copy-start(bf16[4,1,128,2560]{3,2,1,0:T(8,128)(2,1)} %x_ref.15) | copy-start | bytes 7864324
  0.6 145.3 %copy-start.1 = (bf16[1,128,2560]{2,1,0:T(8,128)(2,1)S(1)}, bf16[1,128,2560]{2,1,0:T(8,128)(2,1)}, u32[]{:S(2)}) copy-start(bf16[1,128,2560]{2,1,0:T(8,128)(2,1)} %param.9) | copy-start | bytes 1966084
  2.4 11.2 %collective-permute-start = (bf16[2,160,256]{2,1,0:T(8,128)(2,1)}, bf16[2,160,256]{2,1,0:T(8,128)(2,1)}, u32[]{:S(2)}, u32[]{:S(2)}) collective-permute-start(bf16[2,160,256]{2,1,0:T(8,128)(2,1)} %pad_maximum_fusion.2), channel_id=1, source_target_pairs={{0,1},{1,0},{2,3},{3,2},{4,5},{5,4},{6,7},{7,6},{8,9},{9,8},{10,11... | collective-permute-start | bytes 491528 | tf_op jit(solution)/shard_map/cond/branch_1_fun/ppermute | solution.py:30
  14.6 10.7 %copy-start.4 = (bf16[2,2,160,256]{3,2,1,0:T(8,128)(2,1)}, bf16[2,2,160,256]{3,2,1,0:T(8,128)(2,1)S(1)}, u32[]{:S(2)}) copy-start(bf16[2,2,160,256]{3,2,1,0:T(8,128)(2,1)S(1)} %pad_maximum_fusion.1.refs_0_) | copy-start | bytes 983044 | tf_op jit(solution)/shard_map/cond
  14.6 16.1 %collective-permute-start.4 = (bf16[2,2,160,256]{3,2,1,0:T(8,128)(2,1)S(1)}, bf16[2,2,160,256]{3,2,1,0:T(8,128)(2,1)S(1)}, u32[]{:S(2)}, u32[]{:S(2)}) collective-permute-start(bf16[2,2,160,256]{3,2,1,0:T(8,128)(2,1)S(1)} %pad_maximum_fusion.1.refs_0_), channel_id=1, source_target_pairs={{0,14},{1,15},{2,0},{3,1},{4,2},{5,3},{6,4},{7,5},{8,6},{9,7},{10,... | collective-permute-start | bytes 983048 | tf_op jit(solution)/shard_map/cond/branch_1_fun/ppermute | solution.py:26
  25.3 10.7 %collective-permute-start.1 = (bf16[2,2,160,256]{3,2,1,0:T(8,128)(2,1)S(1)}, bf16[2,2,160,256]{3,2,1,0:T(8,128)(2,1)S(1)}, u32[]{:S(2)}, u32[]{:S(2)}) collective-permute-start(bf16[2,2,160,256]{3,2,1,0:T(8,128)(2,1)S(1)} %pad_maximum_fusion.1.refs_0_), channel_id=1, source_target_pairs={{0,2},{1,3},{2,4},{3,5},{4,6},{5,7},{6,8},{7,9},{8,10},{9,11},{10,... | collective-permute-start | bytes 983048 | tf_op jit(solution)/shard_map/cond/branch_1_fun/ppermute | solution.py:26
  30.7 15.2 %copy-start.7 = (bf16[2,2,160,256]{3,2,1,0:T(8,128)(2,1)}, bf16[2,2,160,256]{3,2,1,0:T(8,128)(2,1)S(1)}, u32[]{:S(2)}) copy-start(bf16[2,2,160,256]{3,2,1,0:T(8,128)(2,1)S(1)} %collective-permute-done.4.refs_4_) | copy-start | bytes 983044 | tf_op jit(solution)/shard_map/cond
  30.7 9.8 %collective-permute-start.5 = (bf16[2,2,160,256]{3,2,1,0:T(8,128)(2,1)S(1)}, bf16[2,2,160,256]{3,2,1,0:T(8,128)(2,1)S(1)}, u32[]{:S(2)}, u32[]{:S(2)}) collective-permute-start(bf16[2,2,160,256]{3,2,1,0:T(8,128)(2,1)S(1)} %collective-permute-done.4.refs_4_), channel_id=1, source_target_pairs={{0,14},{1,15},{2,0},{3,1},{4,2},{5,3},{6,4},{7,5},{8,6},{9,7},{10,... | collective-permute-start | bytes 983048 | tf_op jit(solution)/shard_map/cond/branch_1_fun/ppermute | solution.py:26
  36.0 9.8 %copy-start.8 = (bf16[2,2,160,256]{3,2,1,0:T(8,128)(2,1)}, bf16[2,2,160,256]{3,2,1,0:T(8,128)(2,1)S(1)}, u32[]{:S(2)}) copy-start(bf16[2,2,160,256]{3,2,1,0:T(8,128)(2,1)S(1)} %collective-permute-done.1.refs_1_) | copy-start | bytes 983044 | tf_op jit(solution)/shard_map/cond
  36.0 9.8 %collective-permute-start.2 = (bf16[2,2,160,256]{3,2,1,0:T(8,128)(2,1)S(1)}, bf16[2,2,160,256]{3,2,1,0:T(8,128)(2,1)S(1)}, u32[]{:S(2)}, u32[]{:S(2)}) collective-permute-start(bf16[2,2,160,256]{3,2,1,0:T(8,128)(2,1)S(1)} %collective-permute-done.1.refs_1_), channel_id=1, source_target_pairs={{0,2},{1,3},{2,4},{3,5},{4,6},{5,7},{6,8},{7,9},{8,10},{9,11},{10,... | collective-permute-start | bytes 983048 | tf_op jit(solution)/shard_map/cond/branch_1_fun/ppermute | solution.py:26
  40.5 17.2 %copy-start.9 = (bf16[2,2,160,256]{3,2,1,0:T(8,128)(2,1)}, bf16[2,2,160,256]{3,2,1,0:T(8,128)(2,1)S(1)}, u32[]{:S(2)}) copy-start(bf16[2,2,160,256]{3,2,1,0:T(8,128)(2,1)S(1)} %collective-permute-done.5.refs_5_) | copy-start | bytes 983044 | tf_op jit(solution)/shard_map/cond
  40.5 9.3 %collective-permute-start.6 = (bf16[2,2,160,256]{3,2,1,0:T(8,128)(2,1)S(1)}, bf16[2,2,160,256]{3,2,1,0:T(8,128)(2,1)S(1)}, u32[]{:S(2)}, u32[]{:S(2)}) collective-permute-start(bf16[2,2,160,256]{3,2,1,0:T(8,128)(2,1)S(1)} %collective-permute-done.5.refs_5_), channel_id=1, source_target_pairs={{0,14},{1,15},{2,0},{3,1},{4,2},{5,3},{6,4},{7,5},{8,6},{9,7},{10,... | collective-permute-start | bytes 983048 | tf_op jit(solution)/shard_map/cond/branch_1_fun/ppermute | solution.py:26
  45.8 11.8 %copy-start.10 = (bf16[2,2,160,256]{3,2,1,0:T(8,128)(2,1)}, bf16[2,2,160,256]{3,2,1,0:T(8,128)(2,1)S(1)}, u32[]{:S(2)}) copy-start(bf16[2,2,160,256]{3,2,1,0:T(8,128)(2,1)S(1)} %collective-permute-done.2.refs_2_) | copy-start | bytes 983044 | tf_op jit(solution)/shard_map/cond
  45.8 10.4 %collective-permute-start.3 = (bf16[2,2,160,256]{3,2,1,0:T(8,128)(2,1)S(1)}, bf16[2,2,160,256]{3,2,1,0:T(8,128)(2,1)S(1)}, u32[]{:S(2)}, u32[]{:S(2)}) collective-permute-start(bf16[2,2,160,256]{3,2,1,0:T(8,128)(2,1)S(1)} %collective-permute-done.2.refs_2_), channel_id=1, source_target_pairs={{0,2},{1,3},{2,4},{3,5},{4,6},{5,7},{6,8},{7,9},{8,10},{9,11},{10,... | collective-permute-start | bytes 983048 | tf_op jit(solution)/shard_map/cond/branch_1_fun/ppermute | solution.py:26
  49.8 0.7 copy-start.5
  51.2 8.4 %collective-permute-start.8 = (bf16[1,2,160,256]{3,2,1,0:T(8,128)(2,1)}, bf16[1,2,160,256]{3,2,1,0:T(8,128)(2,1)S(1)}, u32[]{:S(2)}, u32[]{:S(2)}) collective-permute-start(bf16[1,2,160,256]{3,2,1,0:T(8,128)(2,1)} %slice.27), channel_id=1, source_target_pairs={{0,14},{1,15},{2,0},{3,1},{4,2},{5,3},{6,4},{7,5},{8,6},{9,7},{10,... | collective-permute-start | bytes 491528 | tf_op jit(solution)/shard_map/cond/branch_1_fun/ppermute | solution.py:26
  56.2 0.7 copy-start.6
  57.7 7.6 %collective-permute-start.7 = (bf16[1,2,160,256]{3,2,1,0:T(8,128)(2,1)}, bf16[1,2,160,256]{3,2,1,0:T(8,128)(2,1)}, u32[]{:S(2)}, u32[]{:S(2)}) collective-permute-start(bf16[1,2,160,256]{3,2,1,0:T(8,128)(2,1)} %slice.26), channel_id=1, source_target_pairs={{0,2},{1,3},{2,4},{3,5},{4,6},{5,7},{6,8},{7,9},{8,10},{9,11},{10,... | collective-permute-start | bytes 491528 | tf_op jit(solution)/shard_map/cond/branch_1_fun/ppermute | solution.py:26
  59.6 5.6 %copy-start.11 = (bf16[1,2,160,256]{3,2,1,0:T(8,128)(2,1)}, bf16[1,2,160,256]{3,2,1,0:T(8,128)(2,1)S(1)}, u32[]{:S(2)}) copy-start(bf16[1,2,160,256]{3,2,1,0:T(8,128)(2,1)S(1)} %collective-permute-done.8.refs_8_) | copy-start | bytes 491524 | tf_op jit(solution)/shard_map/cond
  149.2 19.9 %collective-permute-start.10 = (bf16[128,2560]{1,0:T(8,128)(2,1)}, bf16[128,2560]{1,0:T(8,128)(2,1)}, u32[]{:S(2)}, u32[]{:S(2)}) collective-permute-start(bf16[128,2560]{1,0:T(8,128)(2,1)} %get-tuple-element.70), channel_id=1, source_target_pairs={{0,496},{32,16},{64,48},{96,80},{128,112},{160,144},{192,176},{224... | collective-permute-start | bytes 1966088 | tf_op jit(solution)/shard_map/ppermute | solution.py:391
  150.5 17.1 %collective-permute-start.9 = (bf16[128,2560]{1,0:T(8,128)(2,1)}, bf16[128,2560]{1,0:T(8,128)(2,1)}, u32[]{:S(2)}, u32[]{:S(2)}) collective-permute-start(bf16[128,2560]{1,0:T(8,128)(2,1)} %get-tuple-element.70), channel_id=1, source_target_pairs={{16,0},{48,32},{80,64},{112,96},{144,128},{176,160},{208,192},{240... | collective-permute-start | bytes 1966088 | tf_op jit(solution)/shard_map/ppermute | solution.py:392
  163.0 4.6 %copy-start.2 = (bf16[2560,256]{1,0:T(8,128)(2,1)S(1)}, bf16[2560,256]{1,0:T(8,128)(2,1)}, u32[]{:S(2)}) copy-start(bf16[2560,256]{1,0:T(8,128)(2,1)} %get-tuple-element.71.second_ref) | copy-start | bytes 3932164
  171.8 3.8 %collective-permute-start.11 = (bf16[128,2560]{1,0:T(8,128)(2,1)S(1)}, bf16[128,2560]{1,0:T(8,128)(2,1)S(1)}, u32[]{:S(2)}, u32[]{:S(2)}) collective-permute-start(bf16[128,2560]{1,0:T(8,128)(2,1)S(1)} %get-tuple-element.77), channel_id=1, source_target_pairs={{16,0},{48,32},{80,64},{112,96},{144,128},{176,160},{208,192},{240... | collective-permute-start | bytes 1966088 | tf_op jit(solution)/shard_map/ppermute | solution.py:413
  173.2 15.8 %collective-permute-start.12 = (bf16[128,2560]{1,0:T(8,128)(2,1)S(1)}, bf16[128,2560]{1,0:T(8,128)(2,1)S(1)}, u32[]{:S(2)}, u32[]{:S(2)}) collective-permute-start(bf16[128,2560]{1,0:T(8,128)(2,1)S(1)} %get-tuple-element.79), channel_id=1, source_target_pairs={{0,496},{32,16},{64,48},{96,80},{128,112},{160,144},{192,176},{224... | collective-permute-start | bytes 1966088 | tf_op jit(solution)/shard_map/ppermute | solution.py:411
  191.4 3.0 %collective-permute-start.13 = (bf16[128,2560]{1,0:T(8,128)(2,1)S(1)}, bf16[128,2560]{1,0:T(8,128)(2,1)S(1)}, u32[]{:S(2)}, u32[]{:S(2)}) collective-permute-start(bf16[128,2560]{1,0:T(8,128)(2,1)S(1)} %get-tuple-element.81), channel_id=1, source_target_pairs={{16,0},{48,32},{80,64},{112,96},{144,128},{176,160},{208,192},{240... | collective-permute-start | bytes 1966088 | tf_op jit(solution)/shard_map/ppermute | solution.py:413
  192.8 15.8 %collective-permute-start.14 = (bf16[128,2560]{1,0:T(8,128)(2,1)S(1)}, bf16[128,2560]{1,0:T(8,128)(2,1)S(1)}, u32[]{:S(2)}, u32[]{:S(2)}) collective-permute-start(bf16[128,2560]{1,0:T(8,128)(2,1)S(1)} %get-tuple-element.83), channel_id=1, source_target_pairs={{0,496},{32,16},{64,48},{96,80},{128,112},{160,144},{192,176},{224... | collective-permute-start | bytes 1966088 | tf_op jit(solution)/shard_map/ppermute | solution.py:411
  211.9 67.8 %collective-permute-start.15 = (bf16[128,2560]{1,0:T(8,128)(2,1)}, bf16[128,2560]{1,0:T(8,128)(2,1)S(1)}, u32[]{:S(2)}, u32[]{:S(2)}) collective-permute-start(bf16[128,2560]{1,0:T(8,128)(2,1)} %get-tuple-element.87), channel_id=1, source_target_pairs={{16,0},{48,32},{80,64},{112,96},{144,128},{176,160},{208,192},{240... | collective-permute-start | bytes 1966088 | tf_op jit(solution)/shard_map/ppermute | solution.py:413
  213.2 67.2 %collective-permute-start.16 = (bf16[128,2560]{1,0:T(8,128)(2,1)}, bf16[128,2560]{1,0:T(8,128)(2,1)S(1)}, u32[]{:S(2)}, u32[]{:S(2)}) collective-permute-start(bf16[128,2560]{1,0:T(8,128)(2,1)} %get-tuple-element.88), channel_id=1, source_target_pairs={{0,496},{32,16},{64,48},{96,80},{128,112},{160,144},{192,176},{224... | collective-permute-start | bytes 1966088 | tf_op jit(solution)/shard_map/ppermute | solution.py:411
  279.6 0.7 copy-start.3

commit v7 on v6

--- a/solution.py
+++ b/solution.py
@@ -13,6 +13,7 @@
 LIMIT = pltpu.CompilerParams(vmem_limit_bytes=24 * 1024 * 1024)
 IN_VMEM = pl.BlockSpec(memory_space=pltpu.VMEM)
 ANYWHERE = pl.BlockSpec(memory_space=pl.ANY)
+COST = pl.CostEstimate(flops=2**32, bytes_accessed=2**23, transcendentals=0)
 SCALAR = pl.BlockSpec(memory_space=pltpu.SMEM)
 
 
@@ -72,8 +73,9 @@
         functools.partial(place_kernel, n_z),
         out_shape=[whole, whole],
         in_specs=[SCALAR] + [ANYWHERE] * len(pieces),
-        out_specs=[ANYWHERE] * 2,
+        out_specs=[IN_VMEM] * 2,
         scratch_shapes=[pltpu.SemaphoreType.DMA((2 * (n_z + 1),))],
+        compiler_params=LIMIT,
         name="place_maps",
     )(z.astype(jnp.int32)[None], *pieces)
 
@@ -116,32 +118,38 @@
     return inverse
 
 
-def first_kernel(x_ref, incoming_ref, map_ref, sent_ref, grad_latent_ref, active_ref, normed_ref):
-    rank = active_ref.shape[1]
+def first_kernel(x_ref, incoming_ref, map_ref, dep_ref, sent_ref, grad_latent_ref, normed_ref):
+    rank = grad_latent_ref.shape[1]
     inverse = normalise(x_ref, normed_ref)
     latent = jnp.dot(normed_ref[...], map_ref[:, :rank], preferred_element_type=F32)
     gate = jax.nn.sigmoid(latent)
-    active_ref[...] = (latent * gate).astype(BF16)
     slope = gate * (1.0 + latent * (1.0 - gate))
     relay(incoming_ref, x_ref, map_ref, latent, slope, inverse, sent_ref, grad_latent_ref)
 
 
-def first_tick(saved_inputs, incoming, maps):
-    ticks, _, rows, width = saved_inputs.shape
+def first_tick(part, saved_inputs, incoming, maps, dep):
+    _, _, rows, width = saved_inputs.shape
+    rows //= 2
     rank = maps.shape[1] // 2
-    wide = jax.ShapeDtypeStruct((rows, width), BF16)
-    narrow = jax.ShapeDtypeStruct((rows, rank), BF16)
     return pl.pallas_call(
         first_kernel,
         grid=(1,),
-        out_shape=[wide, narrow, narrow],
-        in_specs=[pl.BlockSpec((1, 1, rows, width), lambda i: (0, 0, 0, 0)), IN_VMEM, IN_VMEM],
-        out_specs=[IN_VMEM] * 3,
+        out_shape=[
+            jax.ShapeDtypeStruct((rows, width), BF16),
+            jax.ShapeDtypeStruct((rows, rank), BF16),
+        ],
+        in_specs=[
+            pl.BlockSpec((1, 1, rows, width), lambda i: (0, 0, part, 0)),
+            pl.BlockSpec((rows, width), lambda i: (part, 0)),
+            IN_VMEM,
+            ANYWHERE,
+        ],
+        out_specs=[IN_VMEM] * 2,
         scratch_shapes=[pltpu.VMEM((rows, width), BF16)],
         compiler_params=LIMIT,
-        cost_estimate=pl.CostEstimate(flops=6 * rows * width * rank, bytes_accessed=4 * 2 * rows * width, transcendentals=0),
+        cost_estimate=COST,
         name="first_tick",
-    )(saved_inputs, incoming, maps)
+    )(saved_inputs, incoming, maps, dep)
 
 
 def forward_kernel(level_ref, x_ref, first_ref, second_ref, dep_ref, normed_ref, active_ref, latent_ref, slope_ref, inverse_ref):
@@ -192,59 +200,49 @@
     )(levels, saved_inputs, first, second, dep)
 
 
-def tick_kernel(tick, flags_ref, incoming_ref, x_ref, first_ref, second_ref, latent_ref, slope_ref, inverse_ref, dep_ref, sent_ref, grad_latent_ref, x, second, sems):
-    level = flags_ref[1]
-    get_x = pltpu.make_async_copy(x_ref.at[pl.ds(tick, 1)], x, sems.at[0])
-    get_second = pltpu.make_async_copy(second_ref, second, sems.at[1])
-
-    @pl.when(flags_ref[0] == 1)
+def tick_kernel(tick, part, level_ref, incoming_ref, x_ref, first_ref, second_ref, latent_ref, slope_ref, inverse_ref, dep_ref, sent_ref, grad_latent_ref, x, second, sems):
+    level = level_ref[tick]
+    rows = x.shape[2]
+    get_x = pltpu.make_async_copy(
+        x_ref.at[pl.ds(tick, 1), :, pl.ds(part * rows, rows)], x, sems.at[0]
+    )
+    get_x.start()
+
+    @pl.when(level == 0)
     def _():
-        get_x.start()
-
-        @pl.when(level == 0)
+        get_second = pltpu.make_async_copy(second_ref, second, sems.at[1])
+        get_second.start()
+        get_second.wait()
+
+    get_x.wait()
+    for value, map_ref in ((1, first_ref), (0, second)):
+
+        @pl.when(level == value)
         def _():
-            get_second.start()
-            get_second.wait()
-
-        get_x.wait()
-        for value, map_ref in ((1, first_ref), (0, second)):
-
-            @pl.when(level == value)
-            def _():
-                relay(
-                    incoming_ref,
-                    x,
-                    map_ref,
-                    latent_ref[0],
-                    slope_ref[0],
-                    inverse_ref[0][:, :1],
-                    sent_ref,
-                    grad_latent_ref,
-                )
-
-
-def later_tick(tick, works, level, incoming, saved_inputs, first, second, latents, slopes, inverses, dep):
-    _, _, rows, width = saved_inputs.shape
+            relay(
+                incoming_ref,
+                x,
+                map_ref,
+                latent_ref[0],
+                slope_ref[0],
+                inverse_ref[0][:, :1],
+                sent_ref,
+                grad_latent_ref,
+            )
+
+
+def later_tick(tick, part, levels, incoming, saved_inputs, first, second, latents, slopes, inverses, dep):
+    rows, width = incoming.shape
     rank = first.shape[1] // 2
-    narrow = pl.BlockSpec((1, rows, rank), lambda i: (tick, 0, 0))
-    return pl.pallas_call(
-        functools.partial(tick_kernel, tick),
+    narrow = pl.BlockSpec((1, rows, rank), lambda i: (tick, part, 0))
+    return pl.pallas_call(
+        functools.partial(tick_kernel, tick, part),
         grid=(1,),
         out_shape=[
             jax.ShapeDtypeStruct((rows, width), BF16),
             jax.ShapeDtypeStruct((rows, rank), BF16),
         ],
-        in_specs=[
-            SCALAR,
-            IN_VMEM,
-            ANYWHERE,
-            IN_VMEM,
-            ANYWHERE,
-            narrow,
-            narrow,
-            narrow,
-            ANYWHERE,
-        ],
+        in_specs=[SCALAR, IN_VMEM, ANYWHERE, IN_VMEM, ANYWHERE, narrow, narrow, narrow, ANYWHERE],
         out_specs=[IN_VMEM] * 2,
         scratch_shapes=[
             pltpu.VMEM((1, 1, rows, width), BF16),
@@ -252,29 +250,9 @@
             pltpu.SemaphoreType.DMA((2,)),
         ],
         compiler_params=LIMIT,
-        cost_estimate=pl.CostEstimate(
-            flops=40 * rows * width * rank, bytes_accessed=40 * rows * width, transcendentals=0
-        ),
+        cost_estimate=COST,
         name="later_tick",
-    )(
-        jnp.stack([works.astype(jnp.int32), level.astype(jnp.int32)]),
-        incoming,
-        saved_inputs,
-        first,
-        second,
-        latents,
-        slopes,
-        inverses,
-        dep,
-    )
-
-
-def turned(block):
-    share, rank = block.shape
-    room = -(-share // 128) * 128
-    if room != share:
-        block = jnp.concatenate([block, jnp.zeros((room - share, rank), block.dtype)], axis=0)
-    return block.T[:, :share]
+    )(levels, incoming, saved_inputs, first, second, latents, slopes, inverses, dep)
 
 
 def beside_kernel(left_ref, right_ref, out_ref):
@@ -319,32 +297,27 @@
     )(moved)
 
 
-def finish_kernel(even_ref, total_ref, core_ref, over_ref, grad_ref, down_ref, up_ref, sem):
-    for value, source in ((1, core_ref), (0, over_ref)):
-
-        @pl.when(even_ref[0] == value)
-        def _():
-            pltpu.make_async_copy(source, grad_ref.at[0], sem).start()
-
-    rank = down_ref.shape[2]
+def finish_kernel(total_ref, low_ref, high_ref, grad_ref, down_ref, up_ref):
+    rows, rank = low_ref.shape[0], down_ref.shape[3]
+    grad_ref[0, :rows] = low_ref[...]
+    grad_ref[0, rows:] = high_ref[...]
     for i, out in enumerate((down_ref, up_ref)):
         for j, level in enumerate((1, 0)):
             at = (2 * i + j) * rank
-            out[level, 0] = turned(total_ref[:, at : at + rank])
-    pltpu.make_async_copy(core_ref, grad_ref.at[0], sem).wait()
-
-
-def finish(flag, total, core, over, share, rank):
-    made = jax.ShapeDtypeStruct((2, 1, rank, share), F32)
+            out[level, 0] = total_ref[:, at : at + rank]
+
+
+def finish(total, low, high, share, rank):
+    rows, width = low.shape
+    made = jax.ShapeDtypeStruct((2, 1, share, rank), F32)
     return pl.pallas_call(
         finish_kernel,
-        out_shape=[jax.ShapeDtypeStruct((1,) + core.shape, core.dtype), made, made],
-        in_specs=[SCALAR, IN_VMEM, ANYWHERE, ANYWHERE],
-        out_specs=[ANYWHERE, IN_VMEM, IN_VMEM],
-        scratch_shapes=[pltpu.SemaphoreType.DMA],
+        out_shape=[jax.ShapeDtypeStruct((1, 2 * rows, width), low.dtype), made, made],
+        in_specs=[IN_VMEM] * 3,
+        out_specs=[IN_VMEM] * 3,
         compiler_params=LIMIT,
         name="finish",
-    )(flag, total, core, over)
+    )(total, low, high)
 
 
 def on_device(saved_inputs, grad_in, adapter_down, adapter_up):
@@ -355,7 +328,6 @@
     ticks = saved_inputs.shape[0]
     rank, share = adapter_down.shape[2], adapter_down.shape[3]
     width = saved_inputs.shape[3]
-    even = position % 2 == 0
     two_layers = position + ticks - 1 >= n_sec
     levels = [1 - (position + tick) // n_sec for tick in range(ticks)]
 
@@ -377,27 +349,28 @@
         two_layers, gather_two, gather_one, adapter_down[:, 0], adapter_up[:, 0]
     )
 
-    sent, grad_latent, _ = first_tick(saved_inputs, grad_in[0], first)
+    down_one = [(s, (s - 1) % n_sec) for s in range(n_sec)]
+    grads = [grad_in[0]]
+    grad_latents = []
+    moving = []
+    dep = first
+    for part in range(2):
+        sent, dep = first_tick(part, saved_inputs, grad_in[0], first, dep)
+        grad_latents.append(dep)
+        moving.append(lax.ppermute(sent, "section", down_one))
     level_stack = jnp.stack(levels).astype(jnp.int32)
     normeds, actives, latents, slopes, inverses = forward_all(
-        level_stack, saved_inputs, first, second, grad_latent
-    )
-
-    inside = [(s, s - 1) for s in range(1, n_sec, 2)]
-    across = [(s, (s - 1) % n_sec) for s in range(0, n_sec, 2)]
-
-    grads = [grad_in[0]]
-    grad_latents = [grad_latent]
-    over = lax.ppermute(sent, "section", across)
-    core = lax.ppermute(sent, "section", inside)
+        level_stack, saved_inputs, first, second, dep
+    )
     for tick in range(1, ticks):
-
-        def layer(works, incoming, dep):
-            return later_tick(
+        grads += moving
+        arrived, moving = moving, []
+        for part in range(2):
+            sent, dep = later_tick(
                 tick,
-                works,
-                levels[tick],
-                incoming,
+                part,
+                level_stack,
+                arrived[part],
                 saved_inputs,
                 first,
                 second,
@@ -406,14 +379,8 @@
                 inverses,
                 dep,
             )
-
-        sent_even, latent_even = layer(even, core, grad_latent)
-        next_over = lax.ppermute(sent_even, "section", across)
-        sent_odd, latent_odd = layer(~even, over, latent_even)
-        next_core = lax.ppermute(sent_odd, "section", inside)
-        grads.append(jnp.where(even, core, over))
-        grad_latents.append(jnp.where(even, latent_even, latent_odd))
-        over, core = next_over, next_core
+            grad_latents.append(dep)
+            moving.append(lax.ppermute(sent, "section", down_one))
 
     normed_all = normeds.reshape(-1, width)
     grads_all = jnp.concatenate(grads, axis=0)
@@ -439,9 +406,9 @@
 
         return products(split(lats), split(acts))
 
-    total = lax.cond(two_layers, reduce_two, reduce_one, jnp.stack(grad_latents), actives)
-    flag = even.astype(jnp.int32)[None]
-    return tuple(finish(flag, total, core, over, share, rank))
+    total = lax.cond(two_layers, reduce_two, reduce_one, jnp.concatenate(grad_latents).reshape(actives.shape), actives)
+    grad_out, down_grad, up_grad = finish(total, *moving, share, rank)
+    return grad_out, jnp.swapaxes(down_grad, 2, 3), jnp.swapaxes(up_grad, 2, 3)
 
 
 def solution(mesh):

time: 285 us -> 206 us (0.72)
  Pallas kernels: 104 us -> 29.6 us
  waiting for transfers between devices: 44.5 us -> 27.9 us
  local copies, waits for them, and re-layouts: 6.16 us -> 14.4 us
  blocking collectives: 61.6 us -> 68.2 us
  other arithmetic: 3.98 us -> 0.51 us
    pallas_call x1, Pallas kernels: 80.7 us -> 4.27 us  [ring_gather(): pl.pallas_call(functools.partial(place_kernel, n_z), out_shape=[whole, wh...]
    ppermute x8, waiting for transfers between devices: 24 us -> 10.5 us  [on_device(): moving.append(lax.ppermute(sent, 'section', down_one))]
    all_to_all x1, blocking collectives: 61.6 us -> 68.2 us  [products(): lax.all_to_all(both.reshape(n_dp, share, -1), 'dp', 0, 0, tiled=True)]
    cond x16 -> x20, local copies, waits for them, and re-layouts: 1.48 us -> 7.76 us
    unnamed x8 -> x23, local copies, waits for them, and re-layouts: 0.72 us -> 4.12 us
    ppermute x8, starting transfers between devices: 21.5 us -> 24.5 us  [on_device(): moving.append(lax.ppermute(sent, 'section', down_one))]
    pallas_call x8 -> x9, Pallas kernels: 18.7 us -> 20.6 us  [the longest x6 13.8 us: later_tick(): pl.pallas_call(functools.partial(tick_kernel, tick, part), grid=(1,), out...]
  transfers between devices with their start and end apart: 17 -> 17, of which waited for: 8 -> 9; matrix products, arithmetic and copies ran while one was open for 2% -> 3% of each run, Pallas kernels for 4% -> 10%
where the time goes in v7:
time: 206 us; the launch traced here: 205 us
  blocking collectives  68.2 us (33%)
  starting transfers between devices  61 us (30%)
  Pallas kernels  29.6 us (14%)
  waiting for transfers between devices  27.9 us (14%)
  local copies, waits for them, and re-layouts  14.4 us (7%)
  matrix products  2.27 us (1%)
    all_to_all x1, blocking collectives, products(): lax.all_to_all(both.reshape(n_dp, share, -1), 'dp', 0, 0, tiled=True)  68.2 us
    ppermute x8, starting transfers between devices, shifted(): return lax.ppermute(value, 'dp', dp_pairs(n_z, step, 0))  32 us
    ppermute x8, starting transfers between devices, on_device(): moving.append(lax.ppermute(sent, 'section', down_one))  24.5 us
    pallas_call x6, Pallas kernels, later_tick(): pl.pallas_call(functools.partial(tick_kernel, tick, part), grid=(1,), out...  13.8 us
    ppermute x8, waiting for transfers between devices, shifted(): return lax.ppermute(value, 'dp', dp_pairs(n_z, step, 0))  11 us
    ppermute x8, waiting for transfers between devices, on_device(): moving.append(lax.ppermute(sent, 'section', down_one))  10.5 us
    cond x20, local copies, waits for them, and re-layouts  7.76 us
    ppermute x1, waiting for transfers between devices, swapped(): return lax.ppermute(value, 'dp', dp_pairs(n_z, 0, 1))  6.41 us
  transfers between devices with their start and end apart: 17, of which 9 were waited for; matrix products, arithmetic and copies ran while one was open for 3% of the time, Pallas kernels for 10%

profile of v7, /device:TPU:63, one launch (start us, length us, event | category | flops | bytes accessed | tf_op | source)
XLA Modules:
  0.0 205.3 jit_solution(6263867642842388246)
XLA Ops:
  0.6 68.6 %conditional.2 = (bf16[2560,256]{1,0:T(8,128)(2,1)}, bf16[2560,256]{1,0:T(8,128)(2,1)}) conditional(s32[]{:T(128)} %convert_element_type.20, (bf16[2,128,160]{1,2,0:T(8,128)(2,1)}, bf16[2,128,160]{1,2,0:T(8,128)(2,1)}) %tuple.45, (bf16[2,128,160]{1,2,0:T(8,128)(2,1)}, bf16[2,128,160]{1,2,0:T(8,128)(2,1)}) %tuple.46), branch_computations={%region_0.1_spmd, %region_1.2_spmd} | conditional | flops 819222 | bytes 25887592 | solution.py:348
  0.7 1.0 slice_bitcast_fusion.4
  1.7 4.4 %collective-permute-start = (bf16[2,160,256]{2,1,0:T(8,128)(2,1)S(1)}, bf16[2,160,256]{2,1,0:T(8,128)(2,1)S(1)}, u32[]{:S(2)}, u32[]{:S(2)}) collective-permute-start(bf16[2,160,256]{2,1,0:T(8,128)(2,1)S(1)} %pad_maximum_fusion.2), channel_id=1, source_target_pairs={{0,1},{1,0},{2,3},{3,2},{4,5},{5,4},{6,7},{7,6},{8,9},{9,8},{10,11... | collective-permute-start | bytes 491528 | tf_op jit(solution)/shard_map/cond/branch_1_fun/ppermute | solution.py:31
  6.2 6.4 %collective-permute-done = bf16[2,160,256]{2,1,0:T(8,128)(2,1)S(1)} collective-permute-done((bf16[2,160,256]{2,1,0:T(8,128)(2,1)S(1)}, bf16[2,160,256]{2,1,0:T(8,128)(2,1)S(1)}, u32[]{:S(2)}, u32[]{:S(2)}) %collective-permute-start) | collective-permute-done | bytes 163872 | tf_op jit(solution)/shard_map/cond/branch_1_fun/ppermute | solution.py:31
  12.7 4.0 %collective-permute-start.1 = (bf16[2,2,160,256]{3,2,1,0:T(8,128)(2,1)S(1)}, bf16[2,2,160,256]{3,2,1,0:T(8,128)(2,1)S(1)}, u32[]{:S(2)}, u32[]{:S(2)}) collective-permute-start(bf16[2,2,160,256]{3,2,1,0:T(8,128)(2,1)S(1)} %pad_maximum_fusion.1.refs_0_), channel_id=1, source_target_pairs={{0,2},{1,3},{2,4},{3,5},{4,6},{5,7},{6,8},{7,9},{8,10},{9,11},{10,... | collective-permute-start | bytes 983048 | tf_op jit(solution)/shard_map/cond/branch_1_fun/ppermute | solution.py:27
  16.7 8.6 %collective-permute-start.4 = (bf16[2,2,160,256]{3,2,1,0:T(8,128)(2,1)S(1)}, bf16[2,2,160,256]{3,2,1,0:T(8,128)(2,1)S(1)}, u32[]{:S(2)}, u32[]{:S(2)}) collective-permute-start(bf16[2,2,160,256]{3,2,1,0:T(8,128)(2,1)S(1)} %pad_maximum_fusion.1.refs_0_), channel_id=1, source_target_pairs={{0,14},{1,15},{2,0},{3,1},{4,2},{5,3},{6,4},{7,5},{8,6},{9,7},{10,... | collective-permute-start | bytes 983048 | tf_op jit(solution)/shard_map/cond/branch_1_fun/ppermute | solution.py:27
  25.3 4.5 %collective-permute-done.1.refs_1_ = bf16[2,2,160,256]{3,2,1,0:T(8,128)(2,1)S(1)} collective-permute-done((bf16[2,2,160,256]{3,2,1,0:T(8,128)(2,1)S(1)}, bf16[2,2,160,256]{3,2,1,0:T(8,128)(2,1)S(1)}, u32[]{:S(2)}, u32[]{:S(2)}) %collective-permute-start.1) | collective-permute-done | bytes 327712 | tf_op jit(solution)/shard_map/cond/branch_1_fun/ppermute | solution.py:27
  29.8 1.9 collective-permute-start.2
  32.5 4.6 %collective-permute-start.5 = (bf16[2,2,160,256]{3,2,1,0:T(8,128)(2,1)S(1)}, bf16[2,2,160,256]{3,2,1,0:T(8,128)(2,1)S(1)}, u32[]{:S(2)}, u32[]{:S(2)}) collective-permute-start(bf16[2,2,160,256]{3,2,1,0:T(8,128)(2,1)S(1)} %collective-permute-done.4.refs_4_), channel_id=1, source_target_pairs={{0,14},{1,15},{2,0},{3,1},{4,2},{5,3},{6,4},{7,5},{8,6},{9,7},{10,... | collective-permute-start | bytes 983048 | tf_op jit(solution)/shard_map/cond/branch_1_fun/ppermute | solution.py:27
  37.8 2.1 %collective-permute-done.2.refs_2_ = bf16[2,2,160,256]{3,2,1,0:T(8,128)(2,1)S(1)} collective-permute-done((bf16[2,2,160,256]{3,2,1,0:T(8,128)(2,1)S(1)}, bf16[2,2,160,256]{3,2,1,0:T(8,128)(2,1)S(1)}, u32[]{:S(2)}, u32[]{:S(2)}) %collective-permute-start.2) | collective-permute-done | bytes 327712 | tf_op jit(solution)/shard_map/cond/branch_1_fun/ppermute | solution.py:27
  39.9 1.9 collective-permute-start.3
  42.6 4.6 %collective-permute-start.6 = (bf16[2,2,160,256]{3,2,1,0:T(8,128)(2,1)S(1)}, bf16[2,2,160,256]{3,2,1,0:T(8,128)(2,1)S(1)}, u32[]{:S(2)}, u32[]{:S(2)}) collective-permute-start(bf16[2,2,160,256]{3,2,1,0:T(8,128)(2,1)S(1)} %collective-permute-done.5.refs_5_), channel_id=1, source_target_pairs={{0,14},{1,15},{2,0},{3,1},{4,2},{5,3},{6,4},{7,5},{8,6},{9,7},{10,... | collective-permute-start | bytes 983048 | tf_op jit(solution)/shard_map/cond/branch_1_fun/ppermute | solution.py:27
  47.1 1.8 collective-permute-done.3.refs_3_
  49.6 1.9 collective-permute-start.7
  53.0 4.6 %collective-permute-start.8 = (bf16[1,2,160,256]{3,2,1,0:T(8,128)(2,1)}, bf16[1,2,160,256]{3,2,1,0:T(8,128)(2,1)}, u32[]{:S(2)}, u32[]{:S(2)}) collective-permute-start(bf16[1,2,160,256]{3,2,1,0:T(8,128)(2,1)} %slice.27), channel_id=1, source_target_pairs={{0,14},{1,15},{2,0},{3,1},{4,2},{5,3},{6,4},{7,5},{8,6},{9,7},{10,... | collective-permute-start | bytes 491528 | tf_op jit(solution)/shard_map/cond/branch_1_fun/ppermute | solution.py:27
  57.6 2.5 %collective-permute-done.8.refs_8_ = bf16[1,2,160,256]{3,2,1,0:T(8,128)(2,1)} collective-permute-done((bf16[1,2,160,256]{3,2,1,0:T(8,128)(2,1)}, bf16[1,2,160,256]{3,2,1,0:T(8,128)(2,1)}, u32[]{:S(2)}, u32[]{:S(2)}) %collective-permute-start.8) | collective-permute-done | bytes 163872 | tf_op jit(solution)/shard_map/cond/branch_1_fun/ppermute | solution.py:27
  60.1 1.0 copy-done.2
  61.1 1.0 copy-done.6
  62.1 1.0 copy-done.8
  63.1 1.0 copy-done.10
  65.0 4.3 %place_maps.1 = (bf16[16,160,256]{2,1,0:T(8,128)(2,1)}, bf16[16,160,256]{2,1,0:T(8,128)(2,1)}) custom-call(s32[1]{0:T(128)} %bitcast.5.place_ref, bf16[2,2,160,256]{3,2,1,0:T(8,128)(2,1)S(1)} %pad_maximum_fusion.1.refs_0_, bf16[2,2,160,256]{3,2,1,0:T(8,128)(2,1)S(1)} %copy-done.6, bf16[2,2,160,256]{3,2,1,0:T(8,128)(2,1)S(1)} %copy-done.10, ...), custom_call_target="tpu_custom_call" | custom-call | tf_op jit(solution)/shard_map/cond/branch_1_fun/place_maps/pallas_call | solution.py:72
  69.3 1.1 copy-done.3
  70.4 2.8 %first_tick.2 = (bf16[64,2560]{1,0:T(8,128)(2,1)}, bf16[64,128]{1,0:T(8,128)(2,1)S(1)}) custom-call(bf16[4,1,128,2560]{3,2,1,0:T(8,128)(2,1)S(1)} %copy-done, bf16[128,2560]{1,0:T(8,128)(2,1)S(1)} %bitcast.68, bf16[2560,256]{1,0:T(8,128)(2,1)} %get-tuple-element.74.map_ref.dep_ref.first_ref, bf16[2560,256]{1,0:T(8,128)(2,1)} %get-tuple-element.74.map_ref.dep_ref.first_ref), custom_call_target="tpu_custom_call" | custom-call | flops 4294967296 | bytes 8388608 | tf_op jit(solution)/shard_map/first_tick/pallas_call | solution.py:134
  73.2 7.3 %collective-permute-start.9 = (bf16[64,2560]{1,0:T(8,128)(2,1)}, bf16[64,2560]{1,0:T(8,128)(2,1)}, u32[]{:S(2)}, u32[]{:S(2)}) collective-permute-start(bf16[64,2560]{1,0:T(8,128)(2,1)} %get-tuple-element.79), channel_id=1, source_target_pairs={{0,496},{16,0},{32,16},{48,32},{64,48},{80,64},{96,80},{112,96},{1... | collective-permute-start | bytes 983048 | tf_op jit(solution)/shard_map/ppermute | solution.py:360
  80.5 2.9 %first_tick.3 = (bf16[64,2560]{1,0:T(8,128)(2,1)}, bf16[64,128]{1,0:T(8,128)(2,1)S(1)}) custom-call(bf16[4,1,128,2560]{3,2,1,0:T(8,128)(2,1)S(1)} %copy-done, bf16[128,2560]{1,0:T(8,128)(2,1)S(1)} %bitcast.69, bf16[2560,256]{1,0:T(8,128)(2,1)} %get-tuple-element.74.map_ref.dep_ref.first_ref, bf16[64,128]{1,0:T(8,128)(2,1)S(1)} %get-tuple-element.76.dep_ref), custom_call_target="tpu_custom_call" | custom-call | flops 4294967296 | bytes 8388608 | tf_op jit(solution)/shard_map/first_tick/pallas_call | solution.py:134
  83.4 5.7 %collective-permute-start.10 = (bf16[64,2560]{1,0:T(8,128)(2,1)}, bf16[64,2560]{1,0:T(8,128)(2,1)}, u32[]{:S(2)}, u32[]{:S(2)}) collective-permute-start(bf16[64,2560]{1,0:T(8,128)(2,1)} %get-tuple-element.84), channel_id=1, source_target_pairs={{0,496},{16,0},{32,16},{48,32},{64,48},{80,64},{96,80},{112,96},{1... | collective-permute-start | bytes 983048 | tf_op jit(solution)/shard_map/ppermute | solution.py:360
  90.1 4.2 %forward_all.1 = (bf16[4,128,2560]{2,1,0:T(8,128)(2,1)S(1)}, bf16[4,128,128]{2,1,0:T(8,128)(2,1)S(1)}, f32[4,128,128]{2,1,0:T(8,128)S(1)}, f32[4,128,128]{2,1,0:T(8,128)S(1)}, f32[4,128,128]{2,1,0:T(8,128)S(1)}) custom-call(s32[4]{0:T(128)S(1)} %pad_add_fusion.level_ref, bf16[4,1,128,2560]{3,2,1,0:T(8,128)(2,1)S(1)} %copy-done, ...), custom_call_target="tpu_custom_call" | custom-call | flops 335544320 | bytes 5242880 | tf_op jit(solution)/shard_map/forward_all/pallas_call | solution.py:185
  94.4 2.2 %later_tick.6 = (bf16[64,2560]{1,0:T(8,128)(2,1)S(1)}, bf16[64,128]{1,0:T(8,128)(2,1)S(1)}) custom-call(s32[4]{0:T(128)S(1)} %pad_add_fusion.level_ref, bf16[64,2560]{1,0:T(8,128)(2,1)} %collective-permute-done.9.incoming_ref, bf16[4,1,128,2560]{3,2,1,0:T(8,128)(2,1)S(1)} %copy-done, bf16[2560,256]{1,0:T(8,128)(2,1)} %get-tuple-element.74.map_ref.dep_ref.first_ref, ...), custom_call_target="tpu_custom_call" | custom-call | flops 4294967296 | bytes 8388608 | tf_op jit(solution)/shard_map/later_tick/pallas_call | solution.py:238
  96.6 1.9 collective-permute-start.11
  98.6 2.4 %later_tick.7 = (bf16[64,2560]{1,0:T(8,128)(2,1)S(1)}, bf16[64,128]{1,0:T(8,128)(2,1)S(1)}) custom-call(s32[4]{0:T(128)S(1)} %pad_add_fusion.level_ref, bf16[64,2560]{1,0:T(8,128)(2,1)} %collective-permute-done.10.incoming_ref, bf16[4,1,128,2560]{3,2,1,0:T(8,128)(2,1)S(1)} %copy-done, bf16[2560,256]{1,0:T(8,128)(2,1)} %get-tuple-element.74.map_ref.dep_ref.first_ref, ...), custom_call_target="tpu_custom_call" | custom-call | flops 4294967296 | bytes 8388608 | tf_op jit(solution)/shard_map/later_tick/pallas_call | solution.py:238
  101.0 1.9 collective-permute-start.12
  102.9 1.0 constant_dynamic-update-slice_fusion.13
  103.9 1.0 constant_dynamic-update-slice_fusion.12
  104.9 4.0 %collective-permute-done.11.incoming_ref = bf16[64,2560]{1,0:T(8,128)(2,1)S(1)} collective-permute-done((bf16[64,2560]{1,0:T(8,128)(2,1)S(1)}, bf16[64,2560]{1,0:T(8,128)(2,1)S(1)}, u32[]{:S(2)}, u32[]{:S(2)}) %collective-permute-start.11) | collective-permute-done | bytes 327712 | tf_op jit(solution)/shard_map/ppermute | solution.py:383
  108.9 2.1 %later_tick.8 = (bf16[64,2560]{1,0:T(8,128)(2,1)S(1)}, bf16[64,128]{1,0:T(8,128)(2,1)S(1)}) custom-call(s32[4]{0:T(128)S(1)} %pad_add_fusion.level_ref, bf16[64,2560]{1,0:T(8,128)(2,1)S(1)} %collective-permute-done.11.incoming_ref, bf16[4,1,128,2560]{3,2,1,0:T(8,128)(2,1)S(1)} %copy-done, bf16[2560,256]{1,0:T(8,128)(2,1)} %get-tuple-element.74.map_ref.dep_ref.first_ref, ...), custom_call_target="tpu_custom_call" | custom-call | flops 4294967296 | bytes 8388608 | tf_op jit(solution)/shard_map/later_tick/pallas_call | solution.py:238
  111.1 1.9 collective-permute-start.13
  113.3 2.1 %later_tick.9 = (bf16[64,2560]{1,0:T(8,128)(2,1)S(1)}, bf16[64,128]{1,0:T(8,128)(2,1)S(1)}) custom-call(s32[4]{0:T(128)S(1)} %pad_add_fusion.level_ref, bf16[64,2560]{1,0:T(8,128)(2,1)S(1)} %collective-permute-done.12.incoming_ref, bf16[4,1,128,2560]{3,2,1,0:T(8,128)(2,1)S(1)} %copy-done, bf16[2560,256]{1,0:T(8,128)(2,1)} %get-tuple-element.74.map_ref.dep_ref.first_ref, ...), custom_call_target="tpu_custom_call" | custom-call | flops 4294967296 | bytes 8388608 | tf_op jit(solution)/shard_map/later_tick/pallas_call | solution.py:238
  115.4 1.9 collective-permute-start.14
  117.4 6.0 %collective-permute-done.13.incoming_ref = bf16[64,2560]{1,0:T(8,128)(2,1)S(1)} collective-permute-done((bf16[64,2560]{1,0:T(8,128)(2,1)S(1)}, bf16[64,2560]{1,0:T(8,128)(2,1)S(1)}, u32[]{:S(2)}, u32[]{:S(2)}) %collective-permute-start.13) | collective-permute-done | bytes 327712 | tf_op jit(solution)/shard_map/ppermute | solution.py:383
  123.4 2.1 %later_tick.10 = (bf16[64,2560]{1,0:T(8,128)(2,1)S(1)}, bf16[64,128]{1,0:T(8,128)(2,1)S(1)}) custom-call(s32[4]{0:T(128)S(1)} %pad_add_fusion.level_ref, bf16[64,2560]{1,0:T(8,128)(2,1)S(1)} %collective-permute-done.13.incoming_ref, bf16[4,1,128,2560]{3,2,1,0:T(8,128)(2,1)S(1)} %copy-done, bf16[2560,256]{1,0:T(8,128)(2,1)} %get-tuple-element.74.map_ref.dep_ref.first_ref, ...), custom_call_target="tpu_custom_call" | custom-call | flops 4294967296 | bytes 8388608 | tf_op jit(solution)/shard_map/later_tick/pallas_call | solution.py:238
  125.5 1.9 collective-permute-start.15
  127.7 2.8 %later_tick.11 = (bf16[64,2560]{1,0:T(8,128)(2,1)}, bf16[64,128]{1,0:T(8,128)(2,1)S(1)}) custom-call(s32[4]{0:T(128)S(1)} %pad_add_fusion.level_ref, bf16[64,2560]{1,0:T(8,128)(2,1)S(1)} %collective-permute-done.14.incoming_ref, bf16[4,1,128,2560]{3,2,1,0:T(8,128)(2,1)S(1)} %copy-done, bf16[2560,256]{1,0:T(8,128)(2,1)} %get-tuple-element.74.map_ref.dep_ref.first_ref, ...), custom_call_target="tpu_custom_call" | custom-call | flops 4294967296 | bytes 8388608 | tf_op jit(solution)/shard_map/later_tick/pallas_call | solution.py:238
  130.6 1.9 collective-permute-start.16
  132.6 71.7 %conditional.3 = (f32[160,512]{1,0:T(8,128)S(1)}) conditional(s32[]{:T(128)} %convert_element_type.20, (bf16[512,2560]{1,0:T(8,128)(2,1)S(1)}, bf16[512,128]{1,0:T(8,128)(2,1)S(1)}, bf16[4,128,128]{2,1,0:T(8,128)(2,1)S(1)}, bf16[512,2560]{1,0:T(8,128)(2,1)S(1)}) %tuple.41, (s32[4]{0:T(128)S(1)}, bf16[512,128]{1,0:T(8,128)(2,1)S(1)}, ...), branch_computations={%region_2.3_spmd, %region_3.4_spmd} | conditional | flops 1344798720 | bytes 14944304 | solution.py:409
  133.0 1.1 fusion.1.right_ref
  134.3 1.1 fusion.left_ref
  135.7 68.2 %all_to_all.13.moved_ref = bf16[16,160,512]{2,1,0:T(8,128)(2,1)S(1)} all-to-all(bf16[16,160,512]{2,1,0:T(8,128)(2,1)S(1)} %bitcast.66), channel_id=1, replica_groups=mesh['section'=32,'dp'=16] {'dp'}, dimensions={0} | all-to-all | bytes 5242880 | tf_op jit(solution)/shard_map/cond/branch_1_fun/all_to_all | solution.py:393
  204.3 1.0 finish.1
  (63 shorter events, 8.0 us)
Async XLA Ops:
  0.6 68.6 %copy-start = (bf16[4,1,128,2560]{3,2,1,0:T(8,128)(2,1)S(1)}, bf16[4,1,128,2560]{3,2,1,0:T(8,128)(2,1)}, u32[]{:S(2)}) copy-start(bf16[4,1,128,2560]{3,2,1,0:T(8,128)(2,1)} %x_ref.17) | copy-start | bytes 7864324
  1.7 10.9 %collective-permute-start = (bf16[2,160,256]{2,1,0:T(8,128)(2,1)S(1)}, bf16[2,160,256]{2,1,0:T(8,128)(2,1)S(1)}, u32[]{:S(2)}, u32[]{:S(2)}) collective-permute-start(bf16[2,160,256]{2,1,0:T(8,128)(2,1)S(1)} %pad_maximum_fusion.2), channel_id=1, source_target_pairs={{0,1},{1,0},{2,3},{3,2},{4,5},{5,4},{6,7},{7,6},{8,9},{9,8},{10,11... | collective-permute-start | bytes 491528 | tf_op jit(solution)/shard_map/cond/branch_1_fun/ppermute | solution.py:31
  12.7 17.1 %collective-permute-start.1 = (bf16[2,2,160,256]{3,2,1,0:T(8,128)(2,1)S(1)}, bf16[2,2,160,256]{3,2,1,0:T(8,128)(2,1)S(1)}, u32[]{:S(2)}, u32[]{:S(2)}) collective-permute-start(bf16[2,2,160,256]{3,2,1,0:T(8,128)(2,1)S(1)} %pad_maximum_fusion.1.refs_0_), channel_id=1, source_target_pairs={{0,2},{1,3},{2,4},{3,5},{4,6},{5,7},{6,8},{7,9},{8,10},{9,11},{10,... | collective-permute-start | bytes 983048 | tf_op jit(solution)/shard_map/cond/branch_1_fun/ppermute | solution.py:27
  16.7 15.8 %collective-permute-start.4 = (bf16[2,2,160,256]{3,2,1,0:T(8,128)(2,1)S(1)}, bf16[2,2,160,256]{3,2,1,0:T(8,128)(2,1)S(1)}, u32[]{:S(2)}, u32[]{:S(2)}) collective-permute-start(bf16[2,2,160,256]{3,2,1,0:T(8,128)(2,1)S(1)} %pad_maximum_fusion.1.refs_0_), channel_id=1, source_target_pairs={{0,14},{1,15},{2,0},{3,1},{4,2},{5,3},{6,4},{7,5},{8,6},{9,7},{10,... | collective-permute-start | bytes 983048 | tf_op jit(solution)/shard_map/cond/branch_1_fun/ppermute | solution.py:27
  29.8 10.1 %collective-permute-start.2 = (bf16[2,2,160,256]{3,2,1,0:T(8,128)(2,1)S(1)}, bf16[2,2,160,256]{3,2,1,0:T(8,128)(2,1)S(1)}, u32[]{:S(2)}, u32[]{:S(2)}) collective-permute-start(bf16[2,2,160,256]{3,2,1,0:T(8,128)(2,1)S(1)} %collective-permute-done.1.refs_1_), channel_id=1, source_target_pairs={{0,2},{1,3},{2,4},{3,5},{4,6},{5,7},{6,8},{7,9},{8,10},{9,11},{10,... | collective-permute-start | bytes 983048 | tf_op jit(solution)/shard_map/cond/branch_1_fun/ppermute | solution.py:27
  31.7 0.7 copy-start.5
  32.5 10.1 %collective-permute-start.5 = (bf16[2,2,160,256]{3,2,1,0:T(8,128)(2,1)S(1)}, bf16[2,2,160,256]{3,2,1,0:T(8,128)(2,1)S(1)}, u32[]{:S(2)}, u32[]{:S(2)}) collective-permute-start(bf16[2,2,160,256]{3,2,1,0:T(8,128)(2,1)S(1)} %collective-permute-done.4.refs_4_), channel_id=1, source_target_pairs={{0,14},{1,15},{2,0},{3,1},{4,2},{5,3},{6,4},{7,5},{8,6},{9,7},{10,... | collective-permute-start | bytes 983048 | tf_op jit(solution)/shard_map/cond/branch_1_fun/ppermute | solution.py:27
  37.0 0.7 copy-start.7
  39.9 9.0 %collective-permute-start.3 = (bf16[2,2,160,256]{3,2,1,0:T(8,128)(2,1)S(1)}, bf16[2,2,160,256]{3,2,1,0:T(8,128)(2,1)S(1)}, u32[]{:S(2)}, u32[]{:S(2)}) collective-permute-start(bf16[2,2,160,256]{3,2,1,0:T(8,128)(2,1)S(1)} %collective-permute-done.2.refs_2_), channel_id=1, source_target_pairs={{0,2},{1,3},{2,4},{3,5},{4,6},{5,7},{6,8},{7,9},{8,10},{9,11},{10,... | collective-permute-start | bytes 983048 | tf_op jit(solution)/shard_map/cond/branch_1_fun/ppermute | solution.py:27
  41.8 0.7 copy-start.9
  42.6 9.7 %copy-start.11 = (bf16[2,2,160,256]{3,2,1,0:T(8,128)(2,1)}, bf16[2,2,160,256]{3,2,1,0:T(8,128)(2,1)S(1)}, u32[]{:S(2)}) copy-start(bf16[2,2,160,256]{3,2,1,0:T(8,128)(2,1)S(1)} %collective-permute-done.5.refs_5_) | copy-start | bytes 983044 | tf_op jit(solution)/shard_map/cond
  42.6 9.0 %collective-permute-start.6 = (bf16[2,2,160,256]{3,2,1,0:T(8,128)(2,1)S(1)}, bf16[2,2,160,256]{3,2,1,0:T(8,128)(2,1)S(1)}, u32[]{:S(2)}, u32[]{:S(2)}) collective-permute-start(bf16[2,2,160,256]{3,2,1,0:T(8,128)(2,1)S(1)} %collective-permute-done.5.refs_5_), channel_id=1, source_target_pairs={{0,14},{1,15},{2,0},{3,1},{4,2},{5,3},{6,4},{7,5},{8,6},{9,7},{10,... | collective-permute-start | bytes 983048 | tf_op jit(solution)/shard_map/cond/branch_1_fun/ppermute | solution.py:27
  49.6 8.0 %collective-permute-start.7 = (bf16[1,2,160,256]{3,2,1,0:T(8,128)(2,1)}, bf16[1,2,160,256]{3,2,1,0:T(8,128)(2,1)S(1)}, u32[]{:S(2)}, u32[]{:S(2)}) collective-permute-start(bf16[1,2,160,256]{3,2,1,0:T(8,128)(2,1)} %slice.26), channel_id=1, source_target_pairs={{0,2},{1,3},{2,4},{3,5},{4,6},{5,7},{6,8},{7,9},{8,10},{9,11},{10,... | collective-permute-start | bytes 491528 | tf_op jit(solution)/shard_map/cond/branch_1_fun/ppermute | solution.py:27
  52.2 0.7 copy-start.1
  53.0 7.2 %collective-permute-start.8 = (bf16[1,2,160,256]{3,2,1,0:T(8,128)(2,1)}, bf16[1,2,160,256]{3,2,1,0:T(8,128)(2,1)}, u32[]{:S(2)}, u32[]{:S(2)}) collective-permute-start(bf16[1,2,160,256]{3,2,1,0:T(8,128)(2,1)} %slice.27), channel_id=1, source_target_pairs={{0,14},{1,15},{2,0},{3,1},{4,2},{5,3},{6,4},{7,5},{8,6},{9,7},{10,... | collective-permute-start | bytes 491528 | tf_op jit(solution)/shard_map/cond/branch_1_fun/ppermute | solution.py:27
  60.1 1.0 copy-start.2
  61.1 1.0 copy-start.6
  62.1 1.0 copy-start.8
  63.1 1.0 copy-start.10
  64.0 1.0 copy-start.12
  69.3 1.1 copy-start.3
  73.2 21.2 %collective-permute-start.9 = (bf16[64,2560]{1,0:T(8,128)(2,1)}, bf16[64,2560]{1,0:T(8,128)(2,1)}, u32[]{:S(2)}, u32[]{:S(2)}) collective-permute-start(bf16[64,2560]{1,0:T(8,128)(2,1)} %get-tuple-element.79), channel_id=1, source_target_pairs={{0,496},{16,0},{32,16},{48,32},{64,48},{80,64},{96,80},{112,96},{1... | collective-permute-start | bytes 983048 | tf_op jit(solution)/shard_map/ppermute | solution.py:360
  80.5 8.6 %copy-start.4 = (bf16[1,128,2560]{2,1,0:T(8,128)(2,1)S(1)}, bf16[1,128,2560]{2,1,0:T(8,128)(2,1)}, u32[]{:S(2)}) copy-start(bf16[1,128,2560]{2,1,0:T(8,128)(2,1)} %param.9) | copy-start | bytes 1966084
  83.4 15.1 %collective-permute-start.10 = (bf16[64,2560]{1,0:T(8,128)(2,1)}, bf16[64,2560]{1,0:T(8,128)(2,1)}, u32[]{:S(2)}, u32[]{:S(2)}) collective-permute-start(bf16[64,2560]{1,0:T(8,128)(2,1)} %get-tuple-element.84), channel_id=1, source_target_pairs={{0,496},{16,0},{32,16},{48,32},{64,48},{80,64},{96,80},{112,96},{1... | collective-permute-start | bytes 983048 | tf_op jit(solution)/shard_map/ppermute | solution.py:360
  90.1 4.3 %copy-start.14 = (bf16[2560,256]{1,0:T(8,128)(2,1)S(1)}, bf16[2560,256]{1,0:T(8,128)(2,1)}, u32[]{:S(2)}) copy-start(bf16[2560,256]{1,0:T(8,128)(2,1)} %get-tuple-element.75.second_ref) | copy-start | bytes 3932164
  96.6 12.3 %collective-permute-start.11 = (bf16[64,2560]{1,0:T(8,128)(2,1)S(1)}, bf16[64,2560]{1,0:T(8,128)(2,1)S(1)}, u32[]{:S(2)}, u32[]{:S(2)}) collective-permute-start(bf16[64,2560]{1,0:T(8,128)(2,1)S(1)} %get-tuple-element.86), channel_id=1, source_target_pairs={{0,496},{16,0},{32,16},{48,32},{64,48},{80,64},{96,80},{112,96},{1... | collective-permute-start | bytes 983048 | tf_op jit(solution)/shard_map/ppermute | solution.py:383
  98.6 4.3 %copy-start.13 = (bf16[512,2560]{1,0:T(8,128)(2,1)S(1)}, bf16[512,2560]{1,0:T(8,128)(2,1)}, u32[]{:S(2)}) copy-start(bf16[512,2560]{1,0:T(8,128)(2,1)} %constant_dynamic-update-slice_fusion.14) | copy-start | bytes 7864324
  101.0 12.3 %collective-permute-start.12 = (bf16[64,2560]{1,0:T(8,128)(2,1)S(1)}, bf16[64,2560]{1,0:T(8,128)(2,1)S(1)}, u32[]{:S(2)}, u32[]{:S(2)}) collective-permute-start(bf16[64,2560]{1,0:T(8,128)(2,1)S(1)} %get-tuple-element.88), channel_id=1, source_target_pairs={{0,496},{16,0},{32,16},{48,32},{64,48},{80,64},{96,80},{112,96},{1... | collective-permute-start | bytes 983048 | tf_op jit(solution)/shard_map/ppermute | solution.py:383
  111.1 12.3 %collective-permute-start.13 = (bf16[64,2560]{1,0:T(8,128)(2,1)S(1)}, bf16[64,2560]{1,0:T(8,128)(2,1)S(1)}, u32[]{:S(2)}, u32[]{:S(2)}) collective-permute-start(bf16[64,2560]{1,0:T(8,128)(2,1)S(1)} %get-tuple-element.90), channel_id=1, source_target_pairs={{0,496},{16,0},{32,16},{48,32},{64,48},{80,64},{96,80},{112,96},{1... | collective-permute-start | bytes 983048 | tf_op jit(solution)/shard_map/ppermute | solution.py:383
  115.4 12.3 %collective-permute-start.14 = (bf16[64,2560]{1,0:T(8,128)(2,1)S(1)}, bf16[64,2560]{1,0:T(8,128)(2,1)S(1)}, u32[]{:S(2)}, u32[]{:S(2)}) collective-permute-start(bf16[64,2560]{1,0:T(8,128)(2,1)S(1)} %get-tuple-element.92), channel_id=1, source_target_pairs={{0,496},{16,0},{32,16},{48,32},{64,48},{80,64},{96,80},{112,96},{1... | collective-permute-start | bytes 983048 | tf_op jit(solution)/shard_map/ppermute | solution.py:383
  125.5 78.7 %collective-permute-start.15 = (bf16[64,2560]{1,0:T(8,128)(2,1)S(1)}, bf16[64,2560]{1,0:T(8,128)(2,1)S(1)}, u32[]{:S(2)}, u32[]{:S(2)}) collective-permute-start(bf16[64,2560]{1,0:T(8,128)(2,1)S(1)} %get-tuple-element.95), channel_id=1, source_target_pairs={{0,496},{16,0},{32,16},{48,32},{64,48},{80,64},{96,80},{112,96},{1... | collective-permute-start | bytes 983048 | tf_op jit(solution)/shard_map/ppermute | solution.py:383
  130.6 73.7 %collective-permute-start.16 = (bf16[64,2560]{1,0:T(8,128)(2,1)}, bf16[64,2560]{1,0:T(8,128)(2,1)S(1)}, u32[]{:S(2)}, u32[]{:S(2)}) collective-permute-start(bf16[64,2560]{1,0:T(8,128)(2,1)} %get-tuple-element.96), channel_id=1, source_target_pairs={{0,496},{16,0},{32,16},{48,32},{64,48},{80,64},{96,80},{112,96},{1... | collective-permute-start | bytes 983048 | tf_op jit(solution)/shard_map/ppermute | solution.py:383

commit v8 on v7

v8 whole, which is shorter than its diff:
```python
import functools

import jax
import jax.numpy as jnp
from jax import lax
from jax.experimental import pallas as pl
from jax.experimental.pallas import tpu as pltpu
from jax.sharding import PartitionSpec as P

EPS = 1e-06
F32 = jnp.float32
BF16 = jnp.bfloat16
LIMIT = pltpu.CompilerParams(vmem_limit_bytes=24 * 1024 * 1024)
IN_VMEM = pl.BlockSpec(memory_space=pltpu.VMEM)
ANYWHERE = pl.BlockSpec(memory_space=pl.ANY)
COST = pl.CostEstimate(flops=2**32, bytes_accessed=2**23, transcendentals=0)
SCALAR = pl.BlockSpec(memory_space=pltpu.SMEM)


def dp_pairs(n_z, step, flip):
    return [
        (2 * z + h, 2 * ((z + step) % n_z) + (h ^ flip)) for z in range(n_z) for h in range(2)
    ]


def shifted(value, n_z, step):
    return lax.ppermute(value, "dp", dp_pairs(n_z, step, 0))


def swapped(value, n_z):
    return lax.ppermute(value, "dp", dp_pairs(n_z, 0, 1))


def ring_gather(shard, n_z):
    index = lax.axis_index("dp")
    z, h = index // 2, index % 2
    other = swapped(shard, n_z)
    pair = jnp.stack([jnp.where(h == 0, shard, other), jnp.where(h == 0, other, shard)], axis=1)
    half = n_z // 2
    full = unset((2, n_z) + pair.shape[1:], pair.dtype)

    def placed(full, piece, offset):
        return lax.dynamic_update_slice(full, piece[:, None], (0, (z + offset) % n_z, 0, 0, 0))

    full = placed(full, pair, 0)
    right, left = pair, pair
    for step in range(1, half):
        right, left = shifted(right, n_z, 1), shifted(left, n_z, -1)
        full = placed(full, right, -step)
        full = placed(full, left, step)
    right, left = shifted(right[:, :1], n_z, 1), shifted(left[:, 1:], n_z, -1)
    return placed(full, jnp.concatenate([right, left], axis=1), half)


def empty_kernel(out_ref):
    pass


def unset(shape, dtype):
    return pl.pallas_call(
        empty_kernel,
        out_shape=jax.ShapeDtypeStruct(shape, dtype),
        out_specs=ANYWHERE,
        name="unset",
    )()


def norm_kernel(x_ref, normed_ref, inverse_ref):
    x = x_ref[0, 0].astype(F32)
    inverse = lax.rsqrt(jnp.mean(x * x, axis=-1, keepdims=True) + EPS)
    normed_ref[0] = (x * inverse).astype(BF16)
    inverse_ref[0] = jnp.broadcast_to(inverse, inverse_ref.shape[1:])


def norms(saved_inputs):
    ticks, _, rows, width = saved_inputs.shape
    return pl.pallas_call(
        norm_kernel,
        grid=(ticks,),
        out_shape=[
            jax.ShapeDtypeStruct((ticks, rows, width), BF16),
            jax.ShapeDtypeStruct((ticks, rows, 128), F32),
        ],
        in_specs=[pl.BlockSpec((1, 1, rows, width), lambda i: (i, 0, 0, 0))],
        out_specs=[
            pl.BlockSpec((1, rows, width), lambda i: (i, 0, 0)),
            pl.BlockSpec((1, rows, 128), lambda i: (i, 0, 0)),
        ],
        compiler_params=LIMIT,
        cost_estimate=COST,
        name="norms",
    )(saved_inputs)


def forward_values(normed, down):
    latent = jnp.dot(normed, down, preferred_element_type=F32)
    gate = jax.nn.sigmoid(latent)
    active = (latent * gate).astype(BF16)
    return latent, gate * (1.0 + latent * (1.0 - gate)), active


def forward_kernel(levels_ref, normed_ref, maps_ref, dep_ref, latent_ref, slope_ref, active_ref):
    rank = latent_ref.shape[2]
    latent_ref[0], slope_ref[0], active_ref[0] = forward_values(
        normed_ref[0], maps_ref[0, :, :rank]
    )


def forward_rest(levels, normed, maps, dep):
    ticks, rows, width = normed.shape
    rank = maps.shape[2] // 2
    rest = ticks - 1

    def made(dtype):
        return jax.ShapeDtypeStruct((rest, rows, rank), dtype)

    return pl.pallas_call(
        forward_kernel,
        grid_spec=pltpu.PrefetchScalarGridSpec(
            num_scalar_prefetch=1,
            grid=(rest,),
            in_specs=[
                pl.BlockSpec((1, rows, width), lambda i, levels: (i + 1, 0, 0)),
                pl.BlockSpec((1, width, 2 * rank), lambda i, levels: (levels[i + 1], 0, 0)),
                ANYWHERE,
            ],
            out_specs=[pl.BlockSpec((1, rows, rank), lambda i, levels: (i, 0, 0))] * 3,
        ),
        out_shape=[made(F32), made(F32), made(BF16)],
        compiler_params=LIMIT,
        cost_estimate=COST,
        name="forward_rest",
    )(levels, normed, maps, dep)


def tick_kernel(tick, part, levels_ref, incoming_ref, normed_ref, inverse_ref, maps_ref, *refs):
    _, rows, width = normed_ref.shape
    rank = maps_ref.shape[2] // 2
    if tick == 0:
        stack_ref, sent_ref, grad_latent_ref, active_ref, sem = refs[1:]
    else:
        latent_ref, slope_ref = refs[:2]
        stack_ref, sent_ref, grad_latent_ref, sem = refs[3:]
    keep = pltpu.make_async_copy(
        incoming_ref, stack_ref.at[tick, pl.ds(part * rows, rows)], sem
    )
    keep.start()
    if tick == 0:
        latent, slope, active_ref[...] = forward_values(normed_ref[0], maps_ref[0, :, :rank])
    else:
        latent, slope = latent_ref[0], slope_ref[0]
    grad_act = jnp.dot(incoming_ref[...], maps_ref[0, :, rank:], preferred_element_type=F32)
    grad_latent = (grad_act * slope).astype(BF16)
    grad_latent_ref[...] = grad_latent
    inner = jnp.sum(grad_latent.astype(F32) * latent, axis=-1, keepdims=True) / width
    inverse = inverse_ref[0][:, :1]
    scale = inverse * inner
    run = width // 4
    for start in range(0, width, run):
        at = pl.ds(start, run)
        grad_normed = lax.dot_general(
            grad_latent, maps_ref[0, at, :rank], (((1,), (1,)), ((), ())), preferred_element_type=F32
        )
        sent = incoming_ref[:, at].astype(F32) + (
            inverse * grad_normed - normed_ref[0, :, at].astype(F32) * scale
        )
        sent_ref[:, at] = sent.astype(BF16)
    keep.wait()


def tick_layer(tick, part, levels, incoming, normed, inverse, maps, forward, stack):
    _, rows, width = normed.shape
    rows //= 2
    rank = maps.shape[2] // 2
    first = tick == 0
    narrow = jax.ShapeDtypeStruct((rows, rank), BF16)
    incoming_spec = (
        pl.BlockSpec((rows, width), lambda i, levels: (part, 0)) if first else IN_VMEM
    )
    forward_spec = pl.BlockSpec((1, rows, rank), lambda i, levels: (tick - 1, part, 0))
    return pl.pallas_call(
        functools.partial(tick_kernel, tick, part),
        grid_spec=pltpu.PrefetchScalarGridSpec(
            num_scalar_prefetch=1,
            grid=(1,),
            in_specs=[
                incoming_spec,
                pl.BlockSpec((1, rows, width), lambda i, levels: (tick, part, 0)),
                pl.BlockSpec((1, rows, 128), lambda i, levels: (tick, part, 0)),
                pl.BlockSpec((1, width, 2 * rank), lambda i, levels: (levels[tick], 0, 0)),
            ]
            + [forward_spec] * len(forward)
            + [ANYWHERE],
            out_specs=[ANYWHERE, IN_VMEM, IN_VMEM] + [IN_VMEM] * first,
            scratch_shapes=[pltpu.SemaphoreType.DMA],
        ),
        out_shape=[
            jax.ShapeDtypeStruct(stack.shape, stack.dtype),
            jax.ShapeDtypeStruct((rows, width), BF16),
            narrow,
        ]
        + [narrow] * first,
        input_output_aliases={5 + len(forward): 0},
        compiler_params=LIMIT,
        cost_estimate=COST,
        name="tick_layer",
    )(levels, incoming, normed, inverse, maps, *forward, stack)


def beside_kernel(left_ref, right_ref, out_ref):
    lanes = left_ref.shape[1]
    out_ref[:, :lanes] = left_ref[...]
    out_ref[:, lanes:] = right_ref[...]


def beside(left, right):
    rows, lanes = left.shape
    run = rows // 4
    block = pl.BlockSpec((run, lanes), lambda i: (i, 0))
    return pl.pallas_call(
        beside_kernel,
        grid=(rows // run,),
        out_shape=jax.ShapeDtypeStruct((rows, 2 * lanes), left.dtype),
        in_specs=[block, block],
        out_specs=pl.BlockSpec((run, 2 * lanes), lambda i: (i, 0)),
        compiler_params=LIMIT,
        name="side_by_side",
    )(left, right)


def sum_kernel(moved_ref, out_ref):
    total = jnp.sum(moved_ref[...].astype(F32), axis=0)
    if total.shape == out_ref.shape:
        out_ref[...] = total
    else:
        rank = total.shape[1] // 2
        zeros = jnp.zeros((total.shape[0], rank), F32)
        out_ref[...] = jnp.concatenate([total[:, :rank], zeros, total[:, rank:], zeros], axis=1)


def summed(moved, lanes):
    return pl.pallas_call(
        sum_kernel,
        out_shape=jax.ShapeDtypeStruct((moved.shape[1], lanes), F32),
        in_specs=[IN_VMEM],
        out_specs=IN_VMEM,
        compiler_params=LIMIT,
        name="sum_partials",
    )(moved)


def finish_kernel(total_ref, low_ref, high_ref, grad_ref, down_ref, up_ref):
    rows, rank = low_ref.shape[0], down_ref.shape[3]
    grad_ref[0, :rows] = low_ref[...]
    grad_ref[0, rows:] = high_ref[...]
    for i, out in enumerate((down_ref, up_ref)):
        for j, level in enumerate((1, 0)):
            at = (2 * i + j) * rank
            out[level, 0] = total_ref[:, at : at + rank]


def finish(total, low, high, share, rank):
    rows, width = low.shape
    made = jax.ShapeDtypeStruct((2, 1, share, rank), F32)
    return pl.pallas_call(
        finish_kernel,
        out_shape=[jax.ShapeDtypeStruct((1, 2 * rows, width), low.dtype), made, made],
        in_specs=[IN_VMEM] * 3,
        out_specs=[IN_VMEM] * 3,
        compiler_params=LIMIT,
        name="finish",
    )(total, low, high)


def on_device(saved_inputs, grad_in, adapter_down, adapter_up):
    n_sec = lax.axis_size("section")
    n_dp = lax.axis_size("dp")
    n_z = n_dp // 2
    position = lax.axis_index("section")
    ticks = saved_inputs.shape[0]
    rank, share = adapter_down.shape[2], adapter_down.shape[3]
    width = saved_inputs.shape[3]
    two_layers = position + ticks - 1 >= n_sec
    levels = [1 - (position + tick) // n_sec for tick in range(ticks)]

    def shard_of(down, up, level):
        return jnp.concatenate([down[level].T, up[level].T], axis=1)

    def gather_two(down, up, x):
        shards = jnp.stack([shard_of(down, up, level) for level in range(2)])
        full = ring_gather(shards, n_z)
        return full.reshape(2, width, 2 * rank), *norms(x)

    def gather_one(down, up, x):
        shard = shard_of(down, up, 1)
        copies = jnp.broadcast_to(shard[None], (n_dp,) + shard.shape)
        full = lax.all_to_all(copies, "dp", 0, 0, tiled=True)
        both = unset((2, width, 2 * rank), full.dtype)
        both = lax.dynamic_update_index_in_dim(both, full.reshape(width, 2 * rank), 1, 0)
        return both, *norms(x)

    maps, normed, inverse = lax.cond(
        two_layers, gather_two, gather_one, adapter_down[:, 0], adapter_up[:, 0], saved_inputs
    )

    down_one = [(s, (s - 1) % n_sec) for s in range(n_sec)]
    level_stack = jnp.stack(levels).astype(jnp.int32)
    stack = unset(normed.shape, grad_in.dtype)
    grad_latents, first_actives, moving = [], [], []
    for part in range(2):
        stack, sent, grad_latent, active = tick_layer(
            0, part, level_stack, grad_in[0], normed, inverse, maps, [], stack
        )
        grad_latents.append(grad_latent)
        first_actives.append(active)
        moving.append(lax.ppermute(sent, "section", down_one))
    latents, slopes, actives = forward_rest(level_stack, normed, maps, grad_latent)
    for tick in range(1, ticks):
        arrived, moving = moving, []
        for part in range(2):
            stack, sent, grad_latent = tick_layer(
                tick, part, level_stack, arrived[part], normed, inverse, maps, [latents, slopes], stack
            )
            grad_latents.append(grad_latent)
            moving.append(lax.ppermute(sent, "section", down_one))

    normed_all = normed.reshape(-1, width)
    grads_all = stack.reshape(-1, width)
    actives = jnp.concatenate([jnp.concatenate(first_actives)[None], actives], axis=0)

    def products(lats, acts):
        contract = (((0,), (0,)), ((), ()))
        down = lax.dot_general(normed_all, lats, contract, preferred_element_type=F32)
        up = lax.dot_general(grads_all, acts, contract, preferred_element_type=F32)
        both = beside(down.astype(BF16), up.astype(BF16))
        moved = lax.all_to_all(both.reshape(n_dp, share, -1), "dp", 0, 0, tiled=True)
        return summed(moved, 4 * rank)

    def reduce_one(lats, acts):
        return products(lats.reshape(-1, rank), acts.reshape(-1, rank))

    def reduce_two(lats, acts):
        level = level_stack[:, None, None]
        zero = jnp.zeros((), BF16)

        def split(value):
            both = [jnp.where(level == 1, value, zero), jnp.where(level == 0, value, zero)]
            return jnp.concatenate(both, axis=2).reshape(-1, 2 * rank)

        return products(split(lats), split(acts))

    total = lax.cond(two_layers, reduce_two, reduce_one, jnp.concatenate(grad_latents).reshape(actives.shape), actives)
    grad_out, down_grad, up_grad = finish(total, *moving, share, rank)
    return grad_out, jnp.swapaxes(down_grad, 2, 3), jnp.swapaxes(up_grad, 2, 3)


def solution(mesh):
    in_specs = (
        P(None, "section", "dp", None),
        P("section", "dp", None),
        P(None, "section", None, "dp"),
        P(None, "section", None, "dp"),
    )
    out_specs = (
        P("section", "dp", None),
        P(None, "section", None, "dp"),
        P(None, "section", None, "dp"),
    )
    return jax.shard_map(
        on_device, mesh=mesh, in_specs=in_specs, out_specs=out_specs, check_vma=False
    )
```

time: 206 us -> 192 us (0.932)
  local copies, waits for them, and re-layouts: 14.4 us -> 2.74 us
  Pallas kernels: 29.6 us -> 19.6 us
  waiting for transfers between devices: 27.9 us -> 35.3 us
  matrix products: 2.27 us -> 6.46 us
  blocking collectives: 68.2 us -> 64.8 us
  starting transfers between devices: 61 us -> 58.4 us
    pallas_call x10 -> x12, Pallas kernels: 28.1 us -> 18 us  [the longest x8 11.9 us: tick_layer(): pl.pallas_call(functools.partial(tick_kernel, tick, part), grid_spec=pltp...]
    ppermute x8, waiting for transfers between devices: 10.5 us -> 20.5 us  [on_device(): moving.append(lax.ppermute(sent, 'section', down_one))]
    cond x20 -> x6, local copies, waits for them, and re-layouts: 7.76 us -> 1.49 us
    all_to_all x1, blocking collectives: 68.2 us -> 64.8 us  [products(): lax.all_to_all(both.reshape(n_dp, share, -1), 'dp', 0, 0, tiled=True)]
    unnamed x23, local copies, waits for them, and re-layouts: 4.12 us -> 0.96 us
    ppermute x8, waiting for transfers between devices: 11 us -> 8.24 us  [shifted(): return lax.ppermute(value, 'dp', dp_pairs(n_z, step, 0))]
    ppermute x8, starting transfers between devices: 24.5 us -> 22 us  [on_device(): moving.append(lax.ppermute(sent, 'section', down_one))]
    dot_general x1, matrix products: 1.13 us -> 3.58 us  [products(): up = lax.dot_general(grads_all, acts, contract, preferred_element_type=F32)]
  transfers between devices with their start and end apart: 17 -> 17, of which waited for: 9 -> 10; matrix products, arithmetic and copies ran while one was open for 3% -> 4% of each run, Pallas kernels for 10% -> 7%
where the time goes in v8:
time: 192 us; the launch traced here: 191 us
  blocking collectives  64.8 us (34%)
  starting transfers between devices  58.4 us (30%)
  waiting for transfers between devices  35.3 us (18%)
  Pallas kernels  19.6 us (10%)
  matrix products  6.46 us (3%)
  local copies, waits for them, and re-layouts  2.74 us (1%)
  other arithmetic  2.16 us (1%)
    all_to_all x1, blocking collectives, products(): lax.all_to_all(both.reshape(n_dp, share, -1), 'dp', 0, 0, tiled=True)  64.8 us
    ppermute x8, starting transfers between devices, shifted(): return lax.ppermute(value, 'dp', dp_pairs(n_z, step, 0))  32.1 us
    ppermute x8, starting transfers between devices, on_device(): moving.append(lax.ppermute(sent, 'section', down_one))  22 us
    ppermute x8, waiting for transfers between devices, on_device(): moving.append(lax.ppermute(sent, 'section', down_one))  20.5 us
    pallas_call x8, Pallas kernels, tick_layer(): pl.pallas_call(functools.partial(tick_kernel, tick, part), grid_spec=pltp...  11.9 us
    ppermute x8, waiting for transfers between devices, shifted(): return lax.ppermute(value, 'dp', dp_pairs(n_z, step, 0))  8.24 us
    ppermute x1, waiting for transfers between devices, swapped(): return lax.ppermute(value, 'dp', dp_pairs(n_z, 0, 1))  6.54 us
    pallas_call x1, Pallas kernels, norms(): pl.pallas_call(norm_kernel, grid=(ticks,), out_shape=[jax.ShapeDtypeStruc...  4.57 us
  transfers between devices with their start and end apart: 17, of which 10 were waited for; matrix products, arithmetic and copies ran while one was open for 4% of the time, Pallas kernels for 7%

profile of v8, /device:TPU:63, one launch (start us, length us, event | category | flops | bytes accessed | tf_op | source)
XLA Modules:
  0.0 191.4 jit_solution(10918080631246368297)
XLA Ops:
  0.7 0.8 copy-done.7
  1.6 59.7 %conditional.2 = (bf16[2,2560,256]{2,1,0:T(8,128)(2,1)}, bf16[4,128,2560]{2,1,0:T(8,128)(2,1)}, f32[4,128,128]{2,1,0:T(8,128)S(1)}) conditional(s32[]{:T(128)} %convert_element_type.20, (bf16[2,128,160]{1,2,0:T(8,128)(2,1)S(1)}, bf16[2,128,160]{1,2,0:T(8,128)(2,1)S(1)}, bf16[4,1,128,2560]{3,2,1,0:T(8,128)(2,1)}) %tuple.46, ...), branch_computations={%region_0.1_spmd, %region_1.2_spmd} | conditional | flops 4297097216 | bytes 47384412 | solution.py:302
  1.6 0.7 pad_maximum_fusion.2
  2.3 4.4 %collective-permute-start = (bf16[2,160,256]{2,1,0:T(8,128)(2,1)}, bf16[2,160,256]{2,1,0:T(8,128)(2,1)}, u32[]{:S(2)}, u32[]{:S(2)}) collective-permute-start(bf16[2,160,256]{2,1,0:T(8,128)(2,1)} %pad_maximum_fusion.2), channel_id=1, source_target_pairs={{0,1},{1,0},{2,3},{3,2},{4,5},{5,4},{6,7},{7,6},{8,9},{9,8},{10,11... | collective-permute-start | bytes 491528 | tf_op jit(solution)/shard_map/cond/branch_1_fun/ppermute | solution.py:31
  6.9 6.5 %collective-permute-done = bf16[2,160,256]{2,1,0:T(8,128)(2,1)} collective-permute-done((bf16[2,160,256]{2,1,0:T(8,128)(2,1)}, bf16[2,160,256]{2,1,0:T(8,128)(2,1)}, u32[]{:S(2)}, u32[]{:S(2)}) %collective-permute-start) | collective-permute-done | bytes 163872 | tf_op jit(solution)/shard_map/cond/branch_1_fun/ppermute | solution.py:31
  13.5 0.9 select_bitcast_fusion.1
  14.5 4.0 %collective-permute-start.1 = (bf16[2,2,160,256]{3,2,1,0:T(8,128)(2,1)S(1)}, bf16[2,2,160,256]{3,2,1,0:T(8,128)(2,1)S(1)}, u32[]{:S(2)}, u32[]{:S(2)}) collective-permute-start(bf16[2,2,160,256]{3,2,1,0:T(8,128)(2,1)S(1)} %pad_maximum_fusion.1), channel_id=1, source_target_pairs={{0,2},{1,3},{2,4},{3,5},{4,6},{5,7},{6,8},{7,9},{8,10},{9,11},{10,... | collective-permute-start | bytes 983048 | tf_op jit(solution)/shard_map/cond/branch_1_fun/ppermute | solution.py:27
  18.5 8.6 %collective-permute-start.2 = (bf16[2,2,160,256]{3,2,1,0:T(8,128)(2,1)S(1)}, bf16[2,2,160,256]{3,2,1,0:T(8,128)(2,1)S(1)}, u32[]{:S(2)}, u32[]{:S(2)}) collective-permute-start(bf16[2,2,160,256]{3,2,1,0:T(8,128)(2,1)S(1)} %pad_maximum_fusion.1), channel_id=1, source_target_pairs={{0,14},{1,15},{2,0},{3,1},{4,2},{5,3},{6,4},{7,5},{8,6},{9,7},{10,... | collective-permute-start | bytes 983048 | tf_op jit(solution)/shard_map/cond/branch_1_fun/ppermute | solution.py:27
  27.1 4.6 %norms.3 = (bf16[4,128,2560]{2,1,0:T(8,128)(2,1)}, f32[4,128,128]{2,1,0:T(8,128)S(1)}) custom-call(bf16[4,1,128,2560]{3,2,1,0:T(8,128)(2,1)} %get-tuple-element.41.x_ref), custom_call_target="tpu_custom_call" | custom-call | flops 4294967296 | bytes 8388608 | tf_op jit(solution)/shard_map/cond/branch_1_fun/norms/pallas_call | solution.py:77
  31.7 1.9 %collective-permute-start.3 = (bf16[2,2,160,256]{3,2,1,0:T(8,128)(2,1)S(1)}, bf16[2,2,160,256]{3,2,1,0:T(8,128)(2,1)S(1)}, u32[]{:S(2)}, u32[]{:S(2)}) collective-permute-start(bf16[2,2,160,256]{3,2,1,0:T(8,128)(2,1)S(1)} %collective-permute-done.1), channel_id=1, source_target_pairs={{0,2},{1,3},{2,4},{3,5},{4,6},{5,7},{6,8},{7,9},{8,10},{9,11},{10,... | collective-permute-start | bytes 983048 | tf_op jit(solution)/shard_map/cond/branch_1_fun/ppermute | solution.py:27
  33.6 4.6 %collective-permute-start.4 = (bf16[2,2,160,256]{3,2,1,0:T(8,128)(2,1)S(1)}, bf16[2,2,160,256]{3,2,1,0:T(8,128)(2,1)S(1)}, u32[]{:S(2)}, u32[]{:S(2)}) collective-permute-start(bf16[2,2,160,256]{3,2,1,0:T(8,128)(2,1)S(1)} %collective-permute-done.2), channel_id=1, source_target_pairs={{0,14},{1,15},{2,0},{3,1},{4,2},{5,3},{6,4},{7,5},{8,6},{9,7},{10,... | collective-permute-start | bytes 983048 | tf_op jit(solution)/shard_map/cond/branch_1_fun/ppermute | solution.py:27
  38.3 3.6 %collective-permute-done.3 = bf16[2,2,160,256]{3,2,1,0:T(8,128)(2,1)S(1)} collective-permute-done((bf16[2,2,160,256]{3,2,1,0:T(8,128)(2,1)S(1)}, bf16[2,2,160,256]{3,2,1,0:T(8,128)(2,1)S(1)}, u32[]{:S(2)}, u32[]{:S(2)}) %collective-permute-start.3) | collective-permute-done | bytes 327712 | tf_op jit(solution)/shard_map/cond/branch_1_fun/ppermute | solution.py:27
  41.9 1.9 collective-permute-start.5
  43.8 4.6 %collective-permute-start.6 = (bf16[2,2,160,256]{3,2,1,0:T(8,128)(2,1)S(1)}, bf16[2,2,160,256]{3,2,1,0:T(8,128)(2,1)S(1)}, u32[]{:S(2)}, u32[]{:S(2)}) collective-permute-start(bf16[2,2,160,256]{3,2,1,0:T(8,128)(2,1)S(1)} %collective-permute-done.4), channel_id=1, source_target_pairs={{0,14},{1,15},{2,0},{3,1},{4,2},{5,3},{6,4},{7,5},{8,6},{9,7},{10,... | collective-permute-start | bytes 983048 | tf_op jit(solution)/shard_map/cond/branch_1_fun/ppermute | solution.py:27
  48.5 2.4 %collective-permute-done.5 = bf16[2,2,160,256]{3,2,1,0:T(8,128)(2,1)S(1)} collective-permute-done((bf16[2,2,160,256]{3,2,1,0:T(8,128)(2,1)S(1)}, bf16[2,2,160,256]{3,2,1,0:T(8,128)(2,1)S(1)}, u32[]{:S(2)}, u32[]{:S(2)}) %collective-permute-start.5) | collective-permute-done | bytes 327712 | tf_op jit(solution)/shard_map/cond/branch_1_fun/ppermute | solution.py:27
  50.9 1.9 %collective-permute-start.7 = (bf16[2,1,160,256]{3,2,1,0:T(8,128)(2,1)S(1)}, bf16[2,1,160,256]{3,2,1,0:T(8,128)(2,1)S(1)}, u32[]{:S(2)}, u32[]{:S(2)}) collective-permute-start(bf16[2,1,160,256]{3,2,1,0:T(8,128)(2,1)S(1)} %slice.24), channel_id=1, source_target_pairs={{0,2},{1,3},{2,4},{3,5},{4,6},{5,7},{6,8},{7,9},{8,10},{9,11},{10,... | collective-permute-start | bytes 491528 | tf_op jit(solution)/shard_map/cond/branch_1_fun/ppermute | solution.py:27
  52.9 4.6 %collective-permute-start.8 = (bf16[2,1,160,256]{3,2,1,0:T(8,128)(2,1)S(1)}, bf16[2,1,160,256]{3,2,1,0:T(8,128)(2,1)S(1)}, u32[]{:S(2)}, u32[]{:S(2)}) collective-permute-start(bf16[2,1,160,256]{3,2,1,0:T(8,128)(2,1)S(1)} %slice.25), channel_id=1, source_target_pairs={{0,14},{1,15},{2,0},{3,1},{4,2},{5,3},{6,4},{7,5},{8,6},{9,7},{10,... | collective-permute-start | bytes 491528 | tf_op jit(solution)/shard_map/cond/branch_1_fun/ppermute | solution.py:27
  57.6 0.7 collective-permute-done.7
  58.2 1.5 collective-permute-done.8
  59.8 1.5 copy-done.5
  61.3 3.0 %tick_layer.8 = (bf16[4,128,2560]{2,1,0:T(8,128)(2,1)S(1)}, bf16[64,2560]{1,0:T(8,128)(2,1)S(1)}, bf16[64,128]{1,0:T(8,128)(2,1)S(1)}, bf16[64,128]{1,0:T(8,128)(2,1)S(1)}) custom-call(s32[4]{0:T(128)S(1)} %pad_add_fusion.levels_ref, bf16[128,2560]{1,0:T(8,128)(2,1)S(1)} %bitcast.104, ...), custom_call_target="tpu_custom_call", output_to_operand_aliasing={{0}: (5, {})} | custom-call | flops 4294967296 | bytes 8388608 | tf_op jit(solution)/shard_map/tick_layer/pallas_call | solution.py:181
  64.4 7.2 %collective-permute-start.9 = (bf16[64,2560]{1,0:T(8,128)(2,1)S(1)}, bf16[64,2560]{1,0:T(8,128)(2,1)S(1)}, u32[]{:S(2)}, u32[]{:S(2)}) collective-permute-start(bf16[64,2560]{1,0:T(8,128)(2,1)S(1)} %get-tuple-element.97), channel_id=1, source_target_pairs={{0,496},{16,0},{32,16},{48,32},{64,48},{80,64},{96,80},{112,96},{1... | collective-permute-start | bytes 983048 | tf_op jit(solution)/shard_map/ppermute | solution.py:316
  71.7 1.3 tick_layer.9
  73.0 3.2 %collective-permute-start.10 = (bf16[64,2560]{1,0:T(8,128)(2,1)S(1)}, bf16[64,2560]{1,0:T(8,128)(2,1)S(1)}, u32[]{:S(2)}, u32[]{:S(2)}) collective-permute-start(bf16[64,2560]{1,0:T(8,128)(2,1)S(1)} %get-tuple-element.102), channel_id=1, source_target_pairs={{0,496},{16,0},{32,16},{48,32},{64,48},{80,64},{96,80},{112,96},{1... | collective-permute-start | bytes 983048 | tf_op jit(solution)/shard_map/ppermute | solution.py:316
  76.2 1.6 forward_rest.1
  77.9 1.2 tick_layer.10
  79.2 1.9 %collective-permute-start.11 = (bf16[64,2560]{1,0:T(8,128)(2,1)S(1)}, bf16[64,2560]{1,0:T(8,128)(2,1)S(1)}, u32[]{:S(2)}, u32[]{:S(2)}) collective-permute-start(bf16[64,2560]{1,0:T(8,128)(2,1)S(1)} %get-tuple-element.105), channel_id=1, source_target_pairs={{0,496},{16,0},{32,16},{48,32},{64,48},{80,64},{96,80},{112,96},{1... | collective-permute-start | bytes 983048 | tf_op jit(solution)/shard_map/ppermute | solution.py:325
  81.1 4.2 %collective-permute-done.10.incoming_ref = bf16[64,2560]{1,0:T(8,128)(2,1)S(1)} collective-permute-done((bf16[64,2560]{1,0:T(8,128)(2,1)S(1)}, bf16[64,2560]{1,0:T(8,128)(2,1)S(1)}, u32[]{:S(2)}, u32[]{:S(2)}) %collective-permute-start.10) | collective-permute-done | bytes 327712 | tf_op jit(solution)/shard_map/ppermute | solution.py:316
  85.3 1.2 tick_layer.11
  86.6 1.9 %collective-permute-start.12 = (bf16[64,2560]{1,0:T(8,128)(2,1)S(1)}, bf16[64,2560]{1,0:T(8,128)(2,1)S(1)}, u32[]{:S(2)}, u32[]{:S(2)}) collective-permute-start(bf16[64,2560]{1,0:T(8,128)(2,1)S(1)} %get-tuple-element.108), channel_id=1, source_target_pairs={{0,496},{16,0},{32,16},{48,32},{64,48},{80,64},{96,80},{112,96},{1... | collective-permute-start | bytes 983048 | tf_op jit(solution)/shard_map/ppermute | solution.py:325
  88.5 3.0 %collective-permute-done.11.incoming_ref = bf16[64,2560]{1,0:T(8,128)(2,1)S(1)} collective-permute-done((bf16[64,2560]{1,0:T(8,128)(2,1)S(1)}, bf16[64,2560]{1,0:T(8,128)(2,1)S(1)}, u32[]{:S(2)}, u32[]{:S(2)}) %collective-permute-start.11) | collective-permute-done | bytes 327712 | tf_op jit(solution)/shard_map/ppermute | solution.py:325
  91.5 1.2 tick_layer.12
  92.7 1.9 %collective-permute-start.13 = (bf16[64,2560]{1,0:T(8,128)(2,1)S(1)}, bf16[64,2560]{1,0:T(8,128)(2,1)S(1)}, u32[]{:S(2)}, u32[]{:S(2)}) collective-permute-start(bf16[64,2560]{1,0:T(8,128)(2,1)S(1)} %get-tuple-element.111), channel_id=1, source_target_pairs={{0,496},{16,0},{32,16},{48,32},{64,48},{80,64},{96,80},{112,96},{1... | collective-permute-start | bytes 983048 | tf_op jit(solution)/shard_map/ppermute | solution.py:325
  94.7 4.2 %collective-permute-done.12.incoming_ref = bf16[64,2560]{1,0:T(8,128)(2,1)S(1)} collective-permute-done((bf16[64,2560]{1,0:T(8,128)(2,1)S(1)}, bf16[64,2560]{1,0:T(8,128)(2,1)S(1)}, u32[]{:S(2)}, u32[]{:S(2)}) %collective-permute-start.12) | collective-permute-done | bytes 327712 | tf_op jit(solution)/shard_map/ppermute | solution.py:325
  98.9 1.2 tick_layer.13
  100.1 1.9 %collective-permute-start.14 = (bf16[64,2560]{1,0:T(8,128)(2,1)S(1)}, bf16[64,2560]{1,0:T(8,128)(2,1)S(1)}, u32[]{:S(2)}, u32[]{:S(2)}) collective-permute-start(bf16[64,2560]{1,0:T(8,128)(2,1)S(1)} %get-tuple-element.114), channel_id=1, source_target_pairs={{0,496},{16,0},{32,16},{48,32},{64,48},{80,64},{96,80},{112,96},{1... | collective-permute-start | bytes 983048 | tf_op jit(solution)/shard_map/ppermute | solution.py:325
  102.1 3.0 %collective-permute-done.13.incoming_ref = bf16[64,2560]{1,0:T(8,128)(2,1)S(1)} collective-permute-done((bf16[64,2560]{1,0:T(8,128)(2,1)S(1)}, bf16[64,2560]{1,0:T(8,128)(2,1)S(1)}, u32[]{:S(2)}, u32[]{:S(2)}) %collective-permute-start.13) | collective-permute-done | bytes 327712 | tf_op jit(solution)/shard_map/ppermute | solution.py:325
  105.0 1.2 tick_layer.14
  106.3 6.1 %collective-permute-done.14.incoming_ref = bf16[64,2560]{1,0:T(8,128)(2,1)S(1)} collective-permute-done((bf16[64,2560]{1,0:T(8,128)(2,1)S(1)}, bf16[64,2560]{1,0:T(8,128)(2,1)S(1)}, u32[]{:S(2)}, u32[]{:S(2)}) %collective-permute-start.14) | collective-permute-done | bytes 327712 | tf_op jit(solution)/shard_map/ppermute | solution.py:325
  112.4 1.3 tick_layer.15
  113.7 1.9 %collective-permute-start.16 = (bf16[64,2560]{1,0:T(8,128)(2,1)S(1)}, bf16[64,2560]{1,0:T(8,128)(2,1)S(1)}, u32[]{:S(2)}, u32[]{:S(2)}) collective-permute-start(bf16[64,2560]{1,0:T(8,128)(2,1)S(1)} %get-tuple-element.122), channel_id=1, source_target_pairs={{0,496},{16,0},{32,16},{48,32},{64,48},{80,64},{96,80},{112,96},{1... | collective-permute-start | bytes 983048 | tf_op jit(solution)/shard_map/ppermute | solution.py:325
  115.6 1.9 %collective-permute-start.15 = (bf16[64,2560]{1,0:T(8,128)(2,1)S(1)}, bf16[64,2560]{1,0:T(8,128)(2,1)S(1)}, u32[]{:S(2)}, u32[]{:S(2)}) collective-permute-start(bf16[64,2560]{1,0:T(8,128)(2,1)S(1)} %get-tuple-element.121), channel_id=1, source_target_pairs={{0,496},{16,0},{32,16},{48,32},{64,48},{80,64},{96,80},{112,96},{1... | collective-permute-start | bytes 983048 | tf_op jit(solution)/shard_map/ppermute | solution.py:325
  117.6 72.7 %conditional.3 = (f32[160,512]{1,0:T(8,128)S(1)}) conditional(s32[]{:T(128)} %convert_element_type.20, (bf16[512,2560]{1,0:T(8,128)(2,1)S(1)}, bf16[512,128]{1,0:T(8,128)(2,1)S(1)}, bf16[4,128,128]{2,1,0:T(8,128)(2,1)S(1)}, bf16[512,2560]{1,0:T(8,128)(2,1)}) %tuple.42, (s32[4]{0:T(128)S(1)}, bf16[512,128]{1,0:T(8,128)(2,1)S(1)}, ...), branch_computations={%region_2.3_spmd, %region_3.4_spmd} | conditional | flops 1344798720 | bytes 25430092 | solution.py:352
  118.0 3.6 %fusion.2.right_ref = bf16[2560,256]{1,0:T(8,128)(2,1)S(1)} fusion(bf16[512,256]{1,0:T(8,128)(2,1)S(1)} %bitcast.112, bf16[512,2560]{1,0:T(8,128)(2,1)} %get-tuple-element.52), kind=kOutput, calls=%fused_computation.28 | convolution fusion | flops 671744000 | bytes 4194304 | tf_op jit(solution)/shard_map/cond/branch_1_fun/dot_general | solution.py:334
  121.8 2.9 %fusion.1.left_ref = bf16[2560,256]{1,0:T(8,128)(2,1)S(1)} fusion(bf16[512,2560]{1,0:T(8,128)(2,1)} %copy-done.3, bf16[512,128]{1,0:T(8,128)(2,1)S(1)} %get-tuple-element.139, bf16[512,128]{1,0:T(8,128)(2,1)S(1)} %get-tuple-element.138), kind=kOutput, calls=%fused_computation.27 | convolution fusion | flops 672268288 | bytes 4194304 | tf_op jit(solution)/shard_map/cond/branch_1_fun/dot_general | solution.py:333
  125.0 64.8 %all_to_all.13.moved_ref = bf16[16,160,512]{2,1,0:T(8,128)(2,1)S(1)} all-to-all(bf16[16,160,512]{2,1,0:T(8,128)(2,1)S(1)} %bitcast.102), channel_id=1, replica_groups=mesh['section'=32,'dp'=16] {'dp'}, dimensions={0} | all-to-all | bytes 5242880 | tf_op jit(solution)/shard_map/cond/branch_1_fun/all_to_all | solution.py:336
  189.8 0.3 sum_partials.3
  190.4 1.0 finish.1
  (60 shorter events, 1.2 us)
Async XLA Ops:
  0.6 0.9 copy-start.7
  0.6 0.9 copy-start.8
  1.6 59.8 %copy-start = (bf16[1,128,2560]{2,1,0:T(8,128)(2,1)S(1)}, bf16[1,128,2560]{2,1,0:T(8,128)(2,1)}, u32[]{:S(2)}) copy-start(bf16[1,128,2560]{2,1,0:T(8,128)(2,1)} %param.9) | copy-start | bytes 1966084
  2.3 11.2 %collective-permute-start = (bf16[2,160,256]{2,1,0:T(8,128)(2,1)}, bf16[2,160,256]{2,1,0:T(8,128)(2,1)}, u32[]{:S(2)}, u32[]{:S(2)}) collective-permute-start(bf16[2,160,256]{2,1,0:T(8,128)(2,1)} %pad_maximum_fusion.2), channel_id=1, source_target_pairs={{0,1},{1,0},{2,3},{3,2},{4,5},{5,4},{6,7},{7,6},{8,9},{9,8},{10,11... | collective-permute-start | bytes 491528 | tf_op jit(solution)/shard_map/cond/branch_1_fun/ppermute | solution.py:31
  14.5 17.2 %collective-permute-start.1 = (bf16[2,2,160,256]{3,2,1,0:T(8,128)(2,1)S(1)}, bf16[2,2,160,256]{3,2,1,0:T(8,128)(2,1)S(1)}, u32[]{:S(2)}, u32[]{:S(2)}) collective-permute-start(bf16[2,2,160,256]{3,2,1,0:T(8,128)(2,1)S(1)} %pad_maximum_fusion.1), channel_id=1, source_target_pairs={{0,2},{1,3},{2,4},{3,5},{4,6},{5,7},{6,8},{7,9},{8,10},{9,11},{10,... | collective-permute-start | bytes 983048 | tf_op jit(solution)/shard_map/cond/branch_1_fun/ppermute | solution.py:27
  18.5 15.1 %collective-permute-start.2 = (bf16[2,2,160,256]{3,2,1,0:T(8,128)(2,1)S(1)}, bf16[2,2,160,256]{3,2,1,0:T(8,128)(2,1)S(1)}, u32[]{:S(2)}, u32[]{:S(2)}) collective-permute-start(bf16[2,2,160,256]{3,2,1,0:T(8,128)(2,1)S(1)} %pad_maximum_fusion.1), channel_id=1, source_target_pairs={{0,14},{1,15},{2,0},{3,1},{4,2},{5,3},{6,4},{7,5},{8,6},{9,7},{10,... | collective-permute-start | bytes 983048 | tf_op jit(solution)/shard_map/cond/branch_1_fun/ppermute | solution.py:27
  27.1 4.6 %copy-start.4 = (bf16[2,8,2,160,256]{4,3,2,1,0:T(8,128)(2,1)S(1)}, bf16[2,8,2,160,256]{4,3,2,1,0:T(8,128)(2,1)}, u32[]{:S(2)}) copy-start(bf16[2,8,2,160,256]{4,3,2,1,0:T(8,128)(2,1)} %unset.4) | copy-start | bytes 7864324 | tf_op jit(solution)/shard_map/cond
  31.7 10.2 %collective-permute-start.3 = (bf16[2,2,160,256]{3,2,1,0:T(8,128)(2,1)S(1)}, bf16[2,2,160,256]{3,2,1,0:T(8,128)(2,1)S(1)}, u32[]{:S(2)}, u32[]{:S(2)}) collective-permute-start(bf16[2,2,160,256]{3,2,1,0:T(8,128)(2,1)S(1)} %collective-permute-done.1), channel_id=1, source_target_pairs={{0,2},{1,3},{2,4},{3,5},{4,6},{5,7},{6,8},{7,9},{8,10},{9,11},{10,... | collective-permute-start | bytes 983048 | tf_op jit(solution)/shard_map/cond/branch_1_fun/ppermute | solution.py:27
  33.6 10.2 %collective-permute-start.4 = (bf16[2,2,160,256]{3,2,1,0:T(8,128)(2,1)S(1)}, bf16[2,2,160,256]{3,2,1,0:T(8,128)(2,1)S(1)}, u32[]{:S(2)}, u32[]{:S(2)}) collective-permute-start(bf16[2,2,160,256]{3,2,1,0:T(8,128)(2,1)S(1)} %collective-permute-done.2), channel_id=1, source_target_pairs={{0,14},{1,15},{2,0},{3,1},{4,2},{5,3},{6,4},{7,5},{8,6},{9,7},{10,... | collective-permute-start | bytes 983048 | tf_op jit(solution)/shard_map/cond/branch_1_fun/ppermute | solution.py:27
  41.9 9.0 %collective-permute-start.5 = (bf16[2,2,160,256]{3,2,1,0:T(8,128)(2,1)S(1)}, bf16[2,2,160,256]{3,2,1,0:T(8,128)(2,1)S(1)}, u32[]{:S(2)}, u32[]{:S(2)}) collective-permute-start(bf16[2,2,160,256]{3,2,1,0:T(8,128)(2,1)S(1)} %collective-permute-done.3), channel_id=1, source_target_pairs={{0,2},{1,3},{2,4},{3,5},{4,6},{5,7},{6,8},{7,9},{8,10},{9,11},{10,... | collective-permute-start | bytes 983048 | tf_op jit(solution)/shard_map/cond/branch_1_fun/ppermute | solution.py:27
  43.8 9.0 %collective-permute-start.6 = (bf16[2,2,160,256]{3,2,1,0:T(8,128)(2,1)S(1)}, bf16[2,2,160,256]{3,2,1,0:T(8,128)(2,1)S(1)}, u32[]{:S(2)}, u32[]{:S(2)}) collective-permute-start(bf16[2,2,160,256]{3,2,1,0:T(8,128)(2,1)S(1)} %collective-permute-done.4), channel_id=1, source_target_pairs={{0,14},{1,15},{2,0},{3,1},{4,2},{5,3},{6,4},{7,5},{8,6},{9,7},{10,... | collective-permute-start | bytes 983048 | tf_op jit(solution)/shard_map/cond/branch_1_fun/ppermute | solution.py:27
  50.9 7.3 %collective-permute-start.7 = (bf16[2,1,160,256]{3,2,1,0:T(8,128)(2,1)S(1)}, bf16[2,1,160,256]{3,2,1,0:T(8,128)(2,1)S(1)}, u32[]{:S(2)}, u32[]{:S(2)}) collective-permute-start(bf16[2,1,160,256]{3,2,1,0:T(8,128)(2,1)S(1)} %slice.24), channel_id=1, source_target_pairs={{0,2},{1,3},{2,4},{3,5},{4,6},{5,7},{6,8},{7,9},{8,10},{9,11},{10,... | collective-permute-start | bytes 491528 | tf_op jit(solution)/shard_map/cond/branch_1_fun/ppermute | solution.py:27
  52.9 6.8 %collective-permute-start.8 = (bf16[2,1,160,256]{3,2,1,0:T(8,128)(2,1)S(1)}, bf16[2,1,160,256]{3,2,1,0:T(8,128)(2,1)S(1)}, u32[]{:S(2)}, u32[]{:S(2)}) collective-permute-start(bf16[2,1,160,256]{3,2,1,0:T(8,128)(2,1)S(1)} %slice.25), channel_id=1, source_target_pairs={{0,14},{1,15},{2,0},{3,1},{4,2},{5,3},{6,4},{7,5},{8,6},{9,7},{10,... | collective-permute-start | bytes 491528 | tf_op jit(solution)/shard_map/cond/branch_1_fun/ppermute | solution.py:27
  59.7 1.5 copy-start.5
  61.2 10.4 %copy-start.9 = (f32[4,128,128]{2,1,0:T(8,128)}, f32[4,128,128]{2,1,0:T(8,128)S(1)}, u32[]{:S(2)}) copy-start(f32[4,128,128]{2,1,0:T(8,128)S(1)} %get-tuple-element.92.inverse_ref) | copy-start | bytes 786436
  61.3 10.3 %copy-start.2 = (bf16[4,128,2560]{2,1,0:T(8,128)(2,1)S(1)}, bf16[4,128,2560]{2,1,0:T(8,128)(2,1)}, u32[]{:S(2)}) copy-start(bf16[4,128,2560]{2,1,0:T(8,128)(2,1)} %get-tuple-element.91.normed_ref) | copy-start | bytes 7864324
  61.3 10.3 %copy-start.6 = (bf16[2,2560,256]{2,1,0:T(8,128)(2,1)S(1)}, bf16[2,2560,256]{2,1,0:T(8,128)(2,1)}, u32[]{:S(2)}) copy-start(bf16[2,2560,256]{2,1,0:T(8,128)(2,1)} %get-tuple-element.93.maps_ref) | copy-start | bytes 7864324
  64.4 13.5 %collective-permute-start.9 = (bf16[64,2560]{1,0:T(8,128)(2,1)S(1)}, bf16[64,2560]{1,0:T(8,128)(2,1)S(1)}, u32[]{:S(2)}, u32[]{:S(2)}) collective-permute-start(bf16[64,2560]{1,0:T(8,128)(2,1)S(1)} %get-tuple-element.97), channel_id=1, source_target_pairs={{0,496},{16,0},{32,16},{48,32},{64,48},{80,64},{96,80},{112,96},{1... | collective-permute-start | bytes 983048 | tf_op jit(solution)/shard_map/ppermute | solution.py:316
  73.0 12.3 %collective-permute-start.10 = (bf16[64,2560]{1,0:T(8,128)(2,1)S(1)}, bf16[64,2560]{1,0:T(8,128)(2,1)S(1)}, u32[]{:S(2)}, u32[]{:S(2)}) collective-permute-start(bf16[64,2560]{1,0:T(8,128)(2,1)S(1)} %get-tuple-element.102), channel_id=1, source_target_pairs={{0,496},{16,0},{32,16},{48,32},{64,48},{80,64},{96,80},{112,96},{1... | collective-permute-start | bytes 983048 | tf_op jit(solution)/shard_map/ppermute | solution.py:316
  76.2 1.7 copy-start.10
  79.2 12.3 %collective-permute-start.11 = (bf16[64,2560]{1,0:T(8,128)(2,1)S(1)}, bf16[64,2560]{1,0:T(8,128)(2,1)S(1)}, u32[]{:S(2)}, u32[]{:S(2)}) collective-permute-start(bf16[64,2560]{1,0:T(8,128)(2,1)S(1)} %get-tuple-element.105), channel_id=1, source_target_pairs={{0,496},{16,0},{32,16},{48,32},{64,48},{80,64},{96,80},{112,96},{1... | collective-permute-start | bytes 983048 | tf_op jit(solution)/shard_map/ppermute | solution.py:325
  86.6 12.3 %collective-permute-start.12 = (bf16[64,2560]{1,0:T(8,128)(2,1)S(1)}, bf16[64,2560]{1,0:T(8,128)(2,1)S(1)}, u32[]{:S(2)}, u32[]{:S(2)}) collective-permute-start(bf16[64,2560]{1,0:T(8,128)(2,1)S(1)} %get-tuple-element.108), channel_id=1, source_target_pairs={{0,496},{16,0},{32,16},{48,32},{64,48},{80,64},{96,80},{112,96},{1... | collective-permute-start | bytes 983048 | tf_op jit(solution)/shard_map/ppermute | solution.py:325
  92.7 12.3 %collective-permute-start.13 = (bf16[64,2560]{1,0:T(8,128)(2,1)S(1)}, bf16[64,2560]{1,0:T(8,128)(2,1)S(1)}, u32[]{:S(2)}, u32[]{:S(2)}) collective-permute-start(bf16[64,2560]{1,0:T(8,128)(2,1)S(1)} %get-tuple-element.111), channel_id=1, source_target_pairs={{0,496},{16,0},{32,16},{48,32},{64,48},{80,64},{96,80},{112,96},{1... | collective-permute-start | bytes 983048 | tf_op jit(solution)/shard_map/ppermute | solution.py:325
  100.1 12.3 %collective-permute-start.14 = (bf16[64,2560]{1,0:T(8,128)(2,1)S(1)}, bf16[64,2560]{1,0:T(8,128)(2,1)S(1)}, u32[]{:S(2)}, u32[]{:S(2)}) collective-permute-start(bf16[64,2560]{1,0:T(8,128)(2,1)S(1)} %get-tuple-element.114), channel_id=1, source_target_pairs={{0,496},{16,0},{32,16},{48,32},{64,48},{80,64},{96,80},{112,96},{1... | collective-permute-start | bytes 983048 | tf_op jit(solution)/shard_map/ppermute | solution.py:325
  106.3 6.1 %copy-start.1 = (bf16[4,128,2560]{2,1,0:T(8,128)(2,1)}, bf16[4,128,2560]{2,1,0:T(8,128)(2,1)S(1)}, u32[]{:S(2)}) copy-start(bf16[4,128,2560]{2,1,0:T(8,128)(2,1)S(1)} %get-tuple-element.115.refs_2_) | copy-start | bytes 7864324
  113.7 76.6 %collective-permute-start.16 = (bf16[64,2560]{1,0:T(8,128)(2,1)S(1)}, bf16[64,2560]{1,0:T(8,128)(2,1)S(1)}, u32[]{:S(2)}, u32[]{:S(2)}) collective-permute-start(bf16[64,2560]{1,0:T(8,128)(2,1)S(1)} %get-tuple-element.122), channel_id=1, source_target_pairs={{0,496},{16,0},{32,16},{48,32},{64,48},{80,64},{96,80},{112,96},{1... | collective-permute-start | bytes 983048 | tf_op jit(solution)/shard_map/ppermute | solution.py:325
  115.6 74.7 %collective-permute-start.15 = (bf16[64,2560]{1,0:T(8,128)(2,1)S(1)}, bf16[64,2560]{1,0:T(8,128)(2,1)S(1)}, u32[]{:S(2)}, u32[]{:S(2)}) collective-permute-start(bf16[64,2560]{1,0:T(8,128)(2,1)S(1)} %get-tuple-element.121), channel_id=1, source_target_pairs={{0,496},{16,0},{32,16},{48,32},{64,48},{80,64},{96,80},{112,96},{1... | collective-permute-start | bytes 983048 | tf_op jit(solution)/shard_map/ppermute | solution.py:325
  117.8 4.0 %copy-start.3 = (bf16[512,2560]{1,0:T(8,128)(2,1)}, bf16[512,2560]{1,0:T(8,128)(2,1)S(1)}, u32[]{:S(2)}) copy-start(bf16[512,2560]{1,0:T(8,128)(2,1)S(1)} %get-tuple-element.50) | copy-start | bytes 7864324 | tf_op jit(solution)/shard_map/cond

commit v9 on v8

--- a/solution.py
+++ b/solution.py
@@ -31,10 +31,10 @@
     return lax.ppermute(value, "dp", dp_pairs(n_z, 0, 1))
 
 
-def ring_gather(shard, n_z):
+def ring_gather(shard, n_z, beside):
     index = lax.axis_index("dp")
     z, h = index // 2, index % 2
-    other = swapped(shard, n_z)
+    other, *beside = lax.optimization_barrier((swapped(shard, n_z), *beside))
     pair = jnp.stack([jnp.where(h == 0, shard, other), jnp.where(h == 0, other, shard)], axis=1)
     half = n_z // 2
     full = unset((2, n_z) + pair.shape[1:], pair.dtype)
@@ -49,7 +49,7 @@
         full = placed(full, right, -step)
         full = placed(full, left, step)
     right, left = shifted(right[:, :1], n_z, 1), shifted(left[:, 1:], n_z, -1)
-    return placed(full, jnp.concatenate([right, left], axis=1), half)
+    return placed(full, jnp.concatenate([right, left], axis=1), half), beside
 
 
 def empty_kernel(out_ref):
@@ -207,25 +207,34 @@
     )(levels, incoming, normed, inverse, maps, *forward, stack)
 
 
-def beside_kernel(left_ref, right_ref, out_ref):
-    lanes = left_ref.shape[1]
-    out_ref[:, :lanes] = left_ref[...]
-    out_ref[:, lanes:] = right_ref[...]
-
-
-def beside(left, right):
-    rows, lanes = left.shape
+def join_kernel(helps_ref, *refs):
+    down_ref, up_ref = refs[:2]
+    out_ref = refs[-1]
+    lanes = down_ref.shape[1]
+    out_ref[:, :lanes] = down_ref[...]
+    out_ref[:, lanes:] = up_ref[...]
+    if len(refs) == 4:
+        rank = lanes // 2
+        guest_ref = refs[2]
+
+        @pl.when(helps_ref[0] == 1)
+        def _():
+            out_ref[:, rank:lanes] = guest_ref[:, :rank]
+            out_ref[:, lanes + rank :] = guest_ref[:, rank:]
+
+
+def joined(helps, *parts):
+    rows, lanes = parts[0].shape
     run = rows // 4
-    block = pl.BlockSpec((run, lanes), lambda i: (i, 0))
-    return pl.pallas_call(
-        beside_kernel,
+    return pl.pallas_call(
+        join_kernel,
         grid=(rows // run,),
-        out_shape=jax.ShapeDtypeStruct((rows, 2 * lanes), left.dtype),
-        in_specs=[block, block],
+        out_shape=jax.ShapeDtypeStruct((rows, 2 * lanes), parts[0].dtype),
+        in_specs=[SCALAR] + [pl.BlockSpec((run, v.shape[1]), lambda i: (i, 0)) for v in parts],
         out_specs=pl.BlockSpec((run, 2 * lanes), lambda i: (i, 0)),
         compiler_params=LIMIT,
-        name="side_by_side",
-    )(left, right)
+        name="join_parts",
+    )(helps, *parts)
 
 
 def sum_kernel(moved_ref, out_ref):
@@ -249,27 +258,30 @@
     )(moved)
 
 
-def finish_kernel(total_ref, low_ref, high_ref, grad_ref, down_ref, up_ref):
+def finish_kernel(flags_ref, total_ref, guest_ref, low_ref, high_ref, grad_ref, down_ref, up_ref):
     rows, rank = low_ref.shape[0], down_ref.shape[3]
     grad_ref[0, :rows] = low_ref[...]
     grad_ref[0, rows:] = high_ref[...]
+    level = flags_ref[0]
     for i, out in enumerate((down_ref, up_ref)):
-        for j, level in enumerate((1, 0)):
-            at = (2 * i + j) * rank
-            out[level, 0] = total_ref[:, at : at + rank]
-
-
-def finish(total, low, high, share, rank):
+        at = 2 * i * rank
+        out[level, 0] = total_ref[:, at : at + rank]
+        own = total_ref[:, at + rank : at + 2 * rank]
+        own = jnp.where(flags_ref[1] == 1, jnp.zeros_like(own), own)
+        out[1 - level, 0] = own + guest_ref[:, i * rank : (i + 1) * rank]
+
+
+def finish(flags, total, guest, low, high, share, rank):
     rows, width = low.shape
     made = jax.ShapeDtypeStruct((2, 1, share, rank), F32)
     return pl.pallas_call(
         finish_kernel,
         out_shape=[jax.ShapeDtypeStruct((1, 2 * rows, width), low.dtype), made, made],
-        in_specs=[IN_VMEM] * 3,
+        in_specs=[SCALAR] + [IN_VMEM] * 4,
         out_specs=[IN_VMEM] * 3,
         compiler_params=LIMIT,
         name="finish",
-    )(total, low, high)
+    )(flags, total, guest, low, high)
 
 
 def on_device(saved_inputs, grad_in, adapter_down, adapter_up):
@@ -288,8 +300,8 @@
 
     def gather_two(down, up, x):
         shards = jnp.stack([shard_of(down, up, level) for level in range(2)])
-        full = ring_gather(shards, n_z)
-        return full.reshape(2, width, 2 * rank), *norms(x)
+        full, made = ring_gather(shards, n_z, norms(x))
+        return full.reshape(2, width, 2 * rank), *made
 
     def gather_one(down, up, x):
         shard = shard_of(down, up, 1)
@@ -315,6 +327,25 @@
         first_actives.append(active)
         moving.append(lax.ppermute(sent, "section", down_one))
     latents, slopes, actives = forward_rest(level_stack, normed, maps, grad_latent)
+    first_active = jnp.concatenate(first_actives)
+
+    def product(wide, narrow):
+        contract = (((0,), (0,)), ((), ()))
+        return lax.dot_general(wide, narrow, contract, preferred_element_type=F32).astype(BF16)
+
+    guest, helper = n_sec - 1, n_sec - 1 - n_sec // 4
+    is_guest, is_helper = position == guest, position == helper
+    helps = is_helper.astype(jnp.int32)[None]
+    first_latent = jnp.concatenate(grad_latents)
+
+    def guest_parts(lats, acts):
+        return joined(helps, product(normed[0], lats), product(grad_in[0], acts))
+
+    def no_parts(lats, acts):
+        return unset((width, 2 * rank), BF16)
+
+    parts = lax.cond(is_guest, guest_parts, no_parts, first_latent, first_active)
+    guest_in = lax.ppermute(parts, "section", [(guest, helper)])
     for tick in range(1, ticks):
         arrived, moving = moving, []
         for part in range(2):
@@ -326,31 +357,41 @@
 
     normed_all = normed.reshape(-1, width)
     grads_all = stack.reshape(-1, width)
-    actives = jnp.concatenate([jnp.concatenate(first_actives)[None], actives], axis=0)
-
-    def products(lats, acts):
-        contract = (((0,), (0,)), ((), ()))
-        down = lax.dot_general(normed_all, lats, contract, preferred_element_type=F32)
-        up = lax.dot_general(grads_all, acts, contract, preferred_element_type=F32)
-        both = beside(down.astype(BF16), up.astype(BF16))
-        moved = lax.all_to_all(both.reshape(n_dp, share, -1), "dp", 0, 0, tiled=True)
+    actives = jnp.concatenate([first_active[None], actives], axis=0)
+    grad_latents = jnp.concatenate(grad_latents).reshape(actives.shape)
+
+    same = (level_stack == level_stack[-1])[:, None, None]
+    zero = jnp.zeros((), BF16)
+
+    def summed_parts(parts):
+        moved = lax.all_to_all(parts.reshape(n_dp, share, -1), "dp", 0, 0, tiled=True)
         return summed(moved, 4 * rank)
 
-    def reduce_one(lats, acts):
-        return products(lats.reshape(-1, rank), acts.reshape(-1, rank))
-
-    def reduce_two(lats, acts):
-        level = level_stack[:, None, None]
-        zero = jnp.zeros((), BF16)
-
+    def reduce_one(lats, acts, guest_in):
+        def kept(value):
+            return jnp.where(same, value, zero).reshape(-1, rank)
+
+        return summed_parts(
+            joined(helps, product(normed_all, kept(lats)), product(grads_all, kept(acts)))
+        )
+
+    def reduce_two(lats, acts, guest_in):
         def split(value):
-            both = [jnp.where(level == 1, value, zero), jnp.where(level == 0, value, zero)]
+            both = [jnp.where(same, value, zero), jnp.where(same, zero, value)]
             return jnp.concatenate(both, axis=2).reshape(-1, 2 * rank)
 
-        return products(split(lats), split(acts))
-
-    total = lax.cond(two_layers, reduce_two, reduce_one, jnp.concatenate(grad_latents).reshape(actives.shape), actives)
-    grad_out, down_grad, up_grad = finish(total, *moving, share, rank)
+        return summed_parts(
+            joined(
+                helps, product(normed_all, split(lats)), product(grads_all, split(acts)), guest_in
+            )
+        )
+
+    twice = (two_layers & ~is_guest) | is_helper
+    total = lax.cond(twice, reduce_two, reduce_one, grad_latents, actives, guest_in)
+    extra = jnp.concatenate([total[:, rank : 2 * rank], total[:, 3 * rank :]], axis=1)
+    back = lax.ppermute(extra, "section", [(helper, guest)])
+    flags = jnp.stack([level_stack[-1], helps[0]])
+    grad_out, down_grad, up_grad = finish(flags, total, back, *moving, share, rank)
     return grad_out, jnp.swapaxes(down_grad, 2, 3), jnp.swapaxes(up_grad, 2, 3)
 
 

time: 192 us -> 204 us (1.062)
  Pallas kernels: 19.6 us -> 29.2 us
  starting transfers between devices: 58.4 us -> 63.7 us
  local copies, waits for them, and re-layouts: 2.74 us -> 5.12 us
  matrix products: 6.46 us -> 4.11 us
    ppermute x8, waiting for transfers between devices: 20.5 us -> 12.8 us  [on_device(): moving.append(lax.ppermute(sent, 'section', down_one))]
    ppermute x8, waiting for transfers between devices: 8.24 us -> 15.3 us  [shifted(): return lax.ppermute(value, 'dp', dp_pairs(n_z, step, 0))]
    pallas_call x8, Pallas kernels: 11.9 us -> 18.5 us  [tick_layer(): pl.pallas_call(functools.partial(tick_kernel, tick, part), grid_spec=pltp...]
    ppermute x0 -> x2, waiting for transfers between devices: none -> 4.68 us  [the longest x1 4.68 us: on_device(): back = lax.ppermute(extra, 'section', [(helper, guest)])]
    ppermute x1, waiting for transfers between devices: 6.54 us -> 1.96 us  [swapped(): return lax.ppermute(value, 'dp', dp_pairs(n_z, 0, 1))]
    ppermute x0 -> x2, starting transfers between devices: none -> 3.7 us  [the longest x1 2.4 us: on_device(): guest_in = lax.ppermute(parts, 'section', [(guest, helper)])]
    dot_general x2 -> x4, matrix products: 6.46 us -> 4.11 us  [product(): lax.dot_general(wide, narrow, contract, preferred_element_type=F32)]
    pallas_call x1, Pallas kernels: 1.59 us -> 3.86 us  [forward_rest(): pl.pallas_call(forward_kernel, grid_spec=pltpu.PrefetchScalarGridSpec(num...]
  transfers between devices with their start and end apart: 17 -> 19, of which waited for: 10 -> 9; matrix products, arithmetic and copies ran while one was open for 4% -> 3% of each run, Pallas kernels for 7% -> 12%
where the time goes in v9:
time: 204 us; the launch traced here: 202 us
  starting transfers between devices  63.7 us (31%)
  blocking collectives  63.3 us (31%)
  waiting for transfers between devices  34.7 us (17%)
  Pallas kernels  29.2 us (14%)
  local copies, waits for them, and re-layouts  5.12 us (3%)
  matrix products  4.11 us (2%)
    all_to_all x1, blocking collectives, summed_parts(): lax.all_to_all(parts.reshape(n_dp, share, -1), 'dp', 0, 0, tiled=True)  63.3 us
    ppermute x8, starting transfers between devices, shifted(): return lax.ppermute(value, 'dp', dp_pairs(n_z, step, 0))  32.5 us
    ppermute x8, starting transfers between devices, on_device(): moving.append(lax.ppermute(sent, 'section', down_one))  23.1 us
    pallas_call x8, Pallas kernels, tick_layer(): pl.pallas_call(functools.partial(tick_kernel, tick, part), grid_spec=pltp...  18.5 us
    ppermute x8, waiting for transfers between devices, shifted(): return lax.ppermute(value, 'dp', dp_pairs(n_z, step, 0))  15.3 us
    ppermute x8, waiting for transfers between devices, on_device(): moving.append(lax.ppermute(sent, 'section', down_one))  12.8 us
    ppermute x1, waiting for transfers between devices, on_device(): back = lax.ppermute(extra, 'section', [(helper, guest)])  4.68 us
    pallas_call x1, Pallas kernels, norms(): pl.pallas_call(norm_kernel, grid=(ticks,), out_shape=[jax.ShapeDtypeStruc...  4.47 us
  transfers between devices with their start and end apart: 19, of which 9 were waited for; matrix products, arithmetic and copies ran while one was open for 3% of the time, Pallas kernels for 12%

profile of v9, /device:TPU:63, one launch (start us, length us, event | category | flops | bytes accessed | tf_op | source)
XLA Modules:
  0.0 202.4 jit_solution(2977547715830129256)
XLA Ops:
  1.6 62.9 %conditional.3 = (bf16[2,2560,256]{2,1,0:T(8,128)(2,1)}, bf16[4,128,2560]{2,1,0:T(8,128)(2,1)}, f32[4,128,128]{2,1,0:T(8,128)}) conditional(s32[]{:T(128)} %convert_element_type.37, (bf16[2,128,160]{1,2,0:T(8,128)(2,1)S(1)}, bf16[2,128,160]{1,2,0:T(8,128)(2,1)S(1)}, bf16[4,1,128,2560]{3,2,1,0:T(8,128)(2,1)}) %tuple.64, ...), branch_computations={%region_0.1_spmd, %region_1.2_spmd} | conditional | flops 4297097216 | bytes 36898656 | solution.py:314
  1.6 4.4 %collective-permute-start = (bf16[2,160,256]{2,1,0:T(8,128)(2,1)S(1)}, bf16[2,160,256]{2,1,0:T(8,128)(2,1)S(1)}, u32[]{:S(2)}, u32[]{:S(2)}) collective-permute-start(bf16[2,160,256]{2,1,0:T(8,128)(2,1)S(1)} %pad_maximum_fusion.2), channel_id=1, source_target_pairs={{0,1},{1,0},{2,3},{3,2},{4,5},{5,4},{6,7},{7,6},{8,9},{9,8},{10,11... | collective-permute-start | bytes 491528 | tf_op jit(solution)/shard_map/cond/branch_1_fun/ppermute | solution.py:31
  6.1 4.5 %norms.3 = (bf16[4,128,2560]{2,1,0:T(8,128)(2,1)}, f32[4,128,128]{2,1,0:T(8,128)}) custom-call(bf16[4,1,128,2560]{3,2,1,0:T(8,128)(2,1)} %get-tuple-element.61.x_ref), custom_call_target="tpu_custom_call" | custom-call | flops 4294967296 | bytes 8388608 | tf_op jit(solution)/shard_map/cond/branch_1_fun/norms/pallas_call | solution.py:77
  10.6 2.0 collective-permute-done
  12.6 4.0 %collective-permute-start.1 = (bf16[2,2,160,256]{3,2,1,0:T(8,128)(2,1)S(1)}, bf16[2,2,160,256]{3,2,1,0:T(8,128)(2,1)}, u32[]{:S(2)}, u32[]{:S(2)}) collective-permute-start(bf16[2,2,160,256]{3,2,1,0:T(8,128)(2,1)S(1)} %pad_maximum_fusion.1), channel_id=1, source_target_pairs={{0,2},{1,3},{2,4},{3,5},{4,6},{5,7},{6,8},{7,9},{8,10},{9,11},{10,... | collective-permute-start | bytes 983048 | tf_op jit(solution)/shard_map/cond/branch_1_fun/ppermute | solution.py:27
  16.6 8.6 %collective-permute-start.2 = (bf16[2,2,160,256]{3,2,1,0:T(8,128)(2,1)S(1)}, bf16[2,2,160,256]{3,2,1,0:T(8,128)(2,1)}, u32[]{:S(2)}, u32[]{:S(2)}) collective-permute-start(bf16[2,2,160,256]{3,2,1,0:T(8,128)(2,1)S(1)} %pad_maximum_fusion.1), channel_id=1, source_target_pairs={{0,14},{1,15},{2,0},{3,1},{4,2},{5,3},{6,4},{7,5},{8,6},{9,7},{10,... | collective-permute-start | bytes 983048 | tf_op jit(solution)/shard_map/cond/branch_1_fun/ppermute | solution.py:27
  25.4 4.4 %collective-permute-done.1 = bf16[2,2,160,256]{3,2,1,0:T(8,128)(2,1)} collective-permute-done((bf16[2,2,160,256]{3,2,1,0:T(8,128)(2,1)S(1)}, bf16[2,2,160,256]{3,2,1,0:T(8,128)(2,1)}, u32[]{:S(2)}, u32[]{:S(2)}) %collective-permute-start.1) | collective-permute-done | bytes 327712 | tf_op jit(solution)/shard_map/cond/branch_1_fun/ppermute | solution.py:27
  29.8 1.9 collective-permute-start.3
  31.7 4.6 %collective-permute-start.4 = (bf16[2,2,160,256]{3,2,1,0:T(8,128)(2,1)}, bf16[2,2,160,256]{3,2,1,0:T(8,128)(2,1)S(1)}, u32[]{:S(2)}, u32[]{:S(2)}) collective-permute-start(bf16[2,2,160,256]{3,2,1,0:T(8,128)(2,1)} %collective-permute-done.2), channel_id=1, source_target_pairs={{0,14},{1,15},{2,0},{3,1},{4,2},{5,3},{6,4},{7,5},{8,6},{9,7},{10,... | collective-permute-start | bytes 983048 | tf_op jit(solution)/shard_map/cond/branch_1_fun/ppermute | solution.py:27
  36.3 1.0 bitcast_dynamic-update-slice_fusion.6
  37.3 1.0 bitcast_dynamic-update-slice_fusion.5
  38.3 1.7 collective-permute-done.3
  40.0 1.9 collective-permute-start.5
  42.0 4.6 %collective-permute-start.6 = (bf16[2,2,160,256]{3,2,1,0:T(8,128)(2,1)S(1)}, bf16[2,2,160,256]{3,2,1,0:T(8,128)(2,1)S(1)}, u32[]{:S(2)}, u32[]{:S(2)}) collective-permute-start(bf16[2,2,160,256]{3,2,1,0:T(8,128)(2,1)S(1)} %collective-permute-done.4), channel_id=1, source_target_pairs={{0,14},{1,15},{2,0},{3,1},{4,2},{5,3},{6,4},{7,5},{8,6},{9,7},{10,... | collective-permute-start | bytes 983048 | tf_op jit(solution)/shard_map/cond/branch_1_fun/ppermute | solution.py:27
  46.6 3.9 %collective-permute-done.6 = bf16[2,2,160,256]{3,2,1,0:T(8,128)(2,1)S(1)} collective-permute-done((bf16[2,2,160,256]{3,2,1,0:T(8,128)(2,1)S(1)}, bf16[2,2,160,256]{3,2,1,0:T(8,128)(2,1)S(1)}, u32[]{:S(2)}, u32[]{:S(2)}) %collective-permute-start.6) | collective-permute-done | bytes 327712 | tf_op jit(solution)/shard_map/cond/branch_1_fun/ppermute | solution.py:27
  50.5 5.0 %collective-permute-start.8 = (bf16[2,1,160,256]{3,2,1,0:T(8,128)(2,1)S(1)}, bf16[2,1,160,256]{3,2,1,0:T(8,128)(2,1)S(1)}, u32[]{:S(2)}, u32[]{:S(2)}) collective-permute-start(bf16[2,1,160,256]{3,2,1,0:T(8,128)(2,1)S(1)} %slice.36), channel_id=1, source_target_pairs={{0,14},{1,15},{2,0},{3,1},{4,2},{5,3},{6,4},{7,5},{8,6},{9,7},{10,... | collective-permute-start | bytes 491528 | tf_op jit(solution)/shard_map/cond/branch_1_fun/ppermute | solution.py:27
  55.6 1.9 collective-permute-start.7
  57.8 5.1 %collective-permute-done.7 = bf16[2,1,160,256]{3,2,1,0:T(8,128)(2,1)S(1)} collective-permute-done((bf16[2,1,160,256]{3,2,1,0:T(8,128)(2,1)S(1)}, bf16[2,1,160,256]{3,2,1,0:T(8,128)(2,1)S(1)}, u32[]{:S(2)}, u32[]{:S(2)}) %collective-permute-start.7) | collective-permute-done | bytes 163872 | tf_op jit(solution)/shard_map/cond/branch_1_fun/ppermute | solution.py:27
  62.9 1.5 copy-done.5
  64.5 3.1 %tick_layer.8 = (bf16[4,128,2560]{2,1,0:T(8,128)(2,1)}, bf16[64,2560]{1,0:T(8,128)(2,1)S(1)}, bf16[64,128]{1,0:T(8,128)(2,1)S(1)}, bf16[64,128]{1,0:T(8,128)(2,1)S(1)}) custom-call(s32[4]{0:T(128)S(1)} %pad_add_fusion.1.levels_ref, bf16[128,2560]{1,0:T(8,128)(2,1)} %bitcast.130, ...), custom_call_target="tpu_custom_call", output_to_operand_aliasing={{0}: (5, {})} | custom-call | flops 4294967296 | bytes 8388608 | tf_op jit(solution)/shard_map/tick_layer/pallas_call | solution.py:181
  67.6 7.9 %collective-permute-start.9 = (bf16[64,2560]{1,0:T(8,128)(2,1)S(1)}, bf16[64,2560]{1,0:T(8,128)(2,1)S(1)}, u32[]{:S(2)}, u32[]{:S(2)}) collective-permute-start(bf16[64,2560]{1,0:T(8,128)(2,1)S(1)} %get-tuple-element.129), channel_id=1, source_target_pairs={{0,496},{16,0},{32,16},{48,32},{64,48},{80,64},{96,80},{112,96},{1... | collective-permute-start | bytes 983048 | tf_op jit(solution)/shard_map/ppermute | solution.py:328
  75.6 2.1 %tick_layer.9 = (bf16[4,128,2560]{2,1,0:T(8,128)(2,1)}, bf16[64,2560]{1,0:T(8,128)(2,1)S(1)}, bf16[64,128]{1,0:T(8,128)(2,1)S(1)}, bf16[64,128]{1,0:T(8,128)(2,1)S(1)}) custom-call(s32[4]{0:T(128)S(1)} %pad_add_fusion.1.levels_ref, bf16[128,2560]{1,0:T(8,128)(2,1)S(1)} %bitcast.131, ...), custom_call_target="tpu_custom_call", output_to_operand_aliasing={{0}: (5, {})} | custom-call | flops 4294967296 | bytes 8388608 | tf_op jit(solution)/shard_map/tick_layer/pallas_call | solution.py:181
  77.6 3.6 %collective-permute-start.10 = (bf16[64,2560]{1,0:T(8,128)(2,1)S(1)}, bf16[64,2560]{1,0:T(8,128)(2,1)S(1)}, u32[]{:S(2)}, u32[]{:S(2)}) collective-permute-start(bf16[64,2560]{1,0:T(8,128)(2,1)S(1)} %get-tuple-element.134), channel_id=1, source_target_pairs={{0,496},{16,0},{32,16},{48,32},{64,48},{80,64},{96,80},{112,96},{1... | collective-permute-start | bytes 983048 | tf_op jit(solution)/shard_map/ppermute | solution.py:328
  81.3 2.1 %conditional.4 = (bf16[2560,256]{1,0:T(8,128)(2,1)S(1)}) conditional(s32[]{:T(128)} %convert_element_type.38, () %tuple.31, (bf16[4,128,2560]{2,1,0:T(8,128)(2,1)}, bf16[128,128]{1,0:T(8,128)(2,1)S(1)}, bf16[1,128,2560]{2,1,0:T(8,128)(2,1)S(1)}, bf16[128,128]{1,0:T(8,128)(2,1)S(1)}, s32[1]{0:T(128)}) %tuple.59), branch_computations={%region_2.3_spmd, %region_3.4_spmd} | conditional | flops 168427520 | bytes 2686984 | solution.py:347
  81.3 1.5 convolution_convert_fusion.1.refs_0_
  83.4 2.4 %collective-permute-start.15 = (bf16[2560,256]{1,0:T(8,128)(2,1)S(1)}, bf16[2560,256]{1,0:T(8,128)(2,1)}, u32[]{:S(2)}, u32[]{:S(2)}) collective-permute-start(bf16[2560,256]{1,0:T(8,128)(2,1)S(1)} %get-tuple-element.188), channel_id=1, source_target_pairs={{496,368},{497,369},{498,370},{499,371},{500,372},{501,373},{502,3... | collective-permute-start | bytes 3932168 | tf_op jit(solution)/shard_map/ppermute | solution.py:348
  85.8 3.9 %forward_rest.1 = (f32[3,128,128]{2,1,0:T(8,128)S(1)}, f32[3,128,128]{2,1,0:T(8,128)S(1)}, bf16[3,128,128]{2,1,0:T(8,128)(2,1)S(1)}) custom-call(s32[4]{0:T(128)S(1)} %pad_add_fusion.1.levels_ref, bf16[4,128,2560]{2,1,0:T(8,128)(2,1)} %get-tuple-element.123.normed_ref, bf16[2,2560,256]{2,1,0:T(8,128)(2,1)} %get-tuple-element.125.maps_ref, ...), custom_call_target="tpu_custom_call" | custom-call | flops 4294967296 | bytes 8388608 | tf_op jit(solution)/shard_map/forward_rest/pallas_call | solution.py:117
  89.9 3.2 %tick_layer.10 = (bf16[4,128,2560]{2,1,0:T(8,128)(2,1)}, bf16[64,2560]{1,0:T(8,128)(2,1)S(1)}, bf16[64,128]{1,0:T(8,128)(2,1)S(1)}) custom-call(s32[4]{0:T(128)S(1)} %pad_add_fusion.1.levels_ref, bf16[64,2560]{1,0:T(8,128)(2,1)S(1)} %collective-permute-done.9.incoming_ref, ...), custom_call_target="tpu_custom_call", output_to_operand_aliasing={{0}: (7, {})} | custom-call | flops 4294967296 | bytes 8388608 | tf_op jit(solution)/shard_map/tick_layer/pallas_call | solution.py:181
  93.1 1.9 collective-permute-start.11
  95.0 2.0 %tick_layer.11 = (bf16[4,128,2560]{2,1,0:T(8,128)(2,1)}, bf16[64,2560]{1,0:T(8,128)(2,1)S(1)}, bf16[64,128]{1,0:T(8,128)(2,1)S(1)}) custom-call(s32[4]{0:T(128)S(1)} %pad_add_fusion.1.levels_ref, bf16[64,2560]{1,0:T(8,128)(2,1)S(1)} %collective-permute-done.10.incoming_ref, bf16[4,128,2560]{2,1,0:T(8,128)(2,1)S(1)} %copy-done.3, ...), custom_call_target="tpu_custom_call", output_to_operand_aliasing={{0}: (7, {})} | custom-call | flops 4294967296 | bytes 8388608 | tf_op jit(solution)/shard_map/tick_layer/pallas_call | solution.py:181
  97.1 1.9 collective-permute-start.12
  99.1 6.3 %collective-permute-done.11.incoming_ref = bf16[64,2560]{1,0:T(8,128)(2,1)S(1)} collective-permute-done((bf16[64,2560]{1,0:T(8,128)(2,1)S(1)}, bf16[64,2560]{1,0:T(8,128)(2,1)S(1)}, u32[]{:S(2)}, u32[]{:S(2)}) %collective-permute-start.11) | collective-permute-done | bytes 327712 | tf_op jit(solution)/shard_map/ppermute | solution.py:356
  105.4 2.0 %tick_layer.12 = (bf16[4,128,2560]{2,1,0:T(8,128)(2,1)}, bf16[64,2560]{1,0:T(8,128)(2,1)S(1)}, bf16[64,128]{1,0:T(8,128)(2,1)S(1)}) custom-call(s32[4]{0:T(128)S(1)} %pad_add_fusion.1.levels_ref, bf16[64,2560]{1,0:T(8,128)(2,1)S(1)} %collective-permute-done.11.incoming_ref, bf16[4,128,2560]{2,1,0:T(8,128)(2,1)S(1)} %copy-done.3, ...), custom_call_target="tpu_custom_call", output_to_operand_aliasing={{0}: (7, {})} | custom-call | flops 4294967296 | bytes 8388608 | tf_op jit(solution)/shard_map/tick_layer/pallas_call | solution.py:181
  107.4 1.9 collective-permute-start.13
  109.4 2.0 %tick_layer.13 = (bf16[4,128,2560]{2,1,0:T(8,128)(2,1)}, bf16[64,2560]{1,0:T(8,128)(2,1)S(1)}, bf16[64,128]{1,0:T(8,128)(2,1)S(1)}) custom-call(s32[4]{0:T(128)S(1)} %pad_add_fusion.1.levels_ref, bf16[64,2560]{1,0:T(8,128)(2,1)S(1)} %collective-permute-done.12.incoming_ref, bf16[4,128,2560]{2,1,0:T(8,128)(2,1)S(1)} %copy-done.3, ...), custom_call_target="tpu_custom_call", output_to_operand_aliasing={{0}: (7, {})} | custom-call | flops 4294967296 | bytes 8388608 | tf_op jit(solution)/shard_map/tick_layer/pallas_call | solution.py:181
  111.4 1.9 collective-permute-start.14
  113.4 6.3 %collective-permute-done.13.incoming_ref = bf16[64,2560]{1,0:T(8,128)(2,1)S(1)} collective-permute-done((bf16[64,2560]{1,0:T(8,128)(2,1)S(1)}, bf16[64,2560]{1,0:T(8,128)(2,1)S(1)}, u32[]{:S(2)}, u32[]{:S(2)}) %collective-permute-start.13) | collective-permute-done | bytes 327712 | tf_op jit(solution)/shard_map/ppermute | solution.py:356
  119.7 2.0 %tick_layer.14 = (bf16[4,128,2560]{2,1,0:T(8,128)(2,1)}, bf16[64,2560]{1,0:T(8,128)(2,1)S(1)}, bf16[64,128]{1,0:T(8,128)(2,1)S(1)}) custom-call(s32[4]{0:T(128)S(1)} %pad_add_fusion.1.levels_ref, bf16[64,2560]{1,0:T(8,128)(2,1)S(1)} %collective-permute-done.13.incoming_ref, bf16[4,128,2560]{2,1,0:T(8,128)(2,1)S(1)} %copy-done.3, ...), custom_call_target="tpu_custom_call", output_to_operand_aliasing={{0}: (7, {})} | custom-call | flops 4294967296 | bytes 8388608 | tf_op jit(solution)/shard_map/tick_layer/pallas_call | solution.py:181
  121.8 1.9 collective-permute-start.17
  123.7 2.0 %tick_layer.15 = (bf16[4,128,2560]{2,1,0:T(8,128)(2,1)}, bf16[64,2560]{1,0:T(8,128)(2,1)S(1)}, bf16[64,128]{1,0:T(8,128)(2,1)S(1)}) custom-call(s32[4]{0:T(128)S(1)} %pad_add_fusion.1.levels_ref, bf16[64,2560]{1,0:T(8,128)(2,1)S(1)} %collective-permute-done.14.incoming_ref, bf16[4,128,2560]{2,1,0:T(8,128)(2,1)S(1)} %copy-done.3, ...), custom_call_target="tpu_custom_call", output_to_operand_aliasing={{0}: (7, {})} | custom-call | flops 4294967296 | bytes 8388608 | tf_op jit(solution)/shard_map/tick_layer/pallas_call | solution.py:181
  125.8 1.9 collective-permute-start.18
  127.7 66.9 %conditional.5 = (f32[160,512]{1,0:T(8,128)S(1)}) conditional(s32[]{:T(128)} %convert_element_type.36, (pred[4,1,1]{0,2,1:T(4,128)(4,1)S(1)}, bf16[4,128,128]{2,1,0:T(8,128)(2,1)S(1)}, bf16[512,2560]{1,0:T(8,128)(2,1)S(1)}, bf16[4,128,128]{2,1,0:T(8,128)(2,1)S(1)}, bf16[512,2560]{1,0:T(8,128)(2,1)}, /*index=5*/s32[1]{0:T(128)}) %tuple.60, ...), branch_computations={%region_4.5_spmd, %region_5.6_spmd} | conditional | flops 1344798720 | bytes 36438084 | solution.py:390
  127.9 1.1 fusion.4.refs_0_
  129.5 1.2 fusion.5.refs_1_
  131.0 63.3 %all_to_all.12.moved_ref = bf16[16,160,256]{2,1,0:T(8,128)(2,1)S(1)} all-to-all(bf16[16,160,256]{2,1,0:T(8,128)(2,1)S(1)} %bitcast.121), channel_id=1, replica_groups=mesh['section'=32,'dp'=16] {'dp'}, dimensions={0} | all-to-all | bytes 2621440 | tf_op jit(solution)/shard_map/cond/branch_0_fun/all_to_all | solution.py:367
  194.7 1.3 collective-permute-start.16
  196.1 4.7 %collective-permute-done.16.guest_ref = f32[160,256]{1,0:T(8,128)S(1)} collective-permute-done((f32[160,256]{1,0:T(8,128)S(1)}, f32[160,256]{1,0:T(8,128)S(1)}, u32[]{:S(2)}, u32[]{:S(2)}) %collective-permute-start.16) | collective-permute-done | bytes 163872 | tf_op jit(solution)/shard_map/ppermute | solution.py:392
  200.8 1.6 finish.1
  (65 shorter events, 3.6 us)
Async XLA Ops:
  0.6 0.9 copy-start.9
  0.6 0.9 copy-start.10
  1.6 10.9 %collective-permute-start = (bf16[2,160,256]{2,1,0:T(8,128)(2,1)S(1)}, bf16[2,160,256]{2,1,0:T(8,128)(2,1)S(1)}, u32[]{:S(2)}, u32[]{:S(2)}) collective-permute-start(bf16[2,160,256]{2,1,0:T(8,128)(2,1)S(1)} %pad_maximum_fusion.2), channel_id=1, source_target_pairs={{0,1},{1,0},{2,3},{3,2},{4,5},{5,4},{6,7},{7,6},{8,9},{9,8},{10,11... | collective-permute-start | bytes 491528 | tf_op jit(solution)/shard_map/cond/branch_1_fun/ppermute | solution.py:31
  12.6 17.2 %collective-permute-start.1 = (bf16[2,2,160,256]{3,2,1,0:T(8,128)(2,1)S(1)}, bf16[2,2,160,256]{3,2,1,0:T(8,128)(2,1)}, u32[]{:S(2)}, u32[]{:S(2)}) collective-permute-start(bf16[2,2,160,256]{3,2,1,0:T(8,128)(2,1)S(1)} %pad_maximum_fusion.1), channel_id=1, source_target_pairs={{0,2},{1,3},{2,4},{3,5},{4,6},{5,7},{6,8},{7,9},{8,10},{9,11},{10,... | collective-permute-start | bytes 983048 | tf_op jit(solution)/shard_map/cond/branch_1_fun/ppermute | solution.py:27
  16.6 15.1 %collective-permute-start.2 = (bf16[2,2,160,256]{3,2,1,0:T(8,128)(2,1)S(1)}, bf16[2,2,160,256]{3,2,1,0:T(8,128)(2,1)}, u32[]{:S(2)}, u32[]{:S(2)}) collective-permute-start(bf16[2,2,160,256]{3,2,1,0:T(8,128)(2,1)S(1)} %pad_maximum_fusion.1), channel_id=1, source_target_pairs={{0,14},{1,15},{2,0},{3,1},{4,2},{5,3},{6,4},{7,5},{8,6},{9,7},{10,... | collective-permute-start | bytes 983048 | tf_op jit(solution)/shard_map/cond/branch_1_fun/ppermute | solution.py:27
  29.8 10.3 %collective-permute-start.3 = (bf16[2,2,160,256]{3,2,1,0:T(8,128)(2,1)}, bf16[2,2,160,256]{3,2,1,0:T(8,128)(2,1)S(1)}, u32[]{:S(2)}, u32[]{:S(2)}) collective-permute-start(bf16[2,2,160,256]{3,2,1,0:T(8,128)(2,1)} %collective-permute-done.1), channel_id=1, source_target_pairs={{0,2},{1,3},{2,4},{3,5},{4,6},{5,7},{6,8},{7,9},{8,10},{9,11},{10,... | collective-permute-start | bytes 983048 | tf_op jit(solution)/shard_map/cond/branch_1_fun/ppermute | solution.py:27
  31.7 10.3 %collective-permute-start.4 = (bf16[2,2,160,256]{3,2,1,0:T(8,128)(2,1)}, bf16[2,2,160,256]{3,2,1,0:T(8,128)(2,1)S(1)}, u32[]{:S(2)}, u32[]{:S(2)}) collective-permute-start(bf16[2,2,160,256]{3,2,1,0:T(8,128)(2,1)} %collective-permute-done.2), channel_id=1, source_target_pairs={{0,14},{1,15},{2,0},{3,1},{4,2},{5,3},{6,4},{7,5},{8,6},{9,7},{10,... | collective-permute-start | bytes 983048 | tf_op jit(solution)/shard_map/cond/branch_1_fun/ppermute | solution.py:27
  40.0 15.6 %collective-permute-start.5 = (bf16[2,2,160,256]{3,2,1,0:T(8,128)(2,1)S(1)}, bf16[2,2,160,256]{3,2,1,0:T(8,128)(2,1)S(1)}, u32[]{:S(2)}, u32[]{:S(2)}) collective-permute-start(bf16[2,2,160,256]{3,2,1,0:T(8,128)(2,1)S(1)} %collective-permute-done.3), channel_id=1, source_target_pairs={{0,2},{1,3},{2,4},{3,5},{4,6},{5,7},{6,8},{7,9},{8,10},{9,11},{10,... | collective-permute-start | bytes 983048 | tf_op jit(solution)/shard_map/cond/branch_1_fun/ppermute | solution.py:27
  42.0 8.6 %collective-permute-start.6 = (bf16[2,2,160,256]{3,2,1,0:T(8,128)(2,1)S(1)}, bf16[2,2,160,256]{3,2,1,0:T(8,128)(2,1)S(1)}, u32[]{:S(2)}, u32[]{:S(2)}) collective-permute-start(bf16[2,2,160,256]{3,2,1,0:T(8,128)(2,1)S(1)} %collective-permute-done.4), channel_id=1, source_target_pairs={{0,14},{1,15},{2,0},{3,1},{4,2},{5,3},{6,4},{7,5},{8,6},{9,7},{10,... | collective-permute-start | bytes 983048 | tf_op jit(solution)/shard_map/cond/branch_1_fun/ppermute | solution.py:27
  50.5 7.3 %collective-permute-start.8 = (bf16[2,1,160,256]{3,2,1,0:T(8,128)(2,1)S(1)}, bf16[2,1,160,256]{3,2,1,0:T(8,128)(2,1)S(1)}, u32[]{:S(2)}, u32[]{:S(2)}) collective-permute-start(bf16[2,1,160,256]{3,2,1,0:T(8,128)(2,1)S(1)} %slice.36), channel_id=1, source_target_pairs={{0,14},{1,15},{2,0},{3,1},{4,2},{5,3},{6,4},{7,5},{8,6},{9,7},{10,... | collective-permute-start | bytes 491528 | tf_op jit(solution)/shard_map/cond/branch_1_fun/ppermute | solution.py:27
  55.6 7.3 %collective-permute-start.7 = (bf16[2,1,160,256]{3,2,1,0:T(8,128)(2,1)S(1)}, bf16[2,1,160,256]{3,2,1,0:T(8,128)(2,1)S(1)}, u32[]{:S(2)}, u32[]{:S(2)}) collective-permute-start(bf16[2,1,160,256]{3,2,1,0:T(8,128)(2,1)S(1)} %slice.35), channel_id=1, source_target_pairs={{0,2},{1,3},{2,4},{3,5},{4,6},{5,7},{6,8},{7,9},{8,10},{9,11},{10,... | collective-permute-start | bytes 491528 | tf_op jit(solution)/shard_map/cond/branch_1_fun/ppermute | solution.py:27
  62.9 1.5 copy-start.5
  64.5 11.0 %copy-start.2 = (bf16[4,128,2560]{2,1,0:T(8,128)(2,1)S(1)}, bf16[4,128,2560]{2,1,0:T(8,128)(2,1)}, u32[]{:S(2)}) copy-start(bf16[4,128,2560]{2,1,0:T(8,128)(2,1)} %get-tuple-element.123.normed_ref) | copy-start | bytes 7864324
  64.5 11.1 %copy-start.6 = (bf16[2,2560,256]{2,1,0:T(8,128)(2,1)S(1)}, bf16[2,2560,256]{2,1,0:T(8,128)(2,1)}, u32[]{:S(2)}) copy-start(bf16[2,2560,256]{2,1,0:T(8,128)(2,1)} %get-tuple-element.125.maps_ref) | copy-start | bytes 7864324
  64.5 11.1 %copy-start.8 = (bf16[1,128,2560]{2,1,0:T(8,128)(2,1)S(1)}, bf16[1,128,2560]{2,1,0:T(8,128)(2,1)}, u32[]{:S(2)}) copy-start(bf16[1,128,2560]{2,1,0:T(8,128)(2,1)} %param.11) | copy-start | bytes 1966084
  67.6 22.3 %collective-permute-start.9 = (bf16[64,2560]{1,0:T(8,128)(2,1)S(1)}, bf16[64,2560]{1,0:T(8,128)(2,1)S(1)}, u32[]{:S(2)}, u32[]{:S(2)}) collective-permute-start(bf16[64,2560]{1,0:T(8,128)(2,1)S(1)} %get-tuple-element.129), channel_id=1, source_target_pairs={{0,496},{16,0},{32,16},{48,32},{64,48},{80,64},{96,80},{112,96},{1... | collective-permute-start | bytes 983048 | tf_op jit(solution)/shard_map/ppermute | solution.py:328
  77.6 17.4 %collective-permute-start.10 = (bf16[64,2560]{1,0:T(8,128)(2,1)S(1)}, bf16[64,2560]{1,0:T(8,128)(2,1)S(1)}, u32[]{:S(2)}, u32[]{:S(2)}) collective-permute-start(bf16[64,2560]{1,0:T(8,128)(2,1)S(1)} %get-tuple-element.134), channel_id=1, source_target_pairs={{0,496},{16,0},{32,16},{48,32},{64,48},{80,64},{96,80},{112,96},{1... | collective-permute-start | bytes 983048 | tf_op jit(solution)/shard_map/ppermute | solution.py:328
  83.4 44.3 %collective-permute-start.15 = (bf16[2560,256]{1,0:T(8,128)(2,1)S(1)}, bf16[2560,256]{1,0:T(8,128)(2,1)}, u32[]{:S(2)}, u32[]{:S(2)}) collective-permute-start(bf16[2560,256]{1,0:T(8,128)(2,1)S(1)} %get-tuple-element.188), channel_id=1, source_target_pairs={{496,368},{497,369},{498,370},{499,371},{500,372},{501,373},{502,3... | collective-permute-start | bytes 3932168 | tf_op jit(solution)/shard_map/ppermute | solution.py:348
  89.9 5.2 %copy-start.3 = (bf16[4,128,2560]{2,1,0:T(8,128)(2,1)S(1)}, bf16[4,128,2560]{2,1,0:T(8,128)(2,1)}, u32[]{:S(2)}) copy-start(bf16[4,128,2560]{2,1,0:T(8,128)(2,1)} %get-tuple-element.123.normed_ref) | copy-start | bytes 7864324
  89.9 5.2 %copy-start.7 = (bf16[2,2560,256]{2,1,0:T(8,128)(2,1)S(1)}, bf16[2,2560,256]{2,1,0:T(8,128)(2,1)}, u32[]{:S(2)}) copy-start(bf16[2,2560,256]{2,1,0:T(8,128)(2,1)} %get-tuple-element.125.maps_ref) | copy-start | bytes 7864324
  93.1 12.3 %collective-permute-start.11 = (bf16[64,2560]{1,0:T(8,128)(2,1)S(1)}, bf16[64,2560]{1,0:T(8,128)(2,1)S(1)}, u32[]{:S(2)}, u32[]{:S(2)}) collective-permute-start(bf16[64,2560]{1,0:T(8,128)(2,1)S(1)} %get-tuple-element.137), channel_id=1, source_target_pairs={{0,496},{16,0},{32,16},{48,32},{64,48},{80,64},{96,80},{112,96},{1... | collective-permute-start | bytes 983048 | tf_op jit(solution)/shard_map/ppermute | solution.py:356
  97.1 12.3 %collective-permute-start.12 = (bf16[64,2560]{1,0:T(8,128)(2,1)S(1)}, bf16[64,2560]{1,0:T(8,128)(2,1)S(1)}, u32[]{:S(2)}, u32[]{:S(2)}) collective-permute-start(bf16[64,2560]{1,0:T(8,128)(2,1)S(1)} %get-tuple-element.140), channel_id=1, source_target_pairs={{0,496},{16,0},{32,16},{48,32},{64,48},{80,64},{96,80},{112,96},{1... | collective-permute-start | bytes 983048 | tf_op jit(solution)/shard_map/ppermute | solution.py:356
  107.4 12.3 %collective-permute-start.13 = (bf16[64,2560]{1,0:T(8,128)(2,1)S(1)}, bf16[64,2560]{1,0:T(8,128)(2,1)S(1)}, u32[]{:S(2)}, u32[]{:S(2)}) collective-permute-start(bf16[64,2560]{1,0:T(8,128)(2,1)S(1)} %get-tuple-element.143), channel_id=1, source_target_pairs={{0,496},{16,0},{32,16},{48,32},{64,48},{80,64},{96,80},{112,96},{1... | collective-permute-start | bytes 983048 | tf_op jit(solution)/shard_map/ppermute | solution.py:356
  111.4 12.3 %collective-permute-start.14 = (bf16[64,2560]{1,0:T(8,128)(2,1)S(1)}, bf16[64,2560]{1,0:T(8,128)(2,1)S(1)}, u32[]{:S(2)}, u32[]{:S(2)}) collective-permute-start(bf16[64,2560]{1,0:T(8,128)(2,1)S(1)} %get-tuple-element.146), channel_id=1, source_target_pairs={{0,496},{16,0},{32,16},{48,32},{64,48},{80,64},{96,80},{112,96},{1... | collective-permute-start | bytes 983048 | tf_op jit(solution)/shard_map/ppermute | solution.py:356
  121.8 74.3 %collective-permute-start.17 = (bf16[64,2560]{1,0:T(8,128)(2,1)S(1)}, bf16[64,2560]{1,0:T(8,128)(2,1)S(1)}, u32[]{:S(2)}, u32[]{:S(2)}) collective-permute-start(bf16[64,2560]{1,0:T(8,128)(2,1)S(1)} %get-tuple-element.153), channel_id=1, source_target_pairs={{0,496},{16,0},{32,16},{48,32},{64,48},{80,64},{96,80},{112,96},{1... | collective-permute-start | bytes 983048 | tf_op jit(solution)/shard_map/ppermute | solution.py:356
  125.8 70.3 %collective-permute-start.18 = (bf16[64,2560]{1,0:T(8,128)(2,1)S(1)}, bf16[64,2560]{1,0:T(8,128)(2,1)S(1)}, u32[]{:S(2)}, u32[]{:S(2)}) collective-permute-start(bf16[64,2560]{1,0:T(8,128)(2,1)S(1)} %get-tuple-element.154), channel_id=1, source_target_pairs={{0,496},{16,0},{32,16},{48,32},{64,48},{80,64},{96,80},{112,96},{1... | collective-permute-start | bytes 983048 | tf_op jit(solution)/shard_map/ppermute | solution.py:356
  127.8 1.7 copy-start
  194.7 6.1 %collective-permute-start.16 = (f32[160,256]{1,0:T(8,128)S(1)}, f32[160,256]{1,0:T(8,128)S(1)}, u32[]{:S(2)}, u32[]{:S(2)}) collective-permute-start(f32[160,256]{1,0:T(8,128)S(1)} %pad_maximum_fusion.5), channel_id=1, source_target_pairs={{368,496},{369,497},{370,498},{371,499},{372,500},{373,501},{374,5... | collective-permute-start | bytes 491528 | tf_op jit(solution)/shard_map/ppermute | solution.py:392

commit v10 on v8

--- a/solution.py
+++ b/solution.py
@@ -34,22 +34,33 @@
 def ring_gather(shard, n_z):
     index = lax.axis_index("dp")
     z, h = index // 2, index % 2
+    half = n_z // 2
+    full = unset((2, n_z, 2) + shard.shape[1:], shard.dtype)
+
+    def placed(full, piece, offset, side):
+        at = (0, (z + offset) % n_z, side, 0, 0)
+        return lax.dynamic_update_slice(full, piece[:, None, None], at)
+
     other = swapped(shard, n_z)
-    pair = jnp.stack([jnp.where(h == 0, shard, other), jnp.where(h == 0, other, shard)], axis=1)
-    half = n_z // 2
-    full = unset((2, n_z) + pair.shape[1:], pair.dtype)
-
-    def placed(full, piece, offset):
-        return lax.dynamic_update_slice(full, piece[:, None], (0, (z + offset) % n_z, 0, 0, 0))
-
-    full = placed(full, pair, 0)
-    right, left = pair, pair
-    for step in range(1, half):
+    far = shifted(shard, n_z, half)
+    right, left = shifted(shard, n_z, 1), shifted(shard, n_z, -1)
+    full = placed(full, shard, 0, h)
+    full = placed(full, right, -1, h)
+    full = placed(full, left, 1, h)
+    full = placed(full, other, 0, 1 - h)
+    full = placed(full, far, half, h)
+    right, left = jnp.stack([right, other]), jnp.stack([left, other])
+    for step in range(2, half):
         right, left = shifted(right, n_z, 1), shifted(left, n_z, -1)
-        full = placed(full, right, -step)
-        full = placed(full, left, step)
-    right, left = shifted(right[:, :1], n_z, 1), shifted(left[:, 1:], n_z, -1)
-    return placed(full, jnp.concatenate([right, left], axis=1), half)
+        if step == 2:
+            far = swapped(far, n_z)
+        for value, sign in ((right, -1), (left, 1)):
+            full = placed(full, value[0], sign * step, h)
+            full = placed(full, value[1], sign * (step - 1), 1 - h)
+    full = placed(full, far, half, 1 - h)
+    right, left = shifted(right[1], n_z, 1), shifted(left[1], n_z, -1)
+    full = placed(full, right, 1 - half, 1 - h)
+    return placed(full, left, half - 1, 1 - h)
 
 
 def empty_kernel(out_ref):

time: 192 us -> 221 us (1.15)
  local copies, waits for them, and re-layouts: 2.74 us -> 15 us
  starting transfers between devices: 58.4 us -> 68 us
  waiting for transfers between devices: 35.3 us -> 40.2 us
    dynamic_update_slice x6 -> x15, local copies, waits for them, and re-layouts: 0.17 us -> 13.9 us  [placed(): return lax.dynamic_update_slice(full, piece[:, None, None], at)]
    ppermute x1 -> x2, waiting for transfers between devices: 6.54 us -> 16.4 us  [swapped(): return lax.ppermute(value, 'dp', dp_pairs(n_z, 0, 1))]
    ppermute x1 -> x2, starting transfers between devices: 4.42 us -> 12.5 us  [swapped(): return lax.ppermute(value, 'dp', dp_pairs(n_z, 0, 1))]
    ppermute x8 -> x9, waiting for transfers between devices: 8.24 us -> 2.03 us  [shifted(): return lax.ppermute(value, 'dp', dp_pairs(n_z, step, 0))]
    ppermute x8 -> x9, starting transfers between devices: 32.1 us -> 37.3 us  [shifted(): return lax.ppermute(value, 'dp', dp_pairs(n_z, step, 0))]
    ppermute x8, starting transfers between devices: 22 us -> 18.2 us  [on_device(): moving.append(lax.ppermute(sent, 'section', down_one))]
  transfers between devices with their start and end apart: 17 -> 19, of which waited for: 10 -> 9; matrix products, arithmetic and copies ran while one was open for 4% -> 10% of each run, Pallas kernels for 7% -> 6%
where the time goes in v10:
time: 221 us; the launch traced here: 220 us
  starting transfers between devices  68 us (31%)
  blocking collectives  66.1 us (30%)
  waiting for transfers between devices  40.2 us (18%)
  Pallas kernels  19.5 us (9%)
  local copies, waits for them, and re-layouts  15 us (7%)
  matrix products  6.46 us (3%)
  other arithmetic  2.94 us (1%)
    all_to_all x1, blocking collectives, products(): lax.all_to_all(both.reshape(n_dp, share, -1), 'dp', 0, 0, tiled=True)  66.1 us
    ppermute x9, starting transfers between devices, shifted(): return lax.ppermute(value, 'dp', dp_pairs(n_z, step, 0))  37.3 us
    ppermute x8, waiting for transfers between devices, on_device(): moving.append(lax.ppermute(sent, 'section', down_one))  21.8 us
    ppermute x8, starting transfers between devices, on_device(): moving.append(lax.ppermute(sent, 'section', down_one))  18.2 us
    ppermute x2, waiting for transfers between devices, swapped(): return lax.ppermute(value, 'dp', dp_pairs(n_z, 0, 1))  16.4 us
    dynamic_update_slice x15, local copies, waits for them, and re-layouts, placed(): return lax.dynamic_update_slice(full, piece[:, None, None], at)  13.9 us
    ppermute x2, starting transfers between devices, swapped(): return lax.ppermute(value, 'dp', dp_pairs(n_z, 0, 1))  12.5 us
    pallas_call x8, Pallas kernels, tick_layer(): pl.pallas_call(functools.partial(tick_kernel, tick, part), grid_spec=pltp...  11.9 us
  transfers between devices with their start and end apart: 19, of which 9 were waited for; matrix products, arithmetic and copies ran while one was open for 10% of the time, Pallas kernels for 6%

profile of v10, /device:TPU:63, one launch (start us, length us, event | category | flops | bytes accessed | tf_op | source)
XLA Modules:
  0.0 219.8 jit_solution(11639681102598018908)
XLA Ops:
  1.6 89.3 %conditional.2 = (bf16[2,2560,256]{2,1,0:T(8,128)(2,1)}, bf16[4,128,2560]{2,1,0:T(8,128)(2,1)}, f32[4,128,128]{2,1,0:T(8,128)S(1)}) conditional(s32[]{:T(128)} %convert_element_type.20, (bf16[2,128,160]{1,2,0:T(8,128)(2,1)S(1)}, bf16[2,128,160]{1,2,0:T(8,128)(2,1)S(1)}, bf16[4,1,128,2560]{3,2,1,0:T(8,128)(2,1)}) %tuple.46, ...), branch_computations={%region_0.1_spmd, %region_1.2_spmd} | conditional | flops 4296032256 | bytes 27297880 | solution.py:313
  2.3 4.0 %collective-permute-start = (bf16[2,160,256]{2,1,0:T(8,128)(2,1)}, bf16[2,160,256]{2,1,0:T(8,128)(2,1)}, u32[]{:S(2)}, u32[]{:S(2)}) collective-permute-start(bf16[2,160,256]{2,1,0:T(8,128)(2,1)} %pad_maximum_fusion.3), channel_id=1, source_target_pairs={{0,2},{1,3},{2,4},{3,5},{4,6},{5,7},{6,8},{7,9},{8,10},{9,11},{10,... | collective-permute-start | bytes 491528 | tf_op jit(solution)/shard_map/cond/branch_1_fun/ppermute | solution.py:27
  6.3 8.6 %collective-permute-start.1 = (bf16[2,160,256]{2,1,0:T(8,128)(2,1)}, bf16[2,160,256]{2,1,0:T(8,128)(2,1)}, u32[]{:S(2)}, u32[]{:S(2)}) collective-permute-start(bf16[2,160,256]{2,1,0:T(8,128)(2,1)} %pad_maximum_fusion.3), channel_id=1, source_target_pairs={{0,14},{1,15},{2,0},{3,1},{4,2},{5,3},{6,4},{7,5},{8,6},{9,7},{10,... | collective-permute-start | bytes 491528 | tf_op jit(solution)/shard_map/cond/branch_1_fun/ppermute | solution.py:27
  14.9 4.4 %collective-permute-start.2 = (bf16[2,160,256]{2,1,0:T(8,128)(2,1)}, bf16[2,160,256]{2,1,0:T(8,128)(2,1)}, u32[]{:S(2)}, u32[]{:S(2)}) collective-permute-start(bf16[2,160,256]{2,1,0:T(8,128)(2,1)} %pad_maximum_fusion.3), channel_id=1, source_target_pairs={{0,1},{1,0},{2,3},{3,2},{4,5},{5,4},{6,7},{7,6},{8,9},{9,8},{10,11... | collective-permute-start | bytes 491528 | tf_op jit(solution)/shard_map/cond/branch_1_fun/ppermute | solution.py:31
  19.3 4.5 %collective-permute-start.3 = (bf16[2,160,256]{2,1,0:T(8,128)(2,1)}, bf16[2,160,256]{2,1,0:T(8,128)(2,1)}, u32[]{:S(2)}, u32[]{:S(2)}) collective-permute-start(bf16[2,160,256]{2,1,0:T(8,128)(2,1)} %pad_maximum_fusion.3), channel_id=1, source_target_pairs={{0,8},{1,9},{2,10},{3,11},{4,12},{5,13},{6,14},{7,15},{8,0},{9,1},... | collective-permute-start | bytes 491528 | tf_op jit(solution)/shard_map/cond/branch_1_fun/ppermute | solution.py:27
  23.9 4.4 %norms.3 = (bf16[4,128,2560]{2,1,0:T(8,128)(2,1)}, f32[4,128,128]{2,1,0:T(8,128)}) custom-call(bf16[4,1,128,2560]{3,2,1,0:T(8,128)(2,1)} %get-tuple-element.41.x_ref), custom_call_target="tpu_custom_call" | custom-call | flops 4294967296 | bytes 8388608 | tf_op jit(solution)/shard_map/cond/branch_1_fun/norms/pallas_call | solution.py:88
  29.0 16.4 %collective-permute-done.2 = bf16[2,160,256]{2,1,0:T(8,128)(2,1)} collective-permute-done((bf16[2,160,256]{2,1,0:T(8,128)(2,1)}, bf16[2,160,256]{2,1,0:T(8,128)(2,1)}, u32[]{:S(2)}, u32[]{:S(2)}) %collective-permute-start.2) | collective-permute-done | bytes 163872 | tf_op jit(solution)/shard_map/cond/branch_1_fun/ppermute | solution.py:31
  45.4 1.1 pad_maximum_fusion.1
  46.5 1.9 collective-permute-start.4
  48.5 4.6 %collective-permute-start.5 = (bf16[2,2,160,256]{3,2,1,0:T(8,128)(2,1)S(1)}, bf16[2,2,160,256]{3,2,1,0:T(8,128)(2,1)S(1)}, u32[]{:S(2)}, u32[]{:S(2)}) collective-permute-start(bf16[2,2,160,256]{3,2,1,0:T(8,128)(2,1)S(1)} %get-tuple-element.128), channel_id=1, source_target_pairs={{0,14},{1,15},{2,0},{3,1},{4,2},{5,3},{6,4},{7,5},{8,6},{9,7},{10,... | collective-permute-start | bytes 983048 | tf_op jit(solution)/shard_map/cond/branch_1_fun/ppermute | solution.py:27
  53.1 8.0 %collective-permute-start.8 = (bf16[2,160,256]{2,1,0:T(8,128)(2,1)}, bf16[2,160,256]{2,1,0:T(8,128)(2,1)S(1)}, u32[]{:S(2)}, u32[]{:S(2)}) collective-permute-start(bf16[2,160,256]{2,1,0:T(8,128)(2,1)} %collective-permute-done.3), channel_id=1, source_target_pairs={{0,1},{1,0},{2,3},{3,2},{4,5},{5,4},{6,7},{7,6},{8,9},{9,8},{10,11... | collective-permute-start | bytes 491528 | tf_op jit(solution)/shard_map/cond/branch_1_fun/ppermute | solution.py:31
  61.1 1.6 bitcast_dynamic-update-slice_fusion.8
  62.7 1.6 bitcast_dynamic-update-slice_fusion.7
  64.3 1.6 bitcast_dynamic-update-slice_fusion.6
  65.9 1.6 bitcast_dynamic-update-slice_fusion.5
  67.5 1.9 collective-permute-start.6
  70.8 4.6 %collective-permute-start.7 = (bf16[2,2,160,256]{3,2,1,0:T(8,128)(2,1)S(1)}, bf16[2,2,160,256]{3,2,1,0:T(8,128)(2,1)S(1)}, u32[]{:S(2)}, u32[]{:S(2)}) collective-permute-start(bf16[2,2,160,256]{3,2,1,0:T(8,128)(2,1)S(1)} %collective-permute-done.5), channel_id=1, source_target_pairs={{0,14},{1,15},{2,0},{3,1},{4,2},{5,3},{6,4},{7,5},{8,6},{9,7},{10,... | collective-permute-start | bytes 983048 | tf_op jit(solution)/shard_map/cond/branch_1_fun/ppermute | solution.py:27
  76.7 1.7 collective-permute-done.6
  78.5 1.9 collective-permute-start.9
  80.7 5.3 %collective-permute-start.10 = (bf16[2,160,256]{2,1,0:T(8,128)(2,1)S(1)}, bf16[2,160,256]{2,1,0:T(8,128)(2,1)S(1)}, u32[]{:S(2)}, u32[]{:S(2)}) collective-permute-start(bf16[2,160,256]{2,1,0:T(8,128)(2,1)S(1)} %slice_bitcast_fusion.8), channel_id=1, source_target_pairs={{0,14},{1,15},{2,0},{3,1},{4,2},{5,3},{6,4},{7,5},{8,6},{9,7},{10,... | collective-permute-start | bytes 491528 | tf_op jit(solution)/shard_map/cond/branch_1_fun/ppermute | solution.py:27
  90.9 3.0 %tick_layer.8 = (bf16[4,128,2560]{2,1,0:T(8,128)(2,1)S(1)}, bf16[64,2560]{1,0:T(8,128)(2,1)S(1)}, bf16[64,128]{1,0:T(8,128)(2,1)S(1)}, bf16[64,128]{1,0:T(8,128)(2,1)S(1)}) custom-call(s32[4]{0:T(128)S(1)} %pad_add_fusion.levels_ref, bf16[128,2560]{1,0:T(8,128)(2,1)S(1)} %bitcast.147, ...), custom_call_target="tpu_custom_call", output_to_operand_aliasing={{0}: (5, {})} | custom-call | flops 4294967296 | bytes 8388608 | tf_op jit(solution)/shard_map/tick_layer/pallas_call | solution.py:192
  94.0 4.8 %collective-permute-start.11 = (bf16[64,2560]{1,0:T(8,128)(2,1)S(1)}, bf16[64,2560]{1,0:T(8,128)(2,1)S(1)}, u32[]{:S(2)}, u32[]{:S(2)}) collective-permute-start(bf16[64,2560]{1,0:T(8,128)(2,1)S(1)} %get-tuple-element.97), channel_id=1, source_target_pairs={{0,496},{16,0},{32,16},{48,32},{64,48},{80,64},{96,80},{112,96},{1... | collective-permute-start | bytes 983048 | tf_op jit(solution)/shard_map/ppermute | solution.py:327
  98.8 1.3 tick_layer.9
  100.1 1.9 collective-permute-start.12
  102.1 1.6 forward_rest.1
  103.7 2.5 %collective-permute-done.11.incoming_ref = bf16[64,2560]{1,0:T(8,128)(2,1)S(1)} collective-permute-done((bf16[64,2560]{1,0:T(8,128)(2,1)S(1)}, bf16[64,2560]{1,0:T(8,128)(2,1)S(1)}, u32[]{:S(2)}, u32[]{:S(2)}) %collective-permute-start.11) | collective-permute-done | bytes 327712 | tf_op jit(solution)/shard_map/ppermute | solution.py:327
  106.3 1.2 tick_layer.10
  107.5 1.9 collective-permute-start.13
  109.4 3.0 %collective-permute-done.12.incoming_ref = bf16[64,2560]{1,0:T(8,128)(2,1)S(1)} collective-permute-done((bf16[64,2560]{1,0:T(8,128)(2,1)S(1)}, bf16[64,2560]{1,0:T(8,128)(2,1)S(1)}, u32[]{:S(2)}, u32[]{:S(2)}) %collective-permute-start.12) | collective-permute-done | bytes 327712 | tf_op jit(solution)/shard_map/ppermute | solution.py:327
  112.4 1.2 tick_layer.11
  113.7 1.9 collective-permute-start.14
  115.6 4.2 %collective-permute-done.13.incoming_ref = bf16[64,2560]{1,0:T(8,128)(2,1)S(1)} collective-permute-done((bf16[64,2560]{1,0:T(8,128)(2,1)S(1)}, bf16[64,2560]{1,0:T(8,128)(2,1)S(1)}, u32[]{:S(2)}, u32[]{:S(2)}) %collective-permute-start.13) | collective-permute-done | bytes 327712 | tf_op jit(solution)/shard_map/ppermute | solution.py:336
  119.8 1.2 tick_layer.12
  121.1 1.9 collective-permute-start.15
  123.0 3.0 %collective-permute-done.14.incoming_ref = bf16[64,2560]{1,0:T(8,128)(2,1)S(1)} collective-permute-done((bf16[64,2560]{1,0:T(8,128)(2,1)S(1)}, bf16[64,2560]{1,0:T(8,128)(2,1)S(1)}, u32[]{:S(2)}, u32[]{:S(2)}) %collective-permute-start.14) | collective-permute-done | bytes 327712 | tf_op jit(solution)/shard_map/ppermute | solution.py:336
  126.0 1.2 tick_layer.13
  127.2 1.9 collective-permute-start.16
  129.2 4.2 %collective-permute-done.15.incoming_ref = bf16[64,2560]{1,0:T(8,128)(2,1)S(1)} collective-permute-done((bf16[64,2560]{1,0:T(8,128)(2,1)S(1)}, bf16[64,2560]{1,0:T(8,128)(2,1)S(1)}, u32[]{:S(2)}, u32[]{:S(2)}) %collective-permute-start.15) | collective-permute-done | bytes 327712 | tf_op jit(solution)/shard_map/ppermute | solution.py:336
  133.4 1.2 tick_layer.14
  134.6 4.9 %collective-permute-done.16.incoming_ref = bf16[64,2560]{1,0:T(8,128)(2,1)S(1)} collective-permute-done((bf16[64,2560]{1,0:T(8,128)(2,1)S(1)}, bf16[64,2560]{1,0:T(8,128)(2,1)S(1)}, u32[]{:S(2)}, u32[]{:S(2)}) %collective-permute-start.16) | collective-permute-done | bytes 327712 | tf_op jit(solution)/shard_map/ppermute | solution.py:336
  139.5 1.3 tick_layer.15
  140.8 1.9 collective-permute-start.18
  142.8 1.9 collective-permute-start.17
  144.7 74.1 %conditional.3 = (f32[160,512]{1,0:T(8,128)S(1)}) conditional(s32[]{:T(128)} %convert_element_type.20, (bf16[512,2560]{1,0:T(8,128)(2,1)S(1)}, bf16[512,128]{1,0:T(8,128)(2,1)S(1)}, bf16[4,128,128]{2,1,0:T(8,128)(2,1)S(1)}, bf16[512,2560]{1,0:T(8,128)(2,1)}) %tuple.42, (s32[4]{0:T(128)S(1)}, bf16[512,128]{1,0:T(8,128)(2,1)S(1)}, ...), branch_computations={%region_2.3_spmd, %region_3.4_spmd} | conditional | flops 1344798720 | bytes 25430092 | solution.py:363
  145.2 3.6 %fusion.7.right_ref = bf16[2560,256]{1,0:T(8,128)(2,1)S(1)} fusion(bf16[512,256]{1,0:T(8,128)(2,1)S(1)} %bitcast.155, bf16[512,2560]{1,0:T(8,128)(2,1)} %get-tuple-element.52), kind=kOutput, calls=%fused_computation.42 | convolution fusion | flops 671744000 | bytes 4194304 | tf_op jit(solution)/shard_map/cond/branch_1_fun/dot_general | solution.py:345
  149.0 2.9 %fusion.6.left_ref = bf16[2560,256]{1,0:T(8,128)(2,1)S(1)} fusion(bf16[512,2560]{1,0:T(8,128)(2,1)} %copy-done.3, bf16[512,128]{1,0:T(8,128)(2,1)S(1)} %get-tuple-element.139, bf16[512,128]{1,0:T(8,128)(2,1)S(1)} %get-tuple-element.138), kind=kOutput, calls=%fused_computation.41 | convolution fusion | flops 672268288 | bytes 4194304 | tf_op jit(solution)/shard_map/cond/branch_1_fun/dot_general | solution.py:344
  152.1 66.1 %all_to_all.13.moved_ref = bf16[16,160,512]{2,1,0:T(8,128)(2,1)S(1)} all-to-all(bf16[16,160,512]{2,1,0:T(8,128)(2,1)S(1)} %bitcast.145), channel_id=1, replica_groups=mesh['section'=32,'dp'=16] {'dp'}, dimensions={0} | all-to-all | bytes 5242880 | tf_op jit(solution)/shard_map/cond/branch_1_fun/all_to_all | solution.py:347
  218.8 1.0 finish.1
  (69 shorter events, 11.3 us)
Async XLA Ops:
  0.6 0.9 copy-start.5
  0.6 0.9 copy-start.6
  1.6 89.3 %copy-start = (bf16[1,128,2560]{2,1,0:T(8,128)(2,1)S(1)}, bf16[1,128,2560]{2,1,0:T(8,128)(2,1)}, u32[]{:S(2)}) copy-start(bf16[1,128,2560]{2,1,0:T(8,128)(2,1)} %param.9) | copy-start | bytes 1966084
  2.3 26.7 %collective-permute-start = (bf16[2,160,256]{2,1,0:T(8,128)(2,1)}, bf16[2,160,256]{2,1,0:T(8,128)(2,1)}, u32[]{:S(2)}, u32[]{:S(2)}) collective-permute-start(bf16[2,160,256]{2,1,0:T(8,128)(2,1)} %pad_maximum_fusion.3), channel_id=1, source_target_pairs={{0,2},{1,3},{2,4},{3,5},{4,6},{5,7},{6,8},{7,9},{8,10},{9,11},{10,... | collective-permute-start | bytes 491528 | tf_op jit(solution)/shard_map/cond/branch_1_fun/ppermute | solution.py:27
  6.3 22.7 %collective-permute-start.1 = (bf16[2,160,256]{2,1,0:T(8,128)(2,1)}, bf16[2,160,256]{2,1,0:T(8,128)(2,1)}, u32[]{:S(2)}, u32[]{:S(2)}) collective-permute-start(bf16[2,160,256]{2,1,0:T(8,128)(2,1)} %pad_maximum_fusion.3), channel_id=1, source_target_pairs={{0,14},{1,15},{2,0},{3,1},{4,2},{5,3},{6,4},{7,5},{8,6},{9,7},{10,... | collective-permute-start | bytes 491528 | tf_op jit(solution)/shard_map/cond/branch_1_fun/ppermute | solution.py:27
  14.9 30.5 %collective-permute-start.2 = (bf16[2,160,256]{2,1,0:T(8,128)(2,1)}, bf16[2,160,256]{2,1,0:T(8,128)(2,1)}, u32[]{:S(2)}, u32[]{:S(2)}) collective-permute-start(bf16[2,160,256]{2,1,0:T(8,128)(2,1)} %pad_maximum_fusion.3), channel_id=1, source_target_pairs={{0,1},{1,0},{2,3},{3,2},{4,5},{5,4},{6,7},{7,6},{8,9},{9,8},{10,11... | collective-permute-start | bytes 491528 | tf_op jit(solution)/shard_map/cond/branch_1_fun/ppermute | solution.py:31
  19.3 33.7 %collective-permute-start.3 = (bf16[2,160,256]{2,1,0:T(8,128)(2,1)}, bf16[2,160,256]{2,1,0:T(8,128)(2,1)}, u32[]{:S(2)}, u32[]{:S(2)}) collective-permute-start(bf16[2,160,256]{2,1,0:T(8,128)(2,1)} %pad_maximum_fusion.3), channel_id=1, source_target_pairs={{0,8},{1,9},{2,10},{3,11},{4,12},{5,13},{6,14},{7,15},{8,0},{9,1},... | collective-permute-start | bytes 491528 | tf_op jit(solution)/shard_map/cond/branch_1_fun/ppermute | solution.py:27
  46.5 21.0 %collective-permute-start.4 = (bf16[2,2,160,256]{3,2,1,0:T(8,128)(2,1)S(1)}, bf16[2,2,160,256]{3,2,1,0:T(8,128)(2,1)S(1)}, u32[]{:S(2)}, u32[]{:S(2)}) collective-permute-start(bf16[2,2,160,256]{3,2,1,0:T(8,128)(2,1)S(1)} %get-tuple-element.129), channel_id=1, source_target_pairs={{0,2},{1,3},{2,4},{3,5},{4,6},{5,7},{6,8},{7,9},{8,10},{9,11},{10,... | collective-permute-start | bytes 983048 | tf_op jit(solution)/shard_map/cond/branch_1_fun/ppermute | solution.py:27
  48.5 22.3 %collective-permute-start.5 = (bf16[2,2,160,256]{3,2,1,0:T(8,128)(2,1)S(1)}, bf16[2,2,160,256]{3,2,1,0:T(8,128)(2,1)S(1)}, u32[]{:S(2)}, u32[]{:S(2)}) collective-permute-start(bf16[2,2,160,256]{3,2,1,0:T(8,128)(2,1)S(1)} %get-tuple-element.128), channel_id=1, source_target_pairs={{0,14},{1,15},{2,0},{3,1},{4,2},{5,3},{6,4},{7,5},{8,6},{9,7},{10,... | collective-permute-start | bytes 983048 | tf_op jit(solution)/shard_map/cond/branch_1_fun/ppermute | solution.py:27
  53.1 35.7 %collective-permute-start.8 = (bf16[2,160,256]{2,1,0:T(8,128)(2,1)}, bf16[2,160,256]{2,1,0:T(8,128)(2,1)S(1)}, u32[]{:S(2)}, u32[]{:S(2)}) collective-permute-start(bf16[2,160,256]{2,1,0:T(8,128)(2,1)} %collective-permute-done.3), channel_id=1, source_target_pairs={{0,1},{1,0},{2,3},{3,2},{4,5},{5,4},{6,7},{7,6},{8,9},{9,8},{10,11... | collective-permute-start | bytes 491528 | tf_op jit(solution)/shard_map/cond/branch_1_fun/ppermute | solution.py:31
  62.7 28.1 %copy-start.7 = (f32[4,128,128]{2,1,0:T(8,128)S(1)}, f32[4,128,128]{2,1,0:T(8,128)}, u32[]{:S(2)}) copy-start(f32[4,128,128]{2,1,0:T(8,128)} %get-tuple-element.149) | copy-start | bytes 786436 | tf_op jit(solution)/shard_map/cond
  67.5 10.9 %collective-permute-start.6 = (bf16[2,2,160,256]{3,2,1,0:T(8,128)(2,1)S(1)}, bf16[2,2,160,256]{3,2,1,0:T(8,128)(2,1)S(1)}, u32[]{:S(2)}, u32[]{:S(2)}) collective-permute-start(bf16[2,2,160,256]{3,2,1,0:T(8,128)(2,1)S(1)} %collective-permute-done.4), channel_id=1, source_target_pairs={{0,2},{1,3},{2,4},{3,5},{4,6},{5,7},{6,8},{7,9},{8,10},{9,11},{10,... | collective-permute-start | bytes 983048 | tf_op jit(solution)/shard_map/cond/branch_1_fun/ppermute | solution.py:27
  70.8 9.9 %collective-permute-start.7 = (bf16[2,2,160,256]{3,2,1,0:T(8,128)(2,1)S(1)}, bf16[2,2,160,256]{3,2,1,0:T(8,128)(2,1)S(1)}, u32[]{:S(2)}, u32[]{:S(2)}) collective-permute-start(bf16[2,2,160,256]{3,2,1,0:T(8,128)(2,1)S(1)} %collective-permute-done.5), channel_id=1, source_target_pairs={{0,14},{1,15},{2,0},{3,1},{4,2},{5,3},{6,4},{7,5},{8,6},{9,7},{10,... | collective-permute-start | bytes 983048 | tf_op jit(solution)/shard_map/cond/branch_1_fun/ppermute | solution.py:27
  78.5 11.0 %collective-permute-start.9 = (bf16[2,160,256]{2,1,0:T(8,128)(2,1)S(1)}, bf16[2,160,256]{2,1,0:T(8,128)(2,1)S(1)}, u32[]{:S(2)}, u32[]{:S(2)}) collective-permute-start(bf16[2,160,256]{2,1,0:T(8,128)(2,1)S(1)} %slice_bitcast_fusion.9), channel_id=1, source_target_pairs={{0,2},{1,3},{2,4},{3,5},{4,6},{5,7},{6,8},{7,9},{8,10},{9,11},{10,... | collective-permute-start | bytes 491528 | tf_op jit(solution)/shard_map/cond/branch_1_fun/ppermute | solution.py:27
  80.7 9.4 %collective-permute-start.10 = (bf16[2,160,256]{2,1,0:T(8,128)(2,1)S(1)}, bf16[2,160,256]{2,1,0:T(8,128)(2,1)S(1)}, u32[]{:S(2)}, u32[]{:S(2)}) collective-permute-start(bf16[2,160,256]{2,1,0:T(8,128)(2,1)S(1)} %slice_bitcast_fusion.8), channel_id=1, source_target_pairs={{0,14},{1,15},{2,0},{3,1},{4,2},{5,3},{6,4},{7,5},{8,6},{9,7},{10,... | collective-permute-start | bytes 491528 | tf_op jit(solution)/shard_map/cond/branch_1_fun/ppermute | solution.py:27
  90.8 7.9 %copy-start.8 = (f32[4,128,128]{2,1,0:T(8,128)}, f32[4,128,128]{2,1,0:T(8,128)S(1)}, u32[]{:S(2)}) copy-start(f32[4,128,128]{2,1,0:T(8,128)S(1)} %get-tuple-element.92.inverse_ref) | copy-start | bytes 786436
  90.9 7.9 %copy-start.2 = (bf16[4,128,2560]{2,1,0:T(8,128)(2,1)S(1)}, bf16[4,128,2560]{2,1,0:T(8,128)(2,1)}, u32[]{:S(2)}) copy-start(bf16[4,128,2560]{2,1,0:T(8,128)(2,1)} %get-tuple-element.91.normed_ref) | copy-start | bytes 7864324
  90.9 7.9 %copy-start.4 = (bf16[2,2560,256]{2,1,0:T(8,128)(2,1)S(1)}, bf16[2,2560,256]{2,1,0:T(8,128)(2,1)}, u32[]{:S(2)}) copy-start(bf16[2,2560,256]{2,1,0:T(8,128)(2,1)} %get-tuple-element.93.maps_ref) | copy-start | bytes 7864324
  94.0 12.3 %collective-permute-start.11 = (bf16[64,2560]{1,0:T(8,128)(2,1)S(1)}, bf16[64,2560]{1,0:T(8,128)(2,1)S(1)}, u32[]{:S(2)}, u32[]{:S(2)}) collective-permute-start(bf16[64,2560]{1,0:T(8,128)(2,1)S(1)} %get-tuple-element.97), channel_id=1, source_target_pairs={{0,496},{16,0},{32,16},{48,32},{64,48},{80,64},{96,80},{112,96},{1... | collective-permute-start | bytes 983048 | tf_op jit(solution)/shard_map/ppermute | solution.py:327
  100.1 12.3 %collective-permute-start.12 = (bf16[64,2560]{1,0:T(8,128)(2,1)S(1)}, bf16[64,2560]{1,0:T(8,128)(2,1)S(1)}, u32[]{:S(2)}, u32[]{:S(2)}) collective-permute-start(bf16[64,2560]{1,0:T(8,128)(2,1)S(1)} %get-tuple-element.102), channel_id=1, source_target_pairs={{0,496},{16,0},{32,16},{48,32},{64,48},{80,64},{96,80},{112,96},{1... | collective-permute-start | bytes 983048 | tf_op jit(solution)/shard_map/ppermute | solution.py:327
  102.1 4.2 %copy-start.9 = (f32[4,128,128]{2,1,0:T(8,128)S(1)}, f32[4,128,128]{2,1,0:T(8,128)}, u32[]{:S(2)}) copy-start(f32[4,128,128]{2,1,0:T(8,128)} %copy-done.8) | copy-start | bytes 786436
  107.5 12.3 %collective-permute-start.13 = (bf16[64,2560]{1,0:T(8,128)(2,1)S(1)}, bf16[64,2560]{1,0:T(8,128)(2,1)S(1)}, u32[]{:S(2)}, u32[]{:S(2)}) collective-permute-start(bf16[64,2560]{1,0:T(8,128)(2,1)S(1)} %get-tuple-element.105), channel_id=1, source_target_pairs={{0,496},{16,0},{32,16},{48,32},{64,48},{80,64},{96,80},{112,96},{1... | collective-permute-start | bytes 983048 | tf_op jit(solution)/shard_map/ppermute | solution.py:336
  113.7 12.3 %collective-permute-start.14 = (bf16[64,2560]{1,0:T(8,128)(2,1)S(1)}, bf16[64,2560]{1,0:T(8,128)(2,1)S(1)}, u32[]{:S(2)}, u32[]{:S(2)}) collective-permute-start(bf16[64,2560]{1,0:T(8,128)(2,1)S(1)} %get-tuple-element.108), channel_id=1, source_target_pairs={{0,496},{16,0},{32,16},{48,32},{64,48},{80,64},{96,80},{112,96},{1... | collective-permute-start | bytes 983048 | tf_op jit(solution)/shard_map/ppermute | solution.py:336
  121.1 12.3 %collective-permute-start.15 = (bf16[64,2560]{1,0:T(8,128)(2,1)S(1)}, bf16[64,2560]{1,0:T(8,128)(2,1)S(1)}, u32[]{:S(2)}, u32[]{:S(2)}) collective-permute-start(bf16[64,2560]{1,0:T(8,128)(2,1)S(1)} %get-tuple-element.111), channel_id=1, source_target_pairs={{0,496},{16,0},{32,16},{48,32},{64,48},{80,64},{96,80},{112,96},{1... | collective-permute-start | bytes 983048 | tf_op jit(solution)/shard_map/ppermute | solution.py:336
  127.2 12.3 %collective-permute-start.16 = (bf16[64,2560]{1,0:T(8,128)(2,1)S(1)}, bf16[64,2560]{1,0:T(8,128)(2,1)S(1)}, u32[]{:S(2)}, u32[]{:S(2)}) collective-permute-start(bf16[64,2560]{1,0:T(8,128)(2,1)S(1)} %get-tuple-element.114), channel_id=1, source_target_pairs={{0,496},{16,0},{32,16},{48,32},{64,48},{80,64},{96,80},{112,96},{1... | collective-permute-start | bytes 983048 | tf_op jit(solution)/shard_map/ppermute | solution.py:336
  134.6 4.9 %copy-start.1 = (bf16[4,128,2560]{2,1,0:T(8,128)(2,1)}, bf16[4,128,2560]{2,1,0:T(8,128)(2,1)S(1)}, u32[]{:S(2)}) copy-start(bf16[4,128,2560]{2,1,0:T(8,128)(2,1)S(1)} %get-tuple-element.115.refs_2_) | copy-start | bytes 7864324
  140.8 78.0 %collective-permute-start.18 = (bf16[64,2560]{1,0:T(8,128)(2,1)S(1)}, bf16[64,2560]{1,0:T(8,128)(2,1)S(1)}, u32[]{:S(2)}, u32[]{:S(2)}) collective-permute-start(bf16[64,2560]{1,0:T(8,128)(2,1)S(1)} %get-tuple-element.122), channel_id=1, source_target_pairs={{0,496},{16,0},{32,16},{48,32},{64,48},{80,64},{96,80},{112,96},{1... | collective-permute-start | bytes 983048 | tf_op jit(solution)/shard_map/ppermute | solution.py:336
  142.8 76.0 %collective-permute-start.17 = (bf16[64,2560]{1,0:T(8,128)(2,1)S(1)}, bf16[64,2560]{1,0:T(8,128)(2,1)S(1)}, u32[]{:S(2)}, u32[]{:S(2)}) collective-permute-start(bf16[64,2560]{1,0:T(8,128)(2,1)S(1)} %get-tuple-element.121), channel_id=1, source_target_pairs={{0,496},{16,0},{32,16},{48,32},{64,48},{80,64},{96,80},{112,96},{1... | collective-permute-start | bytes 983048 | tf_op jit(solution)/shard_map/ppermute | solution.py:336
  144.9 4.0 %copy-start.3 = (bf16[512,2560]{1,0:T(8,128)(2,1)}, bf16[512,2560]{1,0:T(8,128)(2,1)S(1)}, u32[]{:S(2)}) copy-start(bf16[512,2560]{1,0:T(8,128)(2,1)S(1)} %get-tuple-element.50) | copy-start | bytes 7864324 | tf_op jit(solution)/shard_map/cond

commit v11 on v8

--- a/solution.py
+++ b/solution.py
@@ -140,7 +140,10 @@
         stack_ref, sent_ref, grad_latent_ref, active_ref, sem = refs[1:]
     else:
         latent_ref, slope_ref = refs[:2]
-        stack_ref, sent_ref, grad_latent_ref, sem = refs[3:]
+        stack_ref, sent_ref, grad_latent_ref, sem = refs[-4:]
+    base = sent_ref.shape[0] - rows
+    if base:
+        sent_ref[:base] = refs[2][...]
     keep = pltpu.make_async_copy(
         incoming_ref, stack_ref.at[tick, pl.ds(part * rows, rows)], sem
     )
@@ -164,11 +167,11 @@
         sent = incoming_ref[:, at].astype(F32) + (
             inverse * grad_normed - normed_ref[0, :, at].astype(F32) * scale
         )
-        sent_ref[:, at] = sent.astype(BF16)
+        sent_ref[base:, at] = sent.astype(BF16)
     keep.wait()
 
 
-def tick_layer(tick, part, levels, incoming, normed, inverse, maps, forward, stack):
+def tick_layer(tick, part, levels, incoming, normed, inverse, maps, forward, stack, before=()):
     _, rows, width = normed.shape
     rows //= 2
     rank = maps.shape[2] // 2
@@ -190,21 +193,49 @@
                 pl.BlockSpec((1, width, 2 * rank), lambda i, levels: (levels[tick], 0, 0)),
             ]
             + [forward_spec] * len(forward)
+            + [IN_VMEM] * len(before)
             + [ANYWHERE],
             out_specs=[ANYWHERE, IN_VMEM, IN_VMEM] + [IN_VMEM] * first,
             scratch_shapes=[pltpu.SemaphoreType.DMA],
         ),
         out_shape=[
             jax.ShapeDtypeStruct(stack.shape, stack.dtype),
-            jax.ShapeDtypeStruct((rows, width), BF16),
+            jax.ShapeDtypeStruct((rows * (1 + len(before)), width), BF16),
             narrow,
         ]
         + [narrow] * first,
-        input_output_aliases={5 + len(forward): 0},
+        input_output_aliases={5 + len(forward) + len(before): 0},
         compiler_params=LIMIT,
         cost_estimate=COST,
         name="tick_layer",
-    )(levels, incoming, normed, inverse, maps, *forward, stack)
+    )(levels, incoming, normed, inverse, maps, *forward, *before, stack)
+
+
+def products_kernel(normed_ref, grads_ref, lats_ref, acts_ref, out_ref):
+    lanes = lats_ref.shape[1]
+    contract = (((0,), (0,)), ((), ()))
+    for i, (wide_ref, narrow_ref) in enumerate(((normed_ref, lats_ref), (grads_ref, acts_ref))):
+        wide = wide_ref[...].reshape(-1, wide_ref.shape[2])
+        part = lax.dot_general(wide, narrow_ref[...], contract, preferred_element_type=F32)
+        out_ref[:, i * lanes : (i + 1) * lanes] = part.astype(BF16)
+
+
+def kernel_products(normed, grads, lats, acts):
+    ticks, rows, width = normed.shape
+    lanes = lats.shape[1]
+    run = width // 4
+    by_run = pl.BlockSpec((ticks, rows, run), lambda i: (0, 0, i))
+    whole = pl.BlockSpec((ticks * rows, lanes), lambda i: (0, 0))
+    return pl.pallas_call(
+        products_kernel,
+        grid=(width // run,),
+        out_shape=jax.ShapeDtypeStruct((width, 2 * lanes), BF16),
+        in_specs=[by_run, by_run, whole, whole],
+        out_specs=pl.BlockSpec((run, 2 * lanes), lambda i: (i, 0)),
+        compiler_params=LIMIT,
+        cost_estimate=COST,
+        name="weight_products",
+    )(normed, grads, lats, acts)
 
 
 def beside_kernel(left_ref, right_ref, out_ref):
@@ -249,27 +280,24 @@
     )(moved)
 
 
-def finish_kernel(total_ref, low_ref, high_ref, grad_ref, down_ref, up_ref):
-    rows, rank = low_ref.shape[0], down_ref.shape[3]
-    grad_ref[0, :rows] = low_ref[...]
-    grad_ref[0, rows:] = high_ref[...]
+def finish_kernel(total_ref, down_ref, up_ref):
+    rank = down_ref.shape[3]
     for i, out in enumerate((down_ref, up_ref)):
         for j, level in enumerate((1, 0)):
             at = (2 * i + j) * rank
             out[level, 0] = total_ref[:, at : at + rank]
 
 
-def finish(total, low, high, share, rank):
-    rows, width = low.shape
+def finish(total, share, rank):
     made = jax.ShapeDtypeStruct((2, 1, share, rank), F32)
     return pl.pallas_call(
         finish_kernel,
-        out_shape=[jax.ShapeDtypeStruct((1, 2 * rows, width), low.dtype), made, made],
-        in_specs=[IN_VMEM] * 3,
-        out_specs=[IN_VMEM] * 3,
+        out_shape=[made, made],
+        in_specs=[IN_VMEM],
+        out_specs=[IN_VMEM] * 2,
         compiler_params=LIMIT,
         name="finish",
-    )(total, low, high)
+    )(total)
 
 
 def on_device(saved_inputs, grad_in, adapter_down, adapter_up):
@@ -317,27 +345,42 @@
     latents, slopes, actives = forward_rest(level_stack, normed, maps, grad_latent)
     for tick in range(1, ticks):
         arrived, moving = moving, []
+        before = []
         for part in range(2):
             stack, sent, grad_latent = tick_layer(
-                tick, part, level_stack, arrived[part], normed, inverse, maps, [latents, slopes], stack
+                tick,
+                part,
+                level_stack,
+                arrived[part],
+                normed,
+                inverse,
+                maps,
+                [latents, slopes],
+                stack,
+                before,
             )
             grad_latents.append(grad_latent)
-            moving.append(lax.ppermute(sent, "section", down_one))
+            if tick == ticks - 1 and part == 0:
+                before = [sent]
+            else:
+                moving.append(lax.ppermute(sent, "section", down_one))
 
     normed_all = normed.reshape(-1, width)
     grads_all = stack.reshape(-1, width)
     actives = jnp.concatenate([jnp.concatenate(first_actives)[None], actives], axis=0)
+
+    def summed_parts(parts):
+        moved = lax.all_to_all(parts.reshape(n_dp, share, -1), "dp", 0, 0, tiled=True)
+        return summed(moved, 4 * rank)
 
     def products(lats, acts):
         contract = (((0,), (0,)), ((), ()))
         down = lax.dot_general(normed_all, lats, contract, preferred_element_type=F32)
         up = lax.dot_general(grads_all, acts, contract, preferred_element_type=F32)
-        both = beside(down.astype(BF16), up.astype(BF16))
-        moved = lax.all_to_all(both.reshape(n_dp, share, -1), "dp", 0, 0, tiled=True)
-        return summed(moved, 4 * rank)
+        return beside(down.astype(BF16), up.astype(BF16))
 
     def reduce_one(lats, acts):
-        return products(lats.reshape(-1, rank), acts.reshape(-1, rank))
+        return summed_parts(products(lats.reshape(-1, rank), acts.reshape(-1, rank)))
 
     def reduce_two(lats, acts):
         level = level_stack[:, None, None]
@@ -347,11 +390,11 @@
             both = [jnp.where(level == 1, value, zero), jnp.where(level == 0, value, zero)]
             return jnp.concatenate(both, axis=2).reshape(-1, 2 * rank)
 
-        return products(split(lats), split(acts))
+        return summed_parts(kernel_products(normed, stack, split(lats), split(acts)))
 
     total = lax.cond(two_layers, reduce_two, reduce_one, jnp.concatenate(grad_latents).reshape(actives.shape), actives)
-    grad_out, down_grad, up_grad = finish(total, *moving, share, rank)
-    return grad_out, jnp.swapaxes(down_grad, 2, 3), jnp.swapaxes(up_grad, 2, 3)
+    down_grad, up_grad = finish(total, share, rank)
+    return moving[0][None], jnp.swapaxes(down_grad, 2, 3), jnp.swapaxes(up_grad, 2, 3)
 
 
 def solution(mesh):

time: 192 us -> 202 us (1.052)
  waiting for transfers between devices: 35.3 us -> 44.4 us
  matrix products: 6.46 us -> 0 us
  Pallas kernels: 19.6 us -> 24.8 us
  local copies, waits for them, and re-layouts: 2.74 us -> 5.72 us
    dot_general x2 -> x0, matrix products: 6.46 us -> none  [the longest x1 3.58 us: products(): up = lax.dot_general(grads_all, acts, contract, preferred_element_type=F32)]
    ppermute x8, waiting for transfers between devices: 8.24 us -> 12.8 us  [shifted(): return lax.ppermute(value, 'dp', dp_pairs(n_z, step, 0))]
    ppermute x8 -> x7, waiting for transfers between devices: 20.5 us -> 25 us  [on_device(): moving.append(lax.ppermute(sent, 'section', down_one))]
    pallas_call x2, Pallas kernels: 1.24 us -> 5.69 us  [the longest x1 3.98 us: kernel_products(): pl.pallas_call(products_kernel, grid=(width // run,), out_shape=jax.Shape...]
    ppermute x8 -> x7, starting transfers between devices: 22 us -> 19.6 us  [on_device(): moving.append(lax.ppermute(sent, 'section', down_one))]
  transfers between devices with their start and end apart: 17 -> 16, of which waited for: 10 -> 10; matrix products, arithmetic and copies ran while one was open for 4% -> 0% of each run, Pallas kernels for 7% -> 10%
where the time goes in v11:
time: 202 us; the launch traced here: 201 us
  blocking collectives  65.9 us (33%)
  starting transfers between devices  56.6 us (28%)
  waiting for transfers between devices  44.4 us (22%)
  Pallas kernels  24.8 us (12%)
  local copies, waits for them, and re-layouts  5.72 us (3%)
  other arithmetic  2.19 us (1%)
    all_to_all x1, blocking collectives, summed_parts(): lax.all_to_all(parts.reshape(n_dp, share, -1), 'dp', 0, 0, tiled=True)  65.9 us
    ppermute x8, starting transfers between devices, shifted(): return lax.ppermute(value, 'dp', dp_pairs(n_z, step, 0))  32.5 us
    ppermute x7, waiting for transfers between devices, on_device(): moving.append(lax.ppermute(sent, 'section', down_one))  25 us
    ppermute x7, starting transfers between devices, on_device(): moving.append(lax.ppermute(sent, 'section', down_one))  19.6 us
    ppermute x8, waiting for transfers between devices, shifted(): return lax.ppermute(value, 'dp', dp_pairs(n_z, step, 0))  12.8 us
    pallas_call x8, Pallas kernels, tick_layer(): pl.pallas_call(functools.partial(tick_kernel, tick, part), grid_spec=pltp...  11.9 us
    ppermute x1, waiting for transfers between devices, swapped(): return lax.ppermute(value, 'dp', dp_pairs(n_z, 0, 1))  6.56 us
    pallas_call x1, Pallas kernels, norms(): pl.pallas_call(norm_kernel, grid=(ticks,), out_shape=[jax.ShapeDtypeStruc...  4.57 us
  transfers between devices with their start and end apart: 16, of which 10 were waited for; matrix products, arithmetic and copies ran while one was open for 0% of the time, Pallas kernels for 10%

profile of v11, /device:TPU:63, one launch (start us, length us, event | category | flops | bytes accessed | tf_op | source)
XLA Modules:
  0.0 201.0 jit_solution(14673915392793443260)
XLA Ops:
  0.7 0.8 copy-done.6
  1.6 64.7 %conditional.2 = (bf16[2,2560,256]{2,1,0:T(8,128)(2,1)}, bf16[4,128,2560]{2,1,0:T(8,128)(2,1)}, f32[4,128,128]{2,1,0:T(8,128)S(1)}) conditional(s32[]{:T(128)} %convert_element_type.10, (bf16[2,128,160]{1,2,0:T(8,128)(2,1)S(1)}, bf16[2,128,160]{1,2,0:T(8,128)(2,1)S(1)}, bf16[4,1,128,2560]{3,2,1,0:T(8,128)(2,1)}) %tuple.47, ...), branch_computations={%region_0.1_spmd, %region_1.2_spmd} | conditional | flops 4297097216 | bytes 47384412 | solution.py:330
  1.6 0.7 pad_maximum_fusion.2
  2.3 4.4 %collective-permute-start = (bf16[2,160,256]{2,1,0:T(8,128)(2,1)}, bf16[2,160,256]{2,1,0:T(8,128)(2,1)}, u32[]{:S(2)}, u32[]{:S(2)}) collective-permute-start(bf16[2,160,256]{2,1,0:T(8,128)(2,1)} %pad_maximum_fusion.2), channel_id=1, source_target_pairs={{0,1},{1,0},{2,3},{3,2},{4,5},{5,4},{6,7},{7,6},{8,9},{9,8},{10,11... | collective-permute-start | bytes 491528 | tf_op jit(solution)/shard_map/cond/branch_1_fun/ppermute | solution.py:31
  6.9 6.6 %collective-permute-done = bf16[2,160,256]{2,1,0:T(8,128)(2,1)} collective-permute-done((bf16[2,160,256]{2,1,0:T(8,128)(2,1)}, bf16[2,160,256]{2,1,0:T(8,128)(2,1)}, u32[]{:S(2)}, u32[]{:S(2)}) %collective-permute-start) | collective-permute-done | bytes 163872 | tf_op jit(solution)/shard_map/cond/branch_1_fun/ppermute | solution.py:31
  13.5 0.9 select_bitcast_fusion.1
  14.5 4.0 %collective-permute-start.1 = (bf16[2,2,160,256]{3,2,1,0:T(8,128)(2,1)S(1)}, bf16[2,2,160,256]{3,2,1,0:T(8,128)(2,1)S(1)}, u32[]{:S(2)}, u32[]{:S(2)}) collective-permute-start(bf16[2,2,160,256]{3,2,1,0:T(8,128)(2,1)S(1)} %pad_maximum_fusion.1), channel_id=1, source_target_pairs={{0,2},{1,3},{2,4},{3,5},{4,6},{5,7},{6,8},{7,9},{8,10},{9,11},{10,... | collective-permute-start | bytes 983048 | tf_op jit(solution)/shard_map/cond/branch_1_fun/ppermute | solution.py:27
  18.5 8.6 %collective-permute-start.2 = (bf16[2,2,160,256]{3,2,1,0:T(8,128)(2,1)S(1)}, bf16[2,2,160,256]{3,2,1,0:T(8,128)(2,1)S(1)}, u32[]{:S(2)}, u32[]{:S(2)}) collective-permute-start(bf16[2,2,160,256]{3,2,1,0:T(8,128)(2,1)S(1)} %pad_maximum_fusion.1), channel_id=1, source_target_pairs={{0,14},{1,15},{2,0},{3,1},{4,2},{5,3},{6,4},{7,5},{8,6},{9,7},{10,... | collective-permute-start | bytes 983048 | tf_op jit(solution)/shard_map/cond/branch_1_fun/ppermute | solution.py:27
  27.1 4.6 %norms.3 = (bf16[4,128,2560]{2,1,0:T(8,128)(2,1)}, f32[4,128,128]{2,1,0:T(8,128)S(1)}) custom-call(bf16[4,1,128,2560]{3,2,1,0:T(8,128)(2,1)} %get-tuple-element.43.x_ref), custom_call_target="tpu_custom_call" | custom-call | flops 4294967296 | bytes 8388608 | tf_op jit(solution)/shard_map/cond/branch_1_fun/norms/pallas_call | solution.py:77
  31.7 1.9 collective-permute-start.3
  33.6 4.6 %collective-permute-start.4 = (bf16[2,2,160,256]{3,2,1,0:T(8,128)(2,1)S(1)}, bf16[2,2,160,256]{3,2,1,0:T(8,128)(2,1)S(1)}, u32[]{:S(2)}, u32[]{:S(2)}) collective-permute-start(bf16[2,2,160,256]{3,2,1,0:T(8,128)(2,1)S(1)} %collective-permute-done.2), channel_id=1, source_target_pairs={{0,14},{1,15},{2,0},{3,1},{4,2},{5,3},{6,4},{7,5},{8,6},{9,7},{10,... | collective-permute-start | bytes 983048 | tf_op jit(solution)/shard_map/cond/branch_1_fun/ppermute | solution.py:27
  38.3 3.6 %collective-permute-done.3 = bf16[2,2,160,256]{3,2,1,0:T(8,128)(2,1)S(1)} collective-permute-done((bf16[2,2,160,256]{3,2,1,0:T(8,128)(2,1)S(1)}, bf16[2,2,160,256]{3,2,1,0:T(8,128)(2,1)S(1)}, u32[]{:S(2)}, u32[]{:S(2)}) %collective-permute-start.3) | collective-permute-done | bytes 327712 | tf_op jit(solution)/shard_map/cond/branch_1_fun/ppermute | solution.py:27
  41.9 1.9 collective-permute-start.5
  43.8 4.6 %collective-permute-start.6 = (bf16[2,2,160,256]{3,2,1,0:T(8,128)(2,1)S(1)}, bf16[2,2,160,256]{3,2,1,0:T(8,128)(2,1)S(1)}, u32[]{:S(2)}, u32[]{:S(2)}) collective-permute-start(bf16[2,2,160,256]{3,2,1,0:T(8,128)(2,1)S(1)} %collective-permute-done.4), channel_id=1, source_target_pairs={{0,14},{1,15},{2,0},{3,1},{4,2},{5,3},{6,4},{7,5},{8,6},{9,7},{10,... | collective-permute-start | bytes 983048 | tf_op jit(solution)/shard_map/cond/branch_1_fun/ppermute | solution.py:27
  48.5 3.9 %collective-permute-done.6 = bf16[2,2,160,256]{3,2,1,0:T(8,128)(2,1)S(1)} collective-permute-done((bf16[2,2,160,256]{3,2,1,0:T(8,128)(2,1)S(1)}, bf16[2,2,160,256]{3,2,1,0:T(8,128)(2,1)S(1)}, u32[]{:S(2)}, u32[]{:S(2)}) %collective-permute-start.6) | collective-permute-done | bytes 327712 | tf_op jit(solution)/shard_map/cond/branch_1_fun/ppermute | solution.py:27
  52.4 5.0 %collective-permute-start.8 = (bf16[2,1,160,256]{3,2,1,0:T(8,128)(2,1)S(1)}, bf16[2,1,160,256]{3,2,1,0:T(8,128)(2,1)S(1)}, u32[]{:S(2)}, u32[]{:S(2)}) collective-permute-start(bf16[2,1,160,256]{3,2,1,0:T(8,128)(2,1)S(1)} %slice.25), channel_id=1, source_target_pairs={{0,14},{1,15},{2,0},{3,1},{4,2},{5,3},{6,4},{7,5},{8,6},{9,7},{10,... | collective-permute-start | bytes 491528 | tf_op jit(solution)/shard_map/cond/branch_1_fun/ppermute | solution.py:27
  57.5 1.9 collective-permute-start.7
  59.5 0.2 collective-permute-done.8
  59.7 5.1 %collective-permute-done.7 = bf16[2,1,160,256]{3,2,1,0:T(8,128)(2,1)S(1)} collective-permute-done((bf16[2,1,160,256]{3,2,1,0:T(8,128)(2,1)S(1)}, bf16[2,1,160,256]{3,2,1,0:T(8,128)(2,1)S(1)}, u32[]{:S(2)}, u32[]{:S(2)}) %collective-permute-start.7) | collective-permute-done | bytes 163872 | tf_op jit(solution)/shard_map/cond/branch_1_fun/ppermute | solution.py:27
  64.8 1.5 copy-done.4
  66.4 3.0 %tick_layer.8 = (bf16[4,128,2560]{2,1,0:T(8,128)(2,1)S(1)}, bf16[64,2560]{1,0:T(8,128)(2,1)S(1)}, bf16[64,128]{1,0:T(8,128)(2,1)S(1)}, bf16[64,128]{1,0:T(8,128)(2,1)S(1)}) custom-call(s32[4]{0:T(128)S(1)} %pad_add_fusion.levels_ref, bf16[128,2560]{1,0:T(8,128)(2,1)S(1)} %bitcast.101, ...), custom_call_target="tpu_custom_call", output_to_operand_aliasing={{0}: (5, {})} | custom-call | flops 4294967296 | bytes 8388608 | tf_op jit(solution)/shard_map/tick_layer/pallas_call | solution.py:184
  69.5 1.3 tick_layer.9
  70.8 7.8 %collective-permute-start.9 = (bf16[64,2560]{1,0:T(8,128)(2,1)S(1)}, bf16[64,2560]{1,0:T(8,128)(2,1)S(1)}, u32[]{:S(2)}, u32[]{:S(2)}) collective-permute-start(bf16[64,2560]{1,0:T(8,128)(2,1)S(1)} %get-tuple-element.96), channel_id=1, source_target_pairs={{0,496},{16,0},{32,16},{48,32},{64,48},{80,64},{96,80},{112,96},{1... | collective-permute-start | bytes 983048 | tf_op jit(solution)/shard_map/ppermute | solution.py:344
  78.6 2.2 %collective-permute-start.10 = (bf16[64,2560]{1,0:T(8,128)(2,1)S(1)}, bf16[64,2560]{1,0:T(8,128)(2,1)S(1)}, u32[]{:S(2)}, u32[]{:S(2)}) collective-permute-start(bf16[64,2560]{1,0:T(8,128)(2,1)S(1)} %get-tuple-element.100), channel_id=1, source_target_pairs={{0,496},{16,0},{32,16},{48,32},{64,48},{80,64},{96,80},{112,96},{1... | collective-permute-start | bytes 983048 | tf_op jit(solution)/shard_map/ppermute | solution.py:344
  80.9 1.6 forward_rest.1
  82.5 8.4 %collective-permute-done.10.incoming_ref = bf16[64,2560]{1,0:T(8,128)(2,1)S(1)} collective-permute-done((bf16[64,2560]{1,0:T(8,128)(2,1)S(1)}, bf16[64,2560]{1,0:T(8,128)(2,1)S(1)}, u32[]{:S(2)}, u32[]{:S(2)}) %collective-permute-start.10) | collective-permute-done | bytes 327712 | tf_op jit(solution)/shard_map/ppermute | solution.py:344
  90.9 1.2 tick_layer.10
  92.2 1.9 collective-permute-start.12
  94.1 1.2 tick_layer.11
  95.4 1.9 collective-permute-start.11
  97.3 7.2 %collective-permute-done.12.incoming_ref = bf16[64,2560]{1,0:T(8,128)(2,1)S(1)} collective-permute-done((bf16[64,2560]{1,0:T(8,128)(2,1)S(1)}, bf16[64,2560]{1,0:T(8,128)(2,1)S(1)}, u32[]{:S(2)}, u32[]{:S(2)}) %collective-permute-start.12) | collective-permute-done | bytes 327712 | tf_op jit(solution)/shard_map/ppermute | solution.py:366
  104.5 1.2 tick_layer.12
  105.7 1.9 collective-permute-start.14
  107.6 0.3 collective-permute-done.11.incoming_ref
  108.0 1.2 tick_layer.13
  109.2 1.9 collective-permute-start.13
  111.2 6.9 %collective-permute-done.14.incoming_ref = bf16[64,2560]{1,0:T(8,128)(2,1)S(1)} collective-permute-done((bf16[64,2560]{1,0:T(8,128)(2,1)S(1)}, bf16[64,2560]{1,0:T(8,128)(2,1)S(1)}, u32[]{:S(2)}, u32[]{:S(2)}) %collective-permute-start.14) | collective-permute-done | bytes 327712 | tf_op jit(solution)/shard_map/ppermute | solution.py:366
  118.0 1.2 tick_layer.14
  119.3 2.3 %collective-permute-done.13.incoming_ref = bf16[64,2560]{1,0:T(8,128)(2,1)S(1)} collective-permute-done((bf16[64,2560]{1,0:T(8,128)(2,1)S(1)}, bf16[64,2560]{1,0:T(8,128)(2,1)S(1)}, u32[]{:S(2)}, u32[]{:S(2)}) %collective-permute-start.13) | collective-permute-done | bytes 327712 | tf_op jit(solution)/shard_map/ppermute | solution.py:366
  121.5 1.3 tick_layer.15
  122.8 1.9 collective-permute-start.15
  124.8 72.5 %conditional.3 = (f32[160,512]{1,0:T(8,128)}) conditional(s32[]{:T(128)} %convert_element_type.10, (bf16[4,128,2560]{2,1,0:T(8,128)(2,1)S(1)}, bf16[512,128]{1,0:T(8,128)(2,1)S(1)}, bf16[4,128,2560]{2,1,0:T(8,128)(2,1)S(1)}, bf16[4,128,128]{2,1,0:T(8,128)(2,1)S(1)}) %tuple.43, (s32[4]{0:T(128)S(1)}, bf16[512,128]{1,0:T(8,128)(2,1)S(1)}, ...), branch_computations={%region_2.3_spmd, %region_3.4_spmd} | conditional | flops 4296278016 | bytes 25954380 | solution.py:395
  125.3 1.0 copy-done.2
  126.3 4.0 %weight_products.1 = bf16[2560,512]{1,0:T(8,128)(2,1)S(1)} custom-call(bf16[4,128,2560]{2,1,0:T(8,128)(2,1)} %copy-done.2, bf16[4,128,2560]{2,1,0:T(8,128)(2,1)S(1)} %get-tuple-element.51.grads_ref, bf16[512,256]{1,0:T(8,128)(2,1)S(1)} %pad_maximum_fusion.3.lats_ref, bf16[512,256]{1,0:T(8,128)(2,1)S(1)} %bitcast.100), custom_call_target="tpu_custom_call" | custom-call | flops 4294967296 | bytes 8388608 | tf_op jit(solution)/shard_map/cond/branch_1_fun/weight_products/pallas_call | solution.py:229
  130.3 65.9 %all_to_all.13.moved_ref = bf16[16,160,512]{2,1,0:T(8,128)(2,1)S(1)} all-to-all(bf16[16,160,512]{2,1,0:T(8,128)(2,1)S(1)} %bitcast.99), channel_id=1, replica_groups=mesh['section'=32,'dp'=16] {'dp'}, dimensions={0} | all-to-all | bytes 5242880 | tf_op jit(solution)/shard_map/cond/branch_1_fun/all_to_all | solution.py:373
  196.3 1.1 sum_partials.3
  197.3 1.7 finish.1
  199.0 2.0 copy.58
  (56 shorter events, 1.0 us)
Async XLA Ops:
  0.6 0.9 copy-start.6
  0.6 0.9 copy-start.7
  1.6 64.8 %copy-start = (bf16[1,128,2560]{2,1,0:T(8,128)(2,1)S(1)}, bf16[1,128,2560]{2,1,0:T(8,128)(2,1)}, u32[]{:S(2)}) copy-start(bf16[1,128,2560]{2,1,0:T(8,128)(2,1)} %param.9) | copy-start | bytes 1966084
  2.3 11.2 %collective-permute-start = (bf16[2,160,256]{2,1,0:T(8,128)(2,1)}, bf16[2,160,256]{2,1,0:T(8,128)(2,1)}, u32[]{:S(2)}, u32[]{:S(2)}) collective-permute-start(bf16[2,160,256]{2,1,0:T(8,128)(2,1)} %pad_maximum_fusion.2), channel_id=1, source_target_pairs={{0,1},{1,0},{2,3},{3,2},{4,5},{5,4},{6,7},{7,6},{8,9},{9,8},{10,11... | collective-permute-start | bytes 491528 | tf_op jit(solution)/shard_map/cond/branch_1_fun/ppermute | solution.py:31
  14.5 17.2 %collective-permute-start.1 = (bf16[2,2,160,256]{3,2,1,0:T(8,128)(2,1)S(1)}, bf16[2,2,160,256]{3,2,1,0:T(8,128)(2,1)S(1)}, u32[]{:S(2)}, u32[]{:S(2)}) collective-permute-start(bf16[2,2,160,256]{3,2,1,0:T(8,128)(2,1)S(1)} %pad_maximum_fusion.1), channel_id=1, source_target_pairs={{0,2},{1,3},{2,4},{3,5},{4,6},{5,7},{6,8},{7,9},{8,10},{9,11},{10,... | collective-permute-start | bytes 983048 | tf_op jit(solution)/shard_map/cond/branch_1_fun/ppermute | solution.py:27
  18.5 15.2 %collective-permute-start.2 = (bf16[2,2,160,256]{3,2,1,0:T(8,128)(2,1)S(1)}, bf16[2,2,160,256]{3,2,1,0:T(8,128)(2,1)S(1)}, u32[]{:S(2)}, u32[]{:S(2)}) collective-permute-start(bf16[2,2,160,256]{3,2,1,0:T(8,128)(2,1)S(1)} %pad_maximum_fusion.1), channel_id=1, source_target_pairs={{0,14},{1,15},{2,0},{3,1},{4,2},{5,3},{6,4},{7,5},{8,6},{9,7},{10,... | collective-permute-start | bytes 983048 | tf_op jit(solution)/shard_map/cond/branch_1_fun/ppermute | solution.py:27
  27.1 4.6 %copy-start.3 = (bf16[2,8,2,160,256]{4,3,2,1,0:T(8,128)(2,1)S(1)}, bf16[2,8,2,160,256]{4,3,2,1,0:T(8,128)(2,1)}, u32[]{:S(2)}) copy-start(bf16[2,8,2,160,256]{4,3,2,1,0:T(8,128)(2,1)} %unset.4) | copy-start | bytes 7864324 | tf_op jit(solution)/shard_map/cond
  31.7 10.2 %collective-permute-start.3 = (bf16[2,2,160,256]{3,2,1,0:T(8,128)(2,1)S(1)}, bf16[2,2,160,256]{3,2,1,0:T(8,128)(2,1)S(1)}, u32[]{:S(2)}, u32[]{:S(2)}) collective-permute-start(bf16[2,2,160,256]{3,2,1,0:T(8,128)(2,1)S(1)} %collective-permute-done.1), channel_id=1, source_target_pairs={{0,2},{1,3},{2,4},{3,5},{4,6},{5,7},{6,8},{7,9},{8,10},{9,11},{10,... | collective-permute-start | bytes 983048 | tf_op jit(solution)/shard_map/cond/branch_1_fun/ppermute | solution.py:27
  33.6 10.2 %collective-permute-start.4 = (bf16[2,2,160,256]{3,2,1,0:T(8,128)(2,1)S(1)}, bf16[2,2,160,256]{3,2,1,0:T(8,128)(2,1)S(1)}, u32[]{:S(2)}, u32[]{:S(2)}) collective-permute-start(bf16[2,2,160,256]{3,2,1,0:T(8,128)(2,1)S(1)} %collective-permute-done.2), channel_id=1, source_target_pairs={{0,14},{1,15},{2,0},{3,1},{4,2},{5,3},{6,4},{7,5},{8,6},{9,7},{10,... | collective-permute-start | bytes 983048 | tf_op jit(solution)/shard_map/cond/branch_1_fun/ppermute | solution.py:27
  41.9 15.6 %collective-permute-start.5 = (bf16[2,2,160,256]{3,2,1,0:T(8,128)(2,1)S(1)}, bf16[2,2,160,256]{3,2,1,0:T(8,128)(2,1)S(1)}, u32[]{:S(2)}, u32[]{:S(2)}) collective-permute-start(bf16[2,2,160,256]{3,2,1,0:T(8,128)(2,1)S(1)} %collective-permute-done.3), channel_id=1, source_target_pairs={{0,2},{1,3},{2,4},{3,5},{4,6},{5,7},{6,8},{7,9},{8,10},{9,11},{10,... | collective-permute-start | bytes 983048 | tf_op jit(solution)/shard_map/cond/branch_1_fun/ppermute | solution.py:27
  43.8 8.6 %collective-permute-start.6 = (bf16[2,2,160,256]{3,2,1,0:T(8,128)(2,1)S(1)}, bf16[2,2,160,256]{3,2,1,0:T(8,128)(2,1)S(1)}, u32[]{:S(2)}, u32[]{:S(2)}) collective-permute-start(bf16[2,2,160,256]{3,2,1,0:T(8,128)(2,1)S(1)} %collective-permute-done.4), channel_id=1, source_target_pairs={{0,14},{1,15},{2,0},{3,1},{4,2},{5,3},{6,4},{7,5},{8,6},{9,7},{10,... | collective-permute-start | bytes 983048 | tf_op jit(solution)/shard_map/cond/branch_1_fun/ppermute | solution.py:27
  52.4 7.3 %collective-permute-start.8 = (bf16[2,1,160,256]{3,2,1,0:T(8,128)(2,1)S(1)}, bf16[2,1,160,256]{3,2,1,0:T(8,128)(2,1)S(1)}, u32[]{:S(2)}, u32[]{:S(2)}) collective-permute-start(bf16[2,1,160,256]{3,2,1,0:T(8,128)(2,1)S(1)} %slice.25), channel_id=1, source_target_pairs={{0,14},{1,15},{2,0},{3,1},{4,2},{5,3},{6,4},{7,5},{8,6},{9,7},{10,... | collective-permute-start | bytes 491528 | tf_op jit(solution)/shard_map/cond/branch_1_fun/ppermute | solution.py:27
  57.5 7.3 %collective-permute-start.7 = (bf16[2,1,160,256]{3,2,1,0:T(8,128)(2,1)S(1)}, bf16[2,1,160,256]{3,2,1,0:T(8,128)(2,1)S(1)}, u32[]{:S(2)}, u32[]{:S(2)}) collective-permute-start(bf16[2,1,160,256]{3,2,1,0:T(8,128)(2,1)S(1)} %slice.24), channel_id=1, source_target_pairs={{0,2},{1,3},{2,4},{3,5},{4,6},{5,7},{6,8},{7,9},{8,10},{9,11},{10,... | collective-permute-start | bytes 491528 | tf_op jit(solution)/shard_map/cond/branch_1_fun/ppermute | solution.py:27
  64.8 1.5 copy-start.4
  66.3 3.1 %copy-start.8 = (f32[4,128,128]{2,1,0:T(8,128)}, f32[4,128,128]{2,1,0:T(8,128)S(1)}, u32[]{:S(2)}) copy-start(f32[4,128,128]{2,1,0:T(8,128)S(1)} %get-tuple-element.93.inverse_ref) | copy-start | bytes 786436
  66.4 3.1 %copy-start.1 = (bf16[4,128,2560]{2,1,0:T(8,128)(2,1)S(1)}, bf16[4,128,2560]{2,1,0:T(8,128)(2,1)}, u32[]{:S(2)}) copy-start(bf16[4,128,2560]{2,1,0:T(8,128)(2,1)} %get-tuple-element.92.normed_ref) | copy-start | bytes 7864324
  66.4 3.1 %copy-start.5 = (bf16[2,2560,256]{2,1,0:T(8,128)(2,1)S(1)}, bf16[2,2560,256]{2,1,0:T(8,128)(2,1)}, u32[]{:S(2)}) copy-start(bf16[2,2560,256]{2,1,0:T(8,128)(2,1)} %get-tuple-element.94.maps_ref) | copy-start | bytes 7864324
  70.8 23.3 %collective-permute-start.9 = (bf16[64,2560]{1,0:T(8,128)(2,1)S(1)}, bf16[64,2560]{1,0:T(8,128)(2,1)S(1)}, u32[]{:S(2)}, u32[]{:S(2)}) collective-permute-start(bf16[64,2560]{1,0:T(8,128)(2,1)S(1)} %get-tuple-element.96), channel_id=1, source_target_pairs={{0,496},{16,0},{32,16},{48,32},{64,48},{80,64},{96,80},{112,96},{1... | collective-permute-start | bytes 983048 | tf_op jit(solution)/shard_map/ppermute | solution.py:344
  78.6 12.3 %collective-permute-start.10 = (bf16[64,2560]{1,0:T(8,128)(2,1)S(1)}, bf16[64,2560]{1,0:T(8,128)(2,1)S(1)}, u32[]{:S(2)}, u32[]{:S(2)}) collective-permute-start(bf16[64,2560]{1,0:T(8,128)(2,1)S(1)} %get-tuple-element.100), channel_id=1, source_target_pairs={{0,496},{16,0},{32,16},{48,32},{64,48},{80,64},{96,80},{112,96},{1... | collective-permute-start | bytes 983048 | tf_op jit(solution)/shard_map/ppermute | solution.py:344
  80.9 10.0 %copy-start.9 = (f32[4,128,128]{2,1,0:T(8,128)S(1)}, f32[4,128,128]{2,1,0:T(8,128)}, u32[]{:S(2)}) copy-start(f32[4,128,128]{2,1,0:T(8,128)} %copy-done.8) | copy-start | bytes 786436
  92.2 12.3 %collective-permute-start.12 = (bf16[64,2560]{1,0:T(8,128)(2,1)S(1)}, bf16[64,2560]{1,0:T(8,128)(2,1)S(1)}, u32[]{:S(2)}, u32[]{:S(2)}) collective-permute-start(bf16[64,2560]{1,0:T(8,128)(2,1)S(1)} %get-tuple-element.104), channel_id=1, source_target_pairs={{0,496},{16,0},{32,16},{48,32},{64,48},{80,64},{96,80},{112,96},{1... | collective-permute-start | bytes 983048 | tf_op jit(solution)/shard_map/ppermute | solution.py:366
  95.4 12.6 %collective-permute-start.11 = (bf16[64,2560]{1,0:T(8,128)(2,1)S(1)}, bf16[64,2560]{1,0:T(8,128)(2,1)S(1)}, u32[]{:S(2)}, u32[]{:S(2)}) collective-permute-start(bf16[64,2560]{1,0:T(8,128)(2,1)S(1)} %get-tuple-element.103), channel_id=1, source_target_pairs={{0,496},{16,0},{32,16},{48,32},{64,48},{80,64},{96,80},{112,96},{1... | collective-permute-start | bytes 983048 | tf_op jit(solution)/shard_map/ppermute | solution.py:366
  105.7 12.3 %collective-permute-start.14 = (bf16[64,2560]{1,0:T(8,128)(2,1)S(1)}, bf16[64,2560]{1,0:T(8,128)(2,1)S(1)}, u32[]{:S(2)}, u32[]{:S(2)}) collective-permute-start(bf16[64,2560]{1,0:T(8,128)(2,1)S(1)} %get-tuple-element.108), channel_id=1, source_target_pairs={{0,496},{16,0},{32,16},{48,32},{64,48},{80,64},{96,80},{112,96},{1... | collective-permute-start | bytes 983048 | tf_op jit(solution)/shard_map/ppermute | solution.py:366
  109.2 12.3 %collective-permute-start.13 = (bf16[64,2560]{1,0:T(8,128)(2,1)S(1)}, bf16[64,2560]{1,0:T(8,128)(2,1)S(1)}, u32[]{:S(2)}, u32[]{:S(2)}) collective-permute-start(bf16[64,2560]{1,0:T(8,128)(2,1)S(1)} %get-tuple-element.107), channel_id=1, source_target_pairs={{0,496},{16,0},{32,16},{48,32},{64,48},{80,64},{96,80},{112,96},{1... | collective-permute-start | bytes 983048 | tf_op jit(solution)/shard_map/ppermute | solution.py:366
  122.8 76.2 %collective-permute-start.15 = (bf16[128,2560]{1,0:T(8,128)(2,1)S(1)}, bf16[128,2560]{1,0:T(8,128)(2,1)}, u32[]{:S(2)}, u32[]{:S(2)}) collective-permute-start(bf16[128,2560]{1,0:T(8,128)(2,1)S(1)} %get-tuple-element.112), channel_id=1, source_target_pairs={{0,496},{16,0},{32,16},{48,32},{64,48},{80,64},{96,80},{112,96},{1... | collective-permute-start | bytes 1966088 | tf_op jit(solution)/shard_map/ppermute | solution.py:366
  124.8 1.5 copy-start.2

commit v12 on v8

--- a/solution.py
+++ b/solution.py
@@ -47,9 +47,10 @@
     for step in range(1, half):
         right, left = shifted(right, n_z, 1), shifted(left, n_z, -1)
         full = placed(full, right, -step)
-        full = placed(full, left, step)
-    right, left = shifted(right[:, :1], n_z, 1), shifted(left[:, 1:], n_z, -1)
-    return placed(full, jnp.concatenate([right, left], axis=1), half)
+        if step < half - 1:
+            full = placed(full, left, step)
+    full = placed(full, shifted(right, n_z, 1), -half)
+    return placed(full, left, half - 1)
 
 
 def empty_kernel(out_ref):
@@ -207,6 +208,33 @@
     )(levels, incoming, normed, inverse, maps, *forward, stack)
 
 
+def products_kernel(normed_ref, grads_ref, lats_ref, acts_ref, out_ref):
+    lanes = lats_ref.shape[1]
+    contract = (((0,), (0,)), ((), ()))
+    for i, (wide_ref, narrow_ref) in enumerate(((normed_ref, lats_ref), (grads_ref, acts_ref))):
+        wide = wide_ref[...].reshape(-1, wide_ref.shape[2])
+        part = lax.dot_general(wide, narrow_ref[...], contract, preferred_element_type=F32)
+        out_ref[:, i * lanes : (i + 1) * lanes] = part.astype(BF16)
+
+
+def kernel_products(normed, grads, lats, acts):
+    ticks, rows, width = normed.shape
+    lanes = lats.shape[1]
+    run = width // 4
+    by_run = pl.BlockSpec((ticks, rows, run), lambda i: (0, 0, i))
+    whole = pl.BlockSpec((ticks * rows, lanes), lambda i: (0, 0))
+    return pl.pallas_call(
+        products_kernel,
+        grid=(width // run,),
+        out_shape=jax.ShapeDtypeStruct((width, 2 * lanes), BF16),
+        in_specs=[by_run, by_run, whole, whole],
+        out_specs=pl.BlockSpec((run, 2 * lanes), lambda i: (i, 0)),
+        compiler_params=LIMIT,
+        cost_estimate=COST,
+        name="weight_products",
+    )(normed, grads, lats, acts)
+
+
 def beside_kernel(left_ref, right_ref, out_ref):
     lanes = left_ref.shape[1]
     out_ref[:, :lanes] = left_ref[...]
@@ -328,16 +356,18 @@
     grads_all = stack.reshape(-1, width)
     actives = jnp.concatenate([jnp.concatenate(first_actives)[None], actives], axis=0)
 
+    def summed_parts(parts):
+        moved = lax.all_to_all(parts.reshape(n_dp, share, -1), "dp", 0, 0, tiled=True)
+        return summed(moved, 4 * rank)
+
     def products(lats, acts):
         contract = (((0,), (0,)), ((), ()))
         down = lax.dot_general(normed_all, lats, contract, preferred_element_type=F32)
         up = lax.dot_general(grads_all, acts, contract, preferred_element_type=F32)
-        both = beside(down.astype(BF16), up.astype(BF16))
-        moved = lax.all_to_all(both.reshape(n_dp, share, -1), "dp", 0, 0, tiled=True)
-        return summed(moved, 4 * rank)
+        return beside(down.astype(BF16), up.astype(BF16))
 
     def reduce_one(lats, acts):
-        return products(lats.reshape(-1, rank), acts.reshape(-1, rank))
+        return summed_parts(products(lats.reshape(-1, rank), acts.reshape(-1, rank)))
 
     def reduce_two(lats, acts):
         level = level_stack[:, None, None]
@@ -347,7 +377,7 @@
             both = [jnp.where(level == 1, value, zero), jnp.where(level == 0, value, zero)]
             return jnp.concatenate(both, axis=2).reshape(-1, 2 * rank)
 
-        return products(split(lats), split(acts))
+        return summed_parts(kernel_products(normed, stack, split(lats), split(acts)))
 
     total = lax.cond(two_layers, reduce_two, reduce_one, jnp.concatenate(grad_latents).reshape(actives.shape), actives)
     grad_out, down_grad, up_grad = finish(total, *moving, share, rank)

time: 192 us -> 189 us (0.984)
  matrix products: 6.46 us -> 0 us
  waiting for transfers between devices: 35.3 us -> 40 us
  starting transfers between devices: 58.4 us -> 54 us
  Pallas kernels: 19.6 us -> 23.8 us
    dot_general x2 -> x0, matrix products: 6.46 us -> none  [the longest x1 3.58 us: products(): up = lax.dot_general(grads_all, acts, contract, preferred_element_type=F32)]
    ppermute x8 -> x7, waiting for transfers between devices: 8.24 us -> 13 us  [shifted(): return lax.ppermute(value, 'dp', dp_pairs(n_z, step, 0))]
    ppermute x8 -> x7, starting transfers between devices: 32.1 us -> 27.5 us  [shifted(): return lax.ppermute(value, 'dp', dp_pairs(n_z, step, 0))]
    pallas_call x1, Pallas kernels: 0.24 us -> 4.38 us  [kernel_products(): pl.pallas_call(products_kernel, grid=(width // run,), out_shape=jax.Shape...]
    all_to_all x1, blocking collectives: 64.8 us -> 62.9 us  [summed_parts(): lax.all_to_all(parts.reshape(n_dp, share, -1), 'dp', 0, 0, tiled=True)]
  transfers between devices with their start and end apart: 17 -> 16, of which waited for: 10 -> 9; matrix products, arithmetic and copies ran while one was open for 4% -> 0% of each run, Pallas kernels for 7% -> 10%
where the time goes in v12:
time: 189 us; the launch traced here: 188 us
  blocking collectives  62.9 us (33%)
  starting transfers between devices  54 us (29%)
  waiting for transfers between devices  40 us (21%)
  Pallas kernels  23.8 us (13%)
  local copies, waits for them, and re-layouts  3.76 us (2%)
  other arithmetic  2.17 us (1%)
    all_to_all x1, blocking collectives, summed_parts(): lax.all_to_all(parts.reshape(n_dp, share, -1), 'dp', 0, 0, tiled=True)  62.9 us
    ppermute x7, starting transfers between devices, shifted(): return lax.ppermute(value, 'dp', dp_pairs(n_z, step, 0))  27.5 us
    ppermute x8, starting transfers between devices, on_device(): moving.append(lax.ppermute(sent, 'section', down_one))  22.1 us
    ppermute x8, waiting for transfers between devices, on_device(): moving.append(lax.ppermute(sent, 'section', down_one))  20.4 us
    ppermute x7, waiting for transfers between devices, shifted(): return lax.ppermute(value, 'dp', dp_pairs(n_z, step, 0))  13 us
    pallas_call x8, Pallas kernels, tick_layer(): pl.pallas_call(functools.partial(tick_kernel, tick, part), grid_spec=pltp...  11.9 us
    ppermute x1, waiting for transfers between devices, swapped(): return lax.ppermute(value, 'dp', dp_pairs(n_z, 0, 1))  6.54 us
    pallas_call x1, Pallas kernels, norms(): pl.pallas_call(norm_kernel, grid=(ticks,), out_shape=[jax.ShapeDtypeStruc...  4.57 us
  transfers between devices with their start and end apart: 16, of which 9 were waited for; matrix products, arithmetic and copies ran while one was open for 0% of the time, Pallas kernels for 10%

profile of v12, /device:TPU:63, one launch (start us, length us, event | category | flops | bytes accessed | tf_op | source)
XLA Modules:
  0.0 187.9 jit_solution(3841551534378121350)
XLA Ops:
  0.7 0.8 copy-done.8
  1.6 59.8 %conditional.2 = (bf16[2,2560,256]{2,1,0:T(8,128)(2,1)}, bf16[4,128,2560]{2,1,0:T(8,128)(2,1)}, f32[4,128,128]{2,1,0:T(8,128)S(1)}) conditional(s32[]{:T(128)} %convert_element_type.10, (bf16[2,128,160]{1,2,0:T(8,128)(2,1)S(1)}, bf16[2,128,160]{1,2,0:T(8,128)(2,1)S(1)}, bf16[4,1,128,2560]{3,2,1,0:T(8,128)(2,1)}) %tuple.45, ...), branch_computations={%region_0.1_spmd, %region_1.2_spmd} | conditional | flops 4296441856 | bytes 46729012 | solution.py:330
  1.6 0.7 pad_maximum_fusion.2
  2.3 4.4 %collective-permute-start = (bf16[2,160,256]{2,1,0:T(8,128)(2,1)}, bf16[2,160,256]{2,1,0:T(8,128)(2,1)}, u32[]{:S(2)}, u32[]{:S(2)}) collective-permute-start(bf16[2,160,256]{2,1,0:T(8,128)(2,1)} %pad_maximum_fusion.2), channel_id=1, source_target_pairs={{0,1},{1,0},{2,3},{3,2},{4,5},{5,4},{6,7},{7,6},{8,9},{9,8},{10,11... | collective-permute-start | bytes 491528 | tf_op jit(solution)/shard_map/cond/branch_1_fun/ppermute | solution.py:31
  6.9 6.5 %collective-permute-done = bf16[2,160,256]{2,1,0:T(8,128)(2,1)} collective-permute-done((bf16[2,160,256]{2,1,0:T(8,128)(2,1)}, bf16[2,160,256]{2,1,0:T(8,128)(2,1)}, u32[]{:S(2)}, u32[]{:S(2)}) %collective-permute-start) | collective-permute-done | bytes 163872 | tf_op jit(solution)/shard_map/cond/branch_1_fun/ppermute | solution.py:31
  13.5 0.9 select_bitcast_fusion.1
  14.5 4.0 %collective-permute-start.1 = (bf16[2,2,160,256]{3,2,1,0:T(8,128)(2,1)S(1)}, bf16[2,2,160,256]{3,2,1,0:T(8,128)(2,1)S(1)}, u32[]{:S(2)}, u32[]{:S(2)}) collective-permute-start(bf16[2,2,160,256]{3,2,1,0:T(8,128)(2,1)S(1)} %pad_maximum_fusion.1), channel_id=1, source_target_pairs={{0,2},{1,3},{2,4},{3,5},{4,6},{5,7},{6,8},{7,9},{8,10},{9,11},{10,... | collective-permute-start | bytes 983048 | tf_op jit(solution)/shard_map/cond/branch_1_fun/ppermute | solution.py:27
  18.5 8.6 %collective-permute-start.2 = (bf16[2,2,160,256]{3,2,1,0:T(8,128)(2,1)S(1)}, bf16[2,2,160,256]{3,2,1,0:T(8,128)(2,1)S(1)}, u32[]{:S(2)}, u32[]{:S(2)}) collective-permute-start(bf16[2,2,160,256]{3,2,1,0:T(8,128)(2,1)S(1)} %pad_maximum_fusion.1), channel_id=1, source_target_pairs={{0,14},{1,15},{2,0},{3,1},{4,2},{5,3},{6,4},{7,5},{8,6},{9,7},{10,... | collective-permute-start | bytes 983048 | tf_op jit(solution)/shard_map/cond/branch_1_fun/ppermute | solution.py:27
  27.1 4.6 %norms.3 = (bf16[4,128,2560]{2,1,0:T(8,128)(2,1)}, f32[4,128,128]{2,1,0:T(8,128)S(1)}) custom-call(bf16[4,1,128,2560]{3,2,1,0:T(8,128)(2,1)} %get-tuple-element.43.x_ref), custom_call_target="tpu_custom_call" | custom-call | flops 4294967296 | bytes 8388608 | tf_op jit(solution)/shard_map/cond/branch_1_fun/norms/pallas_call | solution.py:78
  31.6 1.9 %collective-permute-start.3 = (bf16[2,2,160,256]{3,2,1,0:T(8,128)(2,1)S(1)}, bf16[2,2,160,256]{3,2,1,0:T(8,128)(2,1)S(1)}, u32[]{:S(2)}, u32[]{:S(2)}) collective-permute-start(bf16[2,2,160,256]{3,2,1,0:T(8,128)(2,1)S(1)} %collective-permute-done.1), channel_id=1, source_target_pairs={{0,2},{1,3},{2,4},{3,5},{4,6},{5,7},{6,8},{7,9},{8,10},{9,11},{10,... | collective-permute-start | bytes 983048 | tf_op jit(solution)/shard_map/cond/branch_1_fun/ppermute | solution.py:27
  33.6 4.6 %collective-permute-start.4 = (bf16[2,2,160,256]{3,2,1,0:T(8,128)(2,1)S(1)}, bf16[2,2,160,256]{3,2,1,0:T(8,128)(2,1)S(1)}, u32[]{:S(2)}, u32[]{:S(2)}) collective-permute-start(bf16[2,2,160,256]{3,2,1,0:T(8,128)(2,1)S(1)} %collective-permute-done.2), channel_id=1, source_target_pairs={{0,14},{1,15},{2,0},{3,1},{4,2},{5,3},{6,4},{7,5},{8,6},{9,7},{10,... | collective-permute-start | bytes 983048 | tf_op jit(solution)/shard_map/cond/branch_1_fun/ppermute | solution.py:27
  38.2 3.6 %collective-permute-done.3 = bf16[2,2,160,256]{3,2,1,0:T(8,128)(2,1)S(1)} collective-permute-done((bf16[2,2,160,256]{3,2,1,0:T(8,128)(2,1)S(1)}, bf16[2,2,160,256]{3,2,1,0:T(8,128)(2,1)S(1)}, u32[]{:S(2)}, u32[]{:S(2)}) %collective-permute-start.3) | collective-permute-done | bytes 327712 | tf_op jit(solution)/shard_map/cond/branch_1_fun/ppermute | solution.py:27
  41.8 1.9 %collective-permute-start.5 = (bf16[2,2,160,256]{3,2,1,0:T(8,128)(2,1)S(1)}, bf16[2,2,160,256]{3,2,1,0:T(8,128)(2,1)S(1)}, u32[]{:S(2)}, u32[]{:S(2)}) collective-permute-start(bf16[2,2,160,256]{3,2,1,0:T(8,128)(2,1)S(1)} %collective-permute-done.3), channel_id=1, source_target_pairs={{0,2},{1,3},{2,4},{3,5},{4,6},{5,7},{6,8},{7,9},{8,10},{9,11},{10,... | collective-permute-start | bytes 983048 | tf_op jit(solution)/shard_map/cond/branch_1_fun/ppermute | solution.py:27
  43.8 4.6 %collective-permute-start.7 = (bf16[2,2,160,256]{3,2,1,0:T(8,128)(2,1)S(1)}, bf16[2,2,160,256]{3,2,1,0:T(8,128)(2,1)S(1)}, u32[]{:S(2)}, u32[]{:S(2)}) collective-permute-start(bf16[2,2,160,256]{3,2,1,0:T(8,128)(2,1)S(1)} %collective-permute-done.4), channel_id=1, source_target_pairs={{0,14},{1,15},{2,0},{3,1},{4,2},{5,3},{6,4},{7,5},{8,6},{9,7},{10,... | collective-permute-start | bytes 983048 | tf_op jit(solution)/shard_map/cond/branch_1_fun/ppermute | solution.py:27
  48.4 2.4 %collective-permute-done.5 = bf16[2,2,160,256]{3,2,1,0:T(8,128)(2,1)S(1)} collective-permute-done((bf16[2,2,160,256]{3,2,1,0:T(8,128)(2,1)S(1)}, bf16[2,2,160,256]{3,2,1,0:T(8,128)(2,1)S(1)}, u32[]{:S(2)}, u32[]{:S(2)}) %collective-permute-start.5) | collective-permute-done | bytes 327712 | tf_op jit(solution)/shard_map/cond/branch_1_fun/ppermute | solution.py:27
  50.8 1.9 %collective-permute-start.6 = (bf16[2,2,160,256]{3,2,1,0:T(8,128)(2,1)S(1)}, bf16[2,2,160,256]{3,2,1,0:T(8,128)(2,1)S(1)}, u32[]{:S(2)}, u32[]{:S(2)}) collective-permute-start(bf16[2,2,160,256]{3,2,1,0:T(8,128)(2,1)S(1)} %collective-permute-done.5), channel_id=1, source_target_pairs={{0,2},{1,3},{2,4},{3,5},{4,6},{5,7},{6,8},{7,9},{8,10},{9,11},{10,... | collective-permute-start | bytes 983048 | tf_op jit(solution)/shard_map/cond/branch_1_fun/ppermute | solution.py:27
  52.8 7.0 %collective-permute-done.6 = bf16[2,2,160,256]{3,2,1,0:T(8,128)(2,1)S(1)} collective-permute-done((bf16[2,2,160,256]{3,2,1,0:T(8,128)(2,1)S(1)}, bf16[2,2,160,256]{3,2,1,0:T(8,128)(2,1)S(1)}, u32[]{:S(2)}, u32[]{:S(2)}) %collective-permute-start.6) | collective-permute-done | bytes 327712 | tf_op jit(solution)/shard_map/cond/branch_1_fun/ppermute | solution.py:27
  59.9 1.5 copy-done.6
  61.5 3.0 %tick_layer.8 = (bf16[4,128,2560]{2,1,0:T(8,128)(2,1)S(1)}, bf16[64,2560]{1,0:T(8,128)(2,1)S(1)}, bf16[64,128]{1,0:T(8,128)(2,1)S(1)}, bf16[64,128]{1,0:T(8,128)(2,1)S(1)}) custom-call(s32[4]{0:T(128)S(1)} %pad_add_fusion.levels_ref, bf16[128,2560]{1,0:T(8,128)(2,1)S(1)} %bitcast.98, ...), custom_call_target="tpu_custom_call", output_to_operand_aliasing={{0}: (5, {})} | custom-call | flops 4294967296 | bytes 8388608 | tf_op jit(solution)/shard_map/tick_layer/pallas_call | solution.py:182
  64.6 7.3 %collective-permute-start.8 = (bf16[64,2560]{1,0:T(8,128)(2,1)S(1)}, bf16[64,2560]{1,0:T(8,128)(2,1)S(1)}, u32[]{:S(2)}, u32[]{:S(2)}) collective-permute-start(bf16[64,2560]{1,0:T(8,128)(2,1)S(1)} %get-tuple-element.99), channel_id=1, source_target_pairs={{0,496},{16,0},{32,16},{48,32},{64,48},{80,64},{96,80},{112,96},{1... | collective-permute-start | bytes 983048 | tf_op jit(solution)/shard_map/ppermute | solution.py:344
  71.9 1.3 tick_layer.9
  73.2 3.3 %collective-permute-start.9 = (bf16[64,2560]{1,0:T(8,128)(2,1)S(1)}, bf16[64,2560]{1,0:T(8,128)(2,1)S(1)}, u32[]{:S(2)}, u32[]{:S(2)}) collective-permute-start(bf16[64,2560]{1,0:T(8,128)(2,1)S(1)} %get-tuple-element.104), channel_id=1, source_target_pairs={{0,496},{16,0},{32,16},{48,32},{64,48},{80,64},{96,80},{112,96},{1... | collective-permute-start | bytes 983048 | tf_op jit(solution)/shard_map/ppermute | solution.py:344
  76.5 1.6 forward_rest.1
  78.2 1.2 tick_layer.10
  79.4 1.9 %collective-permute-start.10 = (bf16[64,2560]{1,0:T(8,128)(2,1)S(1)}, bf16[64,2560]{1,0:T(8,128)(2,1)S(1)}, u32[]{:S(2)}, u32[]{:S(2)}) collective-permute-start(bf16[64,2560]{1,0:T(8,128)(2,1)S(1)} %get-tuple-element.107), channel_id=1, source_target_pairs={{0,496},{16,0},{32,16},{48,32},{64,48},{80,64},{96,80},{112,96},{1... | collective-permute-start | bytes 983048 | tf_op jit(solution)/shard_map/ppermute | solution.py:353
  81.4 4.1 %collective-permute-done.9.incoming_ref = bf16[64,2560]{1,0:T(8,128)(2,1)S(1)} collective-permute-done((bf16[64,2560]{1,0:T(8,128)(2,1)S(1)}, bf16[64,2560]{1,0:T(8,128)(2,1)S(1)}, u32[]{:S(2)}, u32[]{:S(2)}) %collective-permute-start.9) | collective-permute-done | bytes 327712 | tf_op jit(solution)/shard_map/ppermute | solution.py:344
  85.5 1.2 tick_layer.11
  86.8 1.9 %collective-permute-start.11 = (bf16[64,2560]{1,0:T(8,128)(2,1)S(1)}, bf16[64,2560]{1,0:T(8,128)(2,1)S(1)}, u32[]{:S(2)}, u32[]{:S(2)}) collective-permute-start(bf16[64,2560]{1,0:T(8,128)(2,1)S(1)} %get-tuple-element.110), channel_id=1, source_target_pairs={{0,496},{16,0},{32,16},{48,32},{64,48},{80,64},{96,80},{112,96},{1... | collective-permute-start | bytes 983048 | tf_op jit(solution)/shard_map/ppermute | solution.py:353
  88.7 3.0 %collective-permute-done.10.incoming_ref = bf16[64,2560]{1,0:T(8,128)(2,1)S(1)} collective-permute-done((bf16[64,2560]{1,0:T(8,128)(2,1)S(1)}, bf16[64,2560]{1,0:T(8,128)(2,1)S(1)}, u32[]{:S(2)}, u32[]{:S(2)}) %collective-permute-start.10) | collective-permute-done | bytes 327712 | tf_op jit(solution)/shard_map/ppermute | solution.py:353
  91.7 1.2 tick_layer.12
  93.0 1.9 %collective-permute-start.12 = (bf16[64,2560]{1,0:T(8,128)(2,1)S(1)}, bf16[64,2560]{1,0:T(8,128)(2,1)S(1)}, u32[]{:S(2)}, u32[]{:S(2)}) collective-permute-start(bf16[64,2560]{1,0:T(8,128)(2,1)S(1)} %get-tuple-element.113), channel_id=1, source_target_pairs={{0,496},{16,0},{32,16},{48,32},{64,48},{80,64},{96,80},{112,96},{1... | collective-permute-start | bytes 983048 | tf_op jit(solution)/shard_map/ppermute | solution.py:353
  94.9 4.1 %collective-permute-done.11.incoming_ref = bf16[64,2560]{1,0:T(8,128)(2,1)S(1)} collective-permute-done((bf16[64,2560]{1,0:T(8,128)(2,1)S(1)}, bf16[64,2560]{1,0:T(8,128)(2,1)S(1)}, u32[]{:S(2)}, u32[]{:S(2)}) %collective-permute-start.11) | collective-permute-done | bytes 327712 | tf_op jit(solution)/shard_map/ppermute | solution.py:353
  99.1 1.2 tick_layer.13
  100.3 1.9 %collective-permute-start.13 = (bf16[64,2560]{1,0:T(8,128)(2,1)S(1)}, bf16[64,2560]{1,0:T(8,128)(2,1)S(1)}, u32[]{:S(2)}, u32[]{:S(2)}) collective-permute-start(bf16[64,2560]{1,0:T(8,128)(2,1)S(1)} %get-tuple-element.116), channel_id=1, source_target_pairs={{0,496},{16,0},{32,16},{48,32},{64,48},{80,64},{96,80},{112,96},{1... | collective-permute-start | bytes 983048 | tf_op jit(solution)/shard_map/ppermute | solution.py:353
  102.3 3.0 %collective-permute-done.12.incoming_ref = bf16[64,2560]{1,0:T(8,128)(2,1)S(1)} collective-permute-done((bf16[64,2560]{1,0:T(8,128)(2,1)S(1)}, bf16[64,2560]{1,0:T(8,128)(2,1)S(1)}, u32[]{:S(2)}, u32[]{:S(2)}) %collective-permute-start.12) | collective-permute-done | bytes 327712 | tf_op jit(solution)/shard_map/ppermute | solution.py:353
  105.3 1.2 tick_layer.14
  106.6 6.1 %collective-permute-done.13.incoming_ref = bf16[64,2560]{1,0:T(8,128)(2,1)S(1)} collective-permute-done((bf16[64,2560]{1,0:T(8,128)(2,1)S(1)}, bf16[64,2560]{1,0:T(8,128)(2,1)S(1)}, u32[]{:S(2)}, u32[]{:S(2)}) %collective-permute-start.13) | collective-permute-done | bytes 327712 | tf_op jit(solution)/shard_map/ppermute | solution.py:353
  112.6 1.3 tick_layer.15
  113.9 1.9 %collective-permute-start.15 = (bf16[64,2560]{1,0:T(8,128)(2,1)S(1)}, bf16[64,2560]{1,0:T(8,128)(2,1)S(1)}, u32[]{:S(2)}, u32[]{:S(2)}) collective-permute-start(bf16[64,2560]{1,0:T(8,128)(2,1)S(1)} %get-tuple-element.124), channel_id=1, source_target_pairs={{0,496},{16,0},{32,16},{48,32},{64,48},{80,64},{96,80},{112,96},{1... | collective-permute-start | bytes 983048 | tf_op jit(solution)/shard_map/ppermute | solution.py:353
  115.8 1.9 %collective-permute-start.14 = (bf16[64,2560]{1,0:T(8,128)(2,1)S(1)}, bf16[64,2560]{1,0:T(8,128)(2,1)S(1)}, u32[]{:S(2)}, u32[]{:S(2)}) collective-permute-start(bf16[64,2560]{1,0:T(8,128)(2,1)S(1)} %get-tuple-element.123), channel_id=1, source_target_pairs={{0,496},{16,0},{32,16},{48,32},{64,48},{80,64},{96,80},{112,96},{1... | collective-permute-start | bytes 983048 | tf_op jit(solution)/shard_map/ppermute | solution.py:353
  117.8 69.1 %conditional.3 = (f32[160,512]{1,0:T(8,128)S(1)}) conditional(s32[]{:T(128)} %convert_element_type.10, (bf16[4,128,2560]{2,1,0:T(8,128)(2,1)S(1)}, bf16[512,128]{1,0:T(8,128)(2,1)S(1)}, bf16[4,128,2560]{2,1,0:T(8,128)(2,1)}, bf16[4,128,128]{2,1,0:T(8,128)(2,1)S(1)}) %tuple.41, (s32[4]{0:T(128)S(1)}, bf16[512,128]{1,0:T(8,128)(2,1)S(1)}, ...), branch_computations={%region_2.3_spmd, %region_3.4_spmd} | conditional | flops 4296278016 | bytes 25954380 | solution.py:382
  117.9 0.1 broadcast_select_fusion.1
  118.0 0.2 broadcast_select_fusion.3
  118.3 1.0 copy-done.4
  119.3 4.4 %weight_products.1 = bf16[2560,512]{1,0:T(8,128)(2,1)S(1)} custom-call(bf16[4,128,2560]{2,1,0:T(8,128)(2,1)} %copy-done.4, bf16[4,128,2560]{2,1,0:T(8,128)(2,1)} %get-tuple-element.51.grads_ref, bf16[512,256]{1,0:T(8,128)(2,1)S(1)} %pad_maximum_fusion.3.lats_ref, bf16[512,256]{1,0:T(8,128)(2,1)S(1)} %bitcast.97), custom_call_target="tpu_custom_call" | custom-call | flops 4294967296 | bytes 8388608 | tf_op jit(solution)/shard_map/cond/branch_1_fun/weight_products/pallas_call | solution.py:226
  123.7 62.9 %all_to_all.13.moved_ref = bf16[16,160,512]{2,1,0:T(8,128)(2,1)S(1)} all-to-all(bf16[16,160,512]{2,1,0:T(8,128)(2,1)S(1)} %bitcast.96), channel_id=1, replica_groups=mesh['section'=32,'dp'=16] {'dp'}, dimensions={0} | all-to-all | bytes 5242880 | tf_op jit(solution)/shard_map/cond/branch_1_fun/all_to_all | solution.py:360
  186.6 0.3 sum_partials.3
  186.9 1.0 finish.1
  (55 shorter events, 0.7 us)
Async XLA Ops:
  0.6 0.9 copy-start.8
  0.6 0.9 copy-start.9
  1.6 59.9 %copy-start = (bf16[1,128,2560]{2,1,0:T(8,128)(2,1)S(1)}, bf16[1,128,2560]{2,1,0:T(8,128)(2,1)}, u32[]{:S(2)}) copy-start(bf16[1,128,2560]{2,1,0:T(8,128)(2,1)} %param.9) | copy-start | bytes 1966084
  2.3 11.2 %collective-permute-start = (bf16[2,160,256]{2,1,0:T(8,128)(2,1)}, bf16[2,160,256]{2,1,0:T(8,128)(2,1)}, u32[]{:S(2)}, u32[]{:S(2)}) collective-permute-start(bf16[2,160,256]{2,1,0:T(8,128)(2,1)} %pad_maximum_fusion.2), channel_id=1, source_target_pairs={{0,1},{1,0},{2,3},{3,2},{4,5},{5,4},{6,7},{7,6},{8,9},{9,8},{10,11... | collective-permute-start | bytes 491528 | tf_op jit(solution)/shard_map/cond/branch_1_fun/ppermute | solution.py:31
  14.5 17.2 %collective-permute-start.1 = (bf16[2,2,160,256]{3,2,1,0:T(8,128)(2,1)S(1)}, bf16[2,2,160,256]{3,2,1,0:T(8,128)(2,1)S(1)}, u32[]{:S(2)}, u32[]{:S(2)}) collective-permute-start(bf16[2,2,160,256]{3,2,1,0:T(8,128)(2,1)S(1)} %pad_maximum_fusion.1), channel_id=1, source_target_pairs={{0,2},{1,3},{2,4},{3,5},{4,6},{5,7},{6,8},{7,9},{8,10},{9,11},{10,... | collective-permute-start | bytes 983048 | tf_op jit(solution)/shard_map/cond/branch_1_fun/ppermute | solution.py:27
  18.5 15.1 %collective-permute-start.2 = (bf16[2,2,160,256]{3,2,1,0:T(8,128)(2,1)S(1)}, bf16[2,2,160,256]{3,2,1,0:T(8,128)(2,1)S(1)}, u32[]{:S(2)}, u32[]{:S(2)}) collective-permute-start(bf16[2,2,160,256]{3,2,1,0:T(8,128)(2,1)S(1)} %pad_maximum_fusion.1), channel_id=1, source_target_pairs={{0,14},{1,15},{2,0},{3,1},{4,2},{5,3},{6,4},{7,5},{8,6},{9,7},{10,... | collective-permute-start | bytes 983048 | tf_op jit(solution)/shard_map/cond/branch_1_fun/ppermute | solution.py:27
  27.1 6.5 %copy-start.5 = (bf16[2,8,2,160,256]{4,3,2,1,0:T(8,128)(2,1)S(1)}, bf16[2,8,2,160,256]{4,3,2,1,0:T(8,128)(2,1)}, u32[]{:S(2)}) copy-start(bf16[2,8,2,160,256]{4,3,2,1,0:T(8,128)(2,1)} %unset.4) | copy-start | bytes 7864324 | tf_op jit(solution)/shard_map/cond
  31.6 10.2 %collective-permute-start.3 = (bf16[2,2,160,256]{3,2,1,0:T(8,128)(2,1)S(1)}, bf16[2,2,160,256]{3,2,1,0:T(8,128)(2,1)S(1)}, u32[]{:S(2)}, u32[]{:S(2)}) collective-permute-start(bf16[2,2,160,256]{3,2,1,0:T(8,128)(2,1)S(1)} %collective-permute-done.1), channel_id=1, source_target_pairs={{0,2},{1,3},{2,4},{3,5},{4,6},{5,7},{6,8},{7,9},{8,10},{9,11},{10,... | collective-permute-start | bytes 983048 | tf_op jit(solution)/shard_map/cond/branch_1_fun/ppermute | solution.py:27
  33.6 10.1 %collective-permute-start.4 = (bf16[2,2,160,256]{3,2,1,0:T(8,128)(2,1)S(1)}, bf16[2,2,160,256]{3,2,1,0:T(8,128)(2,1)S(1)}, u32[]{:S(2)}, u32[]{:S(2)}) collective-permute-start(bf16[2,2,160,256]{3,2,1,0:T(8,128)(2,1)S(1)} %collective-permute-done.2), channel_id=1, source_target_pairs={{0,14},{1,15},{2,0},{3,1},{4,2},{5,3},{6,4},{7,5},{8,6},{9,7},{10,... | collective-permute-start | bytes 983048 | tf_op jit(solution)/shard_map/cond/branch_1_fun/ppermute | solution.py:27
  41.8 9.0 %collective-permute-start.5 = (bf16[2,2,160,256]{3,2,1,0:T(8,128)(2,1)S(1)}, bf16[2,2,160,256]{3,2,1,0:T(8,128)(2,1)S(1)}, u32[]{:S(2)}, u32[]{:S(2)}) collective-permute-start(bf16[2,2,160,256]{3,2,1,0:T(8,128)(2,1)S(1)} %collective-permute-done.3), channel_id=1, source_target_pairs={{0,2},{1,3},{2,4},{3,5},{4,6},{5,7},{6,8},{7,9},{8,10},{9,11},{10,... | collective-permute-start | bytes 983048 | tf_op jit(solution)/shard_map/cond/branch_1_fun/ppermute | solution.py:27
  43.8 16.1 %collective-permute-start.7 = (bf16[2,2,160,256]{3,2,1,0:T(8,128)(2,1)S(1)}, bf16[2,2,160,256]{3,2,1,0:T(8,128)(2,1)S(1)}, u32[]{:S(2)}, u32[]{:S(2)}) collective-permute-start(bf16[2,2,160,256]{3,2,1,0:T(8,128)(2,1)S(1)} %collective-permute-done.4), channel_id=1, source_target_pairs={{0,14},{1,15},{2,0},{3,1},{4,2},{5,3},{6,4},{7,5},{8,6},{9,7},{10,... | collective-permute-start | bytes 983048 | tf_op jit(solution)/shard_map/cond/branch_1_fun/ppermute | solution.py:27
  50.8 9.0 %collective-permute-start.6 = (bf16[2,2,160,256]{3,2,1,0:T(8,128)(2,1)S(1)}, bf16[2,2,160,256]{3,2,1,0:T(8,128)(2,1)S(1)}, u32[]{:S(2)}, u32[]{:S(2)}) collective-permute-start(bf16[2,2,160,256]{3,2,1,0:T(8,128)(2,1)S(1)} %collective-permute-done.5), channel_id=1, source_target_pairs={{0,2},{1,3},{2,4},{3,5},{4,6},{5,7},{6,8},{7,9},{8,10},{9,11},{10,... | collective-permute-start | bytes 983048 | tf_op jit(solution)/shard_map/cond/branch_1_fun/ppermute | solution.py:27
  59.9 1.5 copy-start.6
  61.4 10.4 %copy-start.10 = (f32[4,128,128]{2,1,0:T(8,128)}, f32[4,128,128]{2,1,0:T(8,128)S(1)}, u32[]{:S(2)}) copy-start(f32[4,128,128]{2,1,0:T(8,128)S(1)} %get-tuple-element.94.inverse_ref) | copy-start | bytes 786436
  61.5 10.3 %copy-start.3 = (bf16[4,128,2560]{2,1,0:T(8,128)(2,1)S(1)}, bf16[4,128,2560]{2,1,0:T(8,128)(2,1)}, u32[]{:S(2)}) copy-start(bf16[4,128,2560]{2,1,0:T(8,128)(2,1)} %get-tuple-element.93.normed_ref) | copy-start | bytes 7864324
  61.5 10.4 %copy-start.7 = (bf16[2,2560,256]{2,1,0:T(8,128)(2,1)S(1)}, bf16[2,2560,256]{2,1,0:T(8,128)(2,1)}, u32[]{:S(2)}) copy-start(bf16[2,2560,256]{2,1,0:T(8,128)(2,1)} %get-tuple-element.95.maps_ref) | copy-start | bytes 7864324
  64.6 13.6 %collective-permute-start.8 = (bf16[64,2560]{1,0:T(8,128)(2,1)S(1)}, bf16[64,2560]{1,0:T(8,128)(2,1)S(1)}, u32[]{:S(2)}, u32[]{:S(2)}) collective-permute-start(bf16[64,2560]{1,0:T(8,128)(2,1)S(1)} %get-tuple-element.99), channel_id=1, source_target_pairs={{0,496},{16,0},{32,16},{48,32},{64,48},{80,64},{96,80},{112,96},{1... | collective-permute-start | bytes 983048 | tf_op jit(solution)/shard_map/ppermute | solution.py:344
  73.2 12.3 %collective-permute-start.9 = (bf16[64,2560]{1,0:T(8,128)(2,1)S(1)}, bf16[64,2560]{1,0:T(8,128)(2,1)S(1)}, u32[]{:S(2)}, u32[]{:S(2)}) collective-permute-start(bf16[64,2560]{1,0:T(8,128)(2,1)S(1)} %get-tuple-element.104), channel_id=1, source_target_pairs={{0,496},{16,0},{32,16},{48,32},{64,48},{80,64},{96,80},{112,96},{1... | collective-permute-start | bytes 983048 | tf_op jit(solution)/shard_map/ppermute | solution.py:344
  76.5 1.7 copy-start.11
  79.4 12.3 %collective-permute-start.10 = (bf16[64,2560]{1,0:T(8,128)(2,1)S(1)}, bf16[64,2560]{1,0:T(8,128)(2,1)S(1)}, u32[]{:S(2)}, u32[]{:S(2)}) collective-permute-start(bf16[64,2560]{1,0:T(8,128)(2,1)S(1)} %get-tuple-element.107), channel_id=1, source_target_pairs={{0,496},{16,0},{32,16},{48,32},{64,48},{80,64},{96,80},{112,96},{1... | collective-permute-start | bytes 983048 | tf_op jit(solution)/shard_map/ppermute | solution.py:353
  86.8 12.3 %collective-permute-start.11 = (bf16[64,2560]{1,0:T(8,128)(2,1)S(1)}, bf16[64,2560]{1,0:T(8,128)(2,1)S(1)}, u32[]{:S(2)}, u32[]{:S(2)}) collective-permute-start(bf16[64,2560]{1,0:T(8,128)(2,1)S(1)} %get-tuple-element.110), channel_id=1, source_target_pairs={{0,496},{16,0},{32,16},{48,32},{64,48},{80,64},{96,80},{112,96},{1... | collective-permute-start | bytes 983048 | tf_op jit(solution)/shard_map/ppermute | solution.py:353
  93.0 12.3 %collective-permute-start.12 = (bf16[64,2560]{1,0:T(8,128)(2,1)S(1)}, bf16[64,2560]{1,0:T(8,128)(2,1)S(1)}, u32[]{:S(2)}, u32[]{:S(2)}) collective-permute-start(bf16[64,2560]{1,0:T(8,128)(2,1)S(1)} %get-tuple-element.113), channel_id=1, source_target_pairs={{0,496},{16,0},{32,16},{48,32},{64,48},{80,64},{96,80},{112,96},{1... | collective-permute-start | bytes 983048 | tf_op jit(solution)/shard_map/ppermute | solution.py:353
  100.3 12.3 %collective-permute-start.13 = (bf16[64,2560]{1,0:T(8,128)(2,1)S(1)}, bf16[64,2560]{1,0:T(8,128)(2,1)S(1)}, u32[]{:S(2)}, u32[]{:S(2)}) collective-permute-start(bf16[64,2560]{1,0:T(8,128)(2,1)S(1)} %get-tuple-element.116), channel_id=1, source_target_pairs={{0,496},{16,0},{32,16},{48,32},{64,48},{80,64},{96,80},{112,96},{1... | collective-permute-start | bytes 983048 | tf_op jit(solution)/shard_map/ppermute | solution.py:353
  106.5 6.1 %copy-start.1 = (bf16[4,128,2560]{2,1,0:T(8,128)(2,1)}, bf16[4,128,2560]{2,1,0:T(8,128)(2,1)S(1)}, u32[]{:S(2)}) copy-start(bf16[4,128,2560]{2,1,0:T(8,128)(2,1)S(1)} %get-tuple-element.117.refs_2_) | copy-start | bytes 7864324
  113.9 73.0 %collective-permute-start.15 = (bf16[64,2560]{1,0:T(8,128)(2,1)S(1)}, bf16[64,2560]{1,0:T(8,128)(2,1)S(1)}, u32[]{:S(2)}, u32[]{:S(2)}) collective-permute-start(bf16[64,2560]{1,0:T(8,128)(2,1)S(1)} %get-tuple-element.124), channel_id=1, source_target_pairs={{0,496},{16,0},{32,16},{48,32},{64,48},{80,64},{96,80},{112,96},{1... | collective-permute-start | bytes 983048 | tf_op jit(solution)/shard_map/ppermute | solution.py:353
  115.8 71.1 %collective-permute-start.14 = (bf16[64,2560]{1,0:T(8,128)(2,1)S(1)}, bf16[64,2560]{1,0:T(8,128)(2,1)S(1)}, u32[]{:S(2)}, u32[]{:S(2)}) collective-permute-start(bf16[64,2560]{1,0:T(8,128)(2,1)S(1)} %get-tuple-element.123), channel_id=1, source_target_pairs={{0,496},{16,0},{32,16},{48,32},{64,48},{80,64},{96,80},{112,96},{1... | collective-permute-start | bytes 983048 | tf_op jit(solution)/shard_map/ppermute | solution.py:353
  117.8 1.5 copy-start.4

commit v13 on v12

--- a/solution.py
+++ b/solution.py
@@ -31,10 +31,10 @@
     return lax.ppermute(value, "dp", dp_pairs(n_z, 0, 1))
 
 
-def ring_gather(shard, n_z):
+def ring_gather(shard, n_z, made):
     index = lax.axis_index("dp")
     z, h = index // 2, index % 2
-    other = swapped(shard, n_z)
+    other, *made = lax.optimization_barrier((swapped(shard, n_z), *made))
     pair = jnp.stack([jnp.where(h == 0, shard, other), jnp.where(h == 0, other, shard)], axis=1)
     half = n_z // 2
     full = unset((2, n_z) + pair.shape[1:], pair.dtype)
@@ -50,7 +50,7 @@
         if step < half - 1:
             full = placed(full, left, step)
     full = placed(full, shifted(right, n_z, 1), -half)
-    return placed(full, left, half - 1)
+    return placed(full, left, half - 1), made
 
 
 def empty_kernel(out_ref):
@@ -316,8 +316,8 @@
 
     def gather_two(down, up, x):
         shards = jnp.stack([shard_of(down, up, level) for level in range(2)])
-        full = ring_gather(shards, n_z)
-        return full.reshape(2, width, 2 * rank), *norms(x)
+        full, made = ring_gather(shards, n_z, norms(x))
+        return full.reshape(2, width, 2 * rank), *made
 
     def gather_one(down, up, x):
         shard = shard_of(down, up, 1)

time: 189 us -> 189 us (level)
  waiting for transfers between devices: 40 us -> 31.4 us
  local copies, waits for them, and re-layouts: 3.76 us -> 10.6 us
    dynamic_update_slice x7, local copies, waits for them, and re-layouts: 0.2 us -> 7.23 us  [placed(): lax.dynamic_update_slice(full, piece[:, None], (0, (z + offset) % n_z, 0,...]
    ppermute x1, waiting for transfers between devices: 6.54 us -> 2.09 us  [swapped(): return lax.ppermute(value, 'dp', dp_pairs(n_z, 0, 1))]
    ppermute x7, waiting for transfers between devices: 13 us -> 10.4 us  [shifted(): return lax.ppermute(value, 'dp', dp_pairs(n_z, step, 0))]
  transfers between devices with their start and end apart: 16 -> 16, of which waited for: 9 -> 9; matrix products, arithmetic and copies ran while one was open for 0% -> 5% of each run, Pallas kernels for 10% -> 10%
where the time goes in v13:
time: 189 us
  blocking collectives  62 us (33%)
  starting transfers between devices  55.7 us (29%)
  waiting for transfers between devices  31.4 us (17%)
  Pallas kernels  23.6 us (12%)
  local copies, waits for them, and re-layouts  10.6 us (6%)
  other arithmetic  3.95 us (2%)
    all_to_all x1, blocking collectives, summed_parts(): lax.all_to_all(parts.reshape(n_dp, share, -1), 'dp', 0, 0, tiled=True)  62 us
    ppermute x7, starting transfers between devices, shifted(): return lax.ppermute(value, 'dp', dp_pairs(n_z, step, 0))  27.6 us
    ppermute x8, starting transfers between devices, on_device(): moving.append(lax.ppermute(sent, 'section', down_one))  23.7 us
    ppermute x8, waiting for transfers between devices, on_device(): moving.append(lax.ppermute(sent, 'section', down_one))  18.9 us
    pallas_call x8, Pallas kernels, tick_layer(): pl.pallas_call(functools.partial(tick_kernel, tick, part), grid_spec=pltp...  11.9 us
    ppermute x7, waiting for transfers between devices, shifted(): return lax.ppermute(value, 'dp', dp_pairs(n_z, step, 0))  10.4 us
    dynamic_update_slice x7, local copies, waits for them, and re-layouts, placed(): lax.dynamic_update_slice(full, piece[:, None], (0, (z + offset) % n_z, 0,...  7.23 us
    pallas_call x1, Pallas kernels, norms(): pl.pallas_call(norm_kernel, grid=(ticks,), out_shape=[jax.ShapeDtypeStruc...  4.45 us
  transfers between devices with their start and end apart: 16, of which 9 were waited for; matrix products, arithmetic and copies ran while one was open for 5% of the time, Pallas kernels for 10%

profile of v13, /device:TPU:63, one launch (start us, length us, event | category | flops | bytes accessed | tf_op | source)
XLA Modules:
  0.0 188.6 jit_solution(15780744854772525448)
XLA Ops:
  0.7 0.8 copy-done.8
  1.6 61.2 %conditional.2 = (bf16[2,2560,256]{2,1,0:T(8,128)(2,1)}, bf16[4,128,2560]{2,1,0:T(8,128)(2,1)}, f32[4,128,128]{2,1,0:T(8,128)S(1)}) conditional(s32[]{:T(128)} %convert_element_type.10, (bf16[2,128,160]{1,2,0:T(8,128)(2,1)S(1)}, bf16[2,128,160]{1,2,0:T(8,128)(2,1)S(1)}, bf16[4,1,128,2560]{3,2,1,0:T(8,128)(2,1)}) %tuple.46, ...), branch_computations={%region_0.1_spmd, %region_1.2_spmd} | conditional | flops 4296441856 | bytes 27789168 | solution.py:330
  2.3 4.4 %collective-permute-start = (bf16[2,160,256]{2,1,0:T(8,128)(2,1)S(1)}, bf16[2,160,256]{2,1,0:T(8,128)(2,1)}, u32[]{:S(2)}, u32[]{:S(2)}) collective-permute-start(bf16[2,160,256]{2,1,0:T(8,128)(2,1)S(1)} %pad_maximum_fusion.2), channel_id=1, source_target_pairs={{0,1},{1,0},{2,3},{3,2},{4,5},{5,4},{6,7},{7,6},{8,9},{9,8},{10,11... | collective-permute-start | bytes 491528 | tf_op jit(solution)/shard_map/cond/branch_1_fun/ppermute | solution.py:31
  6.7 4.4 %norms.3 = (bf16[4,128,2560]{2,1,0:T(8,128)(2,1)}, f32[4,128,128]{2,1,0:T(8,128)}) custom-call(bf16[4,1,128,2560]{3,2,1,0:T(8,128)(2,1)} %get-tuple-element.43.x_ref), custom_call_target="tpu_custom_call" | custom-call | flops 4294967296 | bytes 8388608 | tf_op jit(solution)/shard_map/cond/branch_1_fun/norms/pallas_call | solution.py:78
  11.2 2.1 %collective-permute-done = bf16[2,160,256]{2,1,0:T(8,128)(2,1)} collective-permute-done((bf16[2,160,256]{2,1,0:T(8,128)(2,1)S(1)}, bf16[2,160,256]{2,1,0:T(8,128)(2,1)}, u32[]{:S(2)}, u32[]{:S(2)}) %collective-permute-start) | collective-permute-done | bytes 163872 | tf_op jit(solution)/shard_map/cond/branch_1_fun/ppermute | solution.py:31
  13.3 1.0 select_bitcast_fusion.1
  14.9 0.8 pad_maximum_fusion.1
  15.7 4.0 %collective-permute-start.1 = (bf16[2,2,160,256]{3,2,1,0:T(8,128)(2,1)}, bf16[2,2,160,256]{3,2,1,0:T(8,128)(2,1)}, u32[]{:S(2)}, u32[]{:S(2)}) collective-permute-start(bf16[2,2,160,256]{3,2,1,0:T(8,128)(2,1)} %pad_maximum_fusion.1), channel_id=1, source_target_pairs={{0,2},{1,3},{2,4},{3,5},{4,6},{5,7},{6,8},{7,9},{8,10},{9,11},{10,... | collective-permute-start | bytes 983048 | tf_op jit(solution)/shard_map/cond/branch_1_fun/ppermute | solution.py:27
  19.7 8.6 %collective-permute-start.2 = (bf16[2,2,160,256]{3,2,1,0:T(8,128)(2,1)}, bf16[2,2,160,256]{3,2,1,0:T(8,128)(2,1)}, u32[]{:S(2)}, u32[]{:S(2)}) collective-permute-start(bf16[2,2,160,256]{3,2,1,0:T(8,128)(2,1)} %pad_maximum_fusion.1), channel_id=1, source_target_pairs={{0,14},{1,15},{2,0},{3,1},{4,2},{5,3},{6,4},{7,5},{8,6},{9,7},{10,... | collective-permute-start | bytes 983048 | tf_op jit(solution)/shard_map/cond/branch_1_fun/ppermute | solution.py:27
  28.5 4.6 %collective-permute-done.1 = bf16[2,2,160,256]{3,2,1,0:T(8,128)(2,1)} collective-permute-done((bf16[2,2,160,256]{3,2,1,0:T(8,128)(2,1)}, bf16[2,2,160,256]{3,2,1,0:T(8,128)(2,1)}, u32[]{:S(2)}, u32[]{:S(2)}) %collective-permute-start.1) | collective-permute-done | bytes 327712 | tf_op jit(solution)/shard_map/cond/branch_1_fun/ppermute | solution.py:27
  33.0 1.9 %collective-permute-start.3 = (bf16[2,2,160,256]{3,2,1,0:T(8,128)(2,1)}, bf16[2,2,160,256]{3,2,1,0:T(8,128)(2,1)S(1)}, u32[]{:S(2)}, u32[]{:S(2)}) collective-permute-start(bf16[2,2,160,256]{3,2,1,0:T(8,128)(2,1)} %collective-permute-done.1), channel_id=1, source_target_pairs={{0,2},{1,3},{2,4},{3,5},{4,6},{5,7},{6,8},{7,9},{8,10},{9,11},{10,... | collective-permute-start | bytes 983048 | tf_op jit(solution)/shard_map/cond/branch_1_fun/ppermute | solution.py:27
  34.9 1.7 bitcast_dynamic-update-slice_fusion.7
  36.6 4.7 %collective-permute-start.4 = (bf16[2,2,160,256]{3,2,1,0:T(8,128)(2,1)}, bf16[2,2,160,256]{3,2,1,0:T(8,128)(2,1)S(1)}, u32[]{:S(2)}, u32[]{:S(2)}) collective-permute-start(bf16[2,2,160,256]{3,2,1,0:T(8,128)(2,1)} %collective-permute-done.2), channel_id=1, source_target_pairs={{0,14},{1,15},{2,0},{3,1},{4,2},{5,3},{6,4},{7,5},{8,6},{9,7},{10,... | collective-permute-start | bytes 983048 | tf_op jit(solution)/shard_map/cond/branch_1_fun/ppermute | solution.py:27
  41.3 1.7 bitcast_dynamic-update-slice_fusion.6
  43.2 1.9 %collective-permute-start.5 = (bf16[2,2,160,256]{3,2,1,0:T(8,128)(2,1)S(1)}, bf16[2,2,160,256]{3,2,1,0:T(8,128)(2,1)S(1)}, u32[]{:S(2)}, u32[]{:S(2)}) collective-permute-start(bf16[2,2,160,256]{3,2,1,0:T(8,128)(2,1)S(1)} %collective-permute-done.3), channel_id=1, source_target_pairs={{0,2},{1,3},{2,4},{3,5},{4,6},{5,7},{6,8},{7,9},{8,10},{9,11},{10,... | collective-permute-start | bytes 983048 | tf_op jit(solution)/shard_map/cond/branch_1_fun/ppermute | solution.py:27
  45.2 1.7 bitcast_dynamic-update-slice_fusion.5
  46.9 4.6 %collective-permute-start.7 = (bf16[2,2,160,256]{3,2,1,0:T(8,128)(2,1)S(1)}, bf16[2,2,160,256]{3,2,1,0:T(8,128)(2,1)S(1)}, u32[]{:S(2)}, u32[]{:S(2)}) collective-permute-start(bf16[2,2,160,256]{3,2,1,0:T(8,128)(2,1)S(1)} %collective-permute-done.4), channel_id=1, source_target_pairs={{0,14},{1,15},{2,0},{3,1},{4,2},{5,3},{6,4},{7,5},{8,6},{9,7},{10,... | collective-permute-start | bytes 983048 | tf_op jit(solution)/shard_map/cond/branch_1_fun/ppermute | solution.py:27
  52.3 1.9 %collective-permute-start.6 = (bf16[2,2,160,256]{3,2,1,0:T(8,128)(2,1)S(1)}, bf16[2,2,160,256]{3,2,1,0:T(8,128)(2,1)S(1)}, u32[]{:S(2)}, u32[]{:S(2)}) collective-permute-start(bf16[2,2,160,256]{3,2,1,0:T(8,128)(2,1)S(1)} %collective-permute-done.5), channel_id=1, source_target_pairs={{0,2},{1,3},{2,4},{3,5},{4,6},{5,7},{6,8},{7,9},{8,10},{9,11},{10,... | collective-permute-start | bytes 983048 | tf_op jit(solution)/shard_map/cond/branch_1_fun/ppermute | solution.py:27
  54.9 0.8 bitcast_dynamic-update-slice_fusion.2
  55.7 5.6 %collective-permute-done.6 = bf16[2,2,160,256]{3,2,1,0:T(8,128)(2,1)S(1)} collective-permute-done((bf16[2,2,160,256]{3,2,1,0:T(8,128)(2,1)S(1)}, bf16[2,2,160,256]{3,2,1,0:T(8,128)(2,1)S(1)}, u32[]{:S(2)}, u32[]{:S(2)}) %collective-permute-start.6) | collective-permute-done | bytes 327712 | tf_op jit(solution)/shard_map/cond/branch_1_fun/ppermute | solution.py:27
  61.3 0.8 bitcast_dynamic-update-slice_fusion.1
  62.9 3.0 %tick_layer.8 = (bf16[4,128,2560]{2,1,0:T(8,128)(2,1)S(1)}, bf16[64,2560]{1,0:T(8,128)(2,1)S(1)}, bf16[64,128]{1,0:T(8,128)(2,1)S(1)}, bf16[64,128]{1,0:T(8,128)(2,1)S(1)}) custom-call(s32[4]{0:T(128)S(1)} %pad_add_fusion.levels_ref, bf16[128,2560]{1,0:T(8,128)(2,1)S(1)} %bitcast.98, ...), custom_call_target="tpu_custom_call", output_to_operand_aliasing={{0}: (5, {})} | custom-call | flops 4294967296 | bytes 8388608 | tf_op jit(solution)/shard_map/tick_layer/pallas_call | solution.py:182
  65.9 7.4 %collective-permute-start.8 = (bf16[64,2560]{1,0:T(8,128)(2,1)S(1)}, bf16[64,2560]{1,0:T(8,128)(2,1)S(1)}, u32[]{:S(2)}, u32[]{:S(2)}) collective-permute-start(bf16[64,2560]{1,0:T(8,128)(2,1)S(1)} %get-tuple-element.102), channel_id=1, source_target_pairs={{0,496},{16,0},{32,16},{48,32},{64,48},{80,64},{96,80},{112,96},{1... | collective-permute-start | bytes 983048 | tf_op jit(solution)/shard_map/ppermute | solution.py:344
  73.4 1.3 tick_layer.9
  74.8 4.8 %collective-permute-start.9 = (bf16[64,2560]{1,0:T(8,128)(2,1)S(1)}, bf16[64,2560]{1,0:T(8,128)(2,1)S(1)}, u32[]{:S(2)}, u32[]{:S(2)}) collective-permute-start(bf16[64,2560]{1,0:T(8,128)(2,1)S(1)} %get-tuple-element.107), channel_id=1, source_target_pairs={{0,496},{16,0},{32,16},{48,32},{64,48},{80,64},{96,80},{112,96},{1... | collective-permute-start | bytes 983048 | tf_op jit(solution)/shard_map/ppermute | solution.py:344
  79.6 1.6 forward_rest.1
  81.2 1.2 tick_layer.10
  82.5 1.9 %collective-permute-start.10 = (bf16[64,2560]{1,0:T(8,128)(2,1)S(1)}, bf16[64,2560]{1,0:T(8,128)(2,1)S(1)}, u32[]{:S(2)}, u32[]{:S(2)}) collective-permute-start(bf16[64,2560]{1,0:T(8,128)(2,1)S(1)} %get-tuple-element.110), channel_id=1, source_target_pairs={{0,496},{16,0},{32,16},{48,32},{64,48},{80,64},{96,80},{112,96},{1... | collective-permute-start | bytes 983048 | tf_op jit(solution)/shard_map/ppermute | solution.py:353
  84.4 2.6 %collective-permute-done.9.incoming_ref = bf16[64,2560]{1,0:T(8,128)(2,1)S(1)} collective-permute-done((bf16[64,2560]{1,0:T(8,128)(2,1)S(1)}, bf16[64,2560]{1,0:T(8,128)(2,1)S(1)}, u32[]{:S(2)}, u32[]{:S(2)}) %collective-permute-start.9) | collective-permute-done | bytes 327712 | tf_op jit(solution)/shard_map/ppermute | solution.py:344
  87.1 1.2 tick_layer.11
  88.3 1.9 %collective-permute-start.11 = (bf16[64,2560]{1,0:T(8,128)(2,1)S(1)}, bf16[64,2560]{1,0:T(8,128)(2,1)S(1)}, u32[]{:S(2)}, u32[]{:S(2)}) collective-permute-start(bf16[64,2560]{1,0:T(8,128)(2,1)S(1)} %get-tuple-element.113), channel_id=1, source_target_pairs={{0,496},{16,0},{32,16},{48,32},{64,48},{80,64},{96,80},{112,96},{1... | collective-permute-start | bytes 983048 | tf_op jit(solution)/shard_map/ppermute | solution.py:353
  90.3 4.5 %collective-permute-done.10.incoming_ref = bf16[64,2560]{1,0:T(8,128)(2,1)S(1)} collective-permute-done((bf16[64,2560]{1,0:T(8,128)(2,1)S(1)}, bf16[64,2560]{1,0:T(8,128)(2,1)S(1)}, u32[]{:S(2)}, u32[]{:S(2)}) %collective-permute-start.10) | collective-permute-done | bytes 327712 | tf_op jit(solution)/shard_map/ppermute | solution.py:353
  94.8 1.2 tick_layer.12
  96.1 1.9 %collective-permute-start.12 = (bf16[64,2560]{1,0:T(8,128)(2,1)S(1)}, bf16[64,2560]{1,0:T(8,128)(2,1)S(1)}, u32[]{:S(2)}, u32[]{:S(2)}) collective-permute-start(bf16[64,2560]{1,0:T(8,128)(2,1)S(1)} %get-tuple-element.116), channel_id=1, source_target_pairs={{0,496},{16,0},{32,16},{48,32},{64,48},{80,64},{96,80},{112,96},{1... | collective-permute-start | bytes 983048 | tf_op jit(solution)/shard_map/ppermute | solution.py:353
  98.0 2.6 %collective-permute-done.11.incoming_ref = bf16[64,2560]{1,0:T(8,128)(2,1)S(1)} collective-permute-done((bf16[64,2560]{1,0:T(8,128)(2,1)S(1)}, bf16[64,2560]{1,0:T(8,128)(2,1)S(1)}, u32[]{:S(2)}, u32[]{:S(2)}) %collective-permute-start.11) | collective-permute-done | bytes 327712 | tf_op jit(solution)/shard_map/ppermute | solution.py:353
  100.6 1.2 tick_layer.13
  101.9 1.9 %collective-permute-start.13 = (bf16[64,2560]{1,0:T(8,128)(2,1)S(1)}, bf16[64,2560]{1,0:T(8,128)(2,1)S(1)}, u32[]{:S(2)}, u32[]{:S(2)}) collective-permute-start(bf16[64,2560]{1,0:T(8,128)(2,1)S(1)} %get-tuple-element.119), channel_id=1, source_target_pairs={{0,496},{16,0},{32,16},{48,32},{64,48},{80,64},{96,80},{112,96},{1... | collective-permute-start | bytes 983048 | tf_op jit(solution)/shard_map/ppermute | solution.py:353
  103.8 4.6 %collective-permute-done.12.incoming_ref = bf16[64,2560]{1,0:T(8,128)(2,1)S(1)} collective-permute-done((bf16[64,2560]{1,0:T(8,128)(2,1)S(1)}, bf16[64,2560]{1,0:T(8,128)(2,1)S(1)}, u32[]{:S(2)}, u32[]{:S(2)}) %collective-permute-start.12) | collective-permute-done | bytes 327712 | tf_op jit(solution)/shard_map/ppermute | solution.py:353
  108.4 1.2 tick_layer.14
  109.6 4.5 %collective-permute-done.13.incoming_ref = bf16[64,2560]{1,0:T(8,128)(2,1)S(1)} collective-permute-done((bf16[64,2560]{1,0:T(8,128)(2,1)S(1)}, bf16[64,2560]{1,0:T(8,128)(2,1)S(1)}, u32[]{:S(2)}, u32[]{:S(2)}) %collective-permute-start.13) | collective-permute-done | bytes 327712 | tf_op jit(solution)/shard_map/ppermute | solution.py:353
  114.2 1.3 tick_layer.15
  115.4 1.9 %collective-permute-start.15 = (bf16[64,2560]{1,0:T(8,128)(2,1)S(1)}, bf16[64,2560]{1,0:T(8,128)(2,1)S(1)}, u32[]{:S(2)}, u32[]{:S(2)}) collective-permute-start(bf16[64,2560]{1,0:T(8,128)(2,1)S(1)} %get-tuple-element.127), channel_id=1, source_target_pairs={{0,496},{16,0},{32,16},{48,32},{64,48},{80,64},{96,80},{112,96},{1... | collective-permute-start | bytes 983048 | tf_op jit(solution)/shard_map/ppermute | solution.py:353
  117.4 1.9 %collective-permute-start.14 = (bf16[64,2560]{1,0:T(8,128)(2,1)S(1)}, bf16[64,2560]{1,0:T(8,128)(2,1)S(1)}, u32[]{:S(2)}, u32[]{:S(2)}) collective-permute-start(bf16[64,2560]{1,0:T(8,128)(2,1)S(1)} %get-tuple-element.126), channel_id=1, source_target_pairs={{0,496},{16,0},{32,16},{48,32},{64,48},{80,64},{96,80},{112,96},{1... | collective-permute-start | bytes 983048 | tf_op jit(solution)/shard_map/ppermute | solution.py:353
  119.3 68.2 %conditional.3 = (f32[160,512]{1,0:T(8,128)S(1)}) conditional(s32[]{:T(128)} %convert_element_type.10, (bf16[4,128,2560]{2,1,0:T(8,128)(2,1)S(1)}, bf16[512,128]{1,0:T(8,128)(2,1)S(1)}, bf16[4,128,2560]{2,1,0:T(8,128)(2,1)}, bf16[4,128,128]{2,1,0:T(8,128)(2,1)S(1)}) %tuple.42, (s32[4]{0:T(128)S(1)}, bf16[512,128]{1,0:T(8,128)(2,1)S(1)}, ...), branch_computations={%region_2.3_spmd, %region_3.4_spmd} | conditional | flops 4296278016 | bytes 25954380 | solution.py:382
  119.8 1.0 copy-done.4
  120.9 4.4 %weight_products.1 = bf16[2560,512]{1,0:T(8,128)(2,1)S(1)} custom-call(bf16[4,128,2560]{2,1,0:T(8,128)(2,1)} %copy-done.4, bf16[4,128,2560]{2,1,0:T(8,128)(2,1)} %get-tuple-element.54.grads_ref, bf16[512,256]{1,0:T(8,128)(2,1)S(1)} %pad_maximum_fusion.3.lats_ref, bf16[512,256]{1,0:T(8,128)(2,1)S(1)} %bitcast.97), custom_call_target="tpu_custom_call" | custom-call | flops 4294967296 | bytes 8388608 | tf_op jit(solution)/shard_map/cond/branch_1_fun/weight_products/pallas_call | solution.py:226
  125.2 62.0 %all_to_all.13.moved_ref = bf16[16,160,512]{2,1,0:T(8,128)(2,1)S(1)} all-to-all(bf16[16,160,512]{2,1,0:T(8,128)(2,1)S(1)} %bitcast.96), channel_id=1, replica_groups=mesh['section'=32,'dp'=16] {'dp'}, dimensions={0} | all-to-all | bytes 5242880 | tf_op jit(solution)/shard_map/cond/branch_1_fun/all_to_all | solution.py:360
  187.6 1.0 finish.1
  (57 shorter events, 4.9 us)
Async XLA Ops:
  0.6 0.9 copy-start.8
  0.6 0.9 copy-start.9
  1.6 61.3 %copy-start = (bf16[1,128,2560]{2,1,0:T(8,128)(2,1)S(1)}, bf16[1,128,2560]{2,1,0:T(8,128)(2,1)}, u32[]{:S(2)}) copy-start(bf16[1,128,2560]{2,1,0:T(8,128)(2,1)} %param.9) | copy-start | bytes 1966084
  1.6 0.6 copy-start.7
  2.3 11.0 %collective-permute-start = (bf16[2,160,256]{2,1,0:T(8,128)(2,1)S(1)}, bf16[2,160,256]{2,1,0:T(8,128)(2,1)}, u32[]{:S(2)}, u32[]{:S(2)}) collective-permute-start(bf16[2,160,256]{2,1,0:T(8,128)(2,1)S(1)} %pad_maximum_fusion.2), channel_id=1, source_target_pairs={{0,1},{1,0},{2,3},{3,2},{4,5},{5,4},{6,7},{7,6},{8,9},{9,8},{10,11... | collective-permute-start | bytes 491528 | tf_op jit(solution)/shard_map/cond/branch_1_fun/ppermute | solution.py:31
  14.2 0.7 copy-start.6
  15.7 17.3 %collective-permute-start.1 = (bf16[2,2,160,256]{3,2,1,0:T(8,128)(2,1)}, bf16[2,2,160,256]{3,2,1,0:T(8,128)(2,1)}, u32[]{:S(2)}, u32[]{:S(2)}) collective-permute-start(bf16[2,2,160,256]{3,2,1,0:T(8,128)(2,1)} %pad_maximum_fusion.1), channel_id=1, source_target_pairs={{0,2},{1,3},{2,4},{3,5},{4,6},{5,7},{6,8},{7,9},{8,10},{9,11},{10,... | collective-permute-start | bytes 983048 | tf_op jit(solution)/shard_map/cond/branch_1_fun/ppermute | solution.py:27
  19.7 17.0 %collective-permute-start.2 = (bf16[2,2,160,256]{3,2,1,0:T(8,128)(2,1)}, bf16[2,2,160,256]{3,2,1,0:T(8,128)(2,1)}, u32[]{:S(2)}, u32[]{:S(2)}) collective-permute-start(bf16[2,2,160,256]{3,2,1,0:T(8,128)(2,1)} %pad_maximum_fusion.1), channel_id=1, source_target_pairs={{0,14},{1,15},{2,0},{3,1},{4,2},{5,3},{6,4},{7,5},{8,6},{9,7},{10,... | collective-permute-start | bytes 983048 | tf_op jit(solution)/shard_map/cond/branch_1_fun/ppermute | solution.py:27
  33.0 10.2 %collective-permute-start.3 = (bf16[2,2,160,256]{3,2,1,0:T(8,128)(2,1)}, bf16[2,2,160,256]{3,2,1,0:T(8,128)(2,1)S(1)}, u32[]{:S(2)}, u32[]{:S(2)}) collective-permute-start(bf16[2,2,160,256]{3,2,1,0:T(8,128)(2,1)} %collective-permute-done.1), channel_id=1, source_target_pairs={{0,2},{1,3},{2,4},{3,5},{4,6},{5,7},{6,8},{7,9},{8,10},{9,11},{10,... | collective-permute-start | bytes 983048 | tf_op jit(solution)/shard_map/cond/branch_1_fun/ppermute | solution.py:27
  36.6 26.2 %copy-start.10 = (f32[4,128,128]{2,1,0:T(8,128)S(1)}, f32[4,128,128]{2,1,0:T(8,128)}, u32[]{:S(2)}) copy-start(f32[4,128,128]{2,1,0:T(8,128)} %get-tuple-element.158) | copy-start | bytes 786436 | tf_op jit(solution)/shard_map/cond
  36.6 10.2 %collective-permute-start.4 = (bf16[2,2,160,256]{3,2,1,0:T(8,128)(2,1)}, bf16[2,2,160,256]{3,2,1,0:T(8,128)(2,1)S(1)}, u32[]{:S(2)}, u32[]{:S(2)}) collective-permute-start(bf16[2,2,160,256]{3,2,1,0:T(8,128)(2,1)} %collective-permute-done.2), channel_id=1, source_target_pairs={{0,14},{1,15},{2,0},{3,1},{4,2},{5,3},{6,4},{7,5},{8,6},{9,7},{10,... | collective-permute-start | bytes 983048 | tf_op jit(solution)/shard_map/cond/branch_1_fun/ppermute | solution.py:27
  43.2 9.0 %collective-permute-start.5 = (bf16[2,2,160,256]{3,2,1,0:T(8,128)(2,1)S(1)}, bf16[2,2,160,256]{3,2,1,0:T(8,128)(2,1)S(1)}, u32[]{:S(2)}, u32[]{:S(2)}) collective-permute-start(bf16[2,2,160,256]{3,2,1,0:T(8,128)(2,1)S(1)} %collective-permute-done.3), channel_id=1, source_target_pairs={{0,2},{1,3},{2,4},{3,5},{4,6},{5,7},{6,8},{7,9},{8,10},{9,11},{10,... | collective-permute-start | bytes 983048 | tf_op jit(solution)/shard_map/cond/branch_1_fun/ppermute | solution.py:27
  46.9 15.2 %collective-permute-start.7 = (bf16[2,2,160,256]{3,2,1,0:T(8,128)(2,1)S(1)}, bf16[2,2,160,256]{3,2,1,0:T(8,128)(2,1)S(1)}, u32[]{:S(2)}, u32[]{:S(2)}) collective-permute-start(bf16[2,2,160,256]{3,2,1,0:T(8,128)(2,1)S(1)} %collective-permute-done.4), channel_id=1, source_target_pairs={{0,14},{1,15},{2,0},{3,1},{4,2},{5,3},{6,4},{7,5},{8,6},{9,7},{10,... | collective-permute-start | bytes 983048 | tf_op jit(solution)/shard_map/cond/branch_1_fun/ppermute | solution.py:27
  52.3 9.0 %collective-permute-start.6 = (bf16[2,2,160,256]{3,2,1,0:T(8,128)(2,1)S(1)}, bf16[2,2,160,256]{3,2,1,0:T(8,128)(2,1)S(1)}, u32[]{:S(2)}, u32[]{:S(2)}) collective-permute-start(bf16[2,2,160,256]{3,2,1,0:T(8,128)(2,1)S(1)} %collective-permute-done.5), channel_id=1, source_target_pairs={{0,2},{1,3},{2,4},{3,5},{4,6},{5,7},{6,8},{7,9},{8,10},{9,11},{10,... | collective-permute-start | bytes 983048 | tf_op jit(solution)/shard_map/cond/branch_1_fun/ppermute | solution.py:27
  62.8 10.6 %copy-start.11 = (f32[4,128,128]{2,1,0:T(8,128)}, f32[4,128,128]{2,1,0:T(8,128)S(1)}, u32[]{:S(2)}) copy-start(f32[4,128,128]{2,1,0:T(8,128)S(1)} %get-tuple-element.97.inverse_ref) | copy-start | bytes 786436
  62.9 10.5 %copy-start.3 = (bf16[4,128,2560]{2,1,0:T(8,128)(2,1)S(1)}, bf16[4,128,2560]{2,1,0:T(8,128)(2,1)}, u32[]{:S(2)}) copy-start(bf16[4,128,2560]{2,1,0:T(8,128)(2,1)} %get-tuple-element.96.normed_ref) | copy-start | bytes 7864324
  62.9 10.5 %copy-start.5 = (bf16[2,2560,256]{2,1,0:T(8,128)(2,1)S(1)}, bf16[2,2560,256]{2,1,0:T(8,128)(2,1)}, u32[]{:S(2)}) copy-start(bf16[2,2560,256]{2,1,0:T(8,128)(2,1)} %get-tuple-element.98.maps_ref) | copy-start | bytes 7864324
  65.9 15.3 %collective-permute-start.8 = (bf16[64,2560]{1,0:T(8,128)(2,1)S(1)}, bf16[64,2560]{1,0:T(8,128)(2,1)S(1)}, u32[]{:S(2)}, u32[]{:S(2)}) collective-permute-start(bf16[64,2560]{1,0:T(8,128)(2,1)S(1)} %get-tuple-element.102), channel_id=1, source_target_pairs={{0,496},{16,0},{32,16},{48,32},{64,48},{80,64},{96,80},{112,96},{1... | collective-permute-start | bytes 983048 | tf_op jit(solution)/shard_map/ppermute | solution.py:344
  74.8 12.3 %collective-permute-start.9 = (bf16[64,2560]{1,0:T(8,128)(2,1)S(1)}, bf16[64,2560]{1,0:T(8,128)(2,1)S(1)}, u32[]{:S(2)}, u32[]{:S(2)}) collective-permute-start(bf16[64,2560]{1,0:T(8,128)(2,1)S(1)} %get-tuple-element.107), channel_id=1, source_target_pairs={{0,496},{16,0},{32,16},{48,32},{64,48},{80,64},{96,80},{112,96},{1... | collective-permute-start | bytes 983048 | tf_op jit(solution)/shard_map/ppermute | solution.py:344
  79.6 1.7 copy-start.12
  82.5 12.3 %collective-permute-start.10 = (bf16[64,2560]{1,0:T(8,128)(2,1)S(1)}, bf16[64,2560]{1,0:T(8,128)(2,1)S(1)}, u32[]{:S(2)}, u32[]{:S(2)}) collective-permute-start(bf16[64,2560]{1,0:T(8,128)(2,1)S(1)} %get-tuple-element.110), channel_id=1, source_target_pairs={{0,496},{16,0},{32,16},{48,32},{64,48},{80,64},{96,80},{112,96},{1... | collective-permute-start | bytes 983048 | tf_op jit(solution)/shard_map/ppermute | solution.py:353
  88.3 12.3 %collective-permute-start.11 = (bf16[64,2560]{1,0:T(8,128)(2,1)S(1)}, bf16[64,2560]{1,0:T(8,128)(2,1)S(1)}, u32[]{:S(2)}, u32[]{:S(2)}) collective-permute-start(bf16[64,2560]{1,0:T(8,128)(2,1)S(1)} %get-tuple-element.113), channel_id=1, source_target_pairs={{0,496},{16,0},{32,16},{48,32},{64,48},{80,64},{96,80},{112,96},{1... | collective-permute-start | bytes 983048 | tf_op jit(solution)/shard_map/ppermute | solution.py:353
  96.1 12.3 %collective-permute-start.12 = (bf16[64,2560]{1,0:T(8,128)(2,1)S(1)}, bf16[64,2560]{1,0:T(8,128)(2,1)S(1)}, u32[]{:S(2)}, u32[]{:S(2)}) collective-permute-start(bf16[64,2560]{1,0:T(8,128)(2,1)S(1)} %get-tuple-element.116), channel_id=1, source_target_pairs={{0,496},{16,0},{32,16},{48,32},{64,48},{80,64},{96,80},{112,96},{1... | collective-permute-start | bytes 983048 | tf_op jit(solution)/shard_map/ppermute | solution.py:353
  101.9 12.3 %collective-permute-start.13 = (bf16[64,2560]{1,0:T(8,128)(2,1)S(1)}, bf16[64,2560]{1,0:T(8,128)(2,1)S(1)}, u32[]{:S(2)}, u32[]{:S(2)}) collective-permute-start(bf16[64,2560]{1,0:T(8,128)(2,1)S(1)} %get-tuple-element.119), channel_id=1, source_target_pairs={{0,496},{16,0},{32,16},{48,32},{64,48},{80,64},{96,80},{112,96},{1... | collective-permute-start | bytes 983048 | tf_op jit(solution)/shard_map/ppermute | solution.py:353
  109.6 4.6 %copy-start.1 = (bf16[4,128,2560]{2,1,0:T(8,128)(2,1)}, bf16[4,128,2560]{2,1,0:T(8,128)(2,1)S(1)}, u32[]{:S(2)}) copy-start(bf16[4,128,2560]{2,1,0:T(8,128)(2,1)S(1)} %get-tuple-element.120.refs_2_) | copy-start | bytes 7864324
  115.4 72.1 %collective-permute-start.15 = (bf16[64,2560]{1,0:T(8,128)(2,1)S(1)}, bf16[64,2560]{1,0:T(8,128)(2,1)S(1)}, u32[]{:S(2)}, u32[]{:S(2)}) collective-permute-start(bf16[64,2560]{1,0:T(8,128)(2,1)S(1)} %get-tuple-element.127), channel_id=1, source_target_pairs={{0,496},{16,0},{32,16},{48,32},{64,48},{80,64},{96,80},{112,96},{1... | collective-permute-start | bytes 983048 | tf_op jit(solution)/shard_map/ppermute | solution.py:353
  117.4 70.2 %collective-permute-start.14 = (bf16[64,2560]{1,0:T(8,128)(2,1)S(1)}, bf16[64,2560]{1,0:T(8,128)(2,1)S(1)}, u32[]{:S(2)}, u32[]{:S(2)}) collective-permute-start(bf16[64,2560]{1,0:T(8,128)(2,1)S(1)} %get-tuple-element.126), channel_id=1, source_target_pairs={{0,496},{16,0},{32,16},{48,32},{64,48},{80,64},{96,80},{112,96},{1... | collective-permute-start | bytes 983048 | tf_op jit(solution)/shard_map/ppermute | solution.py:353
  119.4 1.5 copy-start.4

commit v14 on v12

--- a/solution.py
+++ b/solution.py
@@ -138,7 +138,12 @@
     _, rows, width = normed_ref.shape
     rank = maps_ref.shape[2] // 2
     if tick == 0:
-        stack_ref, sent_ref, grad_latent_ref, active_ref, sem = refs[1:]
+        stack_ref, sent_ref, grad_latent_ref, active_ref, sem, arrived, get_sem = refs[1:]
+        get = pltpu.make_async_copy(incoming_ref.at[pl.ds(part * rows, rows)], arrived, get_sem)
+        get.start()
+        latent, slope, active_ref[...] = forward_values(normed_ref[0], maps_ref[0, :, :rank])
+        get.wait()
+        incoming_ref = arrived
     else:
         latent_ref, slope_ref = refs[:2]
         stack_ref, sent_ref, grad_latent_ref, sem = refs[3:]
@@ -146,9 +151,7 @@
         incoming_ref, stack_ref.at[tick, pl.ds(part * rows, rows)], sem
     )
     keep.start()
-    if tick == 0:
-        latent, slope, active_ref[...] = forward_values(normed_ref[0], maps_ref[0, :, :rank])
-    else:
+    if tick:
         latent, slope = latent_ref[0], slope_ref[0]
     grad_act = jnp.dot(incoming_ref[...], maps_ref[0, :, rank:], preferred_element_type=F32)
     grad_latent = (grad_act * slope).astype(BF16)
@@ -175,9 +178,8 @@
     rank = maps.shape[2] // 2
     first = tick == 0
     narrow = jax.ShapeDtypeStruct((rows, rank), BF16)
-    incoming_spec = (
-        pl.BlockSpec((rows, width), lambda i, levels: (part, 0)) if first else IN_VMEM
-    )
+    incoming_spec = pl.BlockSpec(memory_space=pltpu.HBM) if first else IN_VMEM
+    scratch = [pltpu.VMEM((rows, width), BF16), pltpu.SemaphoreType.DMA] if first else []
     forward_spec = pl.BlockSpec((1, rows, rank), lambda i, levels: (tick - 1, part, 0))
     return pl.pallas_call(
         functools.partial(tick_kernel, tick, part),
@@ -193,7 +195,7 @@
             + [forward_spec] * len(forward)
             + [ANYWHERE],
             out_specs=[ANYWHERE, IN_VMEM, IN_VMEM] + [IN_VMEM] * first,
-            scratch_shapes=[pltpu.SemaphoreType.DMA],
+            scratch_shapes=[pltpu.SemaphoreType.DMA] + scratch,
         ),
         out_shape=[
             jax.ShapeDtypeStruct(stack.shape, stack.dtype),

time: 189 us -> 189 us (level)
  no operation moved by 1% of the time
where the time goes in v14:
time: 189 us; the launch traced here: 188 us
  blocking collectives  62.9 us (33%)
  starting transfers between devices  54 us (29%)
  waiting for transfers between devices  40 us (21%)
  Pallas kernels  24.3 us (13%)
  local copies, waits for them, and re-layouts  3.76 us (2%)
  other arithmetic  2.17 us (1%)
    all_to_all x1, blocking collectives, summed_parts(): lax.all_to_all(parts.reshape(n_dp, share, -1), 'dp', 0, 0, tiled=True)  62.9 us
    ppermute x7, starting transfers between devices, shifted(): return lax.ppermute(value, 'dp', dp_pairs(n_z, step, 0))  27.5 us
    ppermute x8, starting transfers between devices, on_device(): moving.append(lax.ppermute(sent, 'section', down_one))  22.1 us
    ppermute x8, waiting for transfers between devices, on_device(): moving.append(lax.ppermute(sent, 'section', down_one))  20.4 us
    ppermute x7, waiting for transfers between devices, shifted(): return lax.ppermute(value, 'dp', dp_pairs(n_z, step, 0))  13 us
    pallas_call x8, Pallas kernels, tick_layer(): pl.pallas_call(functools.partial(tick_kernel, tick, part), grid_spec=pltp...  12.4 us
    ppermute x1, waiting for transfers between devices, swapped(): return lax.ppermute(value, 'dp', dp_pairs(n_z, 0, 1))  6.54 us
    pallas_call x1, Pallas kernels, norms(): pl.pallas_call(norm_kernel, grid=(ticks,), out_shape=[jax.ShapeDtypeStruc...  4.57 us
  transfers between devices with their start and end apart: 16, of which 9 were waited for; matrix products, arithmetic and copies ran while one was open for 0% of the time, Pallas kernels for 10%

profile of v14, /device:TPU:63, one launch (start us, length us, event | category | flops | bytes accessed | tf_op | source)
XLA Modules:
  0.0 188.4 jit_solution(2525880910546315122)
XLA Ops:
  0.7 0.8 copy-done.8
  1.6 59.8 %conditional.2 = (bf16[2,2560,256]{2,1,0:T(8,128)(2,1)}, bf16[4,128,2560]{2,1,0:T(8,128)(2,1)}, f32[4,128,128]{2,1,0:T(8,128)S(1)}) conditional(s32[]{:T(128)} %convert_element_type.10, (bf16[2,128,160]{1,2,0:T(8,128)(2,1)S(1)}, bf16[2,128,160]{1,2,0:T(8,128)(2,1)S(1)}, bf16[4,1,128,2560]{3,2,1,0:T(8,128)(2,1)}) %tuple.45, ...), branch_computations={%region_0.1_spmd, %region_1.2_spmd} | conditional | flops 4296441856 | bytes 46729012 | solution.py:332
  1.6 0.7 pad_maximum_fusion.2
  2.3 4.4 %collective-permute-start = (bf16[2,160,256]{2,1,0:T(8,128)(2,1)}, bf16[2,160,256]{2,1,0:T(8,128)(2,1)}, u32[]{:S(2)}, u32[]{:S(2)}) collective-permute-start(bf16[2,160,256]{2,1,0:T(8,128)(2,1)} %pad_maximum_fusion.2), channel_id=1, source_target_pairs={{0,1},{1,0},{2,3},{3,2},{4,5},{5,4},{6,7},{7,6},{8,9},{9,8},{10,11... | collective-permute-start | bytes 491528 | tf_op jit(solution)/shard_map/cond/branch_1_fun/ppermute | solution.py:31
  6.9 6.5 %collective-permute-done = bf16[2,160,256]{2,1,0:T(8,128)(2,1)} collective-permute-done((bf16[2,160,256]{2,1,0:T(8,128)(2,1)}, bf16[2,160,256]{2,1,0:T(8,128)(2,1)}, u32[]{:S(2)}, u32[]{:S(2)}) %collective-permute-start) | collective-permute-done | bytes 163872 | tf_op jit(solution)/shard_map/cond/branch_1_fun/ppermute | solution.py:31
  13.5 0.9 select_bitcast_fusion.1
  14.5 4.0 %collective-permute-start.1 = (bf16[2,2,160,256]{3,2,1,0:T(8,128)(2,1)S(1)}, bf16[2,2,160,256]{3,2,1,0:T(8,128)(2,1)S(1)}, u32[]{:S(2)}, u32[]{:S(2)}) collective-permute-start(bf16[2,2,160,256]{3,2,1,0:T(8,128)(2,1)S(1)} %pad_maximum_fusion.1), channel_id=1, source_target_pairs={{0,2},{1,3},{2,4},{3,5},{4,6},{5,7},{6,8},{7,9},{8,10},{9,11},{10,... | collective-permute-start | bytes 983048 | tf_op jit(solution)/shard_map/cond/branch_1_fun/ppermute | solution.py:27
  18.5 8.6 %collective-permute-start.2 = (bf16[2,2,160,256]{3,2,1,0:T(8,128)(2,1)S(1)}, bf16[2,2,160,256]{3,2,1,0:T(8,128)(2,1)S(1)}, u32[]{:S(2)}, u32[]{:S(2)}) collective-permute-start(bf16[2,2,160,256]{3,2,1,0:T(8,128)(2,1)S(1)} %pad_maximum_fusion.1), channel_id=1, source_target_pairs={{0,14},{1,15},{2,0},{3,1},{4,2},{5,3},{6,4},{7,5},{8,6},{9,7},{10,... | collective-permute-start | bytes 983048 | tf_op jit(solution)/shard_map/cond/branch_1_fun/ppermute | solution.py:27
  27.1 4.6 %norms.3 = (bf16[4,128,2560]{2,1,0:T(8,128)(2,1)}, f32[4,128,128]{2,1,0:T(8,128)S(1)}) custom-call(bf16[4,1,128,2560]{3,2,1,0:T(8,128)(2,1)} %get-tuple-element.43.x_ref), custom_call_target="tpu_custom_call" | custom-call | flops 4294967296 | bytes 8388608 | tf_op jit(solution)/shard_map/cond/branch_1_fun/norms/pallas_call | solution.py:78
  31.6 1.9 %collective-permute-start.3 = (bf16[2,2,160,256]{3,2,1,0:T(8,128)(2,1)S(1)}, bf16[2,2,160,256]{3,2,1,0:T(8,128)(2,1)S(1)}, u32[]{:S(2)}, u32[]{:S(2)}) collective-permute-start(bf16[2,2,160,256]{3,2,1,0:T(8,128)(2,1)S(1)} %collective-permute-done.1), channel_id=1, source_target_pairs={{0,2},{1,3},{2,4},{3,5},{4,6},{5,7},{6,8},{7,9},{8,10},{9,11},{10,... | collective-permute-start | bytes 983048 | tf_op jit(solution)/shard_map/cond/branch_1_fun/ppermute | solution.py:27
  33.6 4.6 %collective-permute-start.4 = (bf16[2,2,160,256]{3,2,1,0:T(8,128)(2,1)S(1)}, bf16[2,2,160,256]{3,2,1,0:T(8,128)(2,1)S(1)}, u32[]{:S(2)}, u32[]{:S(2)}) collective-permute-start(bf16[2,2,160,256]{3,2,1,0:T(8,128)(2,1)S(1)} %collective-permute-done.2), channel_id=1, source_target_pairs={{0,14},{1,15},{2,0},{3,1},{4,2},{5,3},{6,4},{7,5},{8,6},{9,7},{10,... | collective-permute-start | bytes 983048 | tf_op jit(solution)/shard_map/cond/branch_1_fun/ppermute | solution.py:27
  38.2 3.6 %collective-permute-done.3 = bf16[2,2,160,256]{3,2,1,0:T(8,128)(2,1)S(1)} collective-permute-done((bf16[2,2,160,256]{3,2,1,0:T(8,128)(2,1)S(1)}, bf16[2,2,160,256]{3,2,1,0:T(8,128)(2,1)S(1)}, u32[]{:S(2)}, u32[]{:S(2)}) %collective-permute-start.3) | collective-permute-done | bytes 327712 | tf_op jit(solution)/shard_map/cond/branch_1_fun/ppermute | solution.py:27
  41.8 1.9 %collective-permute-start.5 = (bf16[2,2,160,256]{3,2,1,0:T(8,128)(2,1)S(1)}, bf16[2,2,160,256]{3,2,1,0:T(8,128)(2,1)S(1)}, u32[]{:S(2)}, u32[]{:S(2)}) collective-permute-start(bf16[2,2,160,256]{3,2,1,0:T(8,128)(2,1)S(1)} %collective-permute-done.3), channel_id=1, source_target_pairs={{0,2},{1,3},{2,4},{3,5},{4,6},{5,7},{6,8},{7,9},{8,10},{9,11},{10,... | collective-permute-start | bytes 983048 | tf_op jit(solution)/shard_map/cond/branch_1_fun/ppermute | solution.py:27
  43.8 4.6 %collective-permute-start.7 = (bf16[2,2,160,256]{3,2,1,0:T(8,128)(2,1)S(1)}, bf16[2,2,160,256]{3,2,1,0:T(8,128)(2,1)S(1)}, u32[]{:S(2)}, u32[]{:S(2)}) collective-permute-start(bf16[2,2,160,256]{3,2,1,0:T(8,128)(2,1)S(1)} %collective-permute-done.4), channel_id=1, source_target_pairs={{0,14},{1,15},{2,0},{3,1},{4,2},{5,3},{6,4},{7,5},{8,6},{9,7},{10,... | collective-permute-start | bytes 983048 | tf_op jit(solution)/shard_map/cond/branch_1_fun/ppermute | solution.py:27
  48.4 2.4 %collective-permute-done.5 = bf16[2,2,160,256]{3,2,1,0:T(8,128)(2,1)S(1)} collective-permute-done((bf16[2,2,160,256]{3,2,1,0:T(8,128)(2,1)S(1)}, bf16[2,2,160,256]{3,2,1,0:T(8,128)(2,1)S(1)}, u32[]{:S(2)}, u32[]{:S(2)}) %collective-permute-start.5) | collective-permute-done | bytes 327712 | tf_op jit(solution)/shard_map/cond/branch_1_fun/ppermute | solution.py:27
  50.8 1.9 %collective-permute-start.6 = (bf16[2,2,160,256]{3,2,1,0:T(8,128)(2,1)S(1)}, bf16[2,2,160,256]{3,2,1,0:T(8,128)(2,1)S(1)}, u32[]{:S(2)}, u32[]{:S(2)}) collective-permute-start(bf16[2,2,160,256]{3,2,1,0:T(8,128)(2,1)S(1)} %collective-permute-done.5), channel_id=1, source_target_pairs={{0,2},{1,3},{2,4},{3,5},{4,6},{5,7},{6,8},{7,9},{8,10},{9,11},{10,... | collective-permute-start | bytes 983048 | tf_op jit(solution)/shard_map/cond/branch_1_fun/ppermute | solution.py:27
  52.8 7.0 %collective-permute-done.6 = bf16[2,2,160,256]{3,2,1,0:T(8,128)(2,1)S(1)} collective-permute-done((bf16[2,2,160,256]{3,2,1,0:T(8,128)(2,1)S(1)}, bf16[2,2,160,256]{3,2,1,0:T(8,128)(2,1)S(1)}, u32[]{:S(2)}, u32[]{:S(2)}) %collective-permute-start.6) | collective-permute-done | bytes 327712 | tf_op jit(solution)/shard_map/cond/branch_1_fun/ppermute | solution.py:27
  59.9 1.5 copy-done.6
  61.5 3.3 %tick_layer.8 = (bf16[4,128,2560]{2,1,0:T(8,128)(2,1)S(1)}, bf16[64,2560]{1,0:T(8,128)(2,1)S(1)}, bf16[64,128]{1,0:T(8,128)(2,1)S(1)}, bf16[64,128]{1,0:T(8,128)(2,1)S(1)}) custom-call(s32[4]{0:T(128)S(1)} %pad_add_fusion.levels_ref, bf16[128,2560]{1,0:T(8,128)(2,1)S(1)} %bitcast.98, ...), custom_call_target="tpu_custom_call", output_to_operand_aliasing={{0}: (5, {})} | custom-call | flops 4294967296 | bytes 8388608 | tf_op jit(solution)/shard_map/tick_layer/pallas_call | solution.py:184
  64.8 7.3 %collective-permute-start.8 = (bf16[64,2560]{1,0:T(8,128)(2,1)S(1)}, bf16[64,2560]{1,0:T(8,128)(2,1)S(1)}, u32[]{:S(2)}, u32[]{:S(2)}) collective-permute-start(bf16[64,2560]{1,0:T(8,128)(2,1)S(1)} %get-tuple-element.99), channel_id=1, source_target_pairs={{0,496},{16,0},{32,16},{48,32},{64,48},{80,64},{96,80},{112,96},{1... | collective-permute-start | bytes 983048 | tf_op jit(solution)/shard_map/ppermute | solution.py:346
  72.1 1.6 tick_layer.9
  73.7 3.3 %collective-permute-start.9 = (bf16[64,2560]{1,0:T(8,128)(2,1)S(1)}, bf16[64,2560]{1,0:T(8,128)(2,1)S(1)}, u32[]{:S(2)}, u32[]{:S(2)}) collective-permute-start(bf16[64,2560]{1,0:T(8,128)(2,1)S(1)} %get-tuple-element.104), channel_id=1, source_target_pairs={{0,496},{16,0},{32,16},{48,32},{64,48},{80,64},{96,80},{112,96},{1... | collective-permute-start | bytes 983048 | tf_op jit(solution)/shard_map/ppermute | solution.py:346
  77.0 1.6 forward_rest.1
  78.7 1.2 tick_layer.10
  80.0 1.9 %collective-permute-start.10 = (bf16[64,2560]{1,0:T(8,128)(2,1)S(1)}, bf16[64,2560]{1,0:T(8,128)(2,1)S(1)}, u32[]{:S(2)}, u32[]{:S(2)}) collective-permute-start(bf16[64,2560]{1,0:T(8,128)(2,1)S(1)} %get-tuple-element.107), channel_id=1, source_target_pairs={{0,496},{16,0},{32,16},{48,32},{64,48},{80,64},{96,80},{112,96},{1... | collective-permute-start | bytes 983048 | tf_op jit(solution)/shard_map/ppermute | solution.py:355
  81.9 4.1 %collective-permute-done.9.incoming_ref = bf16[64,2560]{1,0:T(8,128)(2,1)S(1)} collective-permute-done((bf16[64,2560]{1,0:T(8,128)(2,1)S(1)}, bf16[64,2560]{1,0:T(8,128)(2,1)S(1)}, u32[]{:S(2)}, u32[]{:S(2)}) %collective-permute-start.9) | collective-permute-done | bytes 327712 | tf_op jit(solution)/shard_map/ppermute | solution.py:346
  86.0 1.2 tick_layer.11
  87.3 1.9 %collective-permute-start.11 = (bf16[64,2560]{1,0:T(8,128)(2,1)S(1)}, bf16[64,2560]{1,0:T(8,128)(2,1)S(1)}, u32[]{:S(2)}, u32[]{:S(2)}) collective-permute-start(bf16[64,2560]{1,0:T(8,128)(2,1)S(1)} %get-tuple-element.110), channel_id=1, source_target_pairs={{0,496},{16,0},{32,16},{48,32},{64,48},{80,64},{96,80},{112,96},{1... | collective-permute-start | bytes 983048 | tf_op jit(solution)/shard_map/ppermute | solution.py:355
  89.2 3.0 %collective-permute-done.10.incoming_ref = bf16[64,2560]{1,0:T(8,128)(2,1)S(1)} collective-permute-done((bf16[64,2560]{1,0:T(8,128)(2,1)S(1)}, bf16[64,2560]{1,0:T(8,128)(2,1)S(1)}, u32[]{:S(2)}, u32[]{:S(2)}) %collective-permute-start.10) | collective-permute-done | bytes 327712 | tf_op jit(solution)/shard_map/ppermute | solution.py:355
  92.3 1.2 tick_layer.12
  93.5 1.9 %collective-permute-start.12 = (bf16[64,2560]{1,0:T(8,128)(2,1)S(1)}, bf16[64,2560]{1,0:T(8,128)(2,1)S(1)}, u32[]{:S(2)}, u32[]{:S(2)}) collective-permute-start(bf16[64,2560]{1,0:T(8,128)(2,1)S(1)} %get-tuple-element.113), channel_id=1, source_target_pairs={{0,496},{16,0},{32,16},{48,32},{64,48},{80,64},{96,80},{112,96},{1... | collective-permute-start | bytes 983048 | tf_op jit(solution)/shard_map/ppermute | solution.py:355
  95.4 4.1 %collective-permute-done.11.incoming_ref = bf16[64,2560]{1,0:T(8,128)(2,1)S(1)} collective-permute-done((bf16[64,2560]{1,0:T(8,128)(2,1)S(1)}, bf16[64,2560]{1,0:T(8,128)(2,1)S(1)}, u32[]{:S(2)}, u32[]{:S(2)}) %collective-permute-start.11) | collective-permute-done | bytes 327712 | tf_op jit(solution)/shard_map/ppermute | solution.py:355
  99.6 1.2 tick_layer.13
  100.8 1.9 %collective-permute-start.13 = (bf16[64,2560]{1,0:T(8,128)(2,1)S(1)}, bf16[64,2560]{1,0:T(8,128)(2,1)S(1)}, u32[]{:S(2)}, u32[]{:S(2)}) collective-permute-start(bf16[64,2560]{1,0:T(8,128)(2,1)S(1)} %get-tuple-element.116), channel_id=1, source_target_pairs={{0,496},{16,0},{32,16},{48,32},{64,48},{80,64},{96,80},{112,96},{1... | collective-permute-start | bytes 983048 | tf_op jit(solution)/shard_map/ppermute | solution.py:355
  102.8 3.0 %collective-permute-done.12.incoming_ref = bf16[64,2560]{1,0:T(8,128)(2,1)S(1)} collective-permute-done((bf16[64,2560]{1,0:T(8,128)(2,1)S(1)}, bf16[64,2560]{1,0:T(8,128)(2,1)S(1)}, u32[]{:S(2)}, u32[]{:S(2)}) %collective-permute-start.12) | collective-permute-done | bytes 327712 | tf_op jit(solution)/shard_map/ppermute | solution.py:355
  105.8 1.2 tick_layer.14
  107.1 6.1 %collective-permute-done.13.incoming_ref = bf16[64,2560]{1,0:T(8,128)(2,1)S(1)} collective-permute-done((bf16[64,2560]{1,0:T(8,128)(2,1)S(1)}, bf16[64,2560]{1,0:T(8,128)(2,1)S(1)}, u32[]{:S(2)}, u32[]{:S(2)}) %collective-permute-start.13) | collective-permute-done | bytes 327712 | tf_op jit(solution)/shard_map/ppermute | solution.py:355
  113.1 1.3 tick_layer.15
  114.4 1.9 %collective-permute-start.15 = (bf16[64,2560]{1,0:T(8,128)(2,1)S(1)}, bf16[64,2560]{1,0:T(8,128)(2,1)S(1)}, u32[]{:S(2)}, u32[]{:S(2)}) collective-permute-start(bf16[64,2560]{1,0:T(8,128)(2,1)S(1)} %get-tuple-element.124), channel_id=1, source_target_pairs={{0,496},{16,0},{32,16},{48,32},{64,48},{80,64},{96,80},{112,96},{1... | collective-permute-start | bytes 983048 | tf_op jit(solution)/shard_map/ppermute | solution.py:355
  116.3 1.9 %collective-permute-start.14 = (bf16[64,2560]{1,0:T(8,128)(2,1)S(1)}, bf16[64,2560]{1,0:T(8,128)(2,1)S(1)}, u32[]{:S(2)}, u32[]{:S(2)}) collective-permute-start(bf16[64,2560]{1,0:T(8,128)(2,1)S(1)} %get-tuple-element.123), channel_id=1, source_target_pairs={{0,496},{16,0},{32,16},{48,32},{64,48},{80,64},{96,80},{112,96},{1... | collective-permute-start | bytes 983048 | tf_op jit(solution)/shard_map/ppermute | solution.py:355
  118.3 69.1 %conditional.3 = (f32[160,512]{1,0:T(8,128)S(1)}) conditional(s32[]{:T(128)} %convert_element_type.10, (bf16[4,128,2560]{2,1,0:T(8,128)(2,1)S(1)}, bf16[512,128]{1,0:T(8,128)(2,1)S(1)}, bf16[4,128,2560]{2,1,0:T(8,128)(2,1)}, bf16[4,128,128]{2,1,0:T(8,128)(2,1)S(1)}) %tuple.41, (s32[4]{0:T(128)S(1)}, bf16[512,128]{1,0:T(8,128)(2,1)S(1)}, ...), branch_computations={%region_2.3_spmd, %region_3.4_spmd} | conditional | flops 4296278016 | bytes 25954380 | solution.py:384
  118.4 0.1 broadcast_select_fusion.1
  118.5 0.2 broadcast_select_fusion.3
  118.8 1.0 copy-done.4
  119.8 4.4 %weight_products.1 = bf16[2560,512]{1,0:T(8,128)(2,1)S(1)} custom-call(bf16[4,128,2560]{2,1,0:T(8,128)(2,1)} %copy-done.4, bf16[4,128,2560]{2,1,0:T(8,128)(2,1)} %get-tuple-element.51.grads_ref, bf16[512,256]{1,0:T(8,128)(2,1)S(1)} %pad_maximum_fusion.3.lats_ref, bf16[512,256]{1,0:T(8,128)(2,1)S(1)} %bitcast.97), custom_call_target="tpu_custom_call" | custom-call | flops 4294967296 | bytes 8388608 | tf_op jit(solution)/shard_map/cond/branch_1_fun/weight_products/pallas_call | solution.py:228
  124.2 62.9 %all_to_all.13.moved_ref = bf16[16,160,512]{2,1,0:T(8,128)(2,1)S(1)} all-to-all(bf16[16,160,512]{2,1,0:T(8,128)(2,1)S(1)} %bitcast.96), channel_id=1, replica_groups=mesh['section'=32,'dp'=16] {'dp'}, dimensions={0} | all-to-all | bytes 5242880 | tf_op jit(solution)/shard_map/cond/branch_1_fun/all_to_all | solution.py:362
  187.1 0.3 sum_partials.3
  187.4 1.0 finish.1
  (55 shorter events, 0.7 us)
Async XLA Ops:
  0.6 0.9 copy-start.8
  0.6 0.9 copy-start.9
  1.6 59.9 %copy-start = (bf16[1,128,2560]{2,1,0:T(8,128)(2,1)S(1)}, bf16[1,128,2560]{2,1,0:T(8,128)(2,1)}, u32[]{:S(2)}) copy-start(bf16[1,128,2560]{2,1,0:T(8,128)(2,1)} %param.9) | copy-start | bytes 1966084
  2.3 11.2 %collective-permute-start = (bf16[2,160,256]{2,1,0:T(8,128)(2,1)}, bf16[2,160,256]{2,1,0:T(8,128)(2,1)}, u32[]{:S(2)}, u32[]{:S(2)}) collective-permute-start(bf16[2,160,256]{2,1,0:T(8,128)(2,1)} %pad_maximum_fusion.2), channel_id=1, source_target_pairs={{0,1},{1,0},{2,3},{3,2},{4,5},{5,4},{6,7},{7,6},{8,9},{9,8},{10,11... | collective-permute-start | bytes 491528 | tf_op jit(solution)/shard_map/cond/branch_1_fun/ppermute | solution.py:31
  14.5 17.2 %collective-permute-start.1 = (bf16[2,2,160,256]{3,2,1,0:T(8,128)(2,1)S(1)}, bf16[2,2,160,256]{3,2,1,0:T(8,128)(2,1)S(1)}, u32[]{:S(2)}, u32[]{:S(2)}) collective-permute-start(bf16[2,2,160,256]{3,2,1,0:T(8,128)(2,1)S(1)} %pad_maximum_fusion.1), channel_id=1, source_target_pairs={{0,2},{1,3},{2,4},{3,5},{4,6},{5,7},{6,8},{7,9},{8,10},{9,11},{10,... | collective-permute-start | bytes 983048 | tf_op jit(solution)/shard_map/cond/branch_1_fun/ppermute | solution.py:27
  18.5 15.1 %collective-permute-start.2 = (bf16[2,2,160,256]{3,2,1,0:T(8,128)(2,1)S(1)}, bf16[2,2,160,256]{3,2,1,0:T(8,128)(2,1)S(1)}, u32[]{:S(2)}, u32[]{:S(2)}) collective-permute-start(bf16[2,2,160,256]{3,2,1,0:T(8,128)(2,1)S(1)} %pad_maximum_fusion.1), channel_id=1, source_target_pairs={{0,14},{1,15},{2,0},{3,1},{4,2},{5,3},{6,4},{7,5},{8,6},{9,7},{10,... | collective-permute-start | bytes 983048 | tf_op jit(solution)/shard_map/cond/branch_1_fun/ppermute | solution.py:27
  27.1 6.5 %copy-start.5 = (bf16[2,8,2,160,256]{4,3,2,1,0:T(8,128)(2,1)S(1)}, bf16[2,8,2,160,256]{4,3,2,1,0:T(8,128)(2,1)}, u32[]{:S(2)}) copy-start(bf16[2,8,2,160,256]{4,3,2,1,0:T(8,128)(2,1)} %unset.4) | copy-start | bytes 7864324 | tf_op jit(solution)/shard_map/cond
  31.6 10.2 %collective-permute-start.3 = (bf16[2,2,160,256]{3,2,1,0:T(8,128)(2,1)S(1)}, bf16[2,2,160,256]{3,2,1,0:T(8,128)(2,1)S(1)}, u32[]{:S(2)}, u32[]{:S(2)}) collective-permute-start(bf16[2,2,160,256]{3,2,1,0:T(8,128)(2,1)S(1)} %collective-permute-done.1), channel_id=1, source_target_pairs={{0,2},{1,3},{2,4},{3,5},{4,6},{5,7},{6,8},{7,9},{8,10},{9,11},{10,... | collective-permute-start | bytes 983048 | tf_op jit(solution)/shard_map/cond/branch_1_fun/ppermute | solution.py:27
  33.6 10.1 %collective-permute-start.4 = (bf16[2,2,160,256]{3,2,1,0:T(8,128)(2,1)S(1)}, bf16[2,2,160,256]{3,2,1,0:T(8,128)(2,1)S(1)}, u32[]{:S(2)}, u32[]{:S(2)}) collective-permute-start(bf16[2,2,160,256]{3,2,1,0:T(8,128)(2,1)S(1)} %collective-permute-done.2), channel_id=1, source_target_pairs={{0,14},{1,15},{2,0},{3,1},{4,2},{5,3},{6,4},{7,5},{8,6},{9,7},{10,... | collective-permute-start | bytes 983048 | tf_op jit(solution)/shard_map/cond/branch_1_fun/ppermute | solution.py:27
  41.8 9.0 %collective-permute-start.5 = (bf16[2,2,160,256]{3,2,1,0:T(8,128)(2,1)S(1)}, bf16[2,2,160,256]{3,2,1,0:T(8,128)(2,1)S(1)}, u32[]{:S(2)}, u32[]{:S(2)}) collective-permute-start(bf16[2,2,160,256]{3,2,1,0:T(8,128)(2,1)S(1)} %collective-permute-done.3), channel_id=1, source_target_pairs={{0,2},{1,3},{2,4},{3,5},{4,6},{5,7},{6,8},{7,9},{8,10},{9,11},{10,... | collective-permute-start | bytes 983048 | tf_op jit(solution)/shard_map/cond/branch_1_fun/ppermute | solution.py:27
  43.8 16.1 %collective-permute-start.7 = (bf16[2,2,160,256]{3,2,1,0:T(8,128)(2,1)S(1)}, bf16[2,2,160,256]{3,2,1,0:T(8,128)(2,1)S(1)}, u32[]{:S(2)}, u32[]{:S(2)}) collective-permute-start(bf16[2,2,160,256]{3,2,1,0:T(8,128)(2,1)S(1)} %collective-permute-done.4), channel_id=1, source_target_pairs={{0,14},{1,15},{2,0},{3,1},{4,2},{5,3},{6,4},{7,5},{8,6},{9,7},{10,... | collective-permute-start | bytes 983048 | tf_op jit(solution)/shard_map/cond/branch_1_fun/ppermute | solution.py:27
  50.8 9.0 %collective-permute-start.6 = (bf16[2,2,160,256]{3,2,1,0:T(8,128)(2,1)S(1)}, bf16[2,2,160,256]{3,2,1,0:T(8,128)(2,1)S(1)}, u32[]{:S(2)}, u32[]{:S(2)}) collective-permute-start(bf16[2,2,160,256]{3,2,1,0:T(8,128)(2,1)S(1)} %collective-permute-done.5), channel_id=1, source_target_pairs={{0,2},{1,3},{2,4},{3,5},{4,6},{5,7},{6,8},{7,9},{8,10},{9,11},{10,... | collective-permute-start | bytes 983048 | tf_op jit(solution)/shard_map/cond/branch_1_fun/ppermute | solution.py:27
  59.9 1.5 copy-start.6
  61.4 10.7 %copy-start.10 = (f32[4,128,128]{2,1,0:T(8,128)}, f32[4,128,128]{2,1,0:T(8,128)S(1)}, u32[]{:S(2)}) copy-start(f32[4,128,128]{2,1,0:T(8,128)S(1)} %get-tuple-element.94.inverse_ref) | copy-start | bytes 786436
  61.5 10.6 %copy-start.3 = (bf16[4,128,2560]{2,1,0:T(8,128)(2,1)S(1)}, bf16[4,128,2560]{2,1,0:T(8,128)(2,1)}, u32[]{:S(2)}) copy-start(bf16[4,128,2560]{2,1,0:T(8,128)(2,1)} %get-tuple-element.93.normed_ref) | copy-start | bytes 7864324
  61.5 10.6 %copy-start.7 = (bf16[2,2560,256]{2,1,0:T(8,128)(2,1)S(1)}, bf16[2,2560,256]{2,1,0:T(8,128)(2,1)}, u32[]{:S(2)}) copy-start(bf16[2,2560,256]{2,1,0:T(8,128)(2,1)} %get-tuple-element.95.maps_ref) | copy-start | bytes 7864324
  64.8 13.9 %collective-permute-start.8 = (bf16[64,2560]{1,0:T(8,128)(2,1)S(1)}, bf16[64,2560]{1,0:T(8,128)(2,1)S(1)}, u32[]{:S(2)}, u32[]{:S(2)}) collective-permute-start(bf16[64,2560]{1,0:T(8,128)(2,1)S(1)} %get-tuple-element.99), channel_id=1, source_target_pairs={{0,496},{16,0},{32,16},{48,32},{64,48},{80,64},{96,80},{112,96},{1... | collective-permute-start | bytes 983048 | tf_op jit(solution)/shard_map/ppermute | solution.py:346
  73.7 12.3 %collective-permute-start.9 = (bf16[64,2560]{1,0:T(8,128)(2,1)S(1)}, bf16[64,2560]{1,0:T(8,128)(2,1)S(1)}, u32[]{:S(2)}, u32[]{:S(2)}) collective-permute-start(bf16[64,2560]{1,0:T(8,128)(2,1)S(1)} %get-tuple-element.104), channel_id=1, source_target_pairs={{0,496},{16,0},{32,16},{48,32},{64,48},{80,64},{96,80},{112,96},{1... | collective-permute-start | bytes 983048 | tf_op jit(solution)/shard_map/ppermute | solution.py:346
  77.0 1.7 copy-start.11
  80.0 12.3 %collective-permute-start.10 = (bf16[64,2560]{1,0:T(8,128)(2,1)S(1)}, bf16[64,2560]{1,0:T(8,128)(2,1)S(1)}, u32[]{:S(2)}, u32[]{:S(2)}) collective-permute-start(bf16[64,2560]{1,0:T(8,128)(2,1)S(1)} %get-tuple-element.107), channel_id=1, source_target_pairs={{0,496},{16,0},{32,16},{48,32},{64,48},{80,64},{96,80},{112,96},{1... | collective-permute-start | bytes 983048 | tf_op jit(solution)/shard_map/ppermute | solution.py:355
  87.3 12.3 %collective-permute-start.11 = (bf16[64,2560]{1,0:T(8,128)(2,1)S(1)}, bf16[64,2560]{1,0:T(8,128)(2,1)S(1)}, u32[]{:S(2)}, u32[]{:S(2)}) collective-permute-start(bf16[64,2560]{1,0:T(8,128)(2,1)S(1)} %get-tuple-element.110), channel_id=1, source_target_pairs={{0,496},{16,0},{32,16},{48,32},{64,48},{80,64},{96,80},{112,96},{1... | collective-permute-start | bytes 983048 | tf_op jit(solution)/shard_map/ppermute | solution.py:355
  93.5 12.3 %collective-permute-start.12 = (bf16[64,2560]{1,0:T(8,128)(2,1)S(1)}, bf16[64,2560]{1,0:T(8,128)(2,1)S(1)}, u32[]{:S(2)}, u32[]{:S(2)}) collective-permute-start(bf16[64,2560]{1,0:T(8,128)(2,1)S(1)} %get-tuple-element.113), channel_id=1, source_target_pairs={{0,496},{16,0},{32,16},{48,32},{64,48},{80,64},{96,80},{112,96},{1... | collective-permute-start | bytes 983048 | tf_op jit(solution)/shard_map/ppermute | solution.py:355
  100.8 12.3 %collective-permute-start.13 = (bf16[64,2560]{1,0:T(8,128)(2,1)S(1)}, bf16[64,2560]{1,0:T(8,128)(2,1)S(1)}, u32[]{:S(2)}, u32[]{:S(2)}) collective-permute-start(bf16[64,2560]{1,0:T(8,128)(2,1)S(1)} %get-tuple-element.116), channel_id=1, source_target_pairs={{0,496},{16,0},{32,16},{48,32},{64,48},{80,64},{96,80},{112,96},{1... | collective-permute-start | bytes 983048 | tf_op jit(solution)/shard_map/ppermute | solution.py:355
  107.1 6.1 %copy-start.1 = (bf16[4,128,2560]{2,1,0:T(8,128)(2,1)}, bf16[4,128,2560]{2,1,0:T(8,128)(2,1)S(1)}, u32[]{:S(2)}) copy-start(bf16[4,128,2560]{2,1,0:T(8,128)(2,1)S(1)} %get-tuple-element.117.refs_2_) | copy-start | bytes 7864324
  114.4 73.0 %collective-permute-start.15 = (bf16[64,2560]{1,0:T(8,128)(2,1)S(1)}, bf16[64,2560]{1,0:T(8,128)(2,1)S(1)}, u32[]{:S(2)}, u32[]{:S(2)}) collective-permute-start(bf16[64,2560]{1,0:T(8,128)(2,1)S(1)} %get-tuple-element.124), channel_id=1, source_target_pairs={{0,496},{16,0},{32,16},{48,32},{64,48},{80,64},{96,80},{112,96},{1... | collective-permute-start | bytes 983048 | tf_op jit(solution)/shard_map/ppermute | solution.py:355
  116.3 71.1 %collective-permute-start.14 = (bf16[64,2560]{1,0:T(8,128)(2,1)S(1)}, bf16[64,2560]{1,0:T(8,128)(2,1)S(1)}, u32[]{:S(2)}, u32[]{:S(2)}) collective-permute-start(bf16[64,2560]{1,0:T(8,128)(2,1)S(1)} %get-tuple-element.123), channel_id=1, source_target_pairs={{0,496},{16,0},{32,16},{48,32},{64,48},{80,64},{96,80},{112,96},{1... | collective-permute-start | bytes 983048 | tf_op jit(solution)/shard_map/ppermute | solution.py:355
  118.3 1.5 copy-start.4

commit v15 on v14

--- a/solution.py
+++ b/solution.py
@@ -135,15 +135,20 @@
 
 
 def tick_kernel(tick, part, levels_ref, incoming_ref, normed_ref, inverse_ref, maps_ref, *refs):
-    _, rows, width = normed_ref.shape
+    _, rows, _ = inverse_ref.shape
+    width = maps_ref.shape[1]
     rank = maps_ref.shape[2] // 2
     if tick == 0:
-        stack_ref, sent_ref, grad_latent_ref, active_ref, sem, arrived, get_sem = refs[1:]
-        get = pltpu.make_async_copy(incoming_ref.at[pl.ds(part * rows, rows)], arrived, get_sem)
-        get.start()
-        latent, slope, active_ref[...] = forward_values(normed_ref[0], maps_ref[0, :, :rank])
-        get.wait()
-        incoming_ref = arrived
+        stack_ref, sent_ref, grad_latent_ref, active_ref, sem, arrived, own, get_sems = refs[1:]
+        at = pl.ds(part * rows, rows)
+        get_own = pltpu.make_async_copy(normed_ref.at[pl.ds(0, 1), at], own, get_sems.at[0])
+        get_arrived = pltpu.make_async_copy(incoming_ref.at[at], arrived, get_sems.at[1])
+        get_own.start()
+        get_arrived.start()
+        get_own.wait()
+        latent, slope, active_ref[...] = forward_values(own[0], maps_ref[0, :, :rank])
+        get_arrived.wait()
+        incoming_ref, normed_ref = arrived, own
     else:
         latent_ref, slope_ref = refs[:2]
         stack_ref, sent_ref, grad_latent_ref, sem = refs[3:]
@@ -179,7 +184,15 @@
     first = tick == 0
     narrow = jax.ShapeDtypeStruct((rows, rank), BF16)
     incoming_spec = pl.BlockSpec(memory_space=pltpu.HBM) if first else IN_VMEM
-    scratch = [pltpu.VMEM((rows, width), BF16), pltpu.SemaphoreType.DMA] if first else []
+    normed_spec = pl.BlockSpec((1, rows, width), lambda i, levels: (tick, part, 0))
+    scratch = []
+    if first:
+        normed_spec = pl.BlockSpec(memory_space=pltpu.HBM)
+        scratch = [
+            pltpu.VMEM((rows, width), BF16),
+            pltpu.VMEM((1, rows, width), BF16),
+            pltpu.SemaphoreType.DMA((2,)),
+        ]
     forward_spec = pl.BlockSpec((1, rows, rank), lambda i, levels: (tick - 1, part, 0))
     return pl.pallas_call(
         functools.partial(tick_kernel, tick, part),
@@ -188,7 +201,7 @@
             grid=(1,),
             in_specs=[
                 incoming_spec,
-                pl.BlockSpec((1, rows, width), lambda i, levels: (tick, part, 0)),
+                normed_spec,
                 pl.BlockSpec((1, rows, 128), lambda i, levels: (tick, part, 0)),
                 pl.BlockSpec((1, width, 2 * rank), lambda i, levels: (levels[tick], 0, 0)),
             ]

time: 189 us -> 190 us (level)
  no operation moved by 1% of the time
where the time goes in v15:
time: 190 us; the launch traced here: 189 us
  blocking collectives  62.8 us (33%)
  starting transfers between devices  54 us (28%)
  waiting for transfers between devices  40 us (21%)
  Pallas kernels  25.2 us (13%)
  local copies, waits for them, and re-layouts  3.76 us (2%)
  other arithmetic  2.17 us (1%)
    all_to_all x1, blocking collectives, summed_parts(): lax.all_to_all(parts.reshape(n_dp, share, -1), 'dp', 0, 0, tiled=True)  62.8 us
    ppermute x7, starting transfers between devices, shifted(): return lax.ppermute(value, 'dp', dp_pairs(n_z, step, 0))  27.5 us
    ppermute x8, starting transfers between devices, on_device(): moving.append(lax.ppermute(sent, 'section', down_one))  22.1 us
    ppermute x8, waiting for transfers between devices, on_device(): moving.append(lax.ppermute(sent, 'section', down_one))  20.4 us
    pallas_call x8, Pallas kernels, tick_layer(): pl.pallas_call(functools.partial(tick_kernel, tick, part), grid_spec=pltp...  13.3 us
    ppermute x7, waiting for transfers between devices, shifted(): return lax.ppermute(value, 'dp', dp_pairs(n_z, step, 0))  13 us
    ppermute x1, waiting for transfers between devices, swapped(): return lax.ppermute(value, 'dp', dp_pairs(n_z, 0, 1))  6.54 us
    pallas_call x1, Pallas kernels, norms(): pl.pallas_call(norm_kernel, grid=(ticks,), out_shape=[jax.ShapeDtypeStruc...  4.57 us
  transfers between devices with their start and end apart: 16, of which 9 were waited for; matrix products, arithmetic and copies ran while one was open for 0% of the time, Pallas kernels for 10%

profile of v15, /device:TPU:63, one launch (start us, length us, event | category | flops | bytes accessed | tf_op | source)
XLA Modules:
  0.0 189.3 jit_solution(2306334567591273823)
XLA Ops:
  0.7 0.8 copy-done.8
  1.6 59.8 %conditional.2 = (bf16[2,2560,256]{2,1,0:T(8,128)(2,1)}, bf16[4,128,2560]{2,1,0:T(8,128)(2,1)}, f32[4,128,128]{2,1,0:T(8,128)S(1)}) conditional(s32[]{:T(128)} %convert_element_type.10, (bf16[2,128,160]{1,2,0:T(8,128)(2,1)S(1)}, bf16[2,128,160]{1,2,0:T(8,128)(2,1)S(1)}, bf16[4,1,128,2560]{3,2,1,0:T(8,128)(2,1)}) %tuple.45, ...), branch_computations={%region_0.1_spmd, %region_1.2_spmd} | conditional | flops 4296441856 | bytes 46729012 | solution.py:345
  1.6 0.7 pad_maximum_fusion.2
  2.3 4.4 %collective-permute-start = (bf16[2,160,256]{2,1,0:T(8,128)(2,1)}, bf16[2,160,256]{2,1,0:T(8,128)(2,1)}, u32[]{:S(2)}, u32[]{:S(2)}) collective-permute-start(bf16[2,160,256]{2,1,0:T(8,128)(2,1)} %pad_maximum_fusion.2), channel_id=1, source_target_pairs={{0,1},{1,0},{2,3},{3,2},{4,5},{5,4},{6,7},{7,6},{8,9},{9,8},{10,11... | collective-permute-start | bytes 491528 | tf_op jit(solution)/shard_map/cond/branch_1_fun/ppermute | solution.py:31
  6.9 6.5 %collective-permute-done = bf16[2,160,256]{2,1,0:T(8,128)(2,1)} collective-permute-done((bf16[2,160,256]{2,1,0:T(8,128)(2,1)}, bf16[2,160,256]{2,1,0:T(8,128)(2,1)}, u32[]{:S(2)}, u32[]{:S(2)}) %collective-permute-start) | collective-permute-done | bytes 163872 | tf_op jit(solution)/shard_map/cond/branch_1_fun/ppermute | solution.py:31
  13.5 0.9 select_bitcast_fusion.1
  14.5 4.0 %collective-permute-start.1 = (bf16[2,2,160,256]{3,2,1,0:T(8,128)(2,1)S(1)}, bf16[2,2,160,256]{3,2,1,0:T(8,128)(2,1)S(1)}, u32[]{:S(2)}, u32[]{:S(2)}) collective-permute-start(bf16[2,2,160,256]{3,2,1,0:T(8,128)(2,1)S(1)} %pad_maximum_fusion.1), channel_id=1, source_target_pairs={{0,2},{1,3},{2,4},{3,5},{4,6},{5,7},{6,8},{7,9},{8,10},{9,11},{10,... | collective-permute-start | bytes 983048 | tf_op jit(solution)/shard_map/cond/branch_1_fun/ppermute | solution.py:27
  18.5 8.6 %collective-permute-start.2 = (bf16[2,2,160,256]{3,2,1,0:T(8,128)(2,1)S(1)}, bf16[2,2,160,256]{3,2,1,0:T(8,128)(2,1)S(1)}, u32[]{:S(2)}, u32[]{:S(2)}) collective-permute-start(bf16[2,2,160,256]{3,2,1,0:T(8,128)(2,1)S(1)} %pad_maximum_fusion.1), channel_id=1, source_target_pairs={{0,14},{1,15},{2,0},{3,1},{4,2},{5,3},{6,4},{7,5},{8,6},{9,7},{10,... | collective-permute-start | bytes 983048 | tf_op jit(solution)/shard_map/cond/branch_1_fun/ppermute | solution.py:27
  27.1 4.6 %norms.3 = (bf16[4,128,2560]{2,1,0:T(8,128)(2,1)}, f32[4,128,128]{2,1,0:T(8,128)S(1)}) custom-call(bf16[4,1,128,2560]{3,2,1,0:T(8,128)(2,1)} %get-tuple-element.43.x_ref), custom_call_target="tpu_custom_call" | custom-call | flops 4294967296 | bytes 8388608 | tf_op jit(solution)/shard_map/cond/branch_1_fun/norms/pallas_call | solution.py:78
  31.6 1.9 %collective-permute-start.3 = (bf16[2,2,160,256]{3,2,1,0:T(8,128)(2,1)S(1)}, bf16[2,2,160,256]{3,2,1,0:T(8,128)(2,1)S(1)}, u32[]{:S(2)}, u32[]{:S(2)}) collective-permute-start(bf16[2,2,160,256]{3,2,1,0:T(8,128)(2,1)S(1)} %collective-permute-done.1), channel_id=1, source_target_pairs={{0,2},{1,3},{2,4},{3,5},{4,6},{5,7},{6,8},{7,9},{8,10},{9,11},{10,... | collective-permute-start | bytes 983048 | tf_op jit(solution)/shard_map/cond/branch_1_fun/ppermute | solution.py:27
  33.6 4.6 %collective-permute-start.4 = (bf16[2,2,160,256]{3,2,1,0:T(8,128)(2,1)S(1)}, bf16[2,2,160,256]{3,2,1,0:T(8,128)(2,1)S(1)}, u32[]{:S(2)}, u32[]{:S(2)}) collective-permute-start(bf16[2,2,160,256]{3,2,1,0:T(8,128)(2,1)S(1)} %collective-permute-done.2), channel_id=1, source_target_pairs={{0,14},{1,15},{2,0},{3,1},{4,2},{5,3},{6,4},{7,5},{8,6},{9,7},{10,... | collective-permute-start | bytes 983048 | tf_op jit(solution)/shard_map/cond/branch_1_fun/ppermute | solution.py:27
  38.2 3.6 %collective-permute-done.3 = bf16[2,2,160,256]{3,2,1,0:T(8,128)(2,1)S(1)} collective-permute-done((bf16[2,2,160,256]{3,2,1,0:T(8,128)(2,1)S(1)}, bf16[2,2,160,256]{3,2,1,0:T(8,128)(2,1)S(1)}, u32[]{:S(2)}, u32[]{:S(2)}) %collective-permute-start.3) | collective-permute-done | bytes 327712 | tf_op jit(solution)/shard_map/cond/branch_1_fun/ppermute | solution.py:27
  41.8 1.9 %collective-permute-start.5 = (bf16[2,2,160,256]{3,2,1,0:T(8,128)(2,1)S(1)}, bf16[2,2,160,256]{3,2,1,0:T(8,128)(2,1)S(1)}, u32[]{:S(2)}, u32[]{:S(2)}) collective-permute-start(bf16[2,2,160,256]{3,2,1,0:T(8,128)(2,1)S(1)} %collective-permute-done.3), channel_id=1, source_target_pairs={{0,2},{1,3},{2,4},{3,5},{4,6},{5,7},{6,8},{7,9},{8,10},{9,11},{10,... | collective-permute-start | bytes 983048 | tf_op jit(solution)/shard_map/cond/branch_1_fun/ppermute | solution.py:27
  43.8 4.6 %collective-permute-start.7 = (bf16[2,2,160,256]{3,2,1,0:T(8,128)(2,1)S(1)}, bf16[2,2,160,256]{3,2,1,0:T(8,128)(2,1)S(1)}, u32[]{:S(2)}, u32[]{:S(2)}) collective-permute-start(bf16[2,2,160,256]{3,2,1,0:T(8,128)(2,1)S(1)} %collective-permute-done.4), channel_id=1, source_target_pairs={{0,14},{1,15},{2,0},{3,1},{4,2},{5,3},{6,4},{7,5},{8,6},{9,7},{10,... | collective-permute-start | bytes 983048 | tf_op jit(solution)/shard_map/cond/branch_1_fun/ppermute | solution.py:27
  48.4 2.4 %collective-permute-done.5 = bf16[2,2,160,256]{3,2,1,0:T(8,128)(2,1)S(1)} collective-permute-done((bf16[2,2,160,256]{3,2,1,0:T(8,128)(2,1)S(1)}, bf16[2,2,160,256]{3,2,1,0:T(8,128)(2,1)S(1)}, u32[]{:S(2)}, u32[]{:S(2)}) %collective-permute-start.5) | collective-permute-done | bytes 327712 | tf_op jit(solution)/shard_map/cond/branch_1_fun/ppermute | solution.py:27
  50.8 1.9 %collective-permute-start.6 = (bf16[2,2,160,256]{3,2,1,0:T(8,128)(2,1)S(1)}, bf16[2,2,160,256]{3,2,1,0:T(8,128)(2,1)S(1)}, u32[]{:S(2)}, u32[]{:S(2)}) collective-permute-start(bf16[2,2,160,256]{3,2,1,0:T(8,128)(2,1)S(1)} %collective-permute-done.5), channel_id=1, source_target_pairs={{0,2},{1,3},{2,4},{3,5},{4,6},{5,7},{6,8},{7,9},{8,10},{9,11},{10,... | collective-permute-start | bytes 983048 | tf_op jit(solution)/shard_map/cond/branch_1_fun/ppermute | solution.py:27
  52.8 7.0 %collective-permute-done.6 = bf16[2,2,160,256]{3,2,1,0:T(8,128)(2,1)S(1)} collective-permute-done((bf16[2,2,160,256]{3,2,1,0:T(8,128)(2,1)S(1)}, bf16[2,2,160,256]{3,2,1,0:T(8,128)(2,1)S(1)}, u32[]{:S(2)}, u32[]{:S(2)}) %collective-permute-start.6) | collective-permute-done | bytes 327712 | tf_op jit(solution)/shard_map/cond/branch_1_fun/ppermute | solution.py:27
  59.9 1.5 copy-done.6
  61.5 4.1 %tick_layer.8 = (bf16[4,128,2560]{2,1,0:T(8,128)(2,1)S(1)}, bf16[64,2560]{1,0:T(8,128)(2,1)S(1)}, bf16[64,128]{1,0:T(8,128)(2,1)S(1)}, bf16[64,128]{1,0:T(8,128)(2,1)S(1)}) custom-call(s32[4]{0:T(128)S(1)} %pad_add_fusion.levels_ref, bf16[128,2560]{1,0:T(8,128)(2,1)S(1)} %bitcast.98, ...), custom_call_target="tpu_custom_call", output_to_operand_aliasing={{0}: (5, {})} | custom-call | flops 4294967296 | bytes 8388608 | tf_op jit(solution)/shard_map/tick_layer/pallas_call | solution.py:197
  65.6 7.3 %collective-permute-start.8 = (bf16[64,2560]{1,0:T(8,128)(2,1)S(1)}, bf16[64,2560]{1,0:T(8,128)(2,1)S(1)}, u32[]{:S(2)}, u32[]{:S(2)}) collective-permute-start(bf16[64,2560]{1,0:T(8,128)(2,1)S(1)} %get-tuple-element.99), channel_id=1, source_target_pairs={{0,496},{16,0},{32,16},{48,32},{64,48},{80,64},{96,80},{112,96},{1... | collective-permute-start | bytes 983048 | tf_op jit(solution)/shard_map/ppermute | solution.py:359
  72.9 1.7 tick_layer.9
  74.6 3.3 %collective-permute-start.9 = (bf16[64,2560]{1,0:T(8,128)(2,1)S(1)}, bf16[64,2560]{1,0:T(8,128)(2,1)S(1)}, u32[]{:S(2)}, u32[]{:S(2)}) collective-permute-start(bf16[64,2560]{1,0:T(8,128)(2,1)S(1)} %get-tuple-element.104), channel_id=1, source_target_pairs={{0,496},{16,0},{32,16},{48,32},{64,48},{80,64},{96,80},{112,96},{1... | collective-permute-start | bytes 983048 | tf_op jit(solution)/shard_map/ppermute | solution.py:359
  77.9 1.6 forward_rest.1
  79.6 1.2 tick_layer.10
  80.9 1.9 %collective-permute-start.10 = (bf16[64,2560]{1,0:T(8,128)(2,1)S(1)}, bf16[64,2560]{1,0:T(8,128)(2,1)S(1)}, u32[]{:S(2)}, u32[]{:S(2)}) collective-permute-start(bf16[64,2560]{1,0:T(8,128)(2,1)S(1)} %get-tuple-element.107), channel_id=1, source_target_pairs={{0,496},{16,0},{32,16},{48,32},{64,48},{80,64},{96,80},{112,96},{1... | collective-permute-start | bytes 983048 | tf_op jit(solution)/shard_map/ppermute | solution.py:368
  82.8 4.1 %collective-permute-done.9.incoming_ref = bf16[64,2560]{1,0:T(8,128)(2,1)S(1)} collective-permute-done((bf16[64,2560]{1,0:T(8,128)(2,1)S(1)}, bf16[64,2560]{1,0:T(8,128)(2,1)S(1)}, u32[]{:S(2)}, u32[]{:S(2)}) %collective-permute-start.9) | collective-permute-done | bytes 327712 | tf_op jit(solution)/shard_map/ppermute | solution.py:359
  86.9 1.2 tick_layer.11
  88.2 1.9 %collective-permute-start.11 = (bf16[64,2560]{1,0:T(8,128)(2,1)S(1)}, bf16[64,2560]{1,0:T(8,128)(2,1)S(1)}, u32[]{:S(2)}, u32[]{:S(2)}) collective-permute-start(bf16[64,2560]{1,0:T(8,128)(2,1)S(1)} %get-tuple-element.110), channel_id=1, source_target_pairs={{0,496},{16,0},{32,16},{48,32},{64,48},{80,64},{96,80},{112,96},{1... | collective-permute-start | bytes 983048 | tf_op jit(solution)/shard_map/ppermute | solution.py:368
  90.1 3.0 %collective-permute-done.10.incoming_ref = bf16[64,2560]{1,0:T(8,128)(2,1)S(1)} collective-permute-done((bf16[64,2560]{1,0:T(8,128)(2,1)S(1)}, bf16[64,2560]{1,0:T(8,128)(2,1)S(1)}, u32[]{:S(2)}, u32[]{:S(2)}) %collective-permute-start.10) | collective-permute-done | bytes 327712 | tf_op jit(solution)/shard_map/ppermute | solution.py:368
  93.2 1.2 tick_layer.12
  94.4 1.9 %collective-permute-start.12 = (bf16[64,2560]{1,0:T(8,128)(2,1)S(1)}, bf16[64,2560]{1,0:T(8,128)(2,1)S(1)}, u32[]{:S(2)}, u32[]{:S(2)}) collective-permute-start(bf16[64,2560]{1,0:T(8,128)(2,1)S(1)} %get-tuple-element.113), channel_id=1, source_target_pairs={{0,496},{16,0},{32,16},{48,32},{64,48},{80,64},{96,80},{112,96},{1... | collective-permute-start | bytes 983048 | tf_op jit(solution)/shard_map/ppermute | solution.py:368
  96.3 4.1 %collective-permute-done.11.incoming_ref = bf16[64,2560]{1,0:T(8,128)(2,1)S(1)} collective-permute-done((bf16[64,2560]{1,0:T(8,128)(2,1)S(1)}, bf16[64,2560]{1,0:T(8,128)(2,1)S(1)}, u32[]{:S(2)}, u32[]{:S(2)}) %collective-permute-start.11) | collective-permute-done | bytes 327712 | tf_op jit(solution)/shard_map/ppermute | solution.py:368
  100.5 1.2 tick_layer.13
  101.7 1.9 %collective-permute-start.13 = (bf16[64,2560]{1,0:T(8,128)(2,1)S(1)}, bf16[64,2560]{1,0:T(8,128)(2,1)S(1)}, u32[]{:S(2)}, u32[]{:S(2)}) collective-permute-start(bf16[64,2560]{1,0:T(8,128)(2,1)S(1)} %get-tuple-element.116), channel_id=1, source_target_pairs={{0,496},{16,0},{32,16},{48,32},{64,48},{80,64},{96,80},{112,96},{1... | collective-permute-start | bytes 983048 | tf_op jit(solution)/shard_map/ppermute | solution.py:368
  103.7 3.0 %collective-permute-done.12.incoming_ref = bf16[64,2560]{1,0:T(8,128)(2,1)S(1)} collective-permute-done((bf16[64,2560]{1,0:T(8,128)(2,1)S(1)}, bf16[64,2560]{1,0:T(8,128)(2,1)S(1)}, u32[]{:S(2)}, u32[]{:S(2)}) %collective-permute-start.12) | collective-permute-done | bytes 327712 | tf_op jit(solution)/shard_map/ppermute | solution.py:368
  106.7 1.2 tick_layer.14
  108.0 6.1 %collective-permute-done.13.incoming_ref = bf16[64,2560]{1,0:T(8,128)(2,1)S(1)} collective-permute-done((bf16[64,2560]{1,0:T(8,128)(2,1)S(1)}, bf16[64,2560]{1,0:T(8,128)(2,1)S(1)}, u32[]{:S(2)}, u32[]{:S(2)}) %collective-permute-start.13) | collective-permute-done | bytes 327712 | tf_op jit(solution)/shard_map/ppermute | solution.py:368
  114.0 1.3 tick_layer.15
  115.3 1.9 %collective-permute-start.15 = (bf16[64,2560]{1,0:T(8,128)(2,1)S(1)}, bf16[64,2560]{1,0:T(8,128)(2,1)S(1)}, u32[]{:S(2)}, u32[]{:S(2)}) collective-permute-start(bf16[64,2560]{1,0:T(8,128)(2,1)S(1)} %get-tuple-element.124), channel_id=1, source_target_pairs={{0,496},{16,0},{32,16},{48,32},{64,48},{80,64},{96,80},{112,96},{1... | collective-permute-start | bytes 983048 | tf_op jit(solution)/shard_map/ppermute | solution.py:368
  117.2 1.9 %collective-permute-start.14 = (bf16[64,2560]{1,0:T(8,128)(2,1)S(1)}, bf16[64,2560]{1,0:T(8,128)(2,1)S(1)}, u32[]{:S(2)}, u32[]{:S(2)}) collective-permute-start(bf16[64,2560]{1,0:T(8,128)(2,1)S(1)} %get-tuple-element.123), channel_id=1, source_target_pairs={{0,496},{16,0},{32,16},{48,32},{64,48},{80,64},{96,80},{112,96},{1... | collective-permute-start | bytes 983048 | tf_op jit(solution)/shard_map/ppermute | solution.py:368
  119.2 69.1 %conditional.3 = (f32[160,512]{1,0:T(8,128)S(1)}) conditional(s32[]{:T(128)} %convert_element_type.10, (bf16[4,128,2560]{2,1,0:T(8,128)(2,1)S(1)}, bf16[512,128]{1,0:T(8,128)(2,1)S(1)}, bf16[4,128,2560]{2,1,0:T(8,128)(2,1)}, bf16[4,128,128]{2,1,0:T(8,128)(2,1)S(1)}) %tuple.41, (s32[4]{0:T(128)S(1)}, bf16[512,128]{1,0:T(8,128)(2,1)S(1)}, ...), branch_computations={%region_2.3_spmd, %region_3.4_spmd} | conditional | flops 4296278016 | bytes 25954380 | solution.py:397
  119.3 0.1 broadcast_select_fusion.1
  119.4 0.2 broadcast_select_fusion.3
  119.7 1.0 copy-done.4
  120.7 4.4 %weight_products.1 = bf16[2560,512]{1,0:T(8,128)(2,1)S(1)} custom-call(bf16[4,128,2560]{2,1,0:T(8,128)(2,1)} %copy-done.4, bf16[4,128,2560]{2,1,0:T(8,128)(2,1)} %get-tuple-element.51.grads_ref, bf16[512,256]{1,0:T(8,128)(2,1)S(1)} %pad_maximum_fusion.3.lats_ref, bf16[512,256]{1,0:T(8,128)(2,1)S(1)} %bitcast.97), custom_call_target="tpu_custom_call" | custom-call | flops 4294967296 | bytes 8388608 | tf_op jit(solution)/shard_map/cond/branch_1_fun/weight_products/pallas_call | solution.py:241
  125.1 62.8 %all_to_all.13.moved_ref = bf16[16,160,512]{2,1,0:T(8,128)(2,1)S(1)} all-to-all(bf16[16,160,512]{2,1,0:T(8,128)(2,1)S(1)} %bitcast.96), channel_id=1, replica_groups=mesh['section'=32,'dp'=16] {'dp'}, dimensions={0} | all-to-all | bytes 5242880 | tf_op jit(solution)/shard_map/cond/branch_1_fun/all_to_all | solution.py:375
  188.0 0.3 sum_partials.3
  188.3 1.0 finish.1
  (55 shorter events, 0.7 us)
Async XLA Ops:
  0.6 0.9 copy-start.8
  0.6 0.9 copy-start.9
  1.6 59.9 %copy-start = (bf16[1,128,2560]{2,1,0:T(8,128)(2,1)S(1)}, bf16[1,128,2560]{2,1,0:T(8,128)(2,1)}, u32[]{:S(2)}) copy-start(bf16[1,128,2560]{2,1,0:T(8,128)(2,1)} %param.9) | copy-start | bytes 1966084
  2.3 11.2 %collective-permute-start = (bf16[2,160,256]{2,1,0:T(8,128)(2,1)}, bf16[2,160,256]{2,1,0:T(8,128)(2,1)}, u32[]{:S(2)}, u32[]{:S(2)}) collective-permute-start(bf16[2,160,256]{2,1,0:T(8,128)(2,1)} %pad_maximum_fusion.2), channel_id=1, source_target_pairs={{0,1},{1,0},{2,3},{3,2},{4,5},{5,4},{6,7},{7,6},{8,9},{9,8},{10,11... | collective-permute-start | bytes 491528 | tf_op jit(solution)/shard_map/cond/branch_1_fun/ppermute | solution.py:31
  14.5 17.2 %collective-permute-start.1 = (bf16[2,2,160,256]{3,2,1,0:T(8,128)(2,1)S(1)}, bf16[2,2,160,256]{3,2,1,0:T(8,128)(2,1)S(1)}, u32[]{:S(2)}, u32[]{:S(2)}) collective-permute-start(bf16[2,2,160,256]{3,2,1,0:T(8,128)(2,1)S(1)} %pad_maximum_fusion.1), channel_id=1, source_target_pairs={{0,2},{1,3},{2,4},{3,5},{4,6},{5,7},{6,8},{7,9},{8,10},{9,11},{10,... | collective-permute-start | bytes 983048 | tf_op jit(solution)/shard_map/cond/branch_1_fun/ppermute | solution.py:27
  18.5 15.1 %collective-permute-start.2 = (bf16[2,2,160,256]{3,2,1,0:T(8,128)(2,1)S(1)}, bf16[2,2,160,256]{3,2,1,0:T(8,128)(2,1)S(1)}, u32[]{:S(2)}, u32[]{:S(2)}) collective-permute-start(bf16[2,2,160,256]{3,2,1,0:T(8,128)(2,1)S(1)} %pad_maximum_fusion.1), channel_id=1, source_target_pairs={{0,14},{1,15},{2,0},{3,1},{4,2},{5,3},{6,4},{7,5},{8,6},{9,7},{10,... | collective-permute-start | bytes 983048 | tf_op jit(solution)/shard_map/cond/branch_1_fun/ppermute | solution.py:27
  27.1 6.5 %copy-start.5 = (bf16[2,8,2,160,256]{4,3,2,1,0:T(8,128)(2,1)S(1)}, bf16[2,8,2,160,256]{4,3,2,1,0:T(8,128)(2,1)}, u32[]{:S(2)}) copy-start(bf16[2,8,2,160,256]{4,3,2,1,0:T(8,128)(2,1)} %unset.4) | copy-start | bytes 7864324 | tf_op jit(solution)/shard_map/cond
  31.6 10.2 %collective-permute-start.3 = (bf16[2,2,160,256]{3,2,1,0:T(8,128)(2,1)S(1)}, bf16[2,2,160,256]{3,2,1,0:T(8,128)(2,1)S(1)}, u32[]{:S(2)}, u32[]{:S(2)}) collective-permute-start(bf16[2,2,160,256]{3,2,1,0:T(8,128)(2,1)S(1)} %collective-permute-done.1), channel_id=1, source_target_pairs={{0,2},{1,3},{2,4},{3,5},{4,6},{5,7},{6,8},{7,9},{8,10},{9,11},{10,... | collective-permute-start | bytes 983048 | tf_op jit(solution)/shard_map/cond/branch_1_fun/ppermute | solution.py:27
  33.6 10.1 %collective-permute-start.4 = (bf16[2,2,160,256]{3,2,1,0:T(8,128)(2,1)S(1)}, bf16[2,2,160,256]{3,2,1,0:T(8,128)(2,1)S(1)}, u32[]{:S(2)}, u32[]{:S(2)}) collective-permute-start(bf16[2,2,160,256]{3,2,1,0:T(8,128)(2,1)S(1)} %collective-permute-done.2), channel_id=1, source_target_pairs={{0,14},{1,15},{2,0},{3,1},{4,2},{5,3},{6,4},{7,5},{8,6},{9,7},{10,... | collective-permute-start | bytes 983048 | tf_op jit(solution)/shard_map/cond/branch_1_fun/ppermute | solution.py:27
  41.8 9.0 %collective-permute-start.5 = (bf16[2,2,160,256]{3,2,1,0:T(8,128)(2,1)S(1)}, bf16[2,2,160,256]{3,2,1,0:T(8,128)(2,1)S(1)}, u32[]{:S(2)}, u32[]{:S(2)}) collective-permute-start(bf16[2,2,160,256]{3,2,1,0:T(8,128)(2,1)S(1)} %collective-permute-done.3), channel_id=1, source_target_pairs={{0,2},{1,3},{2,4},{3,5},{4,6},{5,7},{6,8},{7,9},{8,10},{9,11},{10,... | collective-permute-start | bytes 983048 | tf_op jit(solution)/shard_map/cond/branch_1_fun/ppermute | solution.py:27
  43.8 16.1 %collective-permute-start.7 = (bf16[2,2,160,256]{3,2,1,0:T(8,128)(2,1)S(1)}, bf16[2,2,160,256]{3,2,1,0:T(8,128)(2,1)S(1)}, u32[]{:S(2)}, u32[]{:S(2)}) collective-permute-start(bf16[2,2,160,256]{3,2,1,0:T(8,128)(2,1)S(1)} %collective-permute-done.4), channel_id=1, source_target_pairs={{0,14},{1,15},{2,0},{3,1},{4,2},{5,3},{6,4},{7,5},{8,6},{9,7},{10,... | collective-permute-start | bytes 983048 | tf_op jit(solution)/shard_map/cond/branch_1_fun/ppermute | solution.py:27
  50.8 9.0 %collective-permute-start.6 = (bf16[2,2,160,256]{3,2,1,0:T(8,128)(2,1)S(1)}, bf16[2,2,160,256]{3,2,1,0:T(8,128)(2,1)S(1)}, u32[]{:S(2)}, u32[]{:S(2)}) collective-permute-start(bf16[2,2,160,256]{3,2,1,0:T(8,128)(2,1)S(1)} %collective-permute-done.5), channel_id=1, source_target_pairs={{0,2},{1,3},{2,4},{3,5},{4,6},{5,7},{6,8},{7,9},{8,10},{9,11},{10,... | collective-permute-start | bytes 983048 | tf_op jit(solution)/shard_map/cond/branch_1_fun/ppermute | solution.py:27
  59.9 1.5 copy-start.6
  61.4 11.5 %copy-start.10 = (f32[4,128,128]{2,1,0:T(8,128)}, f32[4,128,128]{2,1,0:T(8,128)S(1)}, u32[]{:S(2)}) copy-start(f32[4,128,128]{2,1,0:T(8,128)S(1)} %get-tuple-element.94.inverse_ref) | copy-start | bytes 786436
  61.5 11.4 %copy-start.3 = (bf16[4,128,2560]{2,1,0:T(8,128)(2,1)S(1)}, bf16[4,128,2560]{2,1,0:T(8,128)(2,1)}, u32[]{:S(2)}) copy-start(bf16[4,128,2560]{2,1,0:T(8,128)(2,1)} %get-tuple-element.93.normed_ref) | copy-start | bytes 7864324
  61.5 11.4 %copy-start.7 = (bf16[2,2560,256]{2,1,0:T(8,128)(2,1)S(1)}, bf16[2,2560,256]{2,1,0:T(8,128)(2,1)}, u32[]{:S(2)}) copy-start(bf16[2,2560,256]{2,1,0:T(8,128)(2,1)} %get-tuple-element.95.maps_ref) | copy-start | bytes 7864324
  65.6 14.0 %collective-permute-start.8 = (bf16[64,2560]{1,0:T(8,128)(2,1)S(1)}, bf16[64,2560]{1,0:T(8,128)(2,1)S(1)}, u32[]{:S(2)}, u32[]{:S(2)}) collective-permute-start(bf16[64,2560]{1,0:T(8,128)(2,1)S(1)} %get-tuple-element.99), channel_id=1, source_target_pairs={{0,496},{16,0},{32,16},{48,32},{64,48},{80,64},{96,80},{112,96},{1... | collective-permute-start | bytes 983048 | tf_op jit(solution)/shard_map/ppermute | solution.py:359
  74.6 12.3 %collective-permute-start.9 = (bf16[64,2560]{1,0:T(8,128)(2,1)S(1)}, bf16[64,2560]{1,0:T(8,128)(2,1)S(1)}, u32[]{:S(2)}, u32[]{:S(2)}) collective-permute-start(bf16[64,2560]{1,0:T(8,128)(2,1)S(1)} %get-tuple-element.104), channel_id=1, source_target_pairs={{0,496},{16,0},{32,16},{48,32},{64,48},{80,64},{96,80},{112,96},{1... | collective-permute-start | bytes 983048 | tf_op jit(solution)/shard_map/ppermute | solution.py:359
  77.9 1.7 copy-start.11
  80.9 12.3 %collective-permute-start.10 = (bf16[64,2560]{1,0:T(8,128)(2,1)S(1)}, bf16[64,2560]{1,0:T(8,128)(2,1)S(1)}, u32[]{:S(2)}, u32[]{:S(2)}) collective-permute-start(bf16[64,2560]{1,0:T(8,128)(2,1)S(1)} %get-tuple-element.107), channel_id=1, source_target_pairs={{0,496},{16,0},{32,16},{48,32},{64,48},{80,64},{96,80},{112,96},{1... | collective-permute-start | bytes 983048 | tf_op jit(solution)/shard_map/ppermute | solution.py:368
  88.2 12.3 %collective-permute-start.11 = (bf16[64,2560]{1,0:T(8,128)(2,1)S(1)}, bf16[64,2560]{1,0:T(8,128)(2,1)S(1)}, u32[]{:S(2)}, u32[]{:S(2)}) collective-permute-start(bf16[64,2560]{1,0:T(8,128)(2,1)S(1)} %get-tuple-element.110), channel_id=1, source_target_pairs={{0,496},{16,0},{32,16},{48,32},{64,48},{80,64},{96,80},{112,96},{1... | collective-permute-start | bytes 983048 | tf_op jit(solution)/shard_map/ppermute | solution.py:368
  94.4 12.3 %collective-permute-start.12 = (bf16[64,2560]{1,0:T(8,128)(2,1)S(1)}, bf16[64,2560]{1,0:T(8,128)(2,1)S(1)}, u32[]{:S(2)}, u32[]{:S(2)}) collective-permute-start(bf16[64,2560]{1,0:T(8,128)(2,1)S(1)} %get-tuple-element.113), channel_id=1, source_target_pairs={{0,496},{16,0},{32,16},{48,32},{64,48},{80,64},{96,80},{112,96},{1... | collective-permute-start | bytes 983048 | tf_op jit(solution)/shard_map/ppermute | solution.py:368
  101.7 12.3 %collective-permute-start.13 = (bf16[64,2560]{1,0:T(8,128)(2,1)S(1)}, bf16[64,2560]{1,0:T(8,128)(2,1)S(1)}, u32[]{:S(2)}, u32[]{:S(2)}) collective-permute-start(bf16[64,2560]{1,0:T(8,128)(2,1)S(1)} %get-tuple-element.116), channel_id=1, source_target_pairs={{0,496},{16,0},{32,16},{48,32},{64,48},{80,64},{96,80},{112,96},{1... | collective-permute-start | bytes 983048 | tf_op jit(solution)/shard_map/ppermute | solution.py:368
  108.0 6.1 %copy-start.1 = (bf16[4,128,2560]{2,1,0:T(8,128)(2,1)}, bf16[4,128,2560]{2,1,0:T(8,128)(2,1)S(1)}, u32[]{:S(2)}) copy-start(bf16[4,128,2560]{2,1,0:T(8,128)(2,1)S(1)} %get-tuple-element.117.refs_2_) | copy-start | bytes 7864324
  115.3 73.0 %collective-permute-start.15 = (bf16[64,2560]{1,0:T(8,128)(2,1)S(1)}, bf16[64,2560]{1,0:T(8,128)(2,1)S(1)}, u32[]{:S(2)}, u32[]{:S(2)}) collective-permute-start(bf16[64,2560]{1,0:T(8,128)(2,1)S(1)} %get-tuple-element.124), channel_id=1, source_target_pairs={{0,496},{16,0},{32,16},{48,32},{64,48},{80,64},{96,80},{112,96},{1... | collective-permute-start | bytes 983048 | tf_op jit(solution)/shard_map/ppermute | solution.py:368
  117.2 71.1 %collective-permute-start.14 = (bf16[64,2560]{1,0:T(8,128)(2,1)S(1)}, bf16[64,2560]{1,0:T(8,128)(2,1)S(1)}, u32[]{:S(2)}, u32[]{:S(2)}) collective-permute-start(bf16[64,2560]{1,0:T(8,128)(2,1)S(1)} %get-tuple-element.123), channel_id=1, source_target_pairs={{0,496},{16,0},{32,16},{48,32},{64,48},{80,64},{96,80},{112,96},{1... | collective-permute-start | bytes 983048 | tf_op jit(solution)/shard_map/ppermute | solution.py:368
  119.2 1.5 copy-start.4

commit v16 on v12

--- a/solution.py
+++ b/solution.py
@@ -277,27 +277,25 @@
     )(moved)
 
 
-def finish_kernel(total_ref, low_ref, high_ref, grad_ref, down_ref, up_ref):
-    rows, rank = low_ref.shape[0], down_ref.shape[3]
-    grad_ref[0, :rows] = low_ref[...]
-    grad_ref[0, rows:] = high_ref[...]
+def finish_kernel(total_ref, relayed_ref, grad_ref, down_ref, up_ref):
+    rank = down_ref.shape[3]
+    grad_ref[0] = relayed_ref[...]
     for i, out in enumerate((down_ref, up_ref)):
         for j, level in enumerate((1, 0)):
             at = (2 * i + j) * rank
             out[level, 0] = total_ref[:, at : at + rank]
 
 
-def finish(total, low, high, share, rank):
-    rows, width = low.shape
+def finish(total, relayed, share, rank):
     made = jax.ShapeDtypeStruct((2, 1, share, rank), F32)
     return pl.pallas_call(
         finish_kernel,
-        out_shape=[jax.ShapeDtypeStruct((1, 2 * rows, width), low.dtype), made, made],
-        in_specs=[IN_VMEM] * 3,
+        out_shape=[jax.ShapeDtypeStruct((1,) + relayed.shape, relayed.dtype), made, made],
+        in_specs=[IN_VMEM] * 2,
         out_specs=[IN_VMEM] * 3,
         compiler_params=LIMIT,
         name="finish",
-    )(total, low, high)
+    )(total, relayed)
 
 
 def on_device(saved_inputs, grad_in, adapter_down, adapter_up):
@@ -350,7 +348,8 @@
                 tick, part, level_stack, arrived[part], normed, inverse, maps, [latents, slopes], stack
             )
             grad_latents.append(grad_latent)
-            moving.append(lax.ppermute(sent, "section", down_one))
+            moving.append(sent if tick == ticks - 1 else lax.ppermute(sent, "section", down_one))
+    relayed = lax.ppermute(jnp.concatenate(moving), "section", down_one)
 
     normed_all = normed.reshape(-1, width)
     grads_all = stack.reshape(-1, width)
@@ -380,7 +379,7 @@
         return summed_parts(kernel_products(normed, stack, split(lats), split(acts)))
 
     total = lax.cond(two_layers, reduce_two, reduce_one, jnp.concatenate(grad_latents).reshape(actives.shape), actives)
-    grad_out, down_grad, up_grad = finish(total, *moving, share, rank)
+    grad_out, down_grad, up_grad = finish(total, relayed, share, rank)
     return grad_out, jnp.swapaxes(down_grad, 2, 3), jnp.swapaxes(up_grad, 2, 3)
 
 

time: 189 us -> 193 us (1.021)
  blocking collectives: 62.9 us -> 67 us
  starting transfers between devices: 54 us -> 52 us
    ppermute x0 -> x5, waiting for transfers between devices: none -> 16.3 us  [the longest x4 16.3 us: on_device(): lax.ppermute(sent, 'section', down_one)]
    ppermute x8 -> x2, waiting for transfers between devices: 20.4 us -> 4.15 us  [on_device(): moving.append(lax.ppermute(sent, 'section', down_one))]
    ppermute x8 -> x2, starting transfers between devices: 22.1 us -> 10.5 us  [on_device(): moving.append(lax.ppermute(sent, 'section', down_one))]
    ppermute x0 -> x5, starting transfers between devices: none -> 9.59 us  [the longest x4 7.69 us: on_device(): lax.ppermute(sent, 'section', down_one)]
    all_to_all x1, blocking collectives: 62.9 us -> 67 us  [summed_parts(): lax.all_to_all(parts.reshape(n_dp, share, -1), 'dp', 0, 0, tiled=True)]
  transfers between devices with their start and end apart: 16 -> 15, of which waited for: 9 -> 9; matrix products, arithmetic and copies ran while one was open for 0% -> 0% of each run, Pallas kernels for 10% -> 10%
where the time goes in v16:
time: 193 us; the launch traced here: 192 us
  blocking collectives  67 us (35%)
  starting transfers between devices  52 us (27%)
  waiting for transfers between devices  40.1 us (21%)
  Pallas kernels  25 us (13%)
  local copies, waits for them, and re-layouts  3.73 us (2%)
  other arithmetic  3.05 us (2%)
    all_to_all x1, blocking collectives, summed_parts(): lax.all_to_all(parts.reshape(n_dp, share, -1), 'dp', 0, 0, tiled=True)  67 us
    ppermute x7, starting transfers between devices, shifted(): return lax.ppermute(value, 'dp', dp_pairs(n_z, step, 0))  27.5 us
    ppermute x4, waiting for transfers between devices, on_device(): lax.ppermute(sent, 'section', down_one)  16.3 us
    ppermute x7, waiting for transfers between devices, shifted(): return lax.ppermute(value, 'dp', dp_pairs(n_z, step, 0))  13.1 us
    pallas_call x8, Pallas kernels, tick_layer(): pl.pallas_call(functools.partial(tick_kernel, tick, part), grid_spec=pltp...  11.8 us
    ppermute x2, starting transfers between devices, on_device(): moving.append(lax.ppermute(sent, 'section', down_one))  10.5 us
    ppermute x4, starting transfers between devices, on_device(): lax.ppermute(sent, 'section', down_one)  7.69 us
    ppermute x1, waiting for transfers between devices, swapped(): return lax.ppermute(value, 'dp', dp_pairs(n_z, 0, 1))  6.54 us
  transfers between devices with their start and end apart: 15, of which 9 were waited for; matrix products, arithmetic and copies ran while one was open for 0% of the time, Pallas kernels for 10%

profile of v16, /device:TPU:63, one launch (start us, length us, event | category | flops | bytes accessed | tf_op | source)
XLA Modules:
  0.0 192.2 jit_solution(18133864952531527692)
XLA Ops:
  0.7 0.8 copy-done.6
  1.6 59.9 %conditional.2 = (bf16[2,2560,256]{2,1,0:T(8,128)(2,1)}, bf16[4,128,2560]{2,1,0:T(8,128)(2,1)}, f32[4,128,128]{2,1,0:T(8,128)S(1)}) conditional(s32[]{:T(128)} %convert_element_type.10, (bf16[2,128,160]{1,2,0:T(8,128)(2,1)S(1)}, bf16[2,128,160]{1,2,0:T(8,128)(2,1)S(1)}, bf16[4,1,128,2560]{3,2,1,0:T(8,128)(2,1)}) %tuple.45, ...), branch_computations={%region_0.1_spmd, %region_1.2_spmd} | conditional | flops 4296441856 | bytes 46729012 | solution.py:328
  1.6 0.7 pad_maximum_fusion.2
  2.3 4.4 %collective-permute-start = (bf16[2,160,256]{2,1,0:T(8,128)(2,1)}, bf16[2,160,256]{2,1,0:T(8,128)(2,1)}, u32[]{:S(2)}, u32[]{:S(2)}) collective-permute-start(bf16[2,160,256]{2,1,0:T(8,128)(2,1)} %pad_maximum_fusion.2), channel_id=1, source_target_pairs={{0,1},{1,0},{2,3},{3,2},{4,5},{5,4},{6,7},{7,6},{8,9},{9,8},{10,11... | collective-permute-start | bytes 491528 | tf_op jit(solution)/shard_map/cond/branch_1_fun/ppermute | solution.py:31
  6.9 6.5 %collective-permute-done = bf16[2,160,256]{2,1,0:T(8,128)(2,1)} collective-permute-done((bf16[2,160,256]{2,1,0:T(8,128)(2,1)}, bf16[2,160,256]{2,1,0:T(8,128)(2,1)}, u32[]{:S(2)}, u32[]{:S(2)}) %collective-permute-start) | collective-permute-done | bytes 163872 | tf_op jit(solution)/shard_map/cond/branch_1_fun/ppermute | solution.py:31
  13.5 0.9 select_bitcast_fusion.1
  14.5 4.0 %collective-permute-start.1 = (bf16[2,2,160,256]{3,2,1,0:T(8,128)(2,1)S(1)}, bf16[2,2,160,256]{3,2,1,0:T(8,128)(2,1)S(1)}, u32[]{:S(2)}, u32[]{:S(2)}) collective-permute-start(bf16[2,2,160,256]{3,2,1,0:T(8,128)(2,1)S(1)} %pad_maximum_fusion.1), channel_id=1, source_target_pairs={{0,2},{1,3},{2,4},{3,5},{4,6},{5,7},{6,8},{7,9},{8,10},{9,11},{10,... | collective-permute-start | bytes 983048 | tf_op jit(solution)/shard_map/cond/branch_1_fun/ppermute | solution.py:27
  18.5 8.6 %collective-permute-start.2 = (bf16[2,2,160,256]{3,2,1,0:T(8,128)(2,1)S(1)}, bf16[2,2,160,256]{3,2,1,0:T(8,128)(2,1)S(1)}, u32[]{:S(2)}, u32[]{:S(2)}) collective-permute-start(bf16[2,2,160,256]{3,2,1,0:T(8,128)(2,1)S(1)} %pad_maximum_fusion.1), channel_id=1, source_target_pairs={{0,14},{1,15},{2,0},{3,1},{4,2},{5,3},{6,4},{7,5},{8,6},{9,7},{10,... | collective-permute-start | bytes 983048 | tf_op jit(solution)/shard_map/cond/branch_1_fun/ppermute | solution.py:27
  27.1 4.6 %norms.3 = (bf16[4,128,2560]{2,1,0:T(8,128)(2,1)}, f32[4,128,128]{2,1,0:T(8,128)S(1)}) custom-call(bf16[4,1,128,2560]{3,2,1,0:T(8,128)(2,1)} %get-tuple-element.43.x_ref), custom_call_target="tpu_custom_call" | custom-call | flops 4294967296 | bytes 8388608 | tf_op jit(solution)/shard_map/cond/branch_1_fun/norms/pallas_call | solution.py:78
  31.7 1.9 collective-permute-start.3
  33.6 4.6 %collective-permute-start.4 = (bf16[2,2,160,256]{3,2,1,0:T(8,128)(2,1)S(1)}, bf16[2,2,160,256]{3,2,1,0:T(8,128)(2,1)S(1)}, u32[]{:S(2)}, u32[]{:S(2)}) collective-permute-start(bf16[2,2,160,256]{3,2,1,0:T(8,128)(2,1)S(1)} %collective-permute-done.2), channel_id=1, source_target_pairs={{0,14},{1,15},{2,0},{3,1},{4,2},{5,3},{6,4},{7,5},{8,6},{9,7},{10,... | collective-permute-start | bytes 983048 | tf_op jit(solution)/shard_map/cond/branch_1_fun/ppermute | solution.py:27
  38.3 3.6 %collective-permute-done.3 = bf16[2,2,160,256]{3,2,1,0:T(8,128)(2,1)S(1)} collective-permute-done((bf16[2,2,160,256]{3,2,1,0:T(8,128)(2,1)S(1)}, bf16[2,2,160,256]{3,2,1,0:T(8,128)(2,1)S(1)}, u32[]{:S(2)}, u32[]{:S(2)}) %collective-permute-start.3) | collective-permute-done | bytes 327712 | tf_op jit(solution)/shard_map/cond/branch_1_fun/ppermute | solution.py:27
  41.8 1.9 collective-permute-start.5
  43.8 4.6 %collective-permute-start.7 = (bf16[2,2,160,256]{3,2,1,0:T(8,128)(2,1)S(1)}, bf16[2,2,160,256]{3,2,1,0:T(8,128)(2,1)S(1)}, u32[]{:S(2)}, u32[]{:S(2)}) collective-permute-start(bf16[2,2,160,256]{3,2,1,0:T(8,128)(2,1)S(1)} %collective-permute-done.4), channel_id=1, source_target_pairs={{0,14},{1,15},{2,0},{3,1},{4,2},{5,3},{6,4},{7,5},{8,6},{9,7},{10,... | collective-permute-start | bytes 983048 | tf_op jit(solution)/shard_map/cond/branch_1_fun/ppermute | solution.py:27
  48.4 2.4 %collective-permute-done.5 = bf16[2,2,160,256]{3,2,1,0:T(8,128)(2,1)S(1)} collective-permute-done((bf16[2,2,160,256]{3,2,1,0:T(8,128)(2,1)S(1)}, bf16[2,2,160,256]{3,2,1,0:T(8,128)(2,1)S(1)}, u32[]{:S(2)}, u32[]{:S(2)}) %collective-permute-start.5) | collective-permute-done | bytes 327712 | tf_op jit(solution)/shard_map/cond/branch_1_fun/ppermute | solution.py:27
  50.8 1.9 collective-permute-start.6
  52.8 7.0 %collective-permute-done.6 = bf16[2,2,160,256]{3,2,1,0:T(8,128)(2,1)S(1)} collective-permute-done((bf16[2,2,160,256]{3,2,1,0:T(8,128)(2,1)S(1)}, bf16[2,2,160,256]{3,2,1,0:T(8,128)(2,1)S(1)}, u32[]{:S(2)}, u32[]{:S(2)}) %collective-permute-start.6) | collective-permute-done | bytes 327712 | tf_op jit(solution)/shard_map/cond/branch_1_fun/ppermute | solution.py:27
  60.0 1.5 copy-done.4
  61.5 3.0 %tick_layer.8 = (bf16[4,128,2560]{2,1,0:T(8,128)(2,1)S(1)}, bf16[64,2560]{1,0:T(8,128)(2,1)S(1)}, bf16[64,128]{1,0:T(8,128)(2,1)S(1)}, bf16[64,128]{1,0:T(8,128)(2,1)S(1)}) custom-call(s32[4]{0:T(128)S(1)} %pad_add_fusion.levels_ref, bf16[128,2560]{1,0:T(8,128)(2,1)S(1)} %bitcast.98, ...), custom_call_target="tpu_custom_call", output_to_operand_aliasing={{0}: (5, {})} | custom-call | flops 4294967296 | bytes 8388608 | tf_op jit(solution)/shard_map/tick_layer/pallas_call | solution.py:182
  64.6 7.3 %collective-permute-start.8 = (bf16[64,2560]{1,0:T(8,128)(2,1)S(1)}, bf16[64,2560]{1,0:T(8,128)(2,1)S(1)}, u32[]{:S(2)}, u32[]{:S(2)}) collective-permute-start(bf16[64,2560]{1,0:T(8,128)(2,1)S(1)} %get-tuple-element.99), channel_id=1, source_target_pairs={{0,496},{16,0},{32,16},{48,32},{64,48},{80,64},{96,80},{112,96},{1... | collective-permute-start | bytes 983048 | tf_op jit(solution)/shard_map/ppermute | solution.py:342
  71.9 1.3 tick_layer.9
  73.2 3.3 %collective-permute-start.9 = (bf16[64,2560]{1,0:T(8,128)(2,1)S(1)}, bf16[64,2560]{1,0:T(8,128)(2,1)S(1)}, u32[]{:S(2)}, u32[]{:S(2)}) collective-permute-start(bf16[64,2560]{1,0:T(8,128)(2,1)S(1)} %get-tuple-element.104), channel_id=1, source_target_pairs={{0,496},{16,0},{32,16},{48,32},{64,48},{80,64},{96,80},{112,96},{1... | collective-permute-start | bytes 983048 | tf_op jit(solution)/shard_map/ppermute | solution.py:342
  76.5 1.6 forward_rest.1
  78.2 1.2 tick_layer.10
  79.4 1.9 %collective-permute-start.10 = (bf16[64,2560]{1,0:T(8,128)(2,1)S(1)}, bf16[64,2560]{1,0:T(8,128)(2,1)S(1)}, u32[]{:S(2)}, u32[]{:S(2)}) collective-permute-start(bf16[64,2560]{1,0:T(8,128)(2,1)S(1)} %get-tuple-element.107), channel_id=1, source_target_pairs={{0,496},{16,0},{32,16},{48,32},{64,48},{80,64},{96,80},{112,96},{1... | collective-permute-start | bytes 983048 | tf_op jit(solution)/shard_map/ppermute | solution.py:351
  81.4 4.2 %collective-permute-done.9.incoming_ref = bf16[64,2560]{1,0:T(8,128)(2,1)S(1)} collective-permute-done((bf16[64,2560]{1,0:T(8,128)(2,1)S(1)}, bf16[64,2560]{1,0:T(8,128)(2,1)S(1)}, u32[]{:S(2)}, u32[]{:S(2)}) %collective-permute-start.9) | collective-permute-done | bytes 327712 | tf_op jit(solution)/shard_map/ppermute | solution.py:342
  85.5 1.2 tick_layer.11
  86.8 1.9 collective-permute-start.11
  88.7 3.0 %collective-permute-done.10.incoming_ref = bf16[64,2560]{1,0:T(8,128)(2,1)S(1)} collective-permute-done((bf16[64,2560]{1,0:T(8,128)(2,1)S(1)}, bf16[64,2560]{1,0:T(8,128)(2,1)S(1)}, u32[]{:S(2)}, u32[]{:S(2)}) %collective-permute-start.10) | collective-permute-done | bytes 327712 | tf_op jit(solution)/shard_map/ppermute | solution.py:351
  91.7 1.2 tick_layer.12
  93.0 1.9 collective-permute-start.12
  94.9 4.2 %collective-permute-done.11.incoming_ref = bf16[64,2560]{1,0:T(8,128)(2,1)S(1)} collective-permute-done((bf16[64,2560]{1,0:T(8,128)(2,1)S(1)}, bf16[64,2560]{1,0:T(8,128)(2,1)S(1)}, u32[]{:S(2)}, u32[]{:S(2)}) %collective-permute-start.11) | collective-permute-done | bytes 327712 | tf_op jit(solution)/shard_map/ppermute | solution.py:351
  99.1 1.2 tick_layer.13
  100.3 1.9 collective-permute-start.13
  102.3 3.0 %collective-permute-done.12.incoming_ref = bf16[64,2560]{1,0:T(8,128)(2,1)S(1)} collective-permute-done((bf16[64,2560]{1,0:T(8,128)(2,1)S(1)}, bf16[64,2560]{1,0:T(8,128)(2,1)S(1)}, u32[]{:S(2)}, u32[]{:S(2)}) %collective-permute-start.12) | collective-permute-done | bytes 327712 | tf_op jit(solution)/shard_map/ppermute | solution.py:351
  105.3 1.2 tick_layer.14
  106.5 6.1 %collective-permute-done.13.incoming_ref = bf16[64,2560]{1,0:T(8,128)(2,1)S(1)} collective-permute-done((bf16[64,2560]{1,0:T(8,128)(2,1)S(1)}, bf16[64,2560]{1,0:T(8,128)(2,1)S(1)}, u32[]{:S(2)}, u32[]{:S(2)}) %collective-permute-start.13) | collective-permute-done | bytes 327712 | tf_op jit(solution)/shard_map/ppermute | solution.py:351
  112.6 1.2 tick_layer.15
  113.9 0.9 pad_maximum_fusion.5
  114.8 1.9 collective-permute-start.14
  116.7 73.5 %conditional.3 = (f32[160,512]{1,0:T(8,128)}) conditional(s32[]{:T(128)} %convert_element_type.10, (bf16[4,128,2560]{2,1,0:T(8,128)(2,1)S(1)}, bf16[512,128]{1,0:T(8,128)(2,1)S(1)}, bf16[4,128,2560]{2,1,0:T(8,128)(2,1)S(1)}, bf16[4,128,128]{2,1,0:T(8,128)(2,1)S(1)}) %tuple.41, (s32[4]{0:T(128)S(1)}, bf16[512,128]{1,0:T(8,128)(2,1)S(1)}, ...), branch_computations={%region_2.3_spmd, %region_3.4_spmd} | conditional | flops 4296278016 | bytes 25954380 | solution.py:381
  116.9 0.1 broadcast_select_fusion.1
  117.0 0.2 broadcast_select_fusion.3
  117.3 1.0 copy-done.2
  118.3 4.0 %weight_products.1 = bf16[2560,512]{1,0:T(8,128)(2,1)S(1)} custom-call(bf16[4,128,2560]{2,1,0:T(8,128)(2,1)} %copy-done.2, bf16[4,128,2560]{2,1,0:T(8,128)(2,1)S(1)} %get-tuple-element.51.grads_ref, bf16[512,256]{1,0:T(8,128)(2,1)S(1)} %pad_maximum_fusion.3.lats_ref, bf16[512,256]{1,0:T(8,128)(2,1)S(1)} %bitcast.97), custom_call_target="tpu_custom_call" | custom-call | flops 4294967296 | bytes 8388608 | tf_op jit(solution)/shard_map/cond/branch_1_fun/weight_products/pallas_call | solution.py:226
  122.2 67.0 %all_to_all.13.moved_ref = bf16[16,160,512]{2,1,0:T(8,128)(2,1)S(1)} all-to-all(bf16[16,160,512]{2,1,0:T(8,128)(2,1)S(1)} %bitcast.96), channel_id=1, replica_groups=mesh['section'=32,'dp'=16] {'dp'}, dimensions={0} | all-to-all | bytes 5242880 | tf_op jit(solution)/shard_map/cond/branch_1_fun/all_to_all | solution.py:359
  189.2 1.0 sum_partials.3
  190.3 2.0 %finish.1 = (bf16[1,128,2560]{2,1,0:T(8,128)(2,1)}, f32[2,1,160,128]{3,2,1,0:T(8,128)}, f32[2,1,160,128]{3,2,1,0:T(8,128)}) custom-call(f32[160,512]{1,0:T(8,128)} %get-tuple-element.156.total_ref, bf16[128,2560]{1,0:T(8,128)(2,1)S(1)} %collective-permute-done.14.relayed_ref), custom_call_target="tpu_custom_call" | custom-call | tf_op jit(solution)/shard_map/finish/pallas_call | solution.py:291
  (52 shorter events, 0.7 us)
Async XLA Ops:
  0.6 0.9 copy-start.6
  0.6 0.9 copy-start.7
  1.6 59.9 %copy-start = (bf16[1,128,2560]{2,1,0:T(8,128)(2,1)S(1)}, bf16[1,128,2560]{2,1,0:T(8,128)(2,1)}, u32[]{:S(2)}) copy-start(bf16[1,128,2560]{2,1,0:T(8,128)(2,1)} %param.9) | copy-start | bytes 1966084
  2.3 11.2 %collective-permute-start = (bf16[2,160,256]{2,1,0:T(8,128)(2,1)}, bf16[2,160,256]{2,1,0:T(8,128)(2,1)}, u32[]{:S(2)}, u32[]{:S(2)}) collective-permute-start(bf16[2,160,256]{2,1,0:T(8,128)(2,1)} %pad_maximum_fusion.2), channel_id=1, source_target_pairs={{0,1},{1,0},{2,3},{3,2},{4,5},{5,4},{6,7},{7,6},{8,9},{9,8},{10,11... | collective-permute-start | bytes 491528 | tf_op jit(solution)/shard_map/cond/branch_1_fun/ppermute | solution.py:31
  14.5 17.2 %collective-permute-start.1 = (bf16[2,2,160,256]{3,2,1,0:T(8,128)(2,1)S(1)}, bf16[2,2,160,256]{3,2,1,0:T(8,128)(2,1)S(1)}, u32[]{:S(2)}, u32[]{:S(2)}) collective-permute-start(bf16[2,2,160,256]{3,2,1,0:T(8,128)(2,1)S(1)} %pad_maximum_fusion.1), channel_id=1, source_target_pairs={{0,2},{1,3},{2,4},{3,5},{4,6},{5,7},{6,8},{7,9},{8,10},{9,11},{10,... | collective-permute-start | bytes 983048 | tf_op jit(solution)/shard_map/cond/branch_1_fun/ppermute | solution.py:27
  18.5 15.2 %collective-permute-start.2 = (bf16[2,2,160,256]{3,2,1,0:T(8,128)(2,1)S(1)}, bf16[2,2,160,256]{3,2,1,0:T(8,128)(2,1)S(1)}, u32[]{:S(2)}, u32[]{:S(2)}) collective-permute-start(bf16[2,2,160,256]{3,2,1,0:T(8,128)(2,1)S(1)} %pad_maximum_fusion.1), channel_id=1, source_target_pairs={{0,14},{1,15},{2,0},{3,1},{4,2},{5,3},{6,4},{7,5},{8,6},{9,7},{10,... | collective-permute-start | bytes 983048 | tf_op jit(solution)/shard_map/cond/branch_1_fun/ppermute | solution.py:27
  27.1 6.5 %copy-start.3 = (bf16[2,8,2,160,256]{4,3,2,1,0:T(8,128)(2,1)S(1)}, bf16[2,8,2,160,256]{4,3,2,1,0:T(8,128)(2,1)}, u32[]{:S(2)}) copy-start(bf16[2,8,2,160,256]{4,3,2,1,0:T(8,128)(2,1)} %unset.4) | copy-start | bytes 7864324 | tf_op jit(solution)/shard_map/cond
  31.7 10.2 %collective-permute-start.3 = (bf16[2,2,160,256]{3,2,1,0:T(8,128)(2,1)S(1)}, bf16[2,2,160,256]{3,2,1,0:T(8,128)(2,1)S(1)}, u32[]{:S(2)}, u32[]{:S(2)}) collective-permute-start(bf16[2,2,160,256]{3,2,1,0:T(8,128)(2,1)S(1)} %collective-permute-done.1), channel_id=1, source_target_pairs={{0,2},{1,3},{2,4},{3,5},{4,6},{5,7},{6,8},{7,9},{8,10},{9,11},{10,... | collective-permute-start | bytes 983048 | tf_op jit(solution)/shard_map/cond/branch_1_fun/ppermute | solution.py:27
  33.6 10.2 %collective-permute-start.4 = (bf16[2,2,160,256]{3,2,1,0:T(8,128)(2,1)S(1)}, bf16[2,2,160,256]{3,2,1,0:T(8,128)(2,1)S(1)}, u32[]{:S(2)}, u32[]{:S(2)}) collective-permute-start(bf16[2,2,160,256]{3,2,1,0:T(8,128)(2,1)S(1)} %collective-permute-done.2), channel_id=1, source_target_pairs={{0,14},{1,15},{2,0},{3,1},{4,2},{5,3},{6,4},{7,5},{8,6},{9,7},{10,... | collective-permute-start | bytes 983048 | tf_op jit(solution)/shard_map/cond/branch_1_fun/ppermute | solution.py:27
  41.8 9.0 %collective-permute-start.5 = (bf16[2,2,160,256]{3,2,1,0:T(8,128)(2,1)S(1)}, bf16[2,2,160,256]{3,2,1,0:T(8,128)(2,1)S(1)}, u32[]{:S(2)}, u32[]{:S(2)}) collective-permute-start(bf16[2,2,160,256]{3,2,1,0:T(8,128)(2,1)S(1)} %collective-permute-done.3), channel_id=1, source_target_pairs={{0,2},{1,3},{2,4},{3,5},{4,6},{5,7},{6,8},{7,9},{8,10},{9,11},{10,... | collective-permute-start | bytes 983048 | tf_op jit(solution)/shard_map/cond/branch_1_fun/ppermute | solution.py:27
  43.8 16.1 %collective-permute-start.7 = (bf16[2,2,160,256]{3,2,1,0:T(8,128)(2,1)S(1)}, bf16[2,2,160,256]{3,2,1,0:T(8,128)(2,1)S(1)}, u32[]{:S(2)}, u32[]{:S(2)}) collective-permute-start(bf16[2,2,160,256]{3,2,1,0:T(8,128)(2,1)S(1)} %collective-permute-done.4), channel_id=1, source_target_pairs={{0,14},{1,15},{2,0},{3,1},{4,2},{5,3},{6,4},{7,5},{8,6},{9,7},{10,... | collective-permute-start | bytes 983048 | tf_op jit(solution)/shard_map/cond/branch_1_fun/ppermute | solution.py:27
  50.8 9.0 %collective-permute-start.6 = (bf16[2,2,160,256]{3,2,1,0:T(8,128)(2,1)S(1)}, bf16[2,2,160,256]{3,2,1,0:T(8,128)(2,1)S(1)}, u32[]{:S(2)}, u32[]{:S(2)}) collective-permute-start(bf16[2,2,160,256]{3,2,1,0:T(8,128)(2,1)S(1)} %collective-permute-done.5), channel_id=1, source_target_pairs={{0,2},{1,3},{2,4},{3,5},{4,6},{5,7},{6,8},{7,9},{8,10},{9,11},{10,... | collective-permute-start | bytes 983048 | tf_op jit(solution)/shard_map/cond/branch_1_fun/ppermute | solution.py:27
  59.9 1.5 copy-start.4
  61.4 10.4 %copy-start.8 = (f32[4,128,128]{2,1,0:T(8,128)}, f32[4,128,128]{2,1,0:T(8,128)S(1)}, u32[]{:S(2)}) copy-start(f32[4,128,128]{2,1,0:T(8,128)S(1)} %get-tuple-element.94.inverse_ref) | copy-start | bytes 786436
  61.5 10.3 %copy-start.1 = (bf16[4,128,2560]{2,1,0:T(8,128)(2,1)S(1)}, bf16[4,128,2560]{2,1,0:T(8,128)(2,1)}, u32[]{:S(2)}) copy-start(bf16[4,128,2560]{2,1,0:T(8,128)(2,1)} %get-tuple-element.93.normed_ref) | copy-start | bytes 7864324
  61.5 10.3 %copy-start.5 = (bf16[2,2560,256]{2,1,0:T(8,128)(2,1)S(1)}, bf16[2,2560,256]{2,1,0:T(8,128)(2,1)}, u32[]{:S(2)}) copy-start(bf16[2,2560,256]{2,1,0:T(8,128)(2,1)} %get-tuple-element.95.maps_ref) | copy-start | bytes 7864324
  64.6 13.6 %collective-permute-start.8 = (bf16[64,2560]{1,0:T(8,128)(2,1)S(1)}, bf16[64,2560]{1,0:T(8,128)(2,1)S(1)}, u32[]{:S(2)}, u32[]{:S(2)}) collective-permute-start(bf16[64,2560]{1,0:T(8,128)(2,1)S(1)} %get-tuple-element.99), channel_id=1, source_target_pairs={{0,496},{16,0},{32,16},{48,32},{64,48},{80,64},{96,80},{112,96},{1... | collective-permute-start | bytes 983048 | tf_op jit(solution)/shard_map/ppermute | solution.py:342
  73.2 12.3 %collective-permute-start.9 = (bf16[64,2560]{1,0:T(8,128)(2,1)S(1)}, bf16[64,2560]{1,0:T(8,128)(2,1)S(1)}, u32[]{:S(2)}, u32[]{:S(2)}) collective-permute-start(bf16[64,2560]{1,0:T(8,128)(2,1)S(1)} %get-tuple-element.104), channel_id=1, source_target_pairs={{0,496},{16,0},{32,16},{48,32},{64,48},{80,64},{96,80},{112,96},{1... | collective-permute-start | bytes 983048 | tf_op jit(solution)/shard_map/ppermute | solution.py:342
  76.5 1.7 copy-start.9
  79.4 12.3 %collective-permute-start.10 = (bf16[64,2560]{1,0:T(8,128)(2,1)S(1)}, bf16[64,2560]{1,0:T(8,128)(2,1)S(1)}, u32[]{:S(2)}, u32[]{:S(2)}) collective-permute-start(bf16[64,2560]{1,0:T(8,128)(2,1)S(1)} %get-tuple-element.107), channel_id=1, source_target_pairs={{0,496},{16,0},{32,16},{48,32},{64,48},{80,64},{96,80},{112,96},{1... | collective-permute-start | bytes 983048 | tf_op jit(solution)/shard_map/ppermute | solution.py:351
  86.8 12.3 %collective-permute-start.11 = (bf16[64,2560]{1,0:T(8,128)(2,1)S(1)}, bf16[64,2560]{1,0:T(8,128)(2,1)S(1)}, u32[]{:S(2)}, u32[]{:S(2)}) collective-permute-start(bf16[64,2560]{1,0:T(8,128)(2,1)S(1)} %get-tuple-element.110), channel_id=1, source_target_pairs={{0,496},{16,0},{32,16},{48,32},{64,48},{80,64},{96,80},{112,96},{1... | collective-permute-start | bytes 983048 | tf_op jit(solution)/shard_map/ppermute | solution.py:351
  93.0 12.3 %collective-permute-start.12 = (bf16[64,2560]{1,0:T(8,128)(2,1)S(1)}, bf16[64,2560]{1,0:T(8,128)(2,1)S(1)}, u32[]{:S(2)}, u32[]{:S(2)}) collective-permute-start(bf16[64,2560]{1,0:T(8,128)(2,1)S(1)} %get-tuple-element.113), channel_id=1, source_target_pairs={{0,496},{16,0},{32,16},{48,32},{64,48},{80,64},{96,80},{112,96},{1... | collective-permute-start | bytes 983048 | tf_op jit(solution)/shard_map/ppermute | solution.py:351
  100.3 12.3 %collective-permute-start.13 = (bf16[64,2560]{1,0:T(8,128)(2,1)S(1)}, bf16[64,2560]{1,0:T(8,128)(2,1)S(1)}, u32[]{:S(2)}, u32[]{:S(2)}) collective-permute-start(bf16[64,2560]{1,0:T(8,128)(2,1)S(1)} %get-tuple-element.116), channel_id=1, source_target_pairs={{0,496},{16,0},{32,16},{48,32},{64,48},{80,64},{96,80},{112,96},{1... | collective-permute-start | bytes 983048 | tf_op jit(solution)/shard_map/ppermute | solution.py:351
  114.8 75.5 %collective-permute-start.14 = (bf16[128,2560]{1,0:T(8,128)(2,1)}, bf16[128,2560]{1,0:T(8,128)(2,1)S(1)}, u32[]{:S(2)}, u32[]{:S(2)}) collective-permute-start(bf16[128,2560]{1,0:T(8,128)(2,1)} %pad_maximum_fusion.5), channel_id=1, source_target_pairs={{0,496},{16,0},{32,16},{48,32},{64,48},{80,64},{96,80},{112,96},{1... | collective-permute-start | bytes 1966088 | tf_op jit(solution)/shard_map/ppermute | solution.py:352
  116.8 1.5 copy-start.2
